TPU v7x, 32 devices: a whole 2x2x4 slice. The times are simulated.
32 devices in a mesh: dp: 8 (over z, x), rep: 4 (over y, core).
Axes of the slice: x: 2, y: 2, z: 4, core: 2. Of those that a mesh axis runs over, the one named last changes fastest.
Arguments:
- tokens: bfloat16 [32, 320, 1024], P(('dp', 'rep')), may hold values from -6 to 6
- cotangent: bfloat16 [32, 320, 1024], P(('dp', 'rep')), may hold values from -6 to 6
- lengths: int32 [32], P(('dp', 'rep')), may hold values from 1 to 320, 7680 in all
- norm_gain: float32 [1024], replicated, may hold values from 0.5 to 1.5
- in_weight: bfloat16 [1024, 4096], replicated, may hold values from -0.1875 to 0.1875
- conv_weight: float32 [4, 2048], replicated, may hold values from -3 to 3
- conv_bias: float32 [2048], replicated, may hold values from -3 to 3
- xproj_weight: bfloat16 [2048, 96], replicated, may hold values from -0.125 to 0.125
- dt_weight: bfloat16 [64, 2048], replicated, may hold values from -0.75 to 0.75
- dt_bias: float32 [2048], replicated, may hold values from -4.5 to -1.5
- decay_log: float32 [16, 2048], replicated, may hold values from 0 to 2.5
- skip_gain: float32 [2048], replicated, may hold values from 0.5 to 1.5
- out_weight: bfloat16 [2048, 1024], replicated, may hold values from -0.25 to 0.25
Outputs:
- mixed: bfloat16 [32, 320, 1024], P(('dp', 'rep'))
- grad_tokens: float32 [32, 320, 1024], P(('dp', 'rep'))
- grad_norm_gain: float32 [1024], replicated
- grad_in_weight: float32 [1024, 4096], replicated
- grad_conv_weight: float32 [4, 2048], replicated
- grad_conv_bias: float32 [2048], replicated
- grad_xproj_weight: float32 [2048, 96], replicated
- grad_dt_weight: float32 [64, 2048], replicated
- grad_dt_bias: float32 [2048], replicated
- grad_decay_log: float32 [16, 2048], replicated
- grad_skip_gain: float32 [2048], replicated
- grad_out_weight: float32 [2048, 1024], replicated
Inputs may be any that keep to these rules, and one draw needn't show every extreme that they name: `lengths`: live length of each slot; the largest is exactly 320.
All inputs are finite; a program needn't handle non-finite values. No bound on the sum of `lengths` on one device may be relied on, other than what follows from the above.
Results may differ from a plain program's by a relative error of at most 0.012.
Values sent between devices are 32-bit elements; how exact they have to be, the bound alone decides.
No kernel may reach another device: no remote copies, remote signals or barrier semaphores. Data moves between devices by JAX's collectives and lax.ppermute only.
A program may use at most 256 MiB of HBM per device.

v0:
```python
import jax
import jax.numpy as jnp
from jax import lax
from jax.sharding import PartitionSpec as P

BLOCK = 64


epsilon = 1e-05


def silu_grad(value):
    sigmoid_val = jax.nn.sigmoid(value)
    return sigmoid_val * (1.0 + value * (1.0 - sigmoid_val))


def combine_pairs(earlier, later):
    return (earlier[0] * later[0], later[0] * earlier[1] + later[1])


def scan_block(carried, delta_blk, inputs_blk, write_blk, read_blk, decay_rates):
    factors = jnp.exp(delta_blk[:, None, :] * decay_rates[None, :, :])
    drives = (delta_blk * inputs_blk)[:, None, :] * write_blk[:, :, None]
    first_row = drives[:1] + factors[:1] * carried[None]
    drives = jnp.concatenate([first_row, drives[1:]], axis=0)
    totals = lax.associative_scan(combine_pairs, (factors, drives), axis=0)[1]
    outputs = jnp.sum(totals * read_blk[:, :, None], axis=1)
    return (totals[-1], outputs)


def blocked_view(members):
    length = members[0].shape[0]
    count = length // BLOCK
    return tuple((member.reshape((count, BLOCK) + member.shape[1:]) for member in members))


def forward_scan(step_size, act_float, write_coef, read_coef, decay_rates):
    length, width = step_size.shape
    blocked = blocked_view((step_size, act_float, write_coef, read_coef))

    def forward_one_block(carried, pieces):
        final_state, outputs = scan_block(
            carried, pieces[0], pieces[1], pieces[2], pieces[3], decay_rates
        )
        return (final_state, (carried, outputs))

    start = jnp.zeros((decay_rates.shape[0], width), jnp.float32)
    ignored, collected = lax.scan(forward_one_block, start, blocked)
    starts, outputs = collected
    return (starts, outputs.reshape(length, width))


def backward_scan(starts, step_size, act_float, write_coef, read_coef, decay_rates, grad_outputs):
    length, width = step_size.shape
    blocked = blocked_view((step_size, act_float, write_coef, read_coef, grad_outputs))

    def backward_one_block(carry, pieces):
        grad_carried, grad_decay = carry
        start_state = pieces[0]
        ignored, pullback = jax.vjp(
            scan_block, start_state, pieces[1], pieces[2], pieces[3], pieces[4], decay_rates
        )
        grads = pullback((grad_carried, pieces[5]))
        return ((grads[0], grad_decay + grads[5]), (grads[1], grads[2], grads[3], grads[4]))

    zero_state = jnp.zeros((decay_rates.shape[0], width), jnp.float32)
    carry_out, collected = lax.scan(
        backward_one_block, (zero_state, zero_state), (starts,) + blocked, reverse=True
    )
    grad_decay = carry_out[1]
    grad_step, grad_act, grad_write, grad_read = (
        member.reshape(length, member.shape[2]) for member in collected
    )
    return (grad_step, grad_act, grad_write, grad_read, grad_decay)


def slot_pass(token_row, cotangent_row, mask_row, params):
    (
        norm_gain,
        in_weight,
        conv_weight,
        conv_bias,
        xproj_weight,
        dt_weight,
        dt_bias,
        decay_log,
        skip_gain,
        out_weight,
    ) = params
    length = token_row.shape[0]
    width = in_weight.shape[1] // 2
    rank = dt_weight.shape[0]
    states = decay_log.shape[0]
    taps = conv_weight.shape[0]
    tokens_float = token_row.astype(jnp.float32)
    inverse_rms = lax.rsqrt(jnp.mean(tokens_float * tokens_float, axis=1, keepdims=True) + epsilon)
    unit_rows = tokens_float * inverse_rms
    normed = (unit_rows * norm_gain).astype(jnp.bfloat16)
    projected = jnp.dot(normed, in_weight, preferred_element_type=jnp.float32)
    inner = projected[:, :width]
    gate_pre = projected[:, width:]
    padded = jnp.concatenate([jnp.zeros((taps - 1, width), jnp.float32), inner], axis=0)
    conv_out = conv_bias + sum(
        (conv_weight[offset] * padded[offset : offset + length] for offset in range(taps))
    )
    activated = jax.nn.silu(conv_out).astype(jnp.bfloat16)
    act_float = activated.astype(jnp.float32)
    mixed_proj = jnp.dot(activated, xproj_weight, preferred_element_type=jnp.float32)
    delta_in = mixed_proj[:, :rank].astype(jnp.bfloat16)
    write_coef = mixed_proj[:, rank : rank + states]
    read_coef = mixed_proj[:, rank + states :]
    delta_lin = jnp.dot(delta_in, dt_weight, preferred_element_type=jnp.float32)
    pre_soft = delta_lin + dt_bias
    step_size = jax.nn.softplus(pre_soft)
    decay_rates = -jnp.exp(decay_log)
    starts, scanned = forward_scan(step_size, act_float, write_coef, read_coef, decay_rates)
    summed = scanned + skip_gain * act_float
    gate_act = jax.nn.silu(gate_pre)
    branch = (summed * gate_act).astype(jnp.bfloat16)
    branch_out = jnp.dot(branch, out_weight, preferred_element_type=jnp.float32)
    mixed = (tokens_float + mask_row * branch_out).astype(jnp.bfloat16)
    cotangent_float = cotangent_row.astype(jnp.float32)
    out_grad = (mask_row * cotangent_float).astype(jnp.bfloat16)
    grad_out_weight = jnp.einsum("ti,tj->ij", branch, out_grad, preferred_element_type=jnp.float32)
    grad_branch = jnp.einsum("tj,ij->ti", out_grad, out_weight, preferred_element_type=jnp.float32)
    grad_summed = grad_branch * gate_act
    grad_gate_pre = grad_branch * summed * silu_grad(gate_pre)
    grad_skip = jnp.sum(grad_summed * act_float, axis=0)
    grad_step, grad_act_scan, grad_write, grad_read, grad_decay = backward_scan(
        starts, step_size, act_float, write_coef, read_coef, decay_rates, grad_summed
    )
    grad_pre = grad_step * jax.nn.sigmoid(pre_soft)
    grad_dt_bias = jnp.sum(grad_pre, axis=0)
    grad_lin = grad_pre.astype(jnp.bfloat16)
    grad_dt_weight = jnp.einsum("tr,te->re", delta_in, grad_lin, preferred_element_type=jnp.float32)
    grad_delta_in = jnp.einsum("te,re->tr", grad_lin, dt_weight, preferred_element_type=jnp.float32)
    grad_mixed = jnp.concatenate([grad_delta_in, grad_write, grad_read], axis=1).astype(
        jnp.bfloat16
    )
    grad_xproj = jnp.einsum("te,tc->ec", activated, grad_mixed, preferred_element_type=jnp.float32)
    grad_act_total = (
        grad_summed * skip_gain
        + grad_act_scan
        + jnp.einsum("tc,ec->te", grad_mixed, xproj_weight, preferred_element_type=jnp.float32)
    )
    grad_conv_out = grad_act_total * silu_grad(conv_out)
    grad_conv_bias = jnp.sum(grad_conv_out, axis=0)
    grad_conv_weight = jnp.stack(
        [
            jnp.sum(grad_conv_out * padded[offset : offset + length], axis=0)
            for offset in range(taps)
        ]
    )
    grad_padded = jnp.concatenate(
        [grad_conv_out, jnp.zeros((taps - 1, width), jnp.float32)], axis=0
    )
    grad_inner = sum(
        (
            conv_weight[offset] * grad_padded[taps - 1 - offset : taps - 1 - offset + length]
            for offset in range(taps)
        )
    )
    grad_projected = jnp.concatenate([grad_inner, grad_gate_pre], axis=1).astype(jnp.bfloat16)
    grad_in_weight = jnp.einsum(
        "td,tf->df", normed, grad_projected, preferred_element_type=jnp.float32
    )
    grad_normed = jnp.einsum(
        "tf,df->td", grad_projected, in_weight, preferred_element_type=jnp.float32
    )
    grad_gain = jnp.sum(grad_normed * unit_rows, axis=0)
    grad_unit = grad_normed * norm_gain
    grad_tokens = cotangent_float + inverse_rms * (
        grad_unit - unit_rows * jnp.mean(grad_unit * unit_rows, axis=1, keepdims=True)
    )
    grad_decay_log = grad_decay * decay_rates
    grads = (
        grad_gain,
        grad_in_weight,
        grad_conv_weight,
        grad_conv_bias,
        grad_xproj,
        grad_dt_weight,
        grad_dt_bias,
        grad_decay_log,
        grad_skip,
        grad_out_weight,
    )
    return (mixed, grad_tokens, grads)


def shards(
    tokens,
    cotangent,
    lengths,
    norm_gain,
    in_weight,
    conv_weight,
    conv_bias,
    xproj_weight,
    dt_weight,
    dt_bias,
    decay_log,
    skip_gain,
    out_weight,
):
    params = (
        norm_gain,
        in_weight,
        conv_weight,
        conv_bias,
        xproj_weight,
        dt_weight,
        dt_bias,
        decay_log,
        skip_gain,
        out_weight,
    )
    positions = jnp.arange(tokens.shape[1])
    mask_row = (positions < lengths[0]).astype(jnp.float32)[:, None]
    mixed, grad_tokens, grads = slot_pass(tokens[0], cotangent[0], mask_row, params)
    mixed_rows = [mixed]
    grad_rows = [grad_tokens]
    flat = jnp.concatenate([member.reshape(-1) for member in grads])
    devices_all = lax.axis_size("dp") * lax.axis_size("rep")
    padding = -flat.shape[0] % devices_all
    flat = jnp.concatenate([flat, jnp.zeros((padding,), jnp.float32)])
    across = lax.psum_scatter(flat, "rep", scatter_dimension=0, tiled=True)
    shares = lax.psum_scatter(across, "dp", scatter_dimension=0, tiled=True)
    partial_back = lax.all_gather(shares, "dp", axis=0, tiled=True)
    summed = lax.all_gather(partial_back, "rep", axis=0, tiled=True)
    results = []
    offset = 0
    for member in grads:
        count = member.size
        results.append(summed[offset : offset + count].reshape(member.shape))
        offset = offset + count
    mixed_all = jnp.stack(mixed_rows)
    grad_all = jnp.stack(grad_rows)
    return (
        mixed_all,
        grad_all,
        results[0],
        results[1],
        results[2],
        results[3],
        results[4],
        results[5],
        results[6],
        results[7],
        results[8],
        results[9],
    )


def solution(mesh):
    return jax.shard_map(
        shards,
        mesh=mesh,
        in_specs=(
            P(("dp", "rep"), None, None),
            P(("dp", "rep"), None, None),
            P(("dp", "rep")),
            P(),
            P(),
            P(),
            P(),
            P(),
            P(),
            P(),
            P(),
            P(),
            P(),
        ),
        out_specs=(
            P(("dp", "rep"), None, None),
            P(("dp", "rep"), None, None),
            P(),
            P(),
            P(),
            P(),
            P(),
            P(),
            P(),
            P(),
            P(),
            P(),
        ),
        check_vma=False,
    )
```

profile of v0, /device:TPU:0, one launch (start us, length us, event | category | flops | bytes accessed | tf_op | source)
XLA Modules:
  0.0 4853.7 jit_solution(14237461162082189552)
XLA Ops:
  36.7 806.4 %while.39 = (s32[]{:T(128)}, f32[16,2048]{1,0:T(8,128)S(1)}, f32[5,16,2048]{2,1,0:T(8,128)}, f32[5,64,2048]{2,1,0:T(8,128)}, f32[5,64,2048]{2,1,0:T(8,128)}, /*i...) while((s32[]{:T(128)}, f32[16,2048]{1,0:T(8,128)S(1)}, ...), condition=%wide.region_3.4_spmd, body=%wide.region_1.3_spmd.sunk | while | flops 28475392 | bytes 363373120 | solution.py:48
  135.3 21.0 pad.996
  166.3 21.0 pad.997
  296.5 21.0 pad.996
  327.6 21.0 pad.997
  457.7 21.0 pad.996
  488.8 21.0 pad.997
  619.0 21.0 pad.996
  650.1 21.0 pad.997
  780.3 21.0 pad.996
  811.3 21.0 pad.997
  848.7 2764.1 %while.40 = (s32[]{:T(128)}, f32[16,2048]{1,0:T(8,128)}, f32[16,2048]{1,0:T(8,128)}, f32[5,64,2048]{2,1,0:T(8,128)}, f32[5,64,2048]{2,1,0:T(8,128)}, /*index=5*/...) while((s32[]{:T(128)}, f32[16,2048]{1,0:T(8,128)}, ...), condition=%wide.region_10.11_spmd.clone, body=%wide.region_4.10_spmd.clone.sunk | while | flops 97712128 | bytes 1066374656 | solution.py:67
  1171.9 18.0 multiply_add_fusion.14
  1196.8 21.0 pad.1065
  1217.9 21.1 pad.1066
  1239.0 20.8 pad.1067
  1274.3 21.0 pad.1068
  1295.4 20.6 pad.1069
  1316.0 21.0 pad.1070
  1362.3 21.0 pad.1071
  1389.9 21.0 pad.1072
  1652.5 11.6 pad.1059
  1719.6 18.0 multiply_add_fusion.14
  1744.5 21.0 pad.1065
  1765.5 21.1 pad.1066
  1786.6 20.8 pad.1067
  1822.0 21.0 pad.1068
  1843.0 20.6 pad.1069
  1863.6 21.0 pad.1070
  1909.9 21.0 pad.1071
  1937.5 21.0 pad.1072
  2267.2 18.0 multiply_add_fusion.14
  2292.1 21.0 pad.1065
  2313.1 21.1 pad.1066
  2334.3 20.8 pad.1067
  2369.6 21.0 pad.1068
  2390.6 20.6 pad.1069
  2411.2 21.0 pad.1070
  2457.6 21.0 pad.1071
  2485.2 21.0 pad.1072
  2814.8 18.0 multiply_add_fusion.14
  2839.8 21.0 pad.1065
  2860.8 21.1 pad.1066
  2881.9 20.8 pad.1067
  2917.2 21.0 pad.1068
  2938.3 20.6 pad.1069
  2958.9 21.0 pad.1070
  3005.2 21.0 pad.1071
  3032.8 21.0 pad.1072
  3362.5 18.0 multiply_add_fusion.14
  3387.4 21.0 pad.1065
  3408.4 21.1 pad.1066
  3429.6 20.8 pad.1067
  3464.9 21.0 pad.1068
  3485.9 20.6 pad.1069
  3506.5 21.0 pad.1070
  3552.9 21.0 pad.1071
  3580.4 21.0 pad.1072
  3697.5 448.9 %all-reduce.81.cloned.1.call-done = f32[6667264]{0:T(1024)} async-done(((f32[6667264]{0:T(1024)}), f32[6667264]{0:T(1024)}) %all-reduce.81.cloned.1.call-update) | async-done | bytes 26669072
  4154.6 220.5 %all-reduce.83.cloned.1.call-done = f32[1666816]{0:T(1024)} async-done(((f32[1666816]{0:T(1024)}), f32[1666816]{0:T(1024)}) %all-reduce.83.cloned.1.call-update) | async-done | bytes 6667280
  4381.1 222.1 %all-reduce.79.cloned.1.call-done = f32[1666816]{0:T(1024)} async-done(((f32[1666816]{0:T(1024)}), f32[1666816]{0:T(1024)}) %all-reduce.79.cloned.1.call-update) | async-done | bytes 6667280
  4603.2 26.6 reshape.234
  4638.9 153.3 %all-gather.3.cloned.1.call-done = f32[4,1,1666816]{2,1,0:T(1,128)} async-done(((f32[1,1,1666816]{2,1,0:T(1,128)}), f32[4,1,1666816]{2,1,0:T(1,128)}) %all-gather.3.cloned.1.call-update) | async-done | bytes 26669072 | tf_op jit(solution)/shard_map/all_gather | solution.py:230
  4815.7 18.2 reshape.224
  (1607 shorter events, 2564.1 us)
Async XLA Ops:
  7.2 19.7 copy-start
  7.2 4139.1 %all-reduce.81.cloned.1.call-start = ((), (), s32[]{:S(2)}) async-start(), calls=%async_computation.2 | async-start | bytes 53338112
  15.0 11.8 copy-start.63
  15.1 11.8 copy-start.89
  15.1 11.8 copy-start.91
  15.1 11.8 copy-start.93
  15.1 11.8 copy-start.95
  40.0 12.1 copy-start.6
  166.3 22.0 copy-start.73
  201.3 12.1 copy-start.6
  327.6 22.0 copy-start.73
  362.5 12.1 copy-start.6
  488.8 22.0 copy-start.73
  523.7 12.1 copy-start.6
  650.1 22.0 copy-start.73
  685.0 12.1 copy-start.6
  811.3 22.0 copy-start.73
  848.7 2766.1 %copy-start.86 = (f32[2048]{0:T(1024)S(1)}, f32[2048]{0:T(1024)}, u32[]{:S(2)}) copy-start(f32[2048]{0:T(1024)} %param.28) | copy-start | bytes 24580
  907.5 11.6 copy-start.44
  965.1 11.5 copy-start.29
  965.1 11.5 copy-start.69
  1161.0 10.9 slice-start.2
  1239.0 20.8 slice-start.1
  1316.0 21.0 copy-start.32
  1337.0 10.7 copy-start.70
  1389.9 21.0 copy-start.30
  1455.1 11.6 copy-start.44
  1512.7 11.5 copy-start.29
  1512.7 11.5 copy-start.69
  1708.6 10.9 slice-start.2
  1786.6 20.8 slice-start.1
  1863.6 21.0 copy-start.32
  1884.6 10.7 copy-start.70
  1937.5 21.0 copy-start.30
  2002.7 11.6 copy-start.44
  2060.4 11.5 copy-start.29
  2060.4 11.5 copy-start.69
  2256.3 10.9 slice-start.2
  2334.3 20.8 slice-start.1
  2411.2 21.0 copy-start.32
  2432.2 10.7 copy-start.70
  2485.2 21.0 copy-start.30
  2550.4 11.6 copy-start.44
  2608.0 11.5 copy-start.29
  2608.0 11.5 copy-start.69
  2803.9 10.9 slice-start.2
  2881.9 20.8 slice-start.1
  2958.9 21.0 copy-start.32
  2979.9 10.7 copy-start.70
  3032.8 21.0 copy-start.30
  3098.1 11.6 copy-start.44
  3155.7 11.5 copy-start.29
  3155.7 11.5 copy-start.69
  3351.6 10.9 slice-start.2
  3429.6 20.8 slice-start.1
  3506.5 21.0 copy-start.32
  3527.5 10.7 copy-start.70
  3580.4 21.0 copy-start.30
  3668.9 11.2 copy-start.42
  3678.9 13.2 slice-start.5
  3680.1 12.0 slice-start.6
  3695.6 679.4 %all-reduce.83.cloned.1.call-start = ((), (), s32[]{:S(2)}) async-start(), calls=%async_computation.3 | async-start | bytes 13336576
  4152.0 451.1 %all-reduce.79.cloned.1.call-start = ((), (), s32[]{:S(2)}) async-start(), calls=%async_computation | async-start | bytes 13336576
  4381.0 411.1 %all-gather.3.cloned.1.call-start = ((), (), s32[]{:S(2)}) async-start(), calls=%async_computation.1 | async-start | bytes 33336320 | tf_op jit(solution)/shard_map/all_gather | solution.py:230
  (342 other events, 1146.3 us)
Sparse Core Ops, SparseCore 0:
  3695.7 450.5 all-reduce.80
  4152.2 222.8 all-reduce.82
  4381.2 221.9 all-reduce.78
  4629.9 162.1 all-gather.2
where the time goes:
time: 4900 us; the launch traced here: 4850 us
  local copies, waits for them, and re-layouts  2500 us (51%)
  other arithmetic  1210 us (25%)
  waiting for transfers between devices  1040 us (21%)
    pad x265, local copies, waits for them, and re-layouts, scan_block(): totals = lax.associative_scan(combine_pairs, (factors, drives), axis=0)[1]  2100 us
    unnamed x7, waiting for transfers between devices  891 us
    add x60, other arithmetic, combine_pairs(): return (earlier[0] * later[0], later[0] * earlier[1] + later[1])  226 us
    add_any x25, other arithmetic, combine_pairs(): return (earlier[0] * later[0], later[0] * earlier[1] + later[1])  196 us
    all_gather x1, waiting for transfers between devices, shards(): summed = lax.all_gather(partial_back, 'rep', axis=0, tiled=True)  153 us
    add x50, other arithmetic, scan_block(): totals = lax.associative_scan(combine_pairs, (factors, drives), axis=0)[1]  143 us
    mul x50, other arithmetic, combine_pairs(): return (earlier[0] * later[0], later[0] * earlier[1] + later[1])  142 us
    while x660, local copies, waits for them, and re-layouts  123 us
  transfers between devices with their start and end apart: 4, of which 4 were waited for; matrix products, arithmetic and copies ran while one was open for 0% of the time, Pallas kernels for 0%

commit v1 on v0

v1 whole, which is shorter than its diff:
```python
import functools
import math
import jax
import jax.numpy as jnp
from jax import lax
from jax.experimental import pallas as pl
from jax.experimental.pallas import tpu as pltpu
from jax.sharding import PartitionSpec as P

F32 = jnp.float32
BF16 = jnp.bfloat16
EPS = 1e-05
LANES = 128
SUB = 8
WIDE = 1024
SEG = 16
VMEM = 60 * 1024 * 1024
LOG2E = math.log2(math.e)
CHEAP = pl.CostEstimate(flops=0, bytes_accessed=0, transcendentals=0)


def dot(a, b, dims=((1,), (0,))):
    return lax.dot_general(a, b, (dims, ((), ())), preferred_element_type=F32)


def shifted(value, rows):
    if rows == 0:
        return value
    length = value.shape[0]
    index = lax.broadcasted_iota(jnp.int32, value.shape, 0)
    moved = pltpu.roll(value, rows % length, 0)
    keep = index >= rows if rows > 0 else index < length + rows
    return jnp.where(keep, moved, 0.0)


def conv_of(inner, cw_ref, cb_ref):
    taps = cw_ref.shape[0]
    total = cb_ref[...] + cw_ref[taps - 1 : taps, :] * inner
    for k in range(taps - 1):
        total = total + cw_ref[k : k + 1, :] * shifted(inner, taps - 1 - k)
    return total


def front_kernel(
    len_ref, tok_ref, cot_ref, gain_ref, w_ref, cw_ref, cb_ref, xp_ref,
    normed_ref, send_ref, og_ref, inner_ref, act_ref, mp_ref,
):
    @pl.when(pl.program_id(0) == 0)
    def _():
        x = tok_ref[...].astype(F32)
        inv = lax.rsqrt(jnp.mean(x * x, axis=1, keepdims=True) + EPS)
        normed = (x * inv * gain_ref[...]).astype(BF16)
        normed_ref[...] = normed
        low = x.shape[1] // 2
        send_ref[...] = jnp.where(len_ref[1] == 0, normed[:, low:], normed[:, :low]).astype(F32)
        row = lax.broadcasted_iota(jnp.int32, x.shape, 0)
        og_ref[...] = jnp.where(row < len_ref[0], cot_ref[...].astype(F32), 0.0)
        mp_ref[...] = jnp.zeros_like(mp_ref)

    inner = dot(normed_ref[...], w_ref[...])
    inner_ref[...] = inner
    conv = conv_of(inner, cw_ref, cb_ref)
    act = (conv * jax.nn.sigmoid(conv)).astype(BF16)
    act_ref[...] = act
    mp_ref[...] += dot(act, xp_ref[...], ((1,), (1,)))


def front(tokens, cot, lengths, gain, in_weight, cw, cb, xproj):
    length, model = tokens.shape
    width = cw.shape[1]
    cols = xproj.shape[0]
    blk = 256
    whole = lambda shape: pl.BlockSpec(shape, lambda j: (0, 0))
    part = lambda rows: pl.BlockSpec((rows, blk), lambda j: (0, j))
    return pl.pallas_call(
        front_kernel,
        grid=(width // blk,),
        in_specs=[
            pl.BlockSpec(memory_space=pltpu.SMEM),
            whole((length, model)), whole((length, model)), whole((1, model)),
            part(model), part(cw.shape[0]), part(1),
            part(cols),
        ],
        out_specs=[
            whole((length, model)), whole((length, model // 2)), whole((length, model)),
            part(length), part(length), whole((length, cols)),
        ],
        out_shape=[
            jax.ShapeDtypeStruct((length, model), BF16),
            jax.ShapeDtypeStruct((length, model // 2), F32),
            jax.ShapeDtypeStruct((length, model), F32),
            jax.ShapeDtypeStruct((length, width), F32),
            jax.ShapeDtypeStruct((length, width), BF16),
            jax.ShapeDtypeStruct((length, cols), F32),
        ],
        compiler_params=pltpu.CompilerParams(vmem_limit_bytes=VMEM),
        cost_estimate=CHEAP,
        name="front",
    )(lengths, tokens, cot, gain, in_weight, cw, cb, xproj)


def splat_rows(length, count):
    return -(-length // LANES) * count * LANES


def fill_splats(mp_ref, splat_ref, first, count):
    length, cols = mp_ref.shape
    for g in range(-(-length // LANES)):
        size = min(LANES, length - g * LANES)
        rows = mp_ref[pl.ds(g * LANES, size), :]
        rows = jnp.concatenate([rows, jnp.zeros((size, LANES - cols), F32)], axis=1)
        if size < LANES:
            rows = jnp.concatenate([rows, jnp.zeros((LANES - size, LANES), F32)], axis=0)
        turned = rows.T
        for n in range(count):
            line = jnp.broadcast_to(turned[first + n : first + n + 1, :], (LANES, LANES))
            splat_ref[pl.ds((g * count + n) * LANES, size), :] = line.T[:size]


def splat(splat_ref, tb, count, n, s):
    per = LANES // SUB
    row = tb // per * (count * LANES) + tb % per * SUB + (n * LANES + s)
    return jnp.broadcast_to(splat_ref[pl.ds(row, 1), :], (SUB, LANES))


def tile_rows(tb, s):
    return pl.ds(pl.multiple_of(tb * SUB * SUB, SUB * SUB) + s, SUB, stride=SUB)


def put_tiles(ref, j, value):
    for tb in range(value.shape[0] // SUB):
        ref[pl.ds(tb * SUB * SUB + j * SUB, SUB), :] = value[tb * SUB : (tb + 1) * SUB, :]


def get_tiles(ref, j, length):
    return jnp.concatenate(
        [ref[pl.ds(tb * SUB * SUB + j * SUB, SUB), :] for tb in range(length // SUB)], axis=0
    )


def scan_kernel(
    core_ref, mp_ref, normed_ref, og_ref, act_ref, wg_ref, wo_ref, dtw_ref, dtb_ref, dlog_ref, skip_ref,
    branch_ref, send_ref, ggp_ref, gs_ref, step_ref, mark_ref,
    splat_ref, u_ref, y_ref, a_ref, gate_ref, gb_ref,
):
    length = mp_ref.shape[0]
    rank = dtw_ref.shape[0]
    states = a_ref.shape[0]
    both = 2 * states
    fill_splats(mp_ref, splat_ref, rank, both)
    a_ref[...] = -jnp.exp(dlog_ref[...]) * LOG2E
    delta_in = mp_ref[:, :rank].astype(BF16)
    for j in range(WIDE // LANES):
        cols = pl.ds(j * LANES, LANES)
        pre = dot(delta_in, dtw_ref[:, cols]) + dtb_ref[:, cols]
        step = jnp.maximum(pre, 0.0) + jnp.log1p(jnp.exp(-jnp.abs(pre)))
        put_tiles(step_ref, j, step)
        put_tiles(u_ref, j, step * act_ref[:, cols].astype(F32))

    def body(tb, carry):
        h = list(carry)
        @pl.when(tb % (SEG // SUB) == 0)
        def _():
            base = pl.multiple_of((tb // (SEG // SUB)) * states * SUB, states * SUB)
            for n in range(states):
                mark_ref[pl.ds(base + n * SUB, SUB), :] = h[n]
        for s in range(SUB):
            step = step_ref[tile_rows(tb, s), :]
            u = u_ref[tile_rows(tb, s), :]
            y = None
            for n in range(states):
                f = jnp.exp2(step * a_ref[n])
                h[n] = f * h[n] + u * splat(splat_ref, tb, both, n, s)
                q = h[n] * splat(splat_ref, tb, both, states + n, s)
                y = q if y is None else y + q
            y_ref[tile_rows(tb, s), :] = y
        return tuple(h)

    zero = jnp.zeros((SUB, LANES), F32)
    lax.fori_loop(0, length // SUB, body, (zero,) * states)

    og = og_ref[...].astype(BF16)
    for k in range(WIDE // 256):
        cols = pl.ds(k * 256, 256)
        gate_ref[:, cols] = dot(normed_ref[...], wg_ref[:, cols])
        gb_ref[:, cols] = dot(og, wo_ref[cols, :], ((1,), (1,)))
    for j in range(WIDE // LANES):
        cols = pl.ds(j * LANES, LANES)
        gate = gate_ref[:, cols]
        gb = gb_ref[:, cols]
        summed = get_tiles(y_ref, j, length) + skip_ref[:, cols] * act_ref[:, cols].astype(F32)
        sig = jax.nn.sigmoid(gate)
        gate_act = gate * sig
        branch = (summed * gate_act).astype(BF16)
        branch_ref[:, cols] = branch
        into = pl.ds(j * LANES % (WIDE // 2), LANES)

        @pl.when((core_ref[0] == 0) == (j * LANES >= WIDE // 2))
        def _():
            send_ref[:, into] = branch.astype(F32)
        put_tiles(gs_ref, j, gb * gate_act)
        ggp_ref[:, cols] = gb * summed * (sig * (1.0 + gate * (1.0 - sig)))


def scan(block, core, mp, normed, og, act, in_weight, out_weight, dtw, dtb, dlog, skip):
    length, model = normed.shape
    width = act.shape[1]
    rank = dtw.shape[0]
    states = dlog.shape[0]
    count = width // WIDE
    whole = lambda shape: pl.BlockSpec(shape, lambda i: (0,) * len(shape))
    col = lambda rows, at: pl.BlockSpec((rows, WIDE), lambda i: (0, at))
    tiles = jax.ShapeDtypeStruct((length * SUB, LANES), F32)
    marks = (length // SEG) * states * SUB
    flat = jax.ShapeDtypeStruct((length, WIDE), F32)
    return pl.pallas_call(
        scan_kernel,
        grid=(1,),
        in_specs=[
            pl.BlockSpec(memory_space=pltpu.SMEM), whole(mp.shape), whole(normed.shape), whole(og.shape), col(length, block),
            col(model, count + block), pl.BlockSpec((WIDE, model), lambda i: (block, 0)),
            col(rank, block), col(1, block),
            pl.BlockSpec((states, SUB, LANES), lambda i: (0, block, 0)), col(1, block),
        ],
        out_specs=[whole(flat.shape), whole((length, WIDE // 2)), whole(flat.shape), whole(tiles.shape), whole(tiles.shape), whole((marks, LANES))],
        out_shape=[jax.ShapeDtypeStruct(flat.shape, BF16), jax.ShapeDtypeStruct((length, WIDE // 2), F32), flat, tiles, tiles, jax.ShapeDtypeStruct((marks, LANES), F32)],
        scratch_shapes=[
            pltpu.VMEM((splat_rows(length, 2 * states), LANES), F32),
            pltpu.VMEM((length * SUB, LANES), F32),
            pltpu.VMEM((length * SUB, LANES), F32),
            pltpu.VMEM((states, SUB, LANES), F32),
            pltpu.VMEM((length, WIDE), F32),
            pltpu.VMEM((length, WIDE), F32),
        ],
        compiler_params=pltpu.CompilerParams(vmem_limit_bytes=VMEM),
        cost_estimate=CHEAP,
        name=f"scan{block}",
    )(core, mp, normed, og, act, in_weight, out_weight, dtw, dtb, dlog, skip)


def back_kernel(
    mp_ref, act_ref, step_ref, gs_ref, mark_ref, dtw_ref, dlog_ref,
    gact_ref, glin_ref, gdelta_ref, gdtw_ref, gwr_ref, gdlog_ref, rows_ref,
    splat_ref, act_t_ref, gd_ref, gu_ref, a_ref, f_ref, h_ref, carry_ref, turn_ref, part_ref,
):
    length = mp_ref.shape[0]
    rank = dtw_ref.shape[0]
    states = a_ref.shape[0]
    both = 2 * states
    fill_splats(mp_ref, splat_ref, rank, both)
    rate = -jnp.exp(dlog_ref[...])
    a_ref[...] = rate
    for j in range(WIDE // LANES):
        put_tiles(act_t_ref, j, act_ref[:, pl.ds(j * LANES, LANES)].astype(F32))
    per = SEG // SUB

    groups = states // SUB
    carry_ref[...] = jnp.zeros_like(carry_ref)

    def segment(i, _):
        seg = length // SEG - 1 - i
        for q in range(groups):
            mine = range(q * SUB, (q + 1) * SUB)
            rates = [a_ref[n] for n in mine]
            base = pl.multiple_of(seg * states * SUB, states * SUB)
            start = [mark_ref[pl.ds(base + n * SUB, SUB), :] for n in mine]
            for j in range(SUB):
                h_ref[0, j] = start[j]

            def again(k, hs):
                hs = list(hs)
                tb = seg * per + k
                for s in range(SUB):
                    step = step_ref[tile_rows(tb, s), :]
                    u = step * act_t_ref[tile_rows(tb, s), :]
                    step2 = step * LOG2E
                    for j, n in enumerate(mine):
                        f = jnp.exp2(step2 * rates[j])
                        f_ref[k * SUB + s, j] = f
                        hs[j] = f * hs[j] + u * splat(splat_ref, tb, both, n, s)
                        h_ref[k * SUB + s + 1, j] = hs[j]
                return tuple(hs)

            last = lax.fori_loop(0, per, again, tuple(start))

            def reverse(k2, carry):
                dhs, gas, now = (list(c) for c in carry)
                k = per - 1 - k2
                tb = seg * per + k
                for s in reversed(range(SUB)):
                    g = gs_ref[tile_rows(tb, s), :]
                    step = step_ref[tile_rows(tb, s), :]
                    u = step * act_t_ref[tile_rows(tb, s), :]
                    gd = gu = None
                    ws, rs = [], []
                    for j, n in enumerate(mine):
                        dh = dhs[j] + g * splat(splat_ref, tb, both, states + n, s)
                        before = h_ref[k * SUB + s, j]
                        rs.append(now[j] * g)
                        ws.append(dh * u)
                        t = dh * splat(splat_ref, tb, both, n, s)
                        gu = t if gu is None else gu + t
                        dhs[j] = dh * f_ref[k * SUB + s, j]
                        ga = dhs[j] * before
                        t = ga * rates[j]
                        gd = t if gd is None else gd + t
                        gas[j] = gas[j] + ga * step
                        now[j] = before
                    if q == 0:
                        gd_ref[tile_rows(tb, s), :] = gd
                        gu_ref[tile_rows(tb, s), :] = gu
                    else:
                        gd_ref[tile_rows(tb, s), :] = gd_ref[tile_rows(tb, s), :] + gd
                        gu_ref[tile_rows(tb, s), :] = gu_ref[tile_rows(tb, s), :] + gu
                    for slot, values in ((0, ws), (1, rs)):
                        at = (s * 2 + slot) * SUB * SUB
                        for j in range(SUB):
                            turn_ref[pl.ds(at + j * SUB, SUB), :] = values[j]
                        total = turn_ref[pl.ds(at, SUB, stride=SUB), :]
                        for j in range(1, SUB):
                            total = total + turn_ref[pl.ds(at + j, SUB, stride=SUB), :]
                        row = tb * (both * SUB) + (slot * states + q * SUB) * SUB + s
                        part_ref[pl.ds(row, SUB, stride=SUB), :] = total
                return (tuple(dhs), tuple(gas), tuple(now))

            begin = (
                tuple(carry_ref[0, n] for n in mine), tuple(carry_ref[1, n] for n in mine), last
            )
            dhs, gas, _ = lax.fori_loop(0, per, reverse, begin)
            for j, n in enumerate(mine):
                carry_ref[0, n] = dhs[j]
                carry_ref[1, n] = gas[j]
        return 0

    lax.fori_loop(0, length // SEG, segment, 0)
    for n in range(states):
        gdlog_ref[n] = carry_ref[1, n] * rate[n]

    row = lax.broadcasted_iota(jnp.int32, (2 * LANES, LANES), 0)
    lane = lax.broadcasted_iota(jnp.int32, (2 * LANES, LANES), 1)
    gwr = None
    for n in range(0, both, 2):
        pieces = []
        for k in range(2):
            pieces.append(jnp.concatenate(
                [part_ref[pl.ds((tb * both + n + k) * SUB, SUB), :] for tb in range(length // SUB)], axis=0
            ).astype(BF16))
        into = jnp.where(lane == rank + n + row // LANES, 1.0, 0.0).astype(BF16)
        term = dot(jnp.concatenate(pieces, axis=1), into)
        gwr = term if gwr is None else gwr + term
    gwr_ref[...] = gwr

    for j in range(WIDE // LANES):
        cols = pl.ds(j * LANES, LANES)
        act = act_ref[:, cols].astype(F32)
        step = get_tiles(step_ref, j, length)
        gs = get_tiles(gs_ref, j, length)
        gu = get_tiles(gu_ref, j, length)
        gstep = get_tiles(gd_ref, j, length) + gu * act
        gpre = gstep * (1.0 - jnp.exp(-step))
        glin_ref[:, cols] = gpre.astype(BF16)
        rows_ref[0:1, cols] = jnp.sum(gpre, axis=0, keepdims=True)
        rows_ref[1:2, cols] = jnp.sum(gs * act, axis=0, keepdims=True)
        gact_ref[:, cols] = gu * step
    delta_in = mp_ref[:, :rank].astype(BF16)
    gdtw_ref[...] = dot(delta_in, glin_ref[...], ((0,), (0,)))
    gdelta_ref[...] = dot(glin_ref[...], dtw_ref[...], ((1,), (1,)))


def back(block, mp, act, step, gs, marks, dtw, dlog):
    length = act.shape[0]
    rank = dtw.shape[0]
    states = dlog.shape[0]
    whole = lambda shape: pl.BlockSpec(shape, lambda i: (0,) * len(shape))
    col = lambda rows, at: pl.BlockSpec((rows, WIDE), lambda i: (0, at))
    flat = jax.ShapeDtypeStruct((length, WIDE), F32)
    outs = [
        flat,
        jax.ShapeDtypeStruct((length, WIDE), BF16),
        jax.ShapeDtypeStruct((length, rank), F32),
        jax.ShapeDtypeStruct((rank, WIDE), F32),
        jax.ShapeDtypeStruct((length, LANES), F32),
        jax.ShapeDtypeStruct((states, SUB, LANES), F32),
        jax.ShapeDtypeStruct((2, WIDE), F32),
    ]
    tiles = pltpu.VMEM((length * SUB, LANES), F32)
    return pl.pallas_call(
        back_kernel,
        grid=(1,),
        in_specs=[
            whole(mp.shape), col(length, block), whole(step.shape), whole(gs.shape), whole(marks.shape),
            col(rank, block), pl.BlockSpec((states, SUB, LANES), lambda i: (0, block, 0)),
        ],
        out_specs=[whole(o.shape) for o in outs],
        out_shape=outs,
        scratch_shapes=[
            pltpu.VMEM((splat_rows(length, 2 * states), LANES), F32),
            tiles, tiles, tiles,
            pltpu.VMEM((states, SUB, LANES), F32),
            pltpu.VMEM((SEG, SUB, SUB, LANES), F32),
            pltpu.VMEM((SEG + 1, SUB, SUB, LANES), F32),
            pltpu.VMEM((2, states, SUB, LANES), F32),
            pltpu.VMEM((2 * SUB * SUB * SUB, LANES), F32),
            pltpu.VMEM((length * 2 * states, LANES), F32),
        ],
        compiler_params=pltpu.CompilerParams(vmem_limit_bytes=VMEM),
        cost_estimate=CHEAP,
        name=f"back{block}",
    )(mp, act, step, gs, marks, dtw, dlog)


def post_kernel(
    gmix_ref, gs_ref, gact_ref, act_ref, inner_ref, xp_ref, cw_ref, cb_ref, skip_ref, gdtw_ref, gdlog_ref, two_ref,
    gi_ref, small_ref,
):
    length = act_ref.shape[0]
    taps = cw_ref.shape[0]
    share = dot(gmix_ref[...], xp_ref[...])
    sizes = [xp_ref.shape[0], gdtw_ref.shape[0], gdlog_ref.shape[0], two_ref.shape[0]]
    ends = [sum(sizes[: i + 1]) for i in range(4)]
    small_ref[: ends[0], :] = dot(gmix_ref[...], act_ref[...], ((0,), (0,)))
    small_ref[ends[0] : ends[1], :] = gdtw_ref[...]
    small_ref[ends[1] : ends[2], :] = gdlog_ref[...]
    small_ref[ends[2] : ends[3], :] = two_ref[...]
    small_ref[ends[3] + taps + 1 :, :] = jnp.zeros((small_ref.shape[0] - ends[3] - taps - 1, WIDE), F32)
    for j in range(WIDE // LANES):
        cols = pl.ds(j * LANES, LANES)
        inner = inner_ref[:, cols]
        cw = cw_ref[:, cols]
        conv = conv_of(inner, cw, cb_ref[:, cols])
        sig = jax.nn.sigmoid(conv)
        gact = (
            get_tiles(gs_ref, j, length) * skip_ref[:, cols]
            + gact_ref[:, cols]
            + share[:, j * LANES : (j + 1) * LANES]
        )
        gconv = gact * (sig * (1.0 + conv * (1.0 - sig)))
        at = ends[3]
        small_ref[at + taps : at + taps + 1, cols] = jnp.sum(gconv, axis=0, keepdims=True)
        total = None
        for k in range(taps):
            small_ref[at + k : at + k + 1, cols] = jnp.sum(
                gconv * shifted(inner, taps - 1 - k), axis=0, keepdims=True
            )
            term = cw[k : k + 1, :] * shifted(gconv, k + 1 - taps)
            total = term if total is None else total + term
        gi_ref[:, cols] = total


def post(block, lines, gmix, gs, gact, act, inner, xproj, cw, cb, skip, gdtw, gdlog, two):
    length = act.shape[0]
    cols = xproj.shape[0]
    taps = cw.shape[0]
    whole = lambda shape: pl.BlockSpec(shape, lambda i: (0,) * len(shape))
    col = lambda rows, at: pl.BlockSpec((rows, WIDE), lambda i: (0, at))
    outs = [jax.ShapeDtypeStruct((length, WIDE), F32), jax.ShapeDtypeStruct((lines, WIDE), F32)]
    return pl.pallas_call(
        post_kernel,
        grid=(1,),
        in_specs=[
            whole(gmix.shape), whole(gs.shape), whole(gact.shape), col(length, block), col(length, block),
            col(cols, block), col(taps, block), col(1, block), col(1, block),
            whole(gdtw.shape), whole(gdlog.shape), whole(two.shape),
        ],
        out_specs=[whole(o.shape) for o in outs],
        out_shape=outs,
        compiler_params=pltpu.CompilerParams(vmem_limit_bytes=VMEM),
        cost_estimate=CHEAP,
        name=f"post{block}",
    )(gmix, gs, gact, act, inner, xproj, cw, cb, skip, gdtw, gdlog, two)


def outer(core, own, other, rows, small=()):
    length = own[0][0].shape[0]
    low, cols = own[0][0].shape[1] // 2, own[0][1].shape[1]
    per = 2
    blk = low // per
    ins, specs = [], []
    for c in range(2):
        at = lambda i, c=c: jnp.clip(i - c * per, 0, per - 1)
        ins += [own[c][0], other[c][0], own[c][1], other[c][1]]
        specs += [
            pl.BlockSpec((length, blk), lambda i, ix, at=at: (0, ix[0] * per + at(i))),
            pl.BlockSpec((length, blk), lambda i, ix, at=at: (0, at(i))),
            pl.BlockSpec((length, cols), lambda i, ix: (0, 0)),
            pl.BlockSpec((length, cols), lambda i, ix: (0, 0)),
        ]
    ins += list(small)
    specs += [pl.BlockSpec(v.shape, lambda i, ix: (0, 0)) for v in small]
    rest = rows - 2 * low
    total = 2 * low + (rest > 0) * blk * -(-rest // blk)

    def body(ix, *refs):
        out = refs[-1]
        step = pl.program_id(0)
        for c in range(2):
            @pl.when((step >= c * per) & (step < (c + 1) * per))
            def _():
                l, lo, r, ro = [ref[...].astype(BF16) for ref in refs[4 * c : 4 * c + 4]]
                out[...] = dot(l, r, ((0,), (0,))) + dot(lo, ro, ((0,), (0,)))

        @pl.when(step >= 2 * per)
        def _():
            out[...] = jnp.zeros_like(out)
            if small:
                a, b, got = refs[8:11]
                out[: got.shape[0], :] = jnp.where(ix[0] == 0, a[...], b[...]) + got[...]

    return pl.pallas_call(
        body,
        out_shape=jax.ShapeDtypeStruct((rows, cols), F32),
        grid_spec=pltpu.PrefetchScalarGridSpec(
            num_scalar_prefetch=1, grid=(total // blk,), in_specs=specs,
            out_specs=pl.BlockSpec((blk, cols), lambda i, ix: (i, 0)),
        ),
        compiler_params=pltpu.CompilerParams(vmem_limit_bytes=VMEM),
        cost_estimate=CHEAP,
        name="outer",
    )(core, *ins)


def blank(shape):
    return pl.pallas_call(
        lambda ref: None, out_shape=jax.ShapeDtypeStruct(shape, F32),
        out_specs=pl.BlockSpec(memory_space=pltpu.HBM), name="blank",
        compiler_params=pltpu.CompilerParams(vmem_limit_bytes=VMEM), cost_estimate=CHEAP,
    )()


def put(targets, pieces, spans, flags):
    arrays = [p[0] for p in pieces]
    n = len(targets)
    sems = max(len(spans(p[1], h)) for p in pieces for h in range(2))

    def body(flag_ref, *refs):
        values = refs[n : n + len(arrays)]
        outs, sem = refs[n + len(arrays) : -1], refs[-1]

        def copies(k, h):
            _, chunk, _, at = pieces[k]
            made = []
            for q, (first, rows, target, row, per, col) in enumerate(spans(chunk, h)):
                to = outs[target].at[
                    pl.ds(pl.multiple_of(flag_ref[at] * per + row, SUB), rows), pl.ds(col, arrays[k].shape[1])
                ]
                made.append(pltpu.make_async_copy(values[k].at[pl.ds(first, rows), :], to, sem.at[k * sems + q]))
            return made

        for act in ("start", "wait"):
            for k in range(len(arrays)):
                for h in range(2):
                    @pl.when(flag_ref[pieces[k][2]] == h)
                    def _():
                        for copy in copies(k, h):
                            getattr(copy, act)()

    return pl.pallas_call(
        body,
        out_shape=[jax.ShapeDtypeStruct(t.shape, F32) for t in targets],
        grid_spec=pltpu.PrefetchScalarGridSpec(
            num_scalar_prefetch=1, grid=(1,),
            in_specs=[pl.BlockSpec(memory_space=pltpu.HBM)] * n
            + [pl.BlockSpec(a.shape, lambda i, ix: (0, 0)) for a in arrays],
            out_specs=[pl.BlockSpec(memory_space=pltpu.HBM)] * n,
            scratch_shapes=[pltpu.SemaphoreType.DMA((len(arrays) * sems,))],
        ),
        input_output_aliases={1 + k: k for k in range(n)},
        compiler_params=pltpu.CompilerParams(vmem_limit_bytes=VMEM),
        cost_estimate=CHEAP,
        name="put",
    )(flags, *targets, *arrays)


def bits_of(axis):
    return lax.axis_size(axis).bit_length() - 1


def bit(step):
    return (lax.axis_index(step[0]) >> step[1]) & 1


def swap(value, step):
    axis, place = step
    size = lax.axis_size(axis)
    return lax.ppermute(value, axis, [(i, i ^ (1 << place)) for i in range(size)])


CORE = ("rep", 0)


def orders():
    x, y, z = ("dp", 0), ("rep", 1), ("dp", 1)
    rest = [("dp", b) for b in range(2, bits_of("dp"))] + [("rep", b) for b in range(2, bits_of("rep"))]
    return [[x, y, z] + rest, [y, z, x] + rest, [z, x, y] + rest]


def fits(rows):
    unit = 3 << len(orders()[0])
    return -(-rows // unit) * unit


def slab(value, start, rows):
    return lax.dynamic_slice_in_dim(value, start, rows, 0)


class Order:
    def __init__(self):
        self.last = None

    def tie(self, *values):
        if self.last is None:
            return values
        return lax.optimization_barrier((values, self.last))[0]

    def done(self, value):
        self.last = value


class Reduced:
    def __init__(self, order):
        self.order = order
        self.steps = orders()
        self.count = len(self.steps[0])
        self.k = -1
        self.share = None

    def same(self, k):
        return self.steps[0][k] == self.steps[1][k]

    def send(self, k, values):
        if self.same(k):
            got = swap(jnp.concatenate(values), self.steps[0][k])
            size = values[0].shape[0]
            return [lax.slice_in_dim(got, c * size, (c + 1) * size) for c in range(3)]
        return [swap(v, s[k]) for v, s in zip(values, self.steps)]

    def begin(self, whole):
        rows = whole.shape[0] // 3
        self.kept = [(whole, c * rows, rows) for c in range(3)]
        self.got = None
        self.fold()

    def fold(self):
        k = self.k + 1
        if self.got is None:
            terms = [[v] for v in self.kept]
        else:
            arrays = self.order.tie([v[0] for v in self.kept], self.got)
            terms = [
                [(a, start, rows), (g, 0, rows)]
                for a, (_, start, rows), g in zip(arrays[0], self.kept, arrays[1])
            ]

        def part(term, i, halves):
            values = []
            for value, start, rows in term:
                size = rows // halves
                values.append(slab(value, start + i * size, size))
            return sum(values[1:], values[0])

        if k == self.count:
            self.share = [part(t, 0, 1) for t in terms]
            self.order.done(self.share[0])
            self.got = self.send(k - 1, self.share)
            self.k = k - 1
            return
        index = [bit(s[k]) for s in self.steps]
        sends = [part(t, 1 - i, 2) for t, i in zip(terms, index)]
        self.order.done(sends)
        if self.got is None:
            self.kept = [(v, start + i * (rows // 2), rows // 2) for (v, start, rows), i in zip(self.kept, index)]
            got = self.send(k, sends)
        else:
            got = self.send(k, sends)
            tied = self.order.tie([[v[0] for v in t] for t in terms])[0]
            keeps = [
                part([(a, start, rows) for a, (_, start, rows) in zip(arr, t)], i, 2)
                for arr, t, i in zip(tied, terms, index)
            ]
            self.order.done(keeps)
            self.kept = [(v, 0, v.shape[0]) for v in keeps]
        self.got = got
        self.k = k

    def finish(self):
        while self.share is None:
            self.fold()
        while self.k > 3:
            self.widen()

    def widen(self):
        k = self.k
        share, got = self.order.tie(self.share, self.got)
        wide = []
        for v, g, s in zip(share, got, self.steps):
            first = bit(s[k]) == 0
            wide.append(jnp.where(first, jnp.concatenate([v, g]), jnp.concatenate([g, v])))
        self.share = wide
        self.order.done(wide)
        self.k = k - 1
        self.got = self.send(k - 1, wide)
        if k == 1:
            self.across = [swap(v, CORE) for v in wide]

    def own(self):
        return [(v, c, c, 6) for c, v in enumerate(self.share)] + [(v, c, c, 7) for c, v in enumerate(self.across)]

    def arrived(self):
        return [(v, c, 3 + c, 6) for c, v in enumerate(self.got)] + [(swap(v, CORE), c, 3 + c, 7) for c, v in enumerate(self.got)]

    def flags(self):
        mine = [bit(s[0]) for s in self.steps]
        core = bit(CORE)
        return jnp.stack(mine + [1 - i for i in mine] + [core, 1 - core]).astype(jnp.int32)


def spans_of(total, parts):
    size = total // 6

    def spans(chunk, h):
        low = (2 * chunk + h) * size
        found, start = [], 0
        for rows, target, row, col in parts:
            a, b = max(low, start), min(low + size, start + rows)
            if a < b and target is not None:
                found.append((a - low, b - a, target, row + a - start, rows, col))
            start += rows
        return found

    return spans


SEQUENCE = (
    "front", "scan0", "out0", "scan1", "out1", "p0.f", "back0", "p0.f", "p1.f", "back1", "p0.f", "p1.f", "mix", "post0",
    "post1", "p0.e", "p1.f", "out2", "p1.e", "p0.w", "p1.w", "p2.f", "p0.w", "p1.w", "p2.f", "p0.w", "gn", "p2.f",
    "p1.w", "p0.own", "p2.e", "p0.got", "p1.own", "p2.w", "p1.got", "p2.w", "mixed", "p2.w", "p2.own", "p2.got",
)


def shards(
    tokens, cotangent, lengths, norm_gain, in_weight, conv_weight, conv_bias, xproj_weight,
    dt_weight, dt_bias, decay_log, skip_gain, out_weight,
):
    tok, cot = tokens[0], cotangent[0]
    length, model = tok.shape
    taps, width = conv_weight.shape
    states = decay_log.shape[0]
    rank = dt_weight.shape[0]
    cols = xproj_weight.shape[1]
    row = lambda v: v.reshape(1, -1)
    core = bit(CORE).astype(jnp.int32)[None]
    dlog3 = decay_log.reshape(states, width // LANES, LANES)
    turned = xproj_weight.T
    sizes = [cols, rank, states, 2, taps + 1]
    used = -(-sum(sizes) // SUB) * SUB
    order = Order()
    tie, done = order.tie, order.done
    sets = [Reduced(order) for _ in range(3)]
    heights = [fits(model), fits(model), fits(model + used)]
    low = model // 2
    spans = [
        spans_of(heights[b], [(WIDE // 2, 1, b * WIDE, 0), (low, 0, 0, width + b * WIDE)]) for b in range(2)
    ] + [spans_of(heights[2], [(low, 0, 0, 0), (low, 0, 0, WIDE), (used, 2, 0, 0)])]
    state = {"targets": [blank((model, 2 * width)), blank((width, model)), blank((2 * used, WIDE))]}
    scans, backs, posts, others = {}, {}, {}, {}

    def op_front():
        state["front"] = front(
            tok, cot, jnp.concatenate([lengths, core]), row(norm_gain), in_weight, conv_weight, row(conv_bias), turned
        )
        _, send, og, _, _, mp = state["front"]
        state["og"] = swap(og, CORE)
        state["normed"] = swap(send, CORE)
        done(mp)

    def op_scan(b):
        normed, _, og, _, act, mp = state["front"]
        mp, = tie(mp)
        scans[b] = scan(
            b, core, mp, normed, og, act, in_weight, out_weight, dt_weight, row(dt_bias), dlog3, row(skip_gain)
        )
        done(scans[b][0])
        others[b] = (swap(scans[b][1], CORE), swap(scans[b][2], CORE))

    def op_out(b):
        normed, _, og, _, _, _ = state["front"]
        if b < 2:
            own = [(scans[b][0], og), (normed, scans[b][2])]
            other = [(others[b][0], state["og"]), (state["normed"], others[b][1])]
            small = ()
        else:
            own = [(normed, posts[q][0]) for q in range(2)]
            other = [(state["normed"], others[2 + q]) for q in range(2)]
            small = (posts[0][1], posts[1][1], others["small"])
        own, other, small = tie(own, other, small)
        whole = outer(core, own, other, heights[b], small)
        done(whole)
        sets[b].begin(whole)

    def op_back(b):
        _, _, _, _, act, mp = state["front"]
        mp, = tie(mp)
        backs[b] = back(b, mp, act, scans[b][4], scans[b][3], scans[b][5], dt_weight, dlog3)
        done(backs[b][0])

    def op_mix():
        v = tie(*[[backs[b][2], backs[b][4]] for b in range(2)])
        state["gmix"] = jnp.concatenate([v[0][0] + v[1][0], (v[0][1] + v[1][1])[:, rank:cols]], axis=1).astype(BF16)
        done(state["gmix"])

    def op_post(b):
        _, _, _, inner, act, _ = state["front"]
        gmix, = tie(state["gmix"])
        back_b = backs[b]
        posts[b] = post(
            b, used, gmix, scans[b][3], back_b[0], act, inner, turned, conv_weight, row(conv_bias), row(skip_gain),
            back_b[3], back_b[5].reshape(states, WIDE), back_b[6],
        )
        done(posts[b][0])
        others[2 + b] = swap(posts[b][0], CORE)
        if b == 1:
            others["small"] = swap(jnp.where(core[0] == 0, posts[1][1], posts[0][1]), CORE)

    def op_gn():
        parts = tie(posts[0][0], posts[1][0], scans[0][2], scans[1][2])
        grad_projected = jnp.concatenate([v.astype(BF16) for v in parts], axis=1)
        grad_normed = dot(grad_projected, in_weight, ((1,), (1,)))
        x = tok.astype(F32)
        inv = lax.rsqrt(jnp.mean(x * x, axis=1, keepdims=True) + EPS)
        unit = x * inv
        grad_unit = grad_normed * norm_gain
        state["grad_tokens"] = cot.astype(F32) + inv * (
            grad_unit - unit * jnp.mean(grad_unit * unit, axis=1, keepdims=True)
        )
        done(state["grad_tokens"])

    def op_mixed():
        b0, b1 = tie(scans[0][0], scans[1][0])
        live = (jnp.arange(length) < lengths[0])[:, None]
        total = dot(jnp.concatenate([b0, b1], axis=1), out_weight)
        state["mixed"] = (tok.astype(F32) + jnp.where(live, total, 0.0)).astype(BF16)
        done(state["mixed"])

    def op_put(p, pieces):
        arrays, targets = tie([v[0] for v in pieces], state["targets"])
        pieces = [(a,) + v[1:] for a, v in zip(arrays, pieces)]
        state["targets"] = put(targets, pieces, spans[p], sets[p].flags())
        done(state["targets"][0])

    for name in SEQUENCE:
        if name[0] == "p" and name[2] == ".":
            p, what = int(name[1]), name[3:]
            if what == "f":
                sets[p].fold()
            elif what == "e":
                sets[p].finish()
            elif what == "w":
                sets[p].widen()
            else:
                op_put(p, sets[p].own() if what == "own" else sets[p].arrived())
        elif name[-1] in "012":
            {"scan": op_scan, "out": op_out, "back": op_back, "post": op_post}[name[:-1]](int(name[-1]))
        else:
            {"front": op_front, "mix": op_mix, "gn": op_gn, "mixed": op_mixed}[name]()

    grad_in, grad_out, small = state["targets"]
    grad_gain = jnp.sum(grad_in * in_weight.astype(F32), axis=1) / norm_gain
    small = jnp.concatenate([small[:used], small[used:]], axis=1)
    ends = [sum(sizes[: i + 1]) for i in range(len(sizes))]
    cut = [small[e - n : e] for e, n in zip(ends, sizes)]
    return (
        state["mixed"][None], state["grad_tokens"][None],
        grad_gain, grad_in, cut[4][:taps], cut[4][taps], cut[0].T, cut[1], cut[3][0],
        cut[2], cut[3][1], grad_out,
    )


def solution(mesh):
    rows = P(("dp", "rep"), None, None)
    return jax.shard_map(
        shards,
        mesh=mesh,
        in_specs=(rows, rows, P(("dp", "rep"))) + (P(),) * 10,
        out_specs=(rows, rows) + (P(),) * 10,
        check_vma=False,
    )
```

time: 4900 us -> 497 us (0.10)
  local copies, waits for them, and re-layouts: 2500 us -> 28.9 us
  other arithmetic: 1210 us -> 75.4 us
  waiting for transfers between devices: 1040 us -> 127 us
  Pallas kernels: 0 us -> 169 us
  starting transfers between devices: 0.16 us -> 75.2 us
    pad x265 -> x0, local copies, waits for them, and re-layouts: 2100 us -> none  [scan_block(): totals = lax.associative_scan(combine_pairs, (factors, drives), axis=0)[1]]
    unnamed x7 -> x0, waiting for transfers between devices: 891 us -> none
    add x120 -> x63, other arithmetic: 374 us -> 50.4 us  [the longest x62 49 us: part(): return sum(values[1:], values[0])]
    add_any x60 -> x0, other arithmetic: 264 us -> none  [the longest x25 196 us: combine_pairs(): return (earlier[0] * later[0], later[0] * earlier[1] + later[1])]
    mul x75 -> x0, other arithmetic: 190 us -> none  [the longest x50 142 us: combine_pairs(): return (earlier[0] * later[0], later[0] * earlier[1] + later[1])]
    pallas_call x0 -> x19, Pallas kernels: none -> 169 us  [the longest x2 56.6 us: back(): pl.pallas_call(back_kernel, grid=(1,), in_specs=[whole(mp.shape), col(len...]
    reduce_sum x23 -> x2, other arithmetic: 175 us -> 9.19 us  [the longest x1 8.97 us: shards(): grad_gain = jnp.sum(grad_in * in_weight.astype(F32), axis=1) / norm_gain]
    all_gather x1 -> x0, waiting for transfers between devices: 153 us -> none  [shards(): summed = lax.all_gather(partial_back, 'rep', axis=0, tiled=True)]
  transfers between devices with their start and end apart: 4 -> 87, of which waited for: 4 -> 31; matrix products, arithmetic and copies ran while one was open for 0% -> 15% of each run, Pallas kernels for 0% -> 21%
where the time goes in v1:
time: 497 us; the launch traced here: 487 us
  Pallas kernels  169 us (34%)
  waiting for transfers between devices  127 us (26%)
  other arithmetic  75.4 us (15%)
  starting transfers between devices  75.2 us (15%)
  local copies, waits for them, and re-layouts  28.9 us (6%)
  matrix products  8.77 us (2%)
    ppermute x87, waiting for transfers between devices, swap(): return lax.ppermute(value, axis, [(i, i ^ 1 << place) for i in range(size)])  127 us
    ppermute x87, starting transfers between devices, swap(): return lax.ppermute(value, axis, [(i, i ^ 1 << place) for i in range(size)])  75.2 us
    pallas_call x2, Pallas kernels, back(): pl.pallas_call(back_kernel, grid=(1,), in_specs=[whole(mp.shape), col(len...  56.6 us
    add x62, other arithmetic, part(): return sum(values[1:], values[0])  49 us
    pallas_call x2, Pallas kernels, scan(): pl.pallas_call(scan_kernel, grid=(1,), in_specs=[pl.BlockSpec(memory_spac...  34.5 us
    pallas_call x6, Pallas kernels, put(): pl.pallas_call(body, out_shape=[jax.ShapeDtypeStruct(t.shape, F32) for t...  31 us
    pallas_call x3, Pallas kernels, outer(): pl.pallas_call(body, out_shape=jax.ShapeDtypeStruct((rows, cols), F32), g...  24.3 us
    unnamed x121, local copies, waits for them, and re-layouts  16.7 us
  transfers between devices with their start and end apart: 87, of which 31 were waited for; matrix products, arithmetic and copies ran while one was open for 15% of the time, Pallas kernels for 21%

profile of v1, /device:TPU:0, one launch (start us, length us, event | category | flops | bytes accessed | tf_op | source)
XLA Modules:
  0.0 487.1 jit_solution(11426537009400879462)
XLA Ops:
  1.9 9.9 %front.1 = (bf16[320,1024]{1,0:T(8,128)(2,1)}, f32[320,512]{1,0:T(8,128)}, f32[320,1024]{1,0:T(8,128)}, f32[320,2048]{1,0:T(8,128)}, bf16[320,2048]{1,0:T(8,128)(2,1)}, /*index=5*/f32[320,96]{1,0:T(8,128)}) custom-call(s32[2]{0:T(128)} %pad_add_fusion.len_ref, bf16[320,1024]{1,0:T(8,128)(2,1)} %bitcast.43, bf16[320,1024]{1,0:T(8,128)(2,1)} %bitcast.51, ...), custom_call_target="tpu_custom_call" | custom-call | tf_op jit(solution)/shard_map/front/pallas_call | solution.py:75
  12.4 17.2 %scan0.1 = (bf16[320,1024]{1,0:T(8,128)(2,1)}, f32[320,512]{1,0:T(8,128)}, f32[320,1024]{1,0:T(8,128)}, f32[2560,128]{1,0:T(8,128)}, f32[2560,128]{1,0:T(8,128)}, /*index=5*/f32[2560,128]{1,0:T(8,128)}) custom-call(s32[1]{0:T(128)} %bitcast.2.core_ref.ix, f32[320,96]{1,0:T(8,128)} %get-tuple-element.413.mp_ref, ...), custom_call_target="tpu_custom_call" | custom-call | tf_op jit(solution)/shard_map/scan0/pallas_call | solution.py:216
  30.7 6.2 %collective-permute-done.refs_1_ = f32[320,512]{1,0:T(8,128)} collective-permute-done((f32[320,512]{1,0:T(8,128)}, f32[320,512]{1,0:T(8,128)}, u32[]{:S(2)}, u32[]{:S(2)}) %collective-permute-start) | collective-permute-done | bytes 655392 | tf_op jit(solution)/shard_map/ppermute | solution.py:585
  38.2 7.7 %outer.3 = f32[1056,1024]{1,0:T(8,128)} custom-call(s32[1]{0:T(128)} %bitcast.2.core_ref.ix, bf16[320,1024]{1,0:T(8,128)(2,1)} %get-tuple-element.636.refs_0_, f32[320,512]{1,0:T(8,128)} %collective-permute-done.refs_1_, f32[320,1024]{1,0:T(8,128)} %get-tuple-element.364.og_ref.refs_2_, f32[320,1024]{1,0:T(8,128)} %copy-done.6, ...), custom_call_target="tpu_custom_call" | custom-call | tf_op jit(solution)/shard_map/outer/pallas_call | solution.py:509
  45.9 3.0 constant_dynamic-slice_fusion.6
  48.8 17.3 %scan1.1 = (bf16[320,1024]{1,0:T(8,128)(2,1)}, f32[320,512]{1,0:T(8,128)}, f32[320,1024]{1,0:T(8,128)}, f32[2560,128]{1,0:T(8,128)}, f32[2560,128]{1,0:T(8,128)}, /*index=5*/f32[2560,128]{1,0:T(8,128)}) custom-call(s32[1]{0:T(128)} %bitcast.2.core_ref.ix, f32[320,96]{1,0:T(8,128)} %get-tuple-element.413.mp_ref, ...), custom_call_target="tpu_custom_call" | custom-call | tf_op jit(solution)/shard_map/scan1/pallas_call | solution.py:216
  66.7 2.9 collective-permute-start.4
  71.1 1.6 collective-permute-start.6
  74.2 7.7 %outer.4 = f32[1056,1024]{1,0:T(8,128)} custom-call(s32[1]{0:T(128)} %bitcast.2.core_ref.ix, bf16[320,1024]{1,0:T(8,128)(2,1)} %get-tuple-element.637.refs_0_, f32[320,512]{1,0:T(8,128)} %copy-done.37, f32[320,1024]{1,0:T(8,128)} %get-tuple-element.364.og_ref.refs_2_, f32[320,1024]{1,0:T(8,128)} %copy-done.6, ...), custom_call_target="tpu_custom_call" | custom-call | tf_op jit(solution)/shard_map/outer/pallas_call | solution.py:509
  81.9 2.6 constant_dynamic-slice_fusion.3
  84.5 1.8 collective-permute-done.4
  90.7 1.9 dynamic-slice_add_fusion.16
  92.6 1.6 collective-permute-start.13
  94.2 1.9 dynamic-slice_add_fusion.17
  102.6 28.2 %back0.1 = (f32[320,1024]{1,0:T(8,128)}, bf16[320,1024]{1,0:T(8,128)(2,1)}, f32[320,64]{1,0:T(8,128)}, f32[64,1024]{1,0:T(8,128)}, f32[320,128]{1,0:T(8,128)}, /*index=5*/f32[16,8,128]{2,1,0:T(8,128)}, f32[2,1024]{1,0:T(2,128)}) custom-call(f32[320,96]{1,0:T(8,128)} %get-tuple-element.413.mp_ref, bf16[320,2048]{1,0:T(8,128)(2,1)} %get-tuple-element.345.act_ref, ...), custom_call_target="tpu_custom_call" | custom-call | tf_op jit(solution)/shard_map/back0/pallas_call | solution.py:387
  133.6 1.6 dynamic-slice_add_fusion.34
  135.6 1.7 dynamic-slice_add_fusion.35
  140.2 1.8 collective-permute-start.18
  142.0 1.9 dynamic-slice_add_fusion.9
  143.9 1.9 dynamic-slice_add_fusion.10
  150.3 28.4 %back1.1 = (f32[320,1024]{1,0:T(8,128)}, bf16[320,1024]{1,0:T(8,128)(2,1)}, f32[320,64]{1,0:T(8,128)}, f32[64,1024]{1,0:T(8,128)}, f32[320,128]{1,0:T(8,128)}, /*index=5*/f32[16,8,128]{2,1,0:T(8,128)}, f32[2,1024]{1,0:T(2,128)}) custom-call(f32[320,96]{1,0:T(8,128)} %get-tuple-element.413.mp_ref, bf16[320,2048]{1,0:T(8,128)(2,1)} %get-tuple-element.345.act_ref, ...), custom_call_target="tpu_custom_call" | custom-call | tf_op jit(solution)/shard_map/back1/pallas_call | solution.py:387
  184.2 2.6 collective-permute-start.27
  186.8 1.6 dynamic-slice_add_fusion.49
  191.5 2.1 collective-permute-done.27
  199.2 2.7 collective-permute-start.24
  202.9 6.4 %post0.1 = (f32[320,1024]{1,0:T(8,128)}, f32[184,1024]{1,0:T(8,128)}) custom-call(bf16[320,96]{1,0:T(8,128)(2,1)} %pad_maximum_fusion.6.gmix_ref, f32[2560,128]{1,0:T(8,128)} %get-tuple-element.384.gs_ref, f32[320,1024]{1,0:T(8,128)} %get-tuple-element.388.gact_ref, bf16[320,2048]{1,0:T(8,128)(2,1)} %get-tuple-element.345.act_ref, ...), custom_call_target="tpu_custom_call" | custom-call | tf_op jit(solution)/shard_map/post0/pallas_call | solution.py:457
  209.3 6.3 %post1.1 = (f32[320,1024]{1,0:T(8,128)}, f32[184,1024]{1,0:T(8,128)}) custom-call(bf16[320,96]{1,0:T(8,128)(2,1)} %pad_maximum_fusion.6.gmix_ref, f32[2560,128]{1,0:T(8,128)} %get-tuple-element.415.gs_ref, f32[320,1024]{1,0:T(8,128)} %get-tuple-element.419.gact_ref, bf16[320,2048]{1,0:T(8,128)(2,1)} %get-tuple-element.345.act_ref, ...), custom_call_target="tpu_custom_call" | custom-call | tf_op jit(solution)/shard_map/post1/pallas_call | solution.py:457
  217.5 1.6 collective-permute-start.33
  226.2 12.9 %collective-permute-done.33 = f32[66,1024]{1,0:T(8,128)S(1)} collective-permute-done((f32[66,1024]{1,0:T(8,128)S(1)}, f32[66,1024]{1,0:T(8,128)S(1)}, u32[]{:S(2)}, u32[]{:S(2)}) %collective-permute-start.33) | collective-permute-done | bytes 270368 | tf_op jit(solution)/shard_map/ppermute | solution.py:585
  239.2 6.2 %collective-permute-done.31 = f32[66,1024]{1,0:T(8,128)S(1)} collective-permute-done((f32[66,1024]{1,0:T(8,128)S(1)}, f32[66,1024]{1,0:T(8,128)S(1)}, u32[]{:S(2)}, u32[]{:S(2)}) %collective-permute-start.31) | collective-permute-done | bytes 270368 | tf_op jit(solution)/shard_map/ppermute | solution.py:585
  247.3 8.8 %outer.5 = f32[1248,1024]{1,0:T(8,128)} custom-call(s32[1]{0:T(128)} %bitcast.2.core_ref.ix, bf16[320,1024]{1,0:T(8,128)(2,1)} %get-tuple-element.479.normed_ref.refs_4_.refs_0_, f32[320,512]{1,0:T(8,128)} %copy-done.2, f32[320,1024]{1,0:T(8,128)} %get-tuple-element.550.refs_2_, f32[320,1024]{1,0:T(8,128)} %copy-done.22, ...), custom_call_target="tpu_custom_call" | custom-call | tf_op jit(solution)/shard_map/outer/pallas_call | solution.py:509
  256.2 2.0 constant_dynamic-slice_fusion
  260.4 2.8 collective-permute-start.32
  264.1 20.7 %collective-permute-done.32 = f32[66,1024]{1,0:T(8,128)S(1)} collective-permute-done((f32[66,1024]{1,0:T(8,128)S(1)}, f32[66,1024]{1,0:T(8,128)S(1)}, u32[]{:S(2)}, u32[]{:S(2)}) %collective-permute-start.32) | collective-permute-done | bytes 270368 | tf_op jit(solution)/shard_map/ppermute | solution.py:585
  285.6 1.9 collective-permute-start.40
  292.4 2.5 collective-permute-start.35
  295.0 1.6 collective-permute-start.34
  296.7 1.7 collective-permute-start.48
  299.3 6.4 %collective-permute-done.36 = f32[104,1024]{1,0:T(8,128)S(1)} collective-permute-done((f32[104,1024]{1,0:T(8,128)S(1)}, f32[104,1024]{1,0:T(8,128)S(1)}, u32[]{:S(2)}, u32[]{:S(2)}) %collective-permute-start.36) | collective-permute-done | bytes 426016 | tf_op jit(solution)/shard_map/ppermute | solution.py:585
  308.2 1.8 collective-permute-start.54
  316.0 1.8 collective-permute-start.43
  318.1 1.8 copy-done.5
  322.8 4.2 fusion.14
  334.0 1.7 collective-permute-start.49
  337.1 2.0 collective-permute-start.62
  339.1 1.7 dynamic-slice_add_fusion.36
  340.8 11.2 %collective-permute-done.49 = f32[78,1024]{1,0:T(8,128)} collective-permute-done((f32[78,1024]{1,0:T(8,128)}, f32[78,1024]{1,0:T(8,128)}, u32[]{:S(2)}, u32[]{:S(2)}) %collective-permute-start.49) | collective-permute-done | bytes 319520 | tf_op jit(solution)/shard_map/ppermute | solution.py:585
  352.6 1.6 dynamic-slice_add_fusion.37
  354.2 1.6 dynamic-slice_add_fusion.38
  358.5 2.2 maximum_select_fusion.7.refs_4_
  363.6 7.5 %collective-permute-done.61.refs_4_ = f32[176,1024]{1,0:T(8,128)S(1)} collective-permute-done((f32[176,1024]{1,0:T(8,128)S(1)}, f32[176,1024]{1,0:T(8,128)S(1)}, u32[]{:S(2)}, u32[]{:S(2)}) %collective-permute-start.61) | collective-permute-done | bytes 720928 | tf_op jit(solution)/shard_map/ppermute | solution.py:585
  373.0 1.8 fusion.32
  374.8 5.1 %put.6 = (f32[1024,4096]{1,0:T(8,128)}, f32[2048,1024]{1,0:T(8,128)}, f32[368,1024]{1,0:T(8,128)}) custom-call(s32[8]{0:T(128)} %stack.23.flag_ref, f32[1024,4096]{1,0:T(8,128)} %blank.3.refs_0_, f32[2048,1024]{1,0:T(8,128)} %blank.4.refs_1_, f32[368,1024]{1,0:T(8,128)} %blank.5.refs_2_, ...), custom_call_target="tpu_custom_call", output_to_operand_aliasing={{0}: (1, {}), {1}: (2, {}), {2}: (3, {})} | custom-call | tf_op jit(solution)/shard_map/put/pallas_call | solution.py:557
  385.1 3.5 collective-permute-done.69.refs_3_
  388.6 12.4 %collective-permute-done.56 = f32[78,1024]{1,0:T(8,128)S(1)} collective-permute-done((f32[78,1024]{1,0:T(8,128)S(1)}, f32[78,1024]{1,0:T(8,128)S(1)}, u32[]{:S(2)}, u32[]{:S(2)}) %collective-permute-start.56) | collective-permute-done | bytes 319520 | tf_op jit(solution)/shard_map/ppermute | solution.py:585
  404.1 4.9 %put.7 = (f32[1024,4096]{1,0:T(8,128)}, f32[2048,1024]{1,0:T(8,128)}, f32[368,1024]{1,0:T(8,128)}) custom-call(s32[8]{0:T(128)} %stack.23.flag_ref, f32[1024,4096]{1,0:T(8,128)} %get-tuple-element.590.refs_0_, f32[2048,1024]{1,0:T(8,128)} %get-tuple-element.591.refs_1_, ...), custom_call_target="tpu_custom_call", output_to_operand_aliasing={{0}: (1, {}), {1}: (2, {}), {2}: (3, {})} | custom-call | tf_op jit(solution)/shard_map/put/pallas_call | solution.py:557
  409.1 5.1 %put.8 = (f32[1024,4096]{1,0:T(8,128)}, f32[2048,1024]{1,0:T(8,128)}, f32[368,1024]{1,0:T(8,128)}) custom-call(s32[8]{0:T(128)} %stack.23.flag_ref, f32[1024,4096]{1,0:T(8,128)} %get-tuple-element.602.refs_0_, f32[2048,1024]{1,0:T(8,128)} %get-tuple-element.603.refs_1_, ...), custom_call_target="tpu_custom_call", output_to_operand_aliasing={{0}: (1, {}), {1}: (2, {}), {2}: (3, {})} | custom-call | tf_op jit(solution)/shard_map/put/pallas_call | solution.py:557
  417.6 4.9 %put.9 = (f32[1024,4096]{1,0:T(8,128)}, f32[2048,1024]{1,0:T(8,128)}, f32[368,1024]{1,0:T(8,128)}) custom-call(s32[8]{0:T(128)} %stack.23.flag_ref, f32[1024,4096]{1,0:T(8,128)} %get-tuple-element.620.refs_0_, f32[2048,1024]{1,0:T(8,128)} %get-tuple-element.621.refs_1_, ...), custom_call_target="tpu_custom_call", output_to_operand_aliasing={{0}: (1, {}), {1}: (2, {}), {2}: (3, {})} | custom-call | tf_op jit(solution)/shard_map/put/pallas_call | solution.py:557
  426.6 4.6 fusion.13
  431.2 3.7 collective-permute-done.77
  440.8 17.0 %collective-permute-done.80.refs_5_ = f32[208,1024]{1,0:T(8,128)S(1)} collective-permute-done((f32[208,1024]{1,0:T(8,128)S(1)}, f32[208,1024]{1,0:T(8,128)S(1)}, u32[]{:S(2)}, u32[]{:S(2)}) %collective-permute-start.80) | collective-permute-done | bytes 852000 | tf_op jit(solution)/shard_map/ppermute | solution.py:585
  461.0 5.5 %put.10 = (f32[1024,4096]{1,0:T(8,128)}, f32[2048,1024]{1,0:T(8,128)}, f32[368,1024]{1,0:T(8,128)}) custom-call(s32[8]{0:T(128)} %stack.23.flag_ref, f32[1024,4096]{1,0:T(8,128)} %get-tuple-element.646.refs_0_, f32[2048,1024]{1,0:T(8,128)} %get-tuple-element.647.refs_1_, ...), custom_call_target="tpu_custom_call", output_to_operand_aliasing={{0}: (1, {}), {1}: (2, {}), {2}: (3, {})} | custom-call | tf_op jit(solution)/shard_map/put/pallas_call | solution.py:557
  466.5 5.4 %put.11 = (f32[1024,4096]{1,0:T(8,128)}, f32[2048,1024]{1,0:T(8,128)}, f32[368,1024]{1,0:T(8,128)}) custom-call(s32[8]{0:T(128)} %stack.23.flag_ref, f32[1024,4096]{1,0:T(8,128)} %get-tuple-element.658.refs_0_, f32[2048,1024]{1,0:T(8,128)} %get-tuple-element.659.refs_1_, ...), custom_call_target="tpu_custom_call", output_to_operand_aliasing={{0}: (1, {}), {1}: (2, {}), {2}: (3, {})} | custom-call | tf_op jit(solution)/shard_map/put/pallas_call | solution.py:557
  477.1 9.0 %multiply_reduce_fusion = f32[1024]{0:T(1024)S(1)} fusion(f32[1024,4096]{1,0:T(8,128)} %get-tuple-element.332, bf16[1024,4096]{1,0:T(8,128)(2,1)} %wg_ref.3), kind=kLoop, calls=%fused_computation | loop fusion | flops 12581888 | bytes 25169920 | tf_op jit(solution)/shard_map/reduce_sum | solution.py:867
  (380 shorter events, 123.0 us)
Async XLA Ops:
  66.7 19.6 %collective-permute-start.4 = (f32[176,1024]{1,0:T(8,128)}, f32[176,1024]{1,0:T(8,128)}, u32[]{:S(2)}, u32[]{:S(2)}) collective-permute-start(f32[176,1024]{1,0:T(8,128)} %get-tuple-element.678), channel_id=1, source_target_pairs={{0,4},{4,0},{8,12},{12,8},{16,20},{20,16},{24,28},{28,24},{1,5},{5... | collective-permute-start | bytes 2162696 | tf_op jit(solution)/shard_map/ppermute | solution.py:585
  69.5 18.2 %collective-permute-start.5 = (f32[176,1024]{1,0:T(8,128)}, f32[176,1024]{1,0:T(8,128)}, u32[]{:S(2)}, u32[]{:S(2)}) collective-permute-start(f32[176,1024]{1,0:T(8,128)} %get-tuple-element.677), channel_id=1, source_target_pairs={{0,2},{1,3},{2,0},{3,1},{4,6},{5,7},{6,4},{7,5},{8,10},{9,11},{10,... | collective-permute-start | bytes 2162696 | tf_op jit(solution)/shard_map/ppermute | solution.py:585
  71.1 17.9 %collective-permute-start.6 = (f32[176,1024]{1,0:T(8,128)}, f32[176,1024]{1,0:T(8,128)}, u32[]{:S(2)}, u32[]{:S(2)}) collective-permute-start(f32[176,1024]{1,0:T(8,128)} %get-tuple-element.676), channel_id=1, source_target_pairs={{0,8},{4,12},{8,0},{12,4},{16,24},{20,28},{24,16},{28,20},{1,9},{5... | collective-permute-start | bytes 2162696 | tf_op jit(solution)/shard_map/ppermute | solution.py:585
  92.6 39.7 %collective-permute-start.13 = (f32[88,1024]{1,0:T(8,128)}, f32[88,1024]{1,0:T(8,128)}, u32[]{:S(2)}, u32[]{:S(2)}) collective-permute-start(f32[88,1024]{1,0:T(8,128)} %dynamic-slice_add_fusion.16), channel_id=1, source_target_pairs={{0,8},{4,12},{8,0},{12,4},{16,24},{20,28},{24,16},{28,20},{1,9},{5... | collective-permute-start | bytes 1081352 | tf_op jit(solution)/shard_map/ppermute | solution.py:585
  96.0 36.3 %collective-permute-start.12 = (f32[88,1024]{1,0:T(8,128)}, f32[88,1024]{1,0:T(8,128)}, u32[]{:S(2)}, u32[]{:S(2)}) collective-permute-start(f32[88,1024]{1,0:T(8,128)} %dynamic-slice_add_fusion.17), channel_id=1, source_target_pairs={{0,2},{1,3},{2,0},{3,1},{4,6},{5,7},{6,4},{7,5},{8,10},{9,11},{10,... | collective-permute-start | bytes 1081352 | tf_op jit(solution)/shard_map/ppermute | solution.py:585
  96.5 43.6 %collective-permute-start.10 = (f32[176,1024]{1,0:T(8,128)}, f32[176,1024]{1,0:T(8,128)}, u32[]{:S(2)}, u32[]{:S(2)}) collective-permute-start(f32[176,1024]{1,0:T(8,128)} %get-tuple-element.674), channel_id=1, source_target_pairs={{0,2},{1,3},{2,0},{3,1},{4,6},{5,7},{6,4},{7,5},{8,10},{9,11},{10,... | collective-permute-start | bytes 2162696 | tf_op jit(solution)/shard_map/ppermute | solution.py:585
  98.1 43.9 %collective-permute-start.11 = (f32[176,1024]{1,0:T(8,128)S(1)}, f32[176,1024]{1,0:T(8,128)}, u32[]{:S(2)}, u32[]{:S(2)}) collective-permute-start(f32[176,1024]{1,0:T(8,128)S(1)} %get-tuple-element.673), channel_id=1, source_target_pairs={{0,8},{4,12},{8,0},{12,4},{16,24},{20,28},{24,16},{28,20},{1,9},{5... | collective-permute-start | bytes 2162696 | tf_op jit(solution)/shard_map/ppermute | solution.py:585
  99.9 42.1 %collective-permute-start.9 = (f32[176,1024]{1,0:T(8,128)S(1)}, f32[176,1024]{1,0:T(8,128)}, u32[]{:S(2)}, u32[]{:S(2)}) collective-permute-start(f32[176,1024]{1,0:T(8,128)S(1)} %get-tuple-element.675), channel_id=1, source_target_pairs={{0,4},{4,0},{8,12},{12,8},{16,20},{20,16},{24,28},{28,24},{1,5},{5... | collective-permute-start | bytes 2162696 | tf_op jit(solution)/shard_map/ppermute | solution.py:585
  133.0 45.7 %collective-permute-start.20 = (f32[44,1024]{1,0:T(8,128)}, f32[44,1024]{1,0:T(8,128)S(1)}, u32[]{:S(2)}, u32[]{:S(2)}) collective-permute-start(f32[44,1024]{1,0:T(8,128)} %dynamic-slice_add_fusion.33), channel_id=1, source_target_pairs={{0,2},{1,3},{2,0},{3,1},{4,6},{5,7},{6,4},{7,5},{8,10},{9,11},{10,... | collective-permute-start | bytes 540680 | tf_op jit(solution)/shard_map/ppermute | solution.py:585
  135.2 43.5 %collective-permute-start.19 = (f32[44,1024]{1,0:T(8,128)}, f32[44,1024]{1,0:T(8,128)}, u32[]{:S(2)}, u32[]{:S(2)}) collective-permute-start(f32[44,1024]{1,0:T(8,128)} %dynamic-slice_add_fusion.34), channel_id=1, source_target_pairs={{0,4},{4,0},{8,12},{12,8},{16,20},{20,16},{24,28},{28,24},{1,5},{5... | collective-permute-start | bytes 540680 | tf_op jit(solution)/shard_map/ppermute | solution.py:585
  140.2 38.5 %collective-permute-start.18 = (f32[44,1024]{1,0:T(8,128)}, f32[44,1024]{1,0:T(8,128)}, u32[]{:S(2)}, u32[]{:S(2)}) collective-permute-start(f32[44,1024]{1,0:T(8,128)} %dynamic-slice_add_fusion.35), channel_id=1, source_target_pairs={{0,8},{4,12},{8,0},{12,4},{16,24},{20,28},{24,16},{28,20},{1,9},{5... | collective-permute-start | bytes 540680 | tf_op jit(solution)/shard_map/ppermute | solution.py:585
  180.7 12.9 %collective-permute-start.17 = (f32[88,1024]{1,0:T(8,128)}, f32[88,1024]{1,0:T(8,128)S(1)}, u32[]{:S(2)}, u32[]{:S(2)}) collective-permute-start(f32[88,1024]{1,0:T(8,128)} %dynamic-slice_add_fusion.9), channel_id=1, source_target_pairs={{0,4},{4,0},{8,12},{12,8},{16,20},{20,16},{24,28},{28,24},{1,5},{5... | collective-permute-start | bytes 1081352 | tf_op jit(solution)/shard_map/ppermute | solution.py:585
  182.2 12.8 %collective-permute-start.16 = (f32[88,1024]{1,0:T(8,128)}, f32[88,1024]{1,0:T(8,128)S(1)}, u32[]{:S(2)}, u32[]{:S(2)}) collective-permute-start(f32[88,1024]{1,0:T(8,128)} %dynamic-slice_add_fusion.10), channel_id=1, source_target_pairs={{0,8},{4,12},{8,0},{12,4},{16,24},{20,28},{24,16},{28,20},{1,9},{5... | collective-permute-start | bytes 1081352 | tf_op jit(solution)/shard_map/ppermute | solution.py:585
  182.7 12.4 %collective-permute-start.15 = (f32[88,1024]{1,0:T(8,128)S(1)}, f32[88,1024]{1,0:T(8,128)S(1)}, u32[]{:S(2)}, u32[]{:S(2)}) collective-permute-start(f32[88,1024]{1,0:T(8,128)S(1)} %dynamic-slice_add_fusion.11), channel_id=1, source_target_pairs={{0,2},{1,3},{2,0},{3,1},{4,6},{5,7},{6,4},{7,5},{8,10},{9,11},{10,... | collective-permute-start | bytes 1081352 | tf_op jit(solution)/shard_map/ppermute | solution.py:585
  195.8 21.7 %collective-permute-start.26 = (f32[44,1024]{1,0:T(8,128)}, f32[44,1024]{1,0:T(8,128)}, u32[]{:S(2)}, u32[]{:S(2)}) collective-permute-start(f32[44,1024]{1,0:T(8,128)} %dynamic-slice_add_fusion.27), channel_id=1, source_target_pairs={{0,2},{1,3},{2,0},{3,1},{4,6},{5,7},{6,4},{7,5},{8,10},{9,11},{10,... | collective-permute-start | bytes 540680 | tf_op jit(solution)/shard_map/ppermute | solution.py:585
  197.9 21.2 %collective-permute-start.25 = (f32[44,1024]{1,0:T(8,128)}, f32[44,1024]{1,0:T(8,128)}, u32[]{:S(2)}, u32[]{:S(2)}) collective-permute-start(f32[44,1024]{1,0:T(8,128)} %dynamic-slice_add_fusion.28), channel_id=1, source_target_pairs={{0,4},{4,0},{8,12},{12,8},{16,20},{20,16},{24,28},{28,24},{1,5},{5... | collective-permute-start | bytes 540680 | tf_op jit(solution)/shard_map/ppermute | solution.py:585
  199.2 19.9 %collective-permute-start.24 = (f32[44,1024]{1,0:T(8,128)}, f32[44,1024]{1,0:T(8,128)}, u32[]{:S(2)}, u32[]{:S(2)}) collective-permute-start(f32[44,1024]{1,0:T(8,128)} %dynamic-slice_add_fusion.29), channel_id=1, source_target_pairs={{0,8},{4,12},{8,0},{12,4},{16,24},{20,28},{24,16},{28,20},{1,9},{5... | collective-permute-start | bytes 540680 | tf_op jit(solution)/shard_map/ppermute | solution.py:585
  209.3 36.2 %collective-permute-start.21 = (f32[320,1024]{1,0:T(8,128)}, f32[320,1024]{1,0:T(8,128)S(1)}, u32[]{:S(2)}, u32[]{:S(2)}) collective-permute-start(f32[320,1024]{1,0:T(8,128)} %get-tuple-element.550.refs_2_), channel_id=1, source_target_pairs={{0,1},{1,0},{2,3},{3,2},{4,5},{5,4},{6,7},{7,6},{8,9},{9,8},{10,11... | collective-permute-start | bytes 3932168 | tf_op jit(solution)/shard_map/ppermute | solution.py:585
  215.6 29.8 %collective-permute-start.22 = (f32[320,1024]{1,0:T(8,128)}, f32[320,1024]{1,0:T(8,128)}, u32[]{:S(2)}, u32[]{:S(2)}) collective-permute-start(f32[320,1024]{1,0:T(8,128)} %get-tuple-element.551.refs_6_), channel_id=1, source_target_pairs={{0,1},{1,0},{2,3},{3,2},{4,5},{5,4},{6,7},{7,6},{8,9},{9,8},{10,11... | collective-permute-start | bytes 3932168 | tf_op jit(solution)/shard_map/ppermute | solution.py:585
  217.5 21.6 %collective-permute-start.33 = (f32[66,1024]{1,0:T(8,128)S(1)}, f32[66,1024]{1,0:T(8,128)S(1)}, u32[]{:S(2)}, u32[]{:S(2)}) collective-permute-start(f32[66,1024]{1,0:T(8,128)S(1)} %pad_maximum_fusion.5), channel_id=1, source_target_pairs={{0,16},{4,20},{8,24},{12,28},{16,0},{20,4},{24,8},{28,12},{1,17},{... | collective-permute-start | bytes 811016 | tf_op jit(solution)/shard_map/ppermute | solution.py:585
  219.1 26.3 %collective-permute-start.23 = (f32[184,1024]{1,0:T(8,128)S(1)}, f32[184,1024]{1,0:T(8,128)S(1)}, u32[]{:S(2)}, u32[]{:S(2)}) collective-permute-start(f32[184,1024]{1,0:T(8,128)S(1)} %broadcast_select_fusion), channel_id=1, source_target_pairs={{0,1},{1,0},{2,3},{3,2},{4,5},{5,4},{6,7},{7,6},{8,9},{9,8},{10,11... | collective-permute-start | bytes 2261000 | tf_op jit(solution)/shard_map/ppermute | solution.py:585
  222.0 23.4 %collective-permute-start.31 = (f32[66,1024]{1,0:T(8,128)S(1)}, f32[66,1024]{1,0:T(8,128)S(1)}, u32[]{:S(2)}, u32[]{:S(2)}) collective-permute-start(f32[66,1024]{1,0:T(8,128)S(1)} %pad_maximum_fusion.3), channel_id=1, source_target_pairs={{0,16},{4,20},{8,24},{12,28},{16,0},{20,4},{24,8},{28,12},{1,17},{... | collective-permute-start | bytes 811016 | tf_op jit(solution)/shard_map/ppermute | solution.py:585
  258.2 27.4 %collective-permute-start.28 = (f32[208,1024]{1,0:T(8,128)S(1)}, f32[208,1024]{1,0:T(8,128)S(1)}, u32[]{:S(2)}, u32[]{:S(2)}) collective-permute-start(f32[208,1024]{1,0:T(8,128)S(1)} %get-tuple-element.672), channel_id=1, source_target_pairs={{0,4},{4,0},{8,12},{12,8},{16,20},{20,16},{24,28},{28,24},{1,5},{5... | collective-permute-start | bytes 2555912 | tf_op jit(solution)/shard_map/ppermute | solution.py:585
  259.7 27.7 %collective-permute-start.29 = (f32[208,1024]{1,0:T(8,128)S(1)}, f32[208,1024]{1,0:T(8,128)S(1)}, u32[]{:S(2)}, u32[]{:S(2)}) collective-permute-start(f32[208,1024]{1,0:T(8,128)S(1)} %get-tuple-element.671), channel_id=1, source_target_pairs={{0,2},{1,3},{2,0},{3,1},{4,6},{5,7},{6,4},{7,5},{8,10},{9,11},{10,... | collective-permute-start | bytes 2555912 | tf_op jit(solution)/shard_map/ppermute | solution.py:585
  260.3 28.4 %collective-permute-start.30 = (f32[208,1024]{1,0:T(8,128)S(1)}, f32[208,1024]{1,0:T(8,128)S(1)}, u32[]{:S(2)}, u32[]{:S(2)}) collective-permute-start(f32[208,1024]{1,0:T(8,128)S(1)} %get-tuple-element.670), channel_id=1, source_target_pairs={{0,8},{4,12},{8,0},{12,4},{16,24},{20,28},{24,16},{28,20},{1,9},{5... | collective-permute-start | bytes 2555912 | tf_op jit(solution)/shard_map/ppermute | solution.py:585
  260.4 24.3 %collective-permute-start.32 = (f32[66,1024]{1,0:T(8,128)S(1)}, f32[66,1024]{1,0:T(8,128)S(1)}, u32[]{:S(2)}, u32[]{:S(2)}) collective-permute-start(f32[66,1024]{1,0:T(8,128)S(1)} %pad_maximum_fusion.4), channel_id=1, source_target_pairs={{0,16},{4,20},{8,24},{12,28},{16,0},{20,4},{24,8},{28,12},{1,17},{... | collective-permute-start | bytes 811016 | tf_op jit(solution)/shard_map/ppermute | solution.py:585
  263.3 27.3 %collective-permute-start.42 = (f32[44,1024]{1,0:T(8,128)S(1)}, f32[44,1024]{1,0:T(8,128)S(1)}, u32[]{:S(2)}, u32[]{:S(2)}) collective-permute-start(f32[44,1024]{1,0:T(8,128)S(1)} %maximum_select_fusion.23), channel_id=1, source_target_pairs={{0,2},{1,3},{2,0},{3,1},{4,6},{5,7},{6,4},{7,5},{8,10},{9,11},{10,... | collective-permute-start | bytes 540680 | tf_op jit(solution)/shard_map/ppermute | solution.py:585
  292.4 13.3 %collective-permute-start.36 = (f32[104,1024]{1,0:T(8,128)S(1)}, f32[104,1024]{1,0:T(8,128)S(1)}, u32[]{:S(2)}, u32[]{:S(2)}) collective-permute-start(f32[104,1024]{1,0:T(8,128)S(1)} %dynamic-slice_add_fusion.3), channel_id=1, source_target_pairs={{0,4},{4,0},{8,12},{12,8},{16,20},{20,16},{24,28},{28,24},{1,5},{5... | collective-permute-start | bytes 1277960 | tf_op jit(solution)/shard_map/ppermute | solution.py:585
  292.4 15.2 %collective-permute-start.35 = (f32[104,1024]{1,0:T(8,128)S(1)}, f32[104,1024]{1,0:T(8,128)S(1)}, u32[]{:S(2)}, u32[]{:S(2)}) collective-permute-start(f32[104,1024]{1,0:T(8,128)S(1)} %dynamic-slice_add_fusion.4), channel_id=1, source_target_pairs={{0,8},{4,12},{8,0},{12,4},{16,24},{20,28},{24,16},{28,20},{1,9},{5... | collective-permute-start | bytes 1277960 | tf_op jit(solution)/shard_map/ppermute | solution.py:585
  295.0 13.2 %collective-permute-start.34 = (f32[104,1024]{1,0:T(8,128)S(1)}, f32[104,1024]{1,0:T(8,128)S(1)}, u32[]{:S(2)}, u32[]{:S(2)}) collective-permute-start(f32[104,1024]{1,0:T(8,128)S(1)} %dynamic-slice_add_fusion.5), channel_id=1, source_target_pairs={{0,2},{1,3},{2,0},{3,1},{4,6},{5,7},{6,4},{7,5},{8,10},{9,11},{10,... | collective-permute-start | bytes 1277960 | tf_op jit(solution)/shard_map/ppermute | solution.py:585
  296.7 16.8 %collective-permute-start.48 = (f32[88,1024]{1,0:T(8,128)S(1)}, f32[88,1024]{1,0:T(8,128)S(1)}, u32[]{:S(2)}, u32[]{:S(2)}) collective-permute-start(f32[88,1024]{1,0:T(8,128)S(1)} %maximum_select_fusion.14), channel_id=1, source_target_pairs={{0,4},{4,0},{8,12},{12,8},{16,20},{20,16},{24,28},{28,24},{1,5},{5... | collective-permute-start | bytes 1081352 | tf_op jit(solution)/shard_map/ppermute | solution.py:585
  298.5 16.9 %collective-permute-start.47 = (f32[88,1024]{1,0:T(8,128)S(1)}, f32[88,1024]{1,0:T(8,128)S(1)}, u32[]{:S(2)}, u32[]{:S(2)}) collective-permute-start(f32[88,1024]{1,0:T(8,128)S(1)} %maximum_select_fusion.13), channel_id=1, source_target_pairs={{0,8},{4,12},{8,0},{12,4},{16,24},{20,28},{24,16},{28,20},{1,9},{5... | collective-permute-start | bytes 1081352 | tf_op jit(solution)/shard_map/ppermute | solution.py:585
  307.7 26.3 %collective-permute-start.55 = (f32[88,1024]{1,0:T(8,128)S(1)}, f32[88,1024]{1,0:T(8,128)}, u32[]{:S(2)}, u32[]{:S(2)}) collective-permute-start(f32[88,1024]{1,0:T(8,128)S(1)} %maximum_select_fusion.17), channel_id=1, source_target_pairs={{0,4},{4,0},{8,12},{12,8},{16,20},{20,16},{24,28},{28,24},{1,5},{5... | collective-permute-start | bytes 1081352 | tf_op jit(solution)/shard_map/ppermute | solution.py:585
  308.2 27.4 %collective-permute-start.54 = (f32[88,1024]{1,0:T(8,128)S(1)}, f32[88,1024]{1,0:T(8,128)S(1)}, u32[]{:S(2)}, u32[]{:S(2)}) collective-permute-start(f32[88,1024]{1,0:T(8,128)S(1)} %maximum_select_fusion.16), channel_id=1, source_target_pairs={{0,8},{4,12},{8,0},{12,4},{16,24},{20,28},{24,16},{28,20},{1,9},{5... | collective-permute-start | bytes 1081352 | tf_op jit(solution)/shard_map/ppermute | solution.py:585
  313.4 15.0 %collective-permute-start.45 = (f32[52,1024]{1,0:T(8,128)}, f32[52,1024]{1,0:T(8,128)}, u32[]{:S(2)}, u32[]{:S(2)}) collective-permute-start(f32[52,1024]{1,0:T(8,128)} %dynamic-slice_add_fusion.21), channel_id=1, source_target_pairs={{0,2},{1,3},{2,0},{3,1},{4,6},{5,7},{6,4},{7,5},{8,10},{9,11},{10,... | collective-permute-start | bytes 638984 | tf_op jit(solution)/shard_map/ppermute | solution.py:585
  315.4 14.5 %collective-permute-start.44 = (f32[52,1024]{1,0:T(8,128)}, f32[52,1024]{1,0:T(8,128)}, u32[]{:S(2)}, u32[]{:S(2)}) collective-permute-start(f32[52,1024]{1,0:T(8,128)} %dynamic-slice_add_fusion.22), channel_id=1, source_target_pairs={{0,4},{4,0},{8,12},{12,8},{16,20},{20,16},{24,28},{28,24},{1,5},{5... | collective-permute-start | bytes 638984 | tf_op jit(solution)/shard_map/ppermute | solution.py:585
  316.0 13.9 %collective-permute-start.43 = (f32[52,1024]{1,0:T(8,128)}, f32[52,1024]{1,0:T(8,128)}, u32[]{:S(2)}, u32[]{:S(2)}) collective-permute-start(f32[52,1024]{1,0:T(8,128)} %dynamic-slice_add_fusion.23), channel_id=1, source_target_pairs={{0,8},{4,12},{8,0},{12,4},{16,24},{20,28},{24,16},{28,20},{1,9},{5... | collective-permute-start | bytes 638984 | tf_op jit(solution)/shard_map/ppermute | solution.py:585
  329.9 26.0 %collective-permute-start.52 = (f32[176,1024]{1,0:T(8,128)S(1)}, f32[176,1024]{1,0:T(8,128)}, u32[]{:S(2)}, u32[]{:S(2)}) collective-permute-start(f32[176,1024]{1,0:T(8,128)S(1)} %maximum_select_fusion.5.refs_5_), channel_id=1, source_target_pairs={{0,1},{1,0},{2,3},{3,2},{4,5},{5,4},{6,7},{7,6},{8,9},{9,8},{10,11... | collective-permute-start | bytes 2162696 | tf_op jit(solution)/shard_map/ppermute | solution.py:585
  329.9 28.5 %collective-permute-start.51 = (f32[176,1024]{1,0:T(8,128)S(1)}, f32[176,1024]{1,0:T(8,128)}, u32[]{:S(2)}, u32[]{:S(2)}) collective-permute-start(f32[176,1024]{1,0:T(8,128)S(1)} %maximum_select_fusion.4.refs_4_), channel_id=1, source_target_pairs={{0,1},{1,0},{2,3},{3,2},{4,5},{5,4},{6,7},{7,6},{8,9},{9,8},{10,11... | collective-permute-start | bytes 2162696 | tf_op jit(solution)/shard_map/ppermute | solution.py:585
  334.0 18.0 %collective-permute-start.49 = (f32[78,1024]{1,0:T(8,128)}, f32[78,1024]{1,0:T(8,128)}, u32[]{:S(2)}, u32[]{:S(2)}) collective-permute-start(f32[78,1024]{1,0:T(8,128)} %pad_maximum_fusion), channel_id=1, source_target_pairs={{0,16},{4,20},{8,24},{12,28},{16,0},{20,4},{24,8},{28,12},{1,17},{... | collective-permute-start | bytes 958472 | tf_op jit(solution)/shard_map/ppermute | solution.py:585
  335.6 25.1 %collective-permute-start.50 = (f32[176,1024]{1,0:T(8,128)S(1)}, f32[176,1024]{1,0:T(8,128)}, u32[]{:S(2)}, u32[]{:S(2)}) collective-permute-start(f32[176,1024]{1,0:T(8,128)S(1)} %maximum_select_fusion.3.refs_3_), channel_id=1, source_target_pairs={{0,1},{1,0},{2,3},{3,2},{4,5},{5,4},{6,7},{7,6},{8,9},{9,8},{10,11... | collective-permute-start | bytes 2162696 | tf_op jit(solution)/shard_map/ppermute | solution.py:585
  337.1 24.6 %collective-permute-start.62 = (f32[176,1024]{1,0:T(8,128)S(1)}, f32[176,1024]{1,0:T(8,128)}, u32[]{:S(2)}, u32[]{:S(2)}) collective-permute-start(f32[176,1024]{1,0:T(8,128)S(1)} %maximum_select_fusion.5.refs_5_), channel_id=1, source_target_pairs={{0,8},{4,12},{8,0},{12,4},{16,24},{20,28},{24,16},{28,20},{1,9},{5... | collective-permute-start | bytes 2162696 | tf_op jit(solution)/shard_map/ppermute | solution.py:585
  352.0 19.1 %collective-permute-start.61 = (f32[176,1024]{1,0:T(8,128)S(1)}, f32[176,1024]{1,0:T(8,128)S(1)}, u32[]{:S(2)}, u32[]{:S(2)}) collective-permute-start(f32[176,1024]{1,0:T(8,128)S(1)} %maximum_select_fusion.4.refs_4_), channel_id=1, source_target_pairs={{0,2},{1,3},{2,0},{3,1},{4,6},{5,7},{6,4},{7,5},{8,10},{9,11},{10,... | collective-permute-start | bytes 2162696 | tf_op jit(solution)/shard_map/ppermute | solution.py:585
  355.8 26.9 %collective-permute-start.60 = (f32[176,1024]{1,0:T(8,128)S(1)}, f32[176,1024]{1,0:T(8,128)}, u32[]{:S(2)}, u32[]{:S(2)}) collective-permute-start(f32[176,1024]{1,0:T(8,128)S(1)} %maximum_select_fusion.3.refs_3_), channel_id=1, source_target_pairs={{0,4},{4,0},{8,12},{12,8},{16,20},{20,16},{24,28},{28,24},{1,5},{5... | collective-permute-start | bytes 2162696 | tf_op jit(solution)/shard_map/ppermute | solution.py:585
  358.4 24.5 %collective-permute-start.59 = (f32[176,1024]{1,0:T(8,128)S(1)}, f32[176,1024]{1,0:T(8,128)}, u32[]{:S(2)}, u32[]{:S(2)}) collective-permute-start(f32[176,1024]{1,0:T(8,128)S(1)} %maximum_select_fusion.8.refs_5_), channel_id=1, source_target_pairs={{0,1},{1,0},{2,3},{3,2},{4,5},{5,4},{6,7},{7,6},{8,9},{9,8},{10,11... | collective-permute-start | bytes 2162696 | tf_op jit(solution)/shard_map/ppermute | solution.py:585
  360.7 22.3 %collective-permute-start.71 = (f32[176,1024]{1,0:T(8,128)S(1)}, f32[176,1024]{1,0:T(8,128)}, u32[]{:S(2)}, u32[]{:S(2)}) collective-permute-start(f32[176,1024]{1,0:T(8,128)S(1)} %maximum_select_fusion.8.refs_5_), channel_id=1, source_target_pairs={{0,8},{4,12},{8,0},{12,4},{16,24},{20,28},{24,16},{28,20},{1,9},{5... | collective-permute-start | bytes 2162696 | tf_op jit(solution)/shard_map/ppermute | solution.py:585
  361.7 23.3 %collective-permute-start.70 = (f32[176,1024]{1,0:T(8,128)}, f32[176,1024]{1,0:T(8,128)}, u32[]{:S(2)}, u32[]{:S(2)}) collective-permute-start(f32[176,1024]{1,0:T(8,128)} %maximum_select_fusion.7.refs_4_), channel_id=1, source_target_pairs={{0,2},{1,3},{2,0},{3,1},{4,6},{5,7},{6,4},{7,5},{8,10},{9,11},{10,... | collective-permute-start | bytes 2162696 | tf_op jit(solution)/shard_map/ppermute | solution.py:585
  371.9 16.6 %collective-permute-start.69 = (f32[176,1024]{1,0:T(8,128)S(1)}, f32[176,1024]{1,0:T(8,128)S(1)}, u32[]{:S(2)}, u32[]{:S(2)}) collective-permute-start(f32[176,1024]{1,0:T(8,128)S(1)} %maximum_select_fusion.6.refs_3_), channel_id=1, source_target_pairs={{0,4},{4,0},{8,12},{12,8},{16,20},{20,16},{24,28},{28,24},{1,5},{5... | collective-permute-start | bytes 2162696 | tf_op jit(solution)/shard_map/ppermute | solution.py:585
  382.7 18.2 %collective-permute-start.65 = (f32[176,1024]{1,0:T(8,128)}, f32[176,1024]{1,0:T(8,128)S(1)}, u32[]{:S(2)}, u32[]{:S(2)}) collective-permute-start(f32[176,1024]{1,0:T(8,128)} %collective-permute-done.62.refs_5_), channel_id=1, source_target_pairs={{0,1},{1,0},{2,3},{3,2},{4,5},{5,4},{6,7},{7,6},{8,9},{9,8},{10,11... | collective-permute-start | bytes 2162696 | tf_op jit(solution)/shard_map/ppermute | solution.py:585
  382.9 18.1 %collective-permute-start.56 = (f32[78,1024]{1,0:T(8,128)S(1)}, f32[78,1024]{1,0:T(8,128)S(1)}, u32[]{:S(2)}, u32[]{:S(2)}) collective-permute-start(f32[78,1024]{1,0:T(8,128)S(1)} %pad_maximum_fusion.1), channel_id=1, source_target_pairs={{0,16},{4,20},{8,24},{12,28},{16,0},{20,4},{24,8},{28,12},{1,17},{... | collective-permute-start | bytes 958472 | tf_op jit(solution)/shard_map/ppermute | solution.py:585
  382.9 18.5 %collective-permute-start.64 = (f32[176,1024]{1,0:T(8,128)}, f32[176,1024]{1,0:T(8,128)S(1)}, u32[]{:S(2)}, u32[]{:S(2)}) collective-permute-start(f32[176,1024]{1,0:T(8,128)} %copy-done.30), channel_id=1, source_target_pairs={{0,1},{1,0},{2,3},{3,2},{4,5},{5,4},{6,7},{7,6},{8,9},{9,8},{10,11... | collective-permute-start | bytes 2162696 | tf_op jit(solution)/shard_map/ppermute | solution.py:585
  385.1 17.3 %collective-permute-start.63 = (f32[176,1024]{1,0:T(8,128)}, f32[176,1024]{1,0:T(8,128)S(1)}, u32[]{:S(2)}, u32[]{:S(2)}) collective-permute-start(f32[176,1024]{1,0:T(8,128)} %collective-permute-done.60.refs_3_), channel_id=1, source_target_pairs={{0,1},{1,0},{2,3},{3,2},{4,5},{5,4},{6,7},{7,6},{8,9},{9,8},{10,11... | collective-permute-start | bytes 2162696 | tf_op jit(solution)/shard_map/ppermute | solution.py:585
  388.6 20.5 %collective-permute-start.58 = (f32[176,1024]{1,0:T(8,128)}, f32[176,1024]{1,0:T(8,128)}, u32[]{:S(2)}, u32[]{:S(2)}) collective-permute-start(f32[176,1024]{1,0:T(8,128)} %maximum_select_fusion.7.refs_4_), channel_id=1, source_target_pairs={{0,1},{1,0},{2,3},{3,2},{4,5},{5,4},{6,7},{7,6},{8,9},{9,8},{10,11... | collective-permute-start | bytes 2162696 | tf_op jit(solution)/shard_map/ppermute | solution.py:585
  401.0 15.8 %collective-permute-start.74 = (f32[176,1024]{1,0:T(8,128)}, f32[176,1024]{1,0:T(8,128)S(1)}, u32[]{:S(2)}, u32[]{:S(2)}) collective-permute-start(f32[176,1024]{1,0:T(8,128)} %collective-permute-done.71.refs_5_), channel_id=1, source_target_pairs={{0,1},{1,0},{2,3},{3,2},{4,5},{5,4},{6,7},{7,6},{8,9},{9,8},{10,11... | collective-permute-start | bytes 2162696 | tf_op jit(solution)/shard_map/ppermute | solution.py:585
  401.5 15.4 %collective-permute-start.73 = (f32[176,1024]{1,0:T(8,128)}, f32[176,1024]{1,0:T(8,128)}, u32[]{:S(2)}, u32[]{:S(2)}) collective-permute-start(f32[176,1024]{1,0:T(8,128)} %collective-permute-done.70.refs_4_), channel_id=1, source_target_pairs={{0,1},{1,0},{2,3},{3,2},{4,5},{5,4},{6,7},{7,6},{8,9},{9,8},{10,11... | collective-permute-start | bytes 2162696 | tf_op jit(solution)/shard_map/ppermute | solution.py:585
  403.2 13.7 %collective-permute-start.72 = (f32[176,1024]{1,0:T(8,128)S(1)}, f32[176,1024]{1,0:T(8,128)}, u32[]{:S(2)}, u32[]{:S(2)}) collective-permute-start(f32[176,1024]{1,0:T(8,128)S(1)} %collective-permute-done.69.refs_3_), channel_id=1, source_target_pairs={{0,1},{1,0},{2,3},{3,2},{4,5},{5,4},{6,7},{7,6},{8,9},{9,8},{10,11... | collective-permute-start | bytes 2162696 | tf_op jit(solution)/shard_map/ppermute | solution.py:585
  424.2 10.7 %collective-permute-start.77 = (f32[104,1024]{1,0:T(8,128)S(1)}, f32[104,1024]{1,0:T(8,128)S(1)}, u32[]{:S(2)}, u32[]{:S(2)}) collective-permute-start(f32[104,1024]{1,0:T(8,128)S(1)} %maximum_select_fusion.11), channel_id=1, source_target_pairs={{0,4},{4,0},{8,12},{12,8},{16,20},{20,16},{24,28},{28,24},{1,5},{5... | collective-permute-start | bytes 1277960 | tf_op jit(solution)/shard_map/ppermute | solution.py:585
  425.5 10.4 %collective-permute-start.76 = (f32[104,1024]{1,0:T(8,128)S(1)}, f32[104,1024]{1,0:T(8,128)S(1)}, u32[]{:S(2)}, u32[]{:S(2)}) collective-permute-start(f32[104,1024]{1,0:T(8,128)S(1)} %maximum_select_fusion.10), channel_id=1, source_target_pairs={{0,8},{4,12},{8,0},{12,4},{16,24},{20,28},{24,16},{28,20},{1,9},{5... | collective-permute-start | bytes 1277960 | tf_op jit(solution)/shard_map/ppermute | solution.py:585
  425.9 10.4 %collective-permute-start.75 = (f32[104,1024]{1,0:T(8,128)S(1)}, f32[104,1024]{1,0:T(8,128)S(1)}, u32[]{:S(2)}, u32[]{:S(2)}) collective-permute-start(f32[104,1024]{1,0:T(8,128)S(1)} %maximum_select_fusion.9), channel_id=1, source_target_pairs={{0,2},{1,3},{2,0},{3,1},{4,6},{5,7},{6,4},{7,5},{8,10},{9,11},{10,... | collective-permute-start | bytes 1277960 | tf_op jit(solution)/shard_map/ppermute | solution.py:585
  436.5 21.4 %collective-permute-start.80 = (f32[208,1024]{1,0:T(8,128)S(1)}, f32[208,1024]{1,0:T(8,128)S(1)}, u32[]{:S(2)}, u32[]{:S(2)}) collective-permute-start(f32[208,1024]{1,0:T(8,128)S(1)} %maximum_select_fusion.2.refs_5_), channel_id=1, source_target_pairs={{0,8},{4,12},{8,0},{12,4},{16,24},{20,28},{24,16},{28,20},{1,9},{5... | collective-permute-start | bytes 2555912 | tf_op jit(solution)/shard_map/ppermute | solution.py:585
  438.1 21.2 %collective-permute-start.79 = (f32[208,1024]{1,0:T(8,128)S(1)}, f32[208,1024]{1,0:T(8,128)}, u32[]{:S(2)}, u32[]{:S(2)}) collective-permute-start(f32[208,1024]{1,0:T(8,128)S(1)} %maximum_select_fusion.1.refs_4_), channel_id=1, source_target_pairs={{0,2},{1,3},{2,0},{3,1},{4,6},{5,7},{6,4},{7,5},{8,10},{9,11},{10,... | collective-permute-start | bytes 2555912 | tf_op jit(solution)/shard_map/ppermute | solution.py:585
  438.8 20.9 %collective-permute-start.78 = (f32[208,1024]{1,0:T(8,128)S(1)}, f32[208,1024]{1,0:T(8,128)}, u32[]{:S(2)}, u32[]{:S(2)}) collective-permute-start(f32[208,1024]{1,0:T(8,128)S(1)} %maximum_select_fusion.refs_3_), channel_id=1, source_target_pairs={{0,4},{4,0},{8,12},{12,8},{16,20},{20,16},{24,28},{28,24},{1,5},{5... | collective-permute-start | bytes 2555912 | tf_op jit(solution)/shard_map/ppermute | solution.py:585
  440.3 19.5 %collective-permute-start.85 = (f32[208,1024]{1,0:T(8,128)S(1)}, f32[208,1024]{1,0:T(8,128)S(1)}, u32[]{:S(2)}, u32[]{:S(2)}) collective-permute-start(f32[208,1024]{1,0:T(8,128)S(1)} %maximum_select_fusion.1.refs_4_), channel_id=1, source_target_pairs={{0,1},{1,0},{2,3},{3,2},{4,5},{5,4},{6,7},{7,6},{8,9},{9,8},{10,11... | collective-permute-start | bytes 2555912 | tf_op jit(solution)/shard_map/ppermute | solution.py:585
  440.3 19.5 %collective-permute-start.84 = (f32[208,1024]{1,0:T(8,128)S(1)}, f32[208,1024]{1,0:T(8,128)S(1)}, u32[]{:S(2)}, u32[]{:S(2)}) collective-permute-start(f32[208,1024]{1,0:T(8,128)S(1)} %maximum_select_fusion.refs_3_), channel_id=1, source_target_pairs={{0,1},{1,0},{2,3},{3,2},{4,5},{5,4},{6,7},{7,6},{8,9},{9,8},{10,11... | collective-permute-start | bytes 2555912 | tf_op jit(solution)/shard_map/ppermute | solution.py:585
  (82 other events, 844.8 us)

commit v2 on v1

--- a/solution.py
+++ b/solution.py
@@ -14,9 +14,9 @@
 SUB = 8
 WIDE = 1024
 SEG = 16
-VMEM = 60 * 1024 * 1024
+MIB = 1024 * 1024
 LOG2E = math.log2(math.e)
-CHEAP = pl.CostEstimate(flops=0, bytes_accessed=0, transcendentals=0)
+CHEAP = pl.CostEstimate(flops=1, bytes_accessed=1, transcendentals=0)
 
 
 def dot(a, b, dims=((1,), (0,))):
@@ -69,7 +69,7 @@
     length, model = tokens.shape
     width = cw.shape[1]
     cols = xproj.shape[0]
-    blk = 256
+    blk = 512
     whole = lambda shape: pl.BlockSpec(shape, lambda j: (0, 0))
     part = lambda rows: pl.BlockSpec((rows, blk), lambda j: (0, j))
     return pl.pallas_call(
@@ -93,7 +93,7 @@
             jax.ShapeDtypeStruct((length, width), BF16),
             jax.ShapeDtypeStruct((length, cols), F32),
         ],
-        compiler_params=pltpu.CompilerParams(vmem_limit_bytes=VMEM),
+        compiler_params=pltpu.CompilerParams(vmem_limit_bytes=60 * MIB),
         cost_estimate=CHEAP,
         name="front",
     )(lengths, tokens, cot, gain, in_weight, cw, cb, xproj)
@@ -139,14 +139,24 @@
 
 
 def scan_kernel(
-    core_ref, mp_ref, normed_ref, og_ref, act_ref, wg_ref, wo_ref, dtw_ref, dtb_ref, dlog_ref, skip_ref,
-    branch_ref, send_ref, ggp_ref, gs_ref, step_ref, mark_ref,
-    splat_ref, u_ref, y_ref, a_ref, gate_ref, gb_ref,
+    block, core_ref, mp_ref, act_ref, dtw_ref, dtb_ref, dlog_ref, skip_ref, normed_hbm, og_hbm, win_hbm, wout_hbm,
+    branch_ref, ggp_ref, send_ref, more_ref, gs_ref, step_out, mark_out,
+    splat_ref, u_ref, y_ref, a_ref, gate_ref, gb_ref, normed_ref, og_ref, wg_ref, wo_ref, step_ref, mark_ref, sems,
 ):
     length = mp_ref.shape[0]
     rank = dtw_ref.shape[0]
     states = a_ref.shape[0]
     both = 2 * states
+    width = win_hbm.shape[1] // 2
+    loads = [
+        pltpu.make_async_copy(src, dst, sems.at[k])
+        for k, (src, dst) in enumerate((
+            (normed_hbm, normed_ref), (win_hbm.at[:, pl.ds(width + block * WIDE, WIDE)], wg_ref),
+            (og_hbm, og_ref), (wout_hbm.at[pl.ds(block * WIDE, WIDE), :], wo_ref),
+        ))
+    ]
+    for load in loads:
+        load.start()
     fill_splats(mp_ref, splat_ref, rank, both)
     a_ref[...] = -jnp.exp(dlog_ref[...]) * LOG2E
     delta_in = mp_ref[:, :rank].astype(BF16)
@@ -156,29 +166,40 @@
         step = jnp.maximum(pre, 0.0) + jnp.log1p(jnp.exp(-jnp.abs(pre)))
         put_tiles(step_ref, j, step)
         put_tiles(u_ref, j, step * act_ref[:, cols].astype(F32))
-
-    def body(tb, carry):
+    stores = [
+        pltpu.make_async_copy(step_ref, step_out, sems.at[4]), pltpu.make_async_copy(mark_ref, mark_out, sems.at[5])
+    ]
+    stores[0].start()
+
+    def body(seg, carry):
         h = list(carry)
-        @pl.when(tb % (SEG // SUB) == 0)
-        def _():
-            base = pl.multiple_of((tb // (SEG // SUB)) * states * SUB, states * SUB)
-            for n in range(states):
-                mark_ref[pl.ds(base + n * SUB, SUB), :] = h[n]
-        for s in range(SUB):
-            step = step_ref[tile_rows(tb, s), :]
-            u = u_ref[tile_rows(tb, s), :]
-            y = None
-            for n in range(states):
-                f = jnp.exp2(step * a_ref[n])
-                h[n] = f * h[n] + u * splat(splat_ref, tb, both, n, s)
-                q = h[n] * splat(splat_ref, tb, both, states + n, s)
-                y = q if y is None else y + q
-            y_ref[tile_rows(tb, s), :] = y
-        return tuple(h)
+        base = pl.multiple_of(seg * states * SUB, states * SUB)
+        for n in range(states):
+            mark_ref[pl.ds(base + n * SUB, SUB), :] = h[n]
+
+        def eight(k, h):
+            h = list(h)
+            tb = seg * (SEG // SUB) + k
+            for s in range(SUB):
+                step = step_ref[tile_rows(tb, s), :]
+                u = u_ref[tile_rows(tb, s), :]
+                y = None
+                for n in range(states):
+                    f = jnp.exp2(step * a_ref[n])
+                    h[n] = f * h[n] + u * splat(splat_ref, tb, both, n, s)
+                    q = h[n] * splat(splat_ref, tb, both, states + n, s)
+                    y = q if y is None else y + q
+                y_ref[tile_rows(tb, s), :] = y
+            return tuple(h)
+
+        return lax.fori_loop(0, SEG // SUB, eight, tuple(h))
 
     zero = jnp.zeros((SUB, LANES), F32)
-    lax.fori_loop(0, length // SUB, body, (zero,) * states)
-
+    lax.fori_loop(0, length // SEG, body, (zero,) * states)
+    stores[1].start()
+
+    for load in loads:
+        load.wait()
     og = og_ref[...].astype(BF16)
     for k in range(WIDE // 256):
         cols = pl.ds(k * 256, 256)
@@ -199,63 +220,84 @@
         def _():
             send_ref[:, into] = branch.astype(F32)
         put_tiles(gs_ref, j, gb * gate_act)
-        ggp_ref[:, cols] = gb * summed * (sig * (1.0 + gate * (1.0 - sig)))
+        ggp = (gb * summed * (sig * (1.0 + gate * (1.0 - sig)))).astype(BF16)
+        ggp_ref[:, cols] = ggp
+        to = WIDE // 2 + j * LANES
+        if to < 3 * WIDE // 4:
+            send_ref[:, to : to + LANES] = ggp.astype(F32)
+        else:
+            to = to - 3 * WIDE // 4
+            more_ref[:, to : to + LANES] = ggp.astype(F32)
+    for store in stores:
+        store.wait()
 
 
 def scan(block, core, mp, normed, og, act, in_weight, out_weight, dtw, dtb, dlog, skip):
     length, model = normed.shape
-    width = act.shape[1]
     rank = dtw.shape[0]
     states = dlog.shape[0]
-    count = width // WIDE
     whole = lambda shape: pl.BlockSpec(shape, lambda i: (0,) * len(shape))
-    col = lambda rows, at: pl.BlockSpec((rows, WIDE), lambda i: (0, at))
-    tiles = jax.ShapeDtypeStruct((length * SUB, LANES), F32)
-    marks = (length // SEG) * states * SUB
-    flat = jax.ShapeDtypeStruct((length, WIDE), F32)
+    col = lambda rows: pl.BlockSpec((rows, WIDE), lambda i: (0, block))
+    hbm = pl.BlockSpec(memory_space=pltpu.HBM)
+    tiles = (length * SUB, LANES)
+    marks = (length // SEG * states * SUB, LANES)
+    flat = (length, WIDE)
+    send = (length, 3 * WIDE // 4)
+    shape = jax.ShapeDtypeStruct
     return pl.pallas_call(
-        scan_kernel,
+        functools.partial(scan_kernel, block),
         grid=(1,),
         in_specs=[
-            pl.BlockSpec(memory_space=pltpu.SMEM), whole(mp.shape), whole(normed.shape), whole(og.shape), col(length, block),
-            col(model, count + block), pl.BlockSpec((WIDE, model), lambda i: (block, 0)),
-            col(rank, block), col(1, block),
-            pl.BlockSpec((states, SUB, LANES), lambda i: (0, block, 0)), col(1, block),
+            pl.BlockSpec(memory_space=pltpu.SMEM), whole(mp.shape), col(length), col(rank), col(1),
+            pl.BlockSpec((states, SUB, LANES), lambda i: (0, block, 0)), col(1), hbm, hbm, hbm, hbm,
         ],
-        out_specs=[whole(flat.shape), whole((length, WIDE // 2)), whole(flat.shape), whole(tiles.shape), whole(tiles.shape), whole((marks, LANES))],
-        out_shape=[jax.ShapeDtypeStruct(flat.shape, BF16), jax.ShapeDtypeStruct((length, WIDE // 2), F32), flat, tiles, tiles, jax.ShapeDtypeStruct((marks, LANES), F32)],
+        out_specs=[whole(flat)] * 2 + [whole(send)] * 2 + [whole(tiles), hbm, hbm],
+        out_shape=[shape(flat, BF16)] * 2 + [shape(send, F32)] * 2 + [shape(tiles, F32)] * 2 + [shape(marks, F32)],
         scratch_shapes=[
             pltpu.VMEM((splat_rows(length, 2 * states), LANES), F32),
-            pltpu.VMEM((length * SUB, LANES), F32),
-            pltpu.VMEM((length * SUB, LANES), F32),
+            pltpu.VMEM(tiles, F32),
+            pltpu.VMEM(tiles, F32),
             pltpu.VMEM((states, SUB, LANES), F32),
-            pltpu.VMEM((length, WIDE), F32),
-            pltpu.VMEM((length, WIDE), F32),
+            pltpu.VMEM(flat, F32),
+            pltpu.VMEM(flat, F32),
+            pltpu.VMEM(normed.shape, BF16),
+            pltpu.VMEM(og.shape, F32),
+            pltpu.VMEM((model, WIDE), BF16),
+            pltpu.VMEM((WIDE, model), BF16),
+            pltpu.VMEM(tiles, F32),
+            pltpu.VMEM(marks, F32),
+            pltpu.SemaphoreType.DMA((6,)),
         ],
-        compiler_params=pltpu.CompilerParams(vmem_limit_bytes=VMEM),
+        compiler_params=pltpu.CompilerParams(vmem_limit_bytes=60 * MIB),
         cost_estimate=CHEAP,
         name=f"scan{block}",
-    )(core, mp, normed, og, act, in_weight, out_weight, dtw, dtb, dlog, skip)
+    )(core, mp, act, dtw, dtb, dlog, skip, normed, og, in_weight, out_weight)
 
 
 def back_kernel(
-    mp_ref, act_ref, step_ref, gs_ref, mark_ref, dtw_ref, dlog_ref,
-    gact_ref, glin_ref, gdelta_ref, gdtw_ref, gwr_ref, gdlog_ref, rows_ref,
-    splat_ref, act_t_ref, gd_ref, gu_ref, a_ref, f_ref, h_ref, carry_ref, turn_ref, part_ref,
+    first, mp_ref, act_ref, step_ref, gs_ref, mark_ref, dtw_ref, dlog_ref, *rest,
 ):
+    if not first:
+        carry_in, rest = rest[0], rest[1:]
+    (
+        gact_ref, gdelta_ref, gdtw_ref, gwr_ref, carry_ref, rows_ref, glin_ref,
+        splat_ref, act_t_ref, gd_ref, gu_ref, a_ref, f_ref, h_ref, turn_ref, part_ref,
+    ) = rest
     length = mp_ref.shape[0]
     rank = dtw_ref.shape[0]
     states = a_ref.shape[0]
     both = 2 * states
     fill_splats(mp_ref, splat_ref, rank, both)
-    rate = -jnp.exp(dlog_ref[...])
-    a_ref[...] = rate
+    a_ref[...] = -jnp.exp(dlog_ref[...])
     for j in range(WIDE // LANES):
         put_tiles(act_t_ref, j, act_ref[:, pl.ds(j * LANES, LANES)].astype(F32))
     per = SEG // SUB
 
     groups = states // SUB
-    carry_ref[...] = jnp.zeros_like(carry_ref)
+    if first:
+        carry_ref[...] = jnp.zeros_like(carry_ref)
+    else:
+        carry_ref[...] = carry_in[...]
 
     def segment(i, _):
         seg = length // SEG - 1 - i
@@ -333,9 +375,6 @@
         return 0
 
     lax.fori_loop(0, length // SEG, segment, 0)
-    for n in range(states):
-        gdlog_ref[n] = carry_ref[1, n] * rate[n]
-
     row = lax.broadcasted_iota(jnp.int32, (2 * LANES, LANES), 0)
     lane = lax.broadcasted_iota(jnp.int32, (2 * LANES, LANES), 1)
     gwr = None
@@ -367,61 +406,76 @@
     gdelta_ref[...] = dot(glin_ref[...], dtw_ref[...], ((1,), (1,)))
 
 
-def back(block, mp, act, step, gs, marks, dtw, dlog):
-    length = act.shape[0]
+def back(block, part, parts, mp, act, step, gs, marks, dtw, dlog, carry=None):
+    length = act.shape[0] // parts
     rank = dtw.shape[0]
     states = dlog.shape[0]
+    first = carry is None
     whole = lambda shape: pl.BlockSpec(shape, lambda i: (0,) * len(shape))
-    col = lambda rows, at: pl.BlockSpec((rows, WIDE), lambda i: (0, at))
+    mine = lambda v: pl.BlockSpec((v.shape[0] // parts, v.shape[1]), lambda i: (part, 0))
     flat = jax.ShapeDtypeStruct((length, WIDE), F32)
     outs = [
         flat,
-        jax.ShapeDtypeStruct((length, WIDE), BF16),
         jax.ShapeDtypeStruct((length, rank), F32),
         jax.ShapeDtypeStruct((rank, WIDE), F32),
         jax.ShapeDtypeStruct((length, LANES), F32),
-        jax.ShapeDtypeStruct((states, SUB, LANES), F32),
+        jax.ShapeDtypeStruct((2, states, SUB, LANES), F32),
         jax.ShapeDtypeStruct((2, WIDE), F32),
     ]
     tiles = pltpu.VMEM((length * SUB, LANES), F32)
     return pl.pallas_call(
-        back_kernel,
+        functools.partial(back_kernel, first),
         grid=(1,),
         in_specs=[
-            whole(mp.shape), col(length, block), whole(step.shape), whole(gs.shape), whole(marks.shape),
-            col(rank, block), pl.BlockSpec((states, SUB, LANES), lambda i: (0, block, 0)),
-        ],
+            mine(mp), pl.BlockSpec((length, WIDE), lambda i: (part, block)), mine(step), mine(gs), mine(marks),
+            pl.BlockSpec((rank, WIDE), lambda i: (0, block)),
+            pl.BlockSpec((states, SUB, LANES), lambda i: (0, block, 0)),
+        ] + ([] if first else [whole(carry.shape)]),
         out_specs=[whole(o.shape) for o in outs],
         out_shape=outs,
         scratch_shapes=[
+            pltpu.VMEM((length, WIDE), BF16),
             pltpu.VMEM((splat_rows(length, 2 * states), LANES), F32),
             tiles, tiles, tiles,
             pltpu.VMEM((states, SUB, LANES), F32),
             pltpu.VMEM((SEG, SUB, SUB, LANES), F32),
             pltpu.VMEM((SEG + 1, SUB, SUB, LANES), F32),
-            pltpu.VMEM((2, states, SUB, LANES), F32),
             pltpu.VMEM((2 * SUB * SUB * SUB, LANES), F32),
             pltpu.VMEM((length * 2 * states, LANES), F32),
         ],
-        compiler_params=pltpu.CompilerParams(vmem_limit_bytes=VMEM),
+        compiler_params=pltpu.CompilerParams(vmem_limit_bytes=36 * MIB),
         cost_estimate=CHEAP,
-        name=f"back{block}",
-    )(mp, act, step, gs, marks, dtw, dlog)
+        name=f"back{block}{part}",
+    )(mp, act, step, gs, marks, dtw, dlog, *([] if first else [carry]))
 
 
 def post_kernel(
-    gmix_ref, gs_ref, gact_ref, act_ref, inner_ref, xp_ref, cw_ref, cb_ref, skip_ref, gdtw_ref, gdlog_ref, two_ref,
-    gi_ref, small_ref,
+    parts, gs_ref, act_ref, inner_ref, xp_ref, cw_ref, cb_ref, skip_ref, carry_ref, dlog_ref, *rest,
 ):
+    gact_refs, gdtw_refs, two_refs = rest[:parts], rest[parts : 2 * parts], rest[2 * parts : 3 * parts]
+    gdelta_refs, gwr_refs = rest[3 * parts : 5 * parts], rest[5 * parts : 7 * parts]
+    gi_ref, small_ref = rest[7 * parts :]
+    total_of = lambda refs: sum([ref[...] for ref in refs[1:]], refs[0][...])
     length = act_ref.shape[0]
     taps = cw_ref.shape[0]
-    share = dot(gmix_ref[...], xp_ref[...])
-    sizes = [xp_ref.shape[0], gdtw_ref.shape[0], gdlog_ref.shape[0], two_ref.shape[0]]
+    states = dlog_ref.shape[0]
+    lines = []
+    for k in range(parts):
+        delta = gdelta_refs[k][...] + gdelta_refs[parts + k][...]
+        rest_of = (gwr_refs[k][...] + gwr_refs[parts + k][...])[:, : xp_ref.shape[0]]
+        room = jnp.zeros((delta.shape[0], xp_ref.shape[0] - delta.shape[1]), F32)
+        lines.append(jnp.concatenate([delta, room], axis=1) + rest_of)
+    gmix = jnp.concatenate(lines, axis=0).astype(BF16)
+    share = dot(gmix, xp_ref[...])
+    sizes = [xp_ref.shape[0], gdtw_refs[0].shape[0], states, two_refs[0].shape[0]]
     ends = [sum(sizes[: i + 1]) for i in range(4)]
-    small_ref[: ends[0], :] = dot(gmix_ref[...], act_ref[...], ((0,), (0,)))
-    small_ref[ends[0] : ends[1], :] = gdtw_ref[...]
-    small_ref[ends[1] : ends[2], :] = gdlog_ref[...]
-    small_ref[ends[2] : ends[3], :] = two_ref[...]
+    small_ref[: ends[0], :] = dot(gmix, act_ref[...], ((0,), (0,)))
+    small_ref[ends[0] : ends[1], :] = total_of(gdtw_refs)
+    for n in range(states):
+        for j in range(SUB):
+            small_ref[ends[1] + n : ends[1] + n + 1, j * LANES : (j + 1) * LANES] = carry_ref[1, n, j : j + 1, :]
+    small_ref[ends[1] : ends[2], :] = small_ref[ends[1] : ends[2], :] * -jnp.exp(dlog_ref[...])
+    small_ref[ends[2] : ends[3], :] = total_of(two_refs)
     small_ref[ends[3] + taps + 1 :, :] = jnp.zeros((small_ref.shape[0] - ends[3] - taps - 1, WIDE), F32)
     for j in range(WIDE // LANES):
         cols = pl.ds(j * LANES, LANES)
@@ -431,7 +485,7 @@
         sig = jax.nn.sigmoid(conv)
         gact = (
             get_tiles(gs_ref, j, length) * skip_ref[:, cols]
-            + gact_ref[:, cols]
+            + jnp.concatenate([ref[:, cols] for ref in gact_refs], axis=0)
             + share[:, j * LANES : (j + 1) * LANES]
         )
         gconv = gact * (sig * (1.0 + conv * (1.0 - sig)))
@@ -447,7 +501,7 @@
         gi_ref[:, cols] = total
 
 
-def post(block, lines, gmix, gs, gact, act, inner, xproj, cw, cb, skip, gdtw, gdlog, two):
+def post(block, lines, gs, act, inner, xproj, cw, cb, skip, carry, dlog, gact, gdtw, two, gdelta, gwr):
     length = act.shape[0]
     cols = xproj.shape[0]
     taps = cw.shape[0]
@@ -455,79 +509,244 @@
     col = lambda rows, at: pl.BlockSpec((rows, WIDE), lambda i: (0, at))
     outs = [jax.ShapeDtypeStruct((length, WIDE), F32), jax.ShapeDtypeStruct((lines, WIDE), F32)]
     return pl.pallas_call(
-        post_kernel,
+        functools.partial(post_kernel, len(gact)),
         grid=(1,),
         in_specs=[
-            whole(gmix.shape), whole(gs.shape), whole(gact.shape), col(length, block), col(length, block),
+            whole(gs.shape), col(length, block), col(length, block),
             col(cols, block), col(taps, block), col(1, block), col(1, block),
-            whole(gdtw.shape), whole(gdlog.shape), whole(two.shape),
-        ],
+            whole(carry.shape), col(dlog.shape[0], block),
+        ] + [whole(v.shape) for v in [*gact, *gdtw, *two, *gdelta, *gwr]],
         out_specs=[whole(o.shape) for o in outs],
         out_shape=outs,
-        compiler_params=pltpu.CompilerParams(vmem_limit_bytes=VMEM),
+        compiler_params=pltpu.CompilerParams(vmem_limit_bytes=60 * MIB),
         cost_estimate=CHEAP,
         name=f"post{block}",
-    )(gmix, gs, gact, act, inner, xproj, cw, cb, skip, gdtw, gdlog, two)
-
-
-def outer(core, own, other, rows, small=()):
+    )(gs, act, inner, xproj, cw, cb, skip, carry, dlog, *gact, *gdtw, *two, *gdelta, *gwr)
+
+
+def outer(core, own, other, sizes, flags, weight=None, cols=(), gains=(), small=()):
     length = own[0][0].shape[0]
-    low, cols = own[0][0].shape[1] // 2, own[0][1].shape[1]
-    per = 2
-    blk = low // per
-    ins, specs = [], []
+    low, wide = own[0][0].shape[1] // 2, own[0][1].shape[1]
+    halves = [v // 2 for v in sizes for _ in range(2)]
+    starts = [sum(halves[:k]) for k in range(len(halves))]
+    blk = 256
+    total = sum(sizes)
+    at_core = len(sizes)
+    big, moves = [], []
     for c in range(2):
-        at = lambda i, c=c: jnp.clip(i - c * per, 0, per - 1)
-        ins += [own[c][0], other[c][0], own[c][1], other[c][1]]
-        specs += [
-            pl.BlockSpec((length, blk), lambda i, ix, at=at: (0, ix[0] * per + at(i))),
-            pl.BlockSpec((length, blk), lambda i, ix, at=at: (0, at(i))),
-            pl.BlockSpec((length, cols), lambda i, ix: (0, 0)),
-            pl.BlockSpec((length, cols), lambda i, ix: (0, 0)),
-        ]
-    ins += list(small)
-    specs += [pl.BlockSpec(v.shape, lambda i, ix: (0, 0)) for v in small]
-    rest = rows - 2 * low
-    total = 2 * low + (rest > 0) * blk * -(-rest // blk)
-
-    def body(ix, *refs):
-        out = refs[-1]
-        step = pl.program_id(0)
+        for k, pieces in enumerate(([(own[c][0], None, low)], other[c][0], [(own[c][1], 0, wide)], other[c][1])):
+            to = 0
+            for array, col, count in pieces:
+                moves.append((len(big), 4 * c + k, col, to, count))
+                big.append(array)
+                to += count
+    n_big = len(big)
+    n_buf = 8
+    with_gain = weight is not None
+    extra = ([weight] if with_gain else []) + list(gains) + list(small)
+
+    def body(flag_ref, *refs):
+        ins, refs = refs[: n_big + len(extra)], refs[n_big + len(extra) :]
+        outs, refs = refs[: len(halves) + with_gain], refs[len(halves) + with_gain :]
+        bufs, refs = refs[:n_buf], refs[n_buf:]
+        w_bufs, refs = (refs[: len(cols)], refs[len(cols) :])
+        lefts, rights, result, sem_in, sem_w, sem_out = refs
+        loads = []
+        for k, buf, col, to, count in moves:
+            col = pl.multiple_of(flag_ref[at_core] * low, LANES) if col is None else col
+            loads.append(pltpu.make_async_copy(
+                ins[k].at[:, pl.ds(col, count)], bufs[buf].at[:, pl.ds(to, count)], sem_in.at[k]
+            ))
+            loads[-1].start()
+        w_loads = []
+        for q, (c, col) in enumerate(cols):
+            src = ins[n_big].at[pl.ds(pl.multiple_of(flag_ref[at_core] * low, SUB), low), pl.ds(col, wide)]
+            w_loads.append(pltpu.make_async_copy(src, w_bufs[q], sem_w.at[q]))
+            w_loads[-1].start()
+
+        def copy(k, flip):
+            c, h = k // 2, k % 2
+            return pltpu.make_async_copy(
+                result.at[pl.ds(starts[k], halves[k]), :], outs[2 * c + flip], sem_out.at[k]
+            )
+
+        def each(k, act):
+            c, h = k // 2, k % 2
+            for flip in range(2):
+                @pl.when((flag_ref[c] == h) == bool(flip))
+                def _():
+                    getattr(copy(k, flip), act)()
+
+        ready, sent = 0, 0
+        gain = None
         for c in range(2):
-            @pl.when((step >= c * per) & (step < (c + 1) * per))
-            def _():
-                l, lo, r, ro = [ref[...].astype(BF16) for ref in refs[4 * c : 4 * c + 4]]
-                out[...] = dot(l, r, ((0,), (0,))) + dot(lo, ro, ((0,), (0,)))
-
-        @pl.when(step >= 2 * per)
-        def _():
-            out[...] = jnp.zeros_like(out)
-            if small:
-                a, b, got = refs[8:11]
-                out[: got.shape[0], :] = jnp.where(ix[0] == 0, a[...], b[...]) + got[...]
-
+            for k, buf, _, _, _ in moves:
+                if buf // 4 == c:
+                    loads[k].wait()
+            lefts[:length] = bufs[4 * c][...].astype(BF16)
+            lefts[length:] = bufs[4 * c + 1][...].astype(BF16)
+            rights[:length] = bufs[4 * c + 2][...].astype(BF16)
+            rights[length:] = bufs[4 * c + 3][...].astype(BF16)
+            for m in range(0, low, blk):
+                result[c * low + m : c * low + m + blk, :] = dot(lefts[:, m : m + blk], rights[...], ((0,), (0,)))
+                ready = c * low + m + blk
+                while sent < len(halves) and starts[sent] + halves[sent] <= ready:
+                    each(sent, "start")
+                    sent += 1
+            for q, (pair, _) in enumerate(cols):
+                if pair == c:
+                    w_loads[q].wait()
+                    for j in range(0, wide, LANES):
+                        term = result[c * low : (c + 1) * low, j : j + LANES] * w_bufs[q][:, j : j + LANES].astype(F32)
+                        gain = term if gain is None else gain + term
+        if small:
+            a, b, got = ins[-3:]
+            lines = got.shape[0]
+            result[2 * low : 2 * low + lines, :] = jnp.where(flag_ref[at_core] == 0, a[...], b[...]) + got[...]
+            for ref in ins[n_big + 1 : n_big + 1 + len(gains)]:
+                gain = gain + ref[...]
+            rows = low // (wide // LANES)
+            for j in range(wide // LANES):
+                result[2 * low + lines : 2 * low + lines + rows, j * LANES : (j + 1) * LANES] = gain[j * rows : (j + 1) * rows]
+            if 2 * low + lines + rows < total:
+                result[2 * low + lines + rows :, :] = jnp.zeros((total - 2 * low - lines - rows, wide), F32)
+        elif 2 * low < total:
+            result[2 * low :, :] = jnp.zeros((total - 2 * low, wide), F32)
+        if with_gain:
+            outs[-1][...] = gain
+        while sent < len(halves):
+            each(sent, "start")
+            sent += 1
+        for k in range(len(halves)):
+            each(k, "wait")
+
+    hbm = pl.BlockSpec(memory_space=pltpu.HBM)
+    vmem = lambda v: pl.BlockSpec(v.shape, lambda i, ix: (0, 0))
+    out_shape = [jax.ShapeDtypeStruct((v // 2, wide), F32) for v in sizes for _ in range(2)]
+    out_specs = [hbm] * len(out_shape)
+    if with_gain:
+        out_shape.append(jax.ShapeDtypeStruct((low, LANES), F32))
+        out_specs.append(pl.BlockSpec((low, LANES), lambda i, ix: (0, 0)))
+    buffers = [
+        pltpu.VMEM((length, low if k % 4 < 2 else wide), own[k // 4][k % 4 // 2].dtype if k % 2 == 0 else F32) for k in range(n_buf)
+    ] + [pltpu.VMEM((low, wide), BF16) for _ in cols]
     return pl.pallas_call(
         body,
-        out_shape=jax.ShapeDtypeStruct((rows, cols), F32),
+        out_shape=out_shape,
         grid_spec=pltpu.PrefetchScalarGridSpec(
-            num_scalar_prefetch=1, grid=(total // blk,), in_specs=specs,
-            out_specs=pl.BlockSpec((blk, cols), lambda i, ix: (i, 0)),
+            num_scalar_prefetch=1, grid=(1,),
+            in_specs=[hbm] * n_big + ([hbm] if with_gain else []) + [vmem(v) for v in [*gains, *small]],
+            out_specs=out_specs,
+            scratch_shapes=buffers + [
+                pltpu.VMEM((2 * length, low), BF16), pltpu.VMEM((2 * length, wide), BF16), pltpu.VMEM((total, wide), F32),
+                pltpu.SemaphoreType.DMA((n_big,)), pltpu.SemaphoreType.DMA((max(len(cols), 1),)),
+                pltpu.SemaphoreType.DMA((len(halves),)),
+            ],
         ),
-        compiler_params=pltpu.CompilerParams(vmem_limit_bytes=VMEM),
+        compiler_params=pltpu.CompilerParams(vmem_limit_bytes=60 * MIB),
         cost_estimate=CHEAP,
         name="outer",
-    )(core, *ins)
+    )(flags, *big, *extra)
+
+
+def step_call(body, name, index, ins, in_specs, outs):
+    return pl.pallas_call(
+        body,
+        out_shape=outs,
+        grid_spec=pltpu.PrefetchScalarGridSpec(
+            num_scalar_prefetch=1, grid=(1,), in_specs=in_specs,
+            out_specs=[pl.BlockSpec(o.shape, lambda i, ix: (0, 0)) for o in outs],
+        ),
+        compiler_params=pltpu.CompilerParams(vmem_limit_bytes=20 * MIB),
+        cost_estimate=CHEAP,
+        name=name,
+    )(index, *ins)
+
+
+def rows_of(rows, cols):
+    return jax.ShapeDtypeStruct((rows, cols), F32)
+
+
+def fold_call(index, kept, got, merged):
+    n = len(kept)
+    ins, specs, sends, keeps = [], [], [], []
+    for c in range(n):
+        size, cols = kept[c].shape[0] // 2, kept[c].shape[1]
+        base = 2 * c if len(got) < n else 0
+        for flip in (0, 1):
+            at = lambda i, ix, c=c, flip=flip, base=0: (base + (ix[c] if flip else 1 - ix[c]), 0)
+            ins += [kept[c], got[c % len(got)]]
+            specs += [pl.BlockSpec((size, cols), at), pl.BlockSpec((size, cols), functools.partial(at, base=base))]
+        sends.append(rows_of(size, cols))
+        keeps.append(rows_of(size, cols))
+    sizes = [v.shape[0] for v in sends]
+    if merged:
+        sends = [rows_of(sum(sizes), cols)]
+
+    def body(ix, *refs):
+        outs = refs[4 * n :]
+        for c in range(n):
+            for flip in (0, 1):
+                a, b = refs[4 * c + 2 * flip : 4 * c + 2 * flip + 2]
+                if flip:
+                    outs[len(sends) + c][...] = a[...] + b[...]
+                elif merged:
+                    outs[0][sum(sizes[:c]) : sum(sizes[: c + 1]), :] = a[...] + b[...]
+                else:
+                    outs[c][...] = a[...] + b[...]
+
+    out = step_call(body, "fold", index, ins, specs, sends + keeps)
+    return list(out[: len(sends)]), list(out[len(sends) :])
+
+
+def last_call(index, kept, got):
+    n = len(kept)
+    sizes = [v.shape[0] for v in kept]
+    cols = kept[0].shape[1]
+    specs = [pl.BlockSpec(v.shape, lambda i, ix: (0, 0)) for v in [*kept, *got]]
+
+    def body(ix, *refs):
+        for c in range(n):
+            at = slice(sum(sizes[:c]), sum(sizes[: c + 1]))
+            refs[-1][at, :] = refs[c][...] + (refs[n + c][...] if len(got) == n else refs[n][at, :])
+
+    return step_call(body, "last", index, [*kept, *got], specs, [rows_of(sum(sizes), cols)])[0]
+
+
+def widen_call(index, sizes, share, got, merged):
+    cols = share[0].shape[1]
+    ins = [*share, *got]
+    specs = [pl.BlockSpec(v.shape, lambda i, ix: (0, 0)) for v in ins]
+    n = len(share)
+
+    def body(ix, *refs):
+        outs = refs[n + len(got) :]
+        for c, size in enumerate(sizes):
+            low = sum(sizes[:c])
+            for side, at in ((refs[:n], ix[c]), (refs[n : n + len(got)], 1 - ix[c])):
+                value = side[c][...] if len(side) == len(sizes) else side[0][low : low + size, :]
+                if merged:
+                    outs[0][pl.ds(pl.multiple_of(2 * low + at * size, SUB), size), :] = value
+                else:
+                    outs[c][pl.ds(pl.multiple_of(at * size, SUB), size), :] = value
+
+    outs = [rows_of(2 * sum(sizes), cols)] if merged else [rows_of(2 * s, cols) for s in sizes]
+    return list(step_call(body, "widen", index, ins, specs, outs))
 
 
 def blank(shape):
     return pl.pallas_call(
         lambda ref: None, out_shape=jax.ShapeDtypeStruct(shape, F32),
         out_specs=pl.BlockSpec(memory_space=pltpu.HBM), name="blank",
-        compiler_params=pltpu.CompilerParams(vmem_limit_bytes=VMEM), cost_estimate=CHEAP,
+        compiler_params=pltpu.CompilerParams(vmem_limit_bytes=16 * MIB), cost_estimate=CHEAP,
     )()
 
 
-def put(targets, pieces, spans, flags):
+def put(targets, pieces, parts, sizes, flags):
+    def spans(chunk, h):
+        low = sum(sizes[:chunk]) + h * (sizes[chunk] // 2)
+        return spans_of(parts, low, low + sizes[chunk] // 2)
+
     arrays = [p[0] for p in pieces]
     n = len(targets)
     sems = max(len(spans(p[1], h)) for p in pieces for h in range(2))
@@ -565,7 +784,7 @@
             scratch_shapes=[pltpu.SemaphoreType.DMA((len(arrays) * sems,))],
         ),
         input_output_aliases={1 + k: k for k in range(n)},
-        compiler_params=pltpu.CompilerParams(vmem_limit_bytes=VMEM),
+        compiler_params=pltpu.CompilerParams(vmem_limit_bytes=20 * MIB),
         cost_estimate=CHEAP,
         name="put",
     )(flags, *targets, *arrays)
@@ -588,19 +807,10 @@
 CORE = ("rep", 0)
 
 
-def orders():
-    x, y, z = ("dp", 0), ("rep", 1), ("dp", 1)
+def orders(*heads):
+    axes = {"x": ("dp", 0), "y": ("rep", 1), "z": ("dp", 1)}
     rest = [("dp", b) for b in range(2, bits_of("dp"))] + [("rep", b) for b in range(2, bits_of("rep"))]
-    return [[x, y, z] + rest, [y, z, x] + rest, [z, x, y] + rest]
-
-
-def fits(rows):
-    unit = 3 << len(orders()[0])
-    return -(-rows // unit) * unit
-
-
-def slab(value, start, rows):
-    return lax.dynamic_slice_in_dim(value, start, rows, 0)
+    return [[axes[a] for a in head] + rest for head in heads]
 
 
 class Order:
@@ -617,96 +827,101 @@
 
 
 class Reduced:
-    def __init__(self, order):
+    def __init__(self, order, steps):
         self.order = order
-        self.steps = orders()
-        self.count = len(self.steps[0])
-        self.k = -1
+        self.steps = steps
+        self.count = len(steps[0])
         self.share = None
 
+    def index(self, k):
+        return jnp.stack([bit(s[k]) for s in self.steps]).astype(jnp.int32)
+
     def same(self, k):
-        return self.steps[0][k] == self.steps[1][k]
+        return all(s[k] == self.steps[0][k] for s in self.steps)
 
     def send(self, k, values):
-        if self.same(k):
-            got = swap(jnp.concatenate(values), self.steps[0][k])
-            size = values[0].shape[0]
-            return [lax.slice_in_dim(got, c * size, (c + 1) * size) for c in range(3)]
+        if len(values) == 1:
+            return [swap(values[0], self.steps[0][k])]
         return [swap(v, s[k]) for v, s in zip(values, self.steps)]
 
-    def begin(self, whole):
-        rows = whole.shape[0] // 3
-        self.kept = [(whole, c * rows, rows) for c in range(3)]
-        self.got = None
-        self.fold()
+    def begin(self, sends, keeps):
+        self.k = 0
+        self.kept = keeps
+        self.got = self.send(0, sends)
 
     def fold(self):
         k = self.k + 1
-        if self.got is None:
-            terms = [[v] for v in self.kept]
-        else:
-            arrays = self.order.tie([v[0] for v in self.kept], self.got)
-            terms = [
-                [(a, start, rows), (g, 0, rows)]
-                for a, (_, start, rows), g in zip(arrays[0], self.kept, arrays[1])
-            ]
-
-        def part(term, i, halves):
-            values = []
-            for value, start, rows in term:
-                size = rows // halves
-                values.append(slab(value, start + i * size, size))
-            return sum(values[1:], values[0])
-
+        kept, got = self.order.tie(self.kept, self.got)
         if k == self.count:
-            self.share = [part(t, 0, 1) for t in terms]
+            self.share = [last_call(self.index(0), kept, got)]
+            self.sizes = [v.shape[0] for v in kept]
+            if any(v % SUB for v in self.sizes):
+                cut = [sum(self.sizes[:c]) for c in range(len(kept))]
+                self.share = [lax.slice_in_dim(self.share[0], a, a + n) for a, n in zip(cut, self.sizes)]
             self.order.done(self.share[0])
-            self.got = self.send(k - 1, self.share)
             self.k = k - 1
             return
-        index = [bit(s[k]) for s in self.steps]
-        sends = [part(t, 1 - i, 2) for t, i in zip(terms, index)]
-        self.order.done(sends)
-        if self.got is None:
-            self.kept = [(v, start + i * (rows // 2), rows // 2) for (v, start, rows), i in zip(self.kept, index)]
-            got = self.send(k, sends)
+        equal = len({v.shape[0] for v in kept}) == 1
+        merged = self.same(k) and (equal or k == self.count - 1)
+        if any(v.shape[0] % (2 * SUB) for v in kept):
+            if len(got) < len(kept):
+                size = kept[0].shape[0]
+                got = [lax.slice_in_dim(got[0], c * size, (c + 1) * size) for c in range(len(kept))]
+            total = [a + b for a, b in zip(kept, got)]
+            index = [bit(s[k]) for s in self.steps]
+            half = lambda v, i: lax.dynamic_slice_in_dim(v, i * (v.shape[0] // 2), v.shape[0] // 2, 0)
+            sends = [half(v, 1 - i) for v, i in zip(total, index)]
+            self.kept = [half(v, i) for v, i in zip(total, index)]
         else:
-            got = self.send(k, sends)
-            tied = self.order.tie([[v[0] for v in t] for t in terms])[0]
-            keeps = [
-                part([(a, start, rows) for a, (_, start, rows) in zip(arr, t)], i, 2)
-                for arr, t, i in zip(tied, terms, index)
-            ]
-            self.order.done(keeps)
-            self.kept = [(v, 0, v.shape[0]) for v in keeps]
-        self.got = got
+            sends, self.kept = fold_call(self.index(k), kept, got, merged)
+        self.order.done(self.kept[0])
         self.k = k
+        self.got = self.send(k, sends)
 
     def finish(self):
         while self.share is None:
             self.fold()
+
+    def back(self):
+        self.got = self.send(self.k, self.share)
         while self.k > 3:
             self.widen()
+
+    def origin(self, device, chunk):
+        ranks = {"rep": device % lax.axis_size("rep"), "dp": device // lax.axis_size("rep")}
+        block = 0
+        for axis, place in self.steps[chunk]:
+            block = 2 * block + (ranks[axis] >> place & 1)
+        sizes = [v << self.count for v in self.sizes]
+        return sum(sizes[:chunk]) + block * self.sizes[chunk]
 
     def widen(self):
         k = self.k
         share, got = self.order.tie(self.share, self.got)
-        wide = []
-        for v, g, s in zip(share, got, self.steps):
-            first = bit(s[k]) == 0
-            wide.append(jnp.where(first, jnp.concatenate([v, g]), jnp.concatenate([g, v])))
-        self.share = wide
-        self.order.done(wide)
+        if any(v % SUB for v in self.sizes):
+            pick = [bit(s[k]) == 0 for s in self.steps]
+            self.share = [
+                jnp.where(p, jnp.concatenate([v, g]), jnp.concatenate([g, v])) for p, v, g in zip(pick, share, got)
+            ]
+        else:
+            self.share = widen_call(self.index(k), self.sizes, share, got, self.same(k - 1))
+        self.sizes = [2 * v for v in self.sizes]
+        self.order.done(self.share[0])
         self.k = k - 1
-        self.got = self.send(k - 1, wide)
+        self.got = self.send(k - 1, self.share)
         if k == 1:
-            self.across = [swap(v, CORE) for v in wide]
+            self.across = [swap(v, CORE) for v in self.share]
 
     def own(self):
-        return [(v, c, c, 6) for c, v in enumerate(self.share)] + [(v, c, c, 7) for c, v in enumerate(self.across)]
+        n = len(self.steps)
+        return [(v, c, c, 2 * n) for c, v in enumerate(self.share)] + [(v, c, c, 2 * n + 1) for c, v in enumerate(self.across)]
 
     def arrived(self):
-        return [(v, c, 3 + c, 6) for c, v in enumerate(self.got)] + [(swap(v, CORE), c, 3 + c, 7) for c, v in enumerate(self.got)]
+        n = len(self.steps)
+        got = self.order.tie(*self.got)
+        return [(v, c, n + c, 2 * n) for c, v in enumerate(got)] + [
+            (swap(v, CORE), c, n + c, 2 * n + 1) for c, v in enumerate(got)
+        ]
 
     def flags(self):
         mine = [bit(s[0]) for s in self.steps]
@@ -714,27 +929,71 @@
         return jnp.stack(mine + [1 - i for i in mine] + [core, 1 - core]).astype(jnp.int32)
 
 
-def spans_of(total, parts):
-    size = total // 6
-
-    def spans(chunk, h):
-        low = (2 * chunk + h) * size
-        found, start = [], 0
-        for rows, target, row, col in parts:
-            a, b = max(low, start), min(low + size, start + rows)
-            if a < b and target is not None:
-                found.append((a - low, b - a, target, row + a - start, rows, col))
-            start += rows
-        return found
-
-    return spans
+def spans_of(parts, low, high):
+    found, start = [], 0
+    for rows, target, row, col in parts:
+        a, b = max(low, start), min(high, start + rows)
+        if a < b:
+            found.append((a - low, b - a, target, row + a - start, rows, col))
+        start += rows
+    return found
+
+
+def deal(targets, gathered, sets, parts):
+    n = len(targets)
+    cols = gathered.shape[1]
+    devices = lax.axis_size("dp") * lax.axis_size("rep")
+    per = 4
+    rows = gathered.shape[0] // devices
+    moves = []
+    for device in range(devices):
+        mine, start = [], 0
+        for p, layout in zip(sets, parts):
+            for c, size in enumerate(p.sizes):
+                low = p.origin(device, c)
+                for first, count, target, row, whole, col in spans_of(layout, low, low + size):
+                    mine.append((start + first, count, target, row + device % 2 * whole, col))
+                start += size
+        moves.append(mine)
+    most = max(sum(len(m) for m in moves[g : g + per]) for g in range(0, devices, per))
+
+    def body(*refs):
+        value, outs, sem = refs[n], refs[n + 1 : -1], refs[-1]
+        for g in range(0, devices, per):
+            @pl.when(pl.program_id(0) == g // per)
+            def _():
+                copies = []
+                for d in range(per):
+                    for first, count, target, row, col in moves[g + d]:
+                        copies.append(pltpu.make_async_copy(
+                            value.at[pl.ds(d * rows + first, count), :],
+                            outs[target].at[pl.ds(row, count), pl.ds(col, cols)],
+                            sem.at[len(copies)],
+                        ))
+                        copies[-1].start()
+                for copy in copies:
+                    copy.wait()
+
+    return pl.pallas_call(
+        body,
+        out_shape=[jax.ShapeDtypeStruct(t.shape, F32) for t in targets],
+        grid=(devices // per,),
+        in_specs=[pl.BlockSpec(memory_space=pltpu.HBM)] * n + [pl.BlockSpec((per * rows, cols), lambda i: (i, 0))],
+        out_specs=[pl.BlockSpec(memory_space=pltpu.HBM)] * n,
+        scratch_shapes=[pltpu.SemaphoreType.DMA((most,))],
+        input_output_aliases={k: k for k in range(n)},
+        compiler_params=pltpu.CompilerParams(vmem_limit_bytes=60 * MIB),
+        cost_estimate=CHEAP,
+        name="deal",
+    )(*targets, gathered)
 
 
 SEQUENCE = (
-    "front", "scan0", "out0", "scan1", "out1", "p0.f", "back0", "p0.f", "p1.f", "back1", "p0.f", "p1.f", "mix", "post0",
-    "post1", "p0.e", "p1.f", "out2", "p1.e", "p0.w", "p1.w", "p2.f", "p0.w", "p1.w", "p2.f", "p0.w", "gn", "p2.f",
-    "p1.w", "p0.own", "p2.e", "p0.got", "p1.own", "p2.w", "p1.got", "p2.w", "mixed", "p2.w", "p2.own", "p2.got",
+    "front", "scan0", "out0", "scan1", "mixed", "p0.f", "out1", "back01", "p0.f", "p1.f", "back00", "p0.f", "p1.f", "back11",
+    "p0.e", "p1.f", "back10", "p1.e", "ag", "post0", "post1", "out2", "gn",
+    "p2.f", "p2.f", "p2.f", "p2.e", "p2.b", "p2.w", "p2.w", "p2.w", "deal", "p2.own", "p2.got",
 )
+PARTS = 2
 
 
 def shards(
@@ -753,16 +1012,17 @@
     turned = xproj_weight.T
     sizes = [cols, rank, states, 2, taps + 1]
     used = -(-sum(sizes) // SUB) * SUB
+    gain_rows = model // 2 // (WIDE // LANES)
     order = Order()
     tie, done = order.tie, order.done
-    sets = [Reduced(order) for _ in range(3)]
-    heights = [fits(model), fits(model), fits(model + used)]
+    sets = [Reduced(order, orders(*heads)) for heads in (("xyz", "yxz"), ("xyz", "yzx", "zxy"), ("xyz", "zxy", "yzx"))]
     low = model // 2
-    spans = [
-        spans_of(heights[b], [(WIDE // 2, 1, b * WIDE, 0), (low, 0, 0, width + b * WIDE)]) for b in range(2)
-    ] + [spans_of(heights[2], [(low, 0, 0, 0), (low, 0, 0, WIDE), (used, 2, 0, 0)])]
-    state = {"targets": [blank((model, 2 * width)), blank((width, model)), blank((2 * used, WIDE))]}
-    scans, backs, posts, others = {}, {}, {}, {}
+    third = 3 * model // 8
+    heights = [[low, low], [third, third, model - 2 * third], [third, third, low]]
+    parts = [[(WIDE // 2, 1, b * WIDE, 0), (low, 0, 0, width + b * WIDE)] for b in range(2)]
+    parts.append([(low, 0, 0, 0), (low, 0, 0, WIDE), (used + gain_rows, 2, 0, 0)])
+    state = {"targets": [blank((model, 2 * width)), blank((width, model)), blank((2 * (used + gain_rows), WIDE))]}
+    scans, backs, posts, others, gains = {}, {}, {}, {}, {}
 
     def op_front():
         state["front"] = front(
@@ -780,41 +1040,55 @@
             b, core, mp, normed, og, act, in_weight, out_weight, dt_weight, row(dt_bias), dlog3, row(skip_gain)
         )
         done(scans[b][0])
-        others[b] = (swap(scans[b][1], CORE), swap(scans[b][2], CORE))
+        others[b] = (swap(scans[b][2], CORE), swap(scans[b][3], CORE))
 
     def op_out(b):
         normed, _, og, _, _, _ = state["front"]
         if b < 2:
-            own = [(scans[b][0], og), (normed, scans[b][2])]
-            other = [(others[b][0], state["og"]), (state["normed"], others[b][1])]
+            own = [(scans[b][0], og), (normed, scans[b][1])]
+            one, two = others[b]
+            low = model // 2
+            other = [
+                ([(one, 0, low)], [(state["og"], 0, model)]),
+                ([(state["normed"], 0, low)], [(one, low, one.shape[1] - low), (two, 0, two.shape[1])]),
+            ]
             small = ()
         else:
             own = [(normed, posts[q][0]) for q in range(2)]
-            other = [(state["normed"], others[2 + q]) for q in range(2)]
+            other = [([(state["normed"], 0, model // 2)], [(others[2 + q], 0, WIDE)]) for q in range(2)]
             small = (posts[0][1], posts[1][1], others["small"])
-        own, other, small = tie(own, other, small)
-        whole = outer(core, own, other, heights[b], small)
-        done(whole)
-        sets[b].begin(whole)
-
-    def op_back(b):
+        own, arrays, small = tie(own, [[[p[0] for p in pieces] for pieces in pair] for pair in other], small)
+        other = [
+            [[(a, *p[1:]) for a, p in zip(array, pieces)] for array, pieces in zip(pair, cut)]
+            for pair, cut in zip(arrays, other)
+        ]
+        flags = jnp.concatenate([sets[b].index(0), core])
+        if b < 2:
+            got = outer(core, own, other, heights[b], flags, in_weight, ((1, width + b * WIDE),))
+            gains[b] = got[-1]
+        else:
+            got = outer(
+                core, own, other, heights[b], flags, in_weight, ((0, 0), (1, WIDE)), (gains[0], gains[1]), small
+            )
+        done(got[1])
+        chunks = len(heights[b])
+        sets[b].begin(got[0 : 2 * chunks : 2], got[1 : 2 * chunks : 2])
+
+    def op_back(b, part):
         _, _, _, _, act, mp = state["front"]
         mp, = tie(mp)
-        backs[b] = back(b, mp, act, scans[b][4], scans[b][3], scans[b][5], dt_weight, dlog3)
-        done(backs[b][0])
-
-    def op_mix():
-        v = tie(*[[backs[b][2], backs[b][4]] for b in range(2)])
-        state["gmix"] = jnp.concatenate([v[0][0] + v[1][0], (v[0][1] + v[1][1])[:, rank:cols]], axis=1).astype(BF16)
-        done(state["gmix"])
+        carry = backs[b, part + 1][4] if part < PARTS - 1 else None
+        backs[b, part] = back(
+            b, part, PARTS, mp, act, scans[b][5], scans[b][4], scans[b][6], dt_weight, dlog3, carry
+        )
+        done(backs[b, part][0])
 
     def op_post(b):
         _, _, _, inner, act, _ = state["front"]
-        gmix, = tie(state["gmix"])
-        back_b = backs[b]
+        parts, every = tie([backs[b, k] for k in range(PARTS)], [backs[q, k][1:4:2] for q in range(2) for k in range(PARTS)])
         posts[b] = post(
-            b, used, gmix, scans[b][3], back_b[0], act, inner, turned, conv_weight, row(conv_bias), row(skip_gain),
-            back_b[3], back_b[5].reshape(states, WIDE), back_b[6],
+            b, used, scans[b][4], act, inner, turned, conv_weight, row(conv_bias), row(skip_gain), parts[0][4], decay_log,
+            [p[0] for p in parts], [p[2] for p in parts], [p[5] for p in parts], [v[0] for v in every], [v[1] for v in every],
         )
         done(posts[b][0])
         others[2 + b] = swap(posts[b][0], CORE)
@@ -822,7 +1096,7 @@
             others["small"] = swap(jnp.where(core[0] == 0, posts[1][1], posts[0][1]), CORE)
 
     def op_gn():
-        parts = tie(posts[0][0], posts[1][0], scans[0][2], scans[1][2])
+        parts = tie(posts[0][0], posts[1][0], scans[0][1], scans[1][1])
         grad_projected = jnp.concatenate([v.astype(BF16) for v in parts], axis=1)
         grad_normed = dot(grad_projected, in_weight, ((1,), (1,)))
         x = tok.astype(F32)
@@ -844,8 +1118,29 @@
     def op_put(p, pieces):
         arrays, targets = tie([v[0] for v in pieces], state["targets"])
         pieces = [(a,) + v[1:] for a, v in zip(arrays, pieces)]
-        state["targets"] = put(targets, pieces, spans[p], sets[p].flags())
+        state["targets"] = put(targets, pieces, parts[p], heights[p], sets[p].flags())
         done(state["targets"][0])
+
+    def op_ag():
+        state["split"] = all(v % SUB == 0 for p in sets[:2] for v in p.sizes)
+        if state["split"]:
+            mine = jnp.concatenate([p.share[0] for p in sets[:2]])
+            state["gathered"] = lax.all_gather(mine, ("dp", "rep"), axis=0, tiled=True)
+        else:
+            for p in sets[:2]:
+                p.back()
+
+    def op_deal():
+        if state["split"]:
+            gathered, targets = tie(state["gathered"], state["targets"])
+            state["targets"] = deal(targets, gathered, sets[:2], parts[:2])
+            done(state["targets"][0])
+            return
+        for p in range(2):
+            while sets[p].k > 0:
+                sets[p].widen()
+            op_put(p, sets[p].own())
+            op_put(p, sets[p].arrived())
 
     for name in SEQUENCE:
         if name[0] == "p" and name[2] == ".":
@@ -854,18 +1149,24 @@
                 sets[p].fold()
             elif what == "e":
                 sets[p].finish()
+            elif what == "b":
+                sets[p].back()
             elif what == "w":
                 sets[p].widen()
             else:
                 op_put(p, sets[p].own() if what == "own" else sets[p].arrived())
+        elif name[:4] == "back":
+            op_back(int(name[4]), int(name[5]))
         elif name[-1] in "012":
-            {"scan": op_scan, "out": op_out, "back": op_back, "post": op_post}[name[:-1]](int(name[-1]))
+            {"scan": op_scan, "out": op_out, "post": op_post}[name[:-1]](int(name[-1]))
         else:
-            {"front": op_front, "mix": op_mix, "gn": op_gn, "mixed": op_mixed}[name]()
+            {"front": op_front, "gn": op_gn, "mixed": op_mixed, "ag": op_ag, "deal": op_deal}[name]()
 
     grad_in, grad_out, small = state["targets"]
-    grad_gain = jnp.sum(grad_in * in_weight.astype(F32), axis=1) / norm_gain
-    small = jnp.concatenate([small[:used], small[used:]], axis=1)
+    lines = small.reshape(2, used + gain_rows, WIDE)
+    grad_gain = jnp.sum(lines[:, used:].reshape(2, gain_rows, WIDE // LANES, LANES), axis=3)
+    grad_gain = jnp.swapaxes(grad_gain, 1, 2).reshape(-1) / norm_gain
+    small = jnp.concatenate([lines[0, :used], lines[1, :used]], axis=1)
     ends = [sum(sizes[: i + 1]) for i in range(len(sizes))]
     cut = [small[e - n : e] for e, n in zip(ends, sizes)]
     return (

time: 497 us -> 433 us (0.87)
  other arithmetic: 75.4 us -> 11.3 us
  starting transfers between devices: 75.2 us -> 46.1 us
  waiting for transfers between devices: 127 us -> 145 us
  between operations: 3.05 us -> 15.9 us
    add x62 -> x0, other arithmetic: 49 us -> none  [part(): return sum(values[1:], values[0])]
    ppermute x87 -> x51, starting transfers between devices: 75.2 us -> 46 us  [swap(): return lax.ppermute(value, axis, [(i, i ^ 1 << place) for i in range(size)])]
    pallas_call x9 -> x27, Pallas kernels: 128 us -> 155 us  [the longest x4 59.2 us: back(): pl.pallas_call(functools.partial(back_kernel, first), grid=(1,), in_specs...]
    pallas_call x6 -> x2, Pallas kernels: 31 us -> 8.27 us  [put(): pl.pallas_call(body, out_shape=[jax.ShapeDtypeStruct(t.shape, F32) for t...]
    ppermute x87 -> x51, waiting for transfers between devices: 127 us -> 145 us  [swap(): return lax.ppermute(value, axis, [(i, i ^ 1 << place) for i in range(size)])]
    reduce_sum x1, other arithmetic: 8.97 us -> 0.2 us  [shards(): jnp.sum(lines[:, used:].reshape(2, gain_rows, WIDE // LANES, LANES), axis=3)]
    unnamed x121 -> x162, local copies, waits for them, and re-layouts: 16.7 us -> 25.3 us
    dynamic_slice x3 -> x0, local copies, waits for them, and re-layouts: 7.53 us -> none  [slab(): return lax.dynamic_slice_in_dim(value, start, rows, 0)]
  transfers between devices with their start and end apart: 87 -> 52, of which waited for: 31 -> 21; matrix products, arithmetic and copies ran while one was open for 15% -> 4% of each run, Pallas kernels for 21% -> 34%
where the time goes in v2:
time: 433 us; the launch traced here: 427 us
  Pallas kernels  171 us (39%)
  waiting for transfers between devices  145 us (33%)
  starting transfers between devices  46.1 us (11%)
  local copies, waits for them, and re-layouts  25.6 us (6%)
  between operations  15.9 us (4%)
  matrix products  11.8 us (3%)
  other arithmetic  11.3 us (3%)
    ppermute x51, waiting for transfers between devices, swap(): return lax.ppermute(value, axis, [(i, i ^ 1 << place) for i in range(size)])  145 us
    pallas_call x4, Pallas kernels, back(): pl.pallas_call(functools.partial(back_kernel, first), grid=(1,), in_specs...  59.2 us
    ppermute x51, starting transfers between devices, swap(): return lax.ppermute(value, axis, [(i, i ^ 1 << place) for i in range(size)])  46 us
    pallas_call x2, Pallas kernels, scan(): pl.pallas_call(functools.partial(scan_kernel, block), grid=(1,), in_specs...  29.5 us
    unnamed x162, local copies, waits for them, and re-layouts  25.3 us
    pallas_call x3, Pallas kernels, outer(): pl.pallas_call(body, out_shape=out_shape, grid_spec=pltpu.PrefetchScalarG...  23.3 us
    pallas_call x1, Pallas kernels, deal(): pl.pallas_call(body, out_shape=[jax.ShapeDtypeStruct(t.shape, F32) for t...  15.3 us
    pallas_call x15, Pallas kernels, step_call(): pl.pallas_call(body, out_shape=outs, grid_spec=pltpu.PrefetchScalarGridSp...  14.3 us
  transfers between devices with their start and end apart: 52, of which 21 were waited for; matrix products, arithmetic and copies ran while one was open for 4% of the time, Pallas kernels for 34%

profile of v2, /device:TPU:0, one launch (start us, length us, event | category | flops | bytes accessed | tf_op | source)
XLA Modules:
  0.0 426.9 jit_solution(9466044067685013157)
XLA Ops:
  8.5 7.7 %front.1 = (bf16[320,1024]{1,0:T(8,128)(2,1)}, f32[320,512]{1,0:T(8,128)}, f32[320,1024]{1,0:T(8,128)}, f32[320,2048]{1,0:T(8,128)}, bf16[320,2048]{1,0:T(8,128)(2,1)}, /*index=5*/f32[320,96]{1,0:T(8,128)}) custom-call(s32[2]{0:T(128)} %pad_add_fusion.len_ref, bf16[320,1024]{1,0:T(8,128)(2,1)} %bitcast.54, bf16[320,1024]{1,0:T(8,128)(2,1)} %bitcast.58, ...), custom_call_target="tpu_custom_call" | custom-call | flops 1 | bytes 1 | tf_op jit(solution)/shard_map/front/pallas_call | solution.py:75
  17.3 14.6 %scan0.1 = (bf16[320,1024]{1,0:T(8,128)(2,1)}, bf16[320,1024]{1,0:T(8,128)(2,1)}, f32[320,768]{1,0:T(8,128)}, f32[320,768]{1,0:T(8,128)}, f32[2560,128]{1,0:T(8,...) custom-call(s32[1]{0:T(128)} %bitcast.2.core_ref, f32[320,96]{1,0:T(8,128)} %get-tuple-element.429.mp_ref, ...), custom_call_target="tpu_custom_call" | custom-call | flops 1 | bytes 1 | tf_op jit(solution)/shard_map/scan0/pallas_call | solution.py:247
  33.2 3.9 collective-permute-done.2.refs_5_.refs_1_
  38.8 6.6 %outer.3 = (f32[256,1024]{1,0:T(8,128)}, f32[256,1024]{1,0:T(8,128)}, f32[256,1024]{1,0:T(8,128)}, f32[256,1024]{1,0:T(8,128)}, f32[512,128]{1,0:T(8,128)}) custom-call(s32[3]{0:T(128)} %pad_add_fusion.1.flag_ref, bf16[320,1024]{1,0:T(8,128)(2,1)} %get-tuple-element.328.refs_0_, f32[320,768]{1,0:T(8,128)} %copy-done.70, ...), custom_call_target="tpu_custom_call" | custom-call | flops 1 | bytes 1 | tf_op jit(solution)/shard_map/outer/pallas_call | solution.py:633
  45.3 2.7 collective-permute-start.6
  48.0 1.6 collective-permute-start.7
  49.6 14.9 %scan1.1 = (bf16[320,1024]{1,0:T(8,128)(2,1)}, bf16[320,1024]{1,0:T(8,128)(2,1)}, f32[320,768]{1,0:T(8,128)}, f32[320,768]{1,0:T(8,128)}, f32[2560,128]{1,0:T(8,...) custom-call(s32[1]{0:T(128)} %bitcast.2.core_ref, f32[320,96]{1,0:T(8,128)} %get-tuple-element.429.mp_ref, ...), custom_call_target="tpu_custom_call" | custom-call | flops 1 | bytes 1 | tf_op jit(solution)/shard_map/scan1/pallas_call | solution.py:247
  65.8 4.9 %fusion.13 = bf16[320,1024]{1,0:T(8,128)(2,1)} fusion(bf16[2048,1024]{1,0:T(8,128)(2,1)} %wout_hbm.3, bf16[320,1024]{1,0:T(8,128)(2,1)} %get-tuple-element.343.refs_0_, bf16[320,1024]{1,0:T(8,128)(2,1)S(1)} %copy-done.77, pred[320]{0:T(512)(128)(4,1)S(1)} %iota_compare_fusion, bf16[1,320,1024]{2,1,0:T(8,128)(2,1)S(1)} %copy-done.64), kind=kOutput, calls=%fused_computation.23 | convolution fusion | flops 1346109440 | bytes 6816064 | tf_op jit(solution)/shard_map/dot_general | solution.py:23
  70.7 1.3 collective-permute-done.6.refs_1_.refs_3_
  71.9 1.5 collective-permute-done.7.refs_5_.refs_7_
  76.7 6.9 %outer.4 = (f32[192,1024]{1,0:T(8,128)}, f32[192,1024]{1,0:T(8,128)}, f32[192,1024]{1,0:T(8,128)}, f32[192,1024]{1,0:T(8,128)}, f32[128,1024]{1,0:T(8,128)}, /*index=5*/f32[128,1024]{1,0:T(8,128)}, f32[512,128]{1,0:T(8,128)}) custom-call(s32[4]{0:T(128)} %add_add_fusion.1.flag_ref, bf16[320,1024]{1,0:T(8,128)(2,1)} %get-tuple-element.343.refs_0_, ...), custom_call_target="tpu_custom_call" | custom-call | flops 1 | bytes 1 | tf_op jit(solution)/shard_map/outer/pallas_call | solution.py:633
  84.1 1.7 collective-permute-start.9
  86.1 1.7 collective-permute-start.12
  87.8 1.6 collective-permute-start.10
  89.5 1.3 copy-done.11
  90.8 1.3 copy-done.13
  92.1 12.6 %back01.1 = (f32[160,1024]{1,0:T(8,128)S(1)}, f32[160,64]{1,0:T(8,128)S(1)}, f32[64,1024]{1,0:T(8,128)S(1)}, f32[160,128]{1,0:T(8,128)S(1)}, f32[2,16,8,128]{3,2,1,0:T(8,128)S(1)}, /*index=5*/f32[2,1024]{1,0:T(2,128)S(1)}) custom-call(f32[320,96]{1,0:T(8,128)S(1)} %copy-done.7, bf16[320,2048]{1,0:T(8,128)(2,1)S(1)} %copy-done, f32[2560,128]{1,0:T(8,128)S(1)} %copy-done.11, ...), custom_call_target="tpu_custom_call" | custom-call | flops 1 | bytes 1 | tf_op jit(solution)/shard_map/back01/pallas_call | solution.py:426
  104.8 9.5 %collective-permute-done.11.refs_1_.refs_3_ = f32[128,1024]{1,0:T(8,128)S(1)} collective-permute-done((f32[128,1024]{1,0:T(8,128)}, f32[128,1024]{1,0:T(8,128)S(1)}, u32[]{:S(2)}, u32[]{:S(2)}) %collective-permute-start.11) | collective-permute-done | bytes 524320 | tf_op jit(solution)/shard_map/ppermute | solution.py:804
  114.3 1.5 fold.10
  115.8 1.6 collective-permute-start.16
  117.5 1.6 fold.11
  121.3 1.6 collective-permute-start.13
  123.3 1.4 collective-permute-start.15
  125.7 1.3 copy-done.12
  127.1 1.3 copy-done.14
  129.3 12.6 %back00.1 = (f32[160,1024]{1,0:T(8,128)S(1)}, f32[160,64]{1,0:T(8,128)S(1)}, f32[64,1024]{1,0:T(8,128)S(1)}, f32[160,128]{1,0:T(8,128)S(1)}, f32[2,16,8,128]{3,2,1,0:T(8,128)S(1)}, /*index=5*/f32[2,1024]{1,0:T(2,128)S(1)}) custom-call(f32[320,96]{1,0:T(8,128)S(1)} %copy-done.8, bf16[320,2048]{1,0:T(8,128)(2,1)S(1)} %copy-done, f32[2560,128]{1,0:T(8,128)S(1)} %copy-done.12, ...), custom_call_target="tpu_custom_call" | custom-call | flops 1 | bytes 1 | tf_op jit(solution)/shard_map/back00/pallas_call | solution.py:426
  142.9 2.6 collective-permute-start.20
  145.6 2.2 fold.13
  147.8 1.7 collective-permute-start.17
  150.6 12.6 %back11.1 = (f32[160,1024]{1,0:T(8,128)S(1)}, f32[160,64]{1,0:T(8,128)S(1)}, f32[64,1024]{1,0:T(8,128)S(1)}, f32[160,128]{1,0:T(8,128)S(1)}, f32[2,16,8,128]{3,2,1,0:T(8,128)S(1)}, /*index=5*/f32[2,1024]{1,0:T(2,128)S(1)}) custom-call(f32[320,96]{1,0:T(8,128)S(1)} %copy-done.8, bf16[320,2048]{1,0:T(8,128)(2,1)S(1)} %copy-done, f32[2560,128]{1,0:T(8,128)S(1)} %copy-done.9, ...), custom_call_target="tpu_custom_call" | custom-call | flops 1 | bytes 1 | tf_op jit(solution)/shard_map/back11/pallas_call | solution.py:426
  165.9 21.3 %back10.1 = (f32[160,1024]{1,0:T(8,128)S(1)}, f32[160,64]{1,0:T(8,128)S(1)}, f32[64,1024]{1,0:T(8,128)S(1)}, f32[160,128]{1,0:T(8,128)S(1)}, f32[2,16,8,128]{3,2,1,0:T(8,128)S(1)}, /*index=5*/f32[2,1024]{1,0:T(2,128)S(1)}) custom-call(f32[320,96]{1,0:T(8,128)S(1)} %copy-done.8, bf16[320,2048]{1,0:T(8,128)(2,1)S(1)} %copy-done, f32[2560,128]{1,0:T(8,128)S(1)} %copy-done.9, ...), custom_call_target="tpu_custom_call" | custom-call | flops 1 | bytes 1 | tf_op jit(solution)/shard_map/back10/pallas_call | solution.py:426
  191.6 6.6 %post0.1 = (f32[320,1024]{1,0:T(8,128)}, f32[184,1024]{1,0:T(8,128)}) custom-call(f32[2560,128]{1,0:T(8,128)} %get-tuple-element.330.gs_ref, bf16[320,2048]{1,0:T(8,128)(2,1)} %get-tuple-element.308.act_ref, f32[320,2048]{1,0:T(8,128)} %get-tuple-element.331.inner_ref, bf16[96,2048]{1,0:T(8,128)(2,1)} %bitcast.56, f32[4,2048]{1,0:T(4,128)} %cw_ref.5, ...), custom_call_target="tpu_custom_call" | custom-call | flops 1 | bytes 1 | tf_op jit(solution)/shard_map/post0/pallas_call | solution.py:511
  198.2 7.0 %post1.1 = (f32[320,1024]{1,0:T(8,128)}, f32[184,1024]{1,0:T(8,128)}) custom-call(f32[2560,128]{1,0:T(8,128)} %get-tuple-element.416.gs_ref, bf16[320,2048]{1,0:T(8,128)(2,1)} %get-tuple-element.308.act_ref, f32[320,2048]{1,0:T(8,128)} %get-tuple-element.331.inner_ref, bf16[96,2048]{1,0:T(8,128)(2,1)} %bitcast.57, f32[4,2048]{1,0:T(4,128)} %cw_ref.5, ...), custom_call_target="tpu_custom_call" | custom-call | flops 1 | bytes 1 | tf_op jit(solution)/shard_map/post1/pallas_call | solution.py:511
  208.0 3.3 collective-permute-done.24.refs_13_
  212.2 9.9 %outer.5 = (f32[192,1024]{1,0:T(8,128)}, f32[192,1024]{1,0:T(8,128)}, f32[192,1024]{1,0:T(8,128)}, f32[192,1024]{1,0:T(8,128)}, f32[256,1024]{1,0:T(8,128)}, /*index=5*/f32[256,1024]{1,0:T(8,128)}, f32[512,128]{1,0:T(8,128)}) custom-call(s32[4]{0:T(128)} %add_add_fusion.3.flag_ref, bf16[320,1024]{1,0:T(8,128)(2,1)} %get-tuple-element.486.normed_hbm.refs_4_.refs_0_, ...), custom_call_target="tpu_custom_call" | custom-call | flops 1 | bytes 1 | tf_op jit(solution)/shard_map/outer/pallas_call | solution.py:633
  223.7 1.5 collective-permute-start.27
  225.2 1.4 collective-permute-start.25
  227.2 6.9 %fusion.14 = (f32[320]{0:T(512)S(1)}, f32[320,1024]{1,0:T(8,128)S(1)}) fusion(f32[320]{0:T(512)S(1)} %add_rsqrt_fusion, bf16[1,320,1024]{2,1,0:T(8,128)(2,1)S(1)} %copy-done.65, f32[1024]{0:T(1024)S(1)} %copy-done.78, bf16[1024,4096]{1,0:T(8,128)(2,1)} %refs_8_.1, bf16[320,1024]{1,0:T(8,128)(2,1)S(1)} %copy-done.76, bf16[320,1024]{1,0:T(8,128)(2,1)S(1)} %copy-done.75, ...), kind=kOutput, calls=%fused_computation.24 | convolution fusion | flops 2696478464 | bytes 12982784 | tf_op jit(solution)/shard_map/dot_general | solution.py:23
  234.2 1.4 fusion.17
  235.6 19.3 %collective-permute-done.25.refs_1_.refs_3_ = f32[192,1024]{1,0:T(8,128)S(1)} collective-permute-done((f32[192,1024]{1,0:T(8,128)}, f32[192,1024]{1,0:T(8,128)S(1)}, u32[]{:S(2)}, u32[]{:S(2)}) %collective-permute-start.25) | collective-permute-done | bytes 786464 | tf_op jit(solution)/shard_map/ppermute | solution.py:804
  254.9 7.6 %collective-permute-done.26.refs_5_.refs_7_ = f32[192,1024]{1,0:T(8,128)S(1)} collective-permute-done((f32[192,1024]{1,0:T(8,128)}, f32[192,1024]{1,0:T(8,128)S(1)}, u32[]{:S(2)}, u32[]{:S(2)}) %collective-permute-start.26) | collective-permute-done | bytes 786464 | tf_op jit(solution)/shard_map/ppermute | solution.py:804
  264.0 2.4 collective-permute-start.29
  266.4 12.6 %collective-permute-done.28.refs_1_.refs_3_ = f32[96,1024]{1,0:T(8,128)S(1)} collective-permute-done((f32[96,1024]{1,0:T(8,128)S(1)}, f32[96,1024]{1,0:T(8,128)S(1)}, u32[]{:S(2)}, u32[]{:S(2)}) %collective-permute-start.28) | collective-permute-done | bytes 393248 | tf_op jit(solution)/shard_map/ppermute | solution.py:804
  279.0 3.3 collective-permute-done.29.refs_5_.refs_7_
  282.2 15.4 %collective-permute-done.30.refs_9_.refs_11_ = f32[128,1024]{1,0:T(8,128)S(1)} collective-permute-done((f32[128,1024]{1,0:T(8,128)S(1)}, f32[128,1024]{1,0:T(8,128)S(1)}, u32[]{:S(2)}, u32[]{:S(2)}) %collective-permute-start.30) | collective-permute-done | bytes 524320 | tf_op jit(solution)/shard_map/ppermute | solution.py:804
  298.3 2.1 collective-permute-start.33
  300.5 1.5 collective-permute-start.32
  301.9 11.3 %collective-permute-done.31.refs_1_.refs_3_ = f32[48,1024]{1,0:T(8,128)S(1)} collective-permute-done((f32[48,1024]{1,0:T(8,128)S(1)}, f32[48,1024]{1,0:T(8,128)S(1)}, u32[]{:S(2)}, u32[]{:S(2)}) %collective-permute-start.31) | collective-permute-done | bytes 196640 | tf_op jit(solution)/shard_map/ppermute | solution.py:804
  314.0 26.4 %collective-permute-done.34.refs_3_ = f32[80,1024]{1,0:T(8,128)S(1)} collective-permute-done((f32[80,1024]{1,0:T(8,128)S(1)}, f32[80,1024]{1,0:T(8,128)S(1)}, u32[]{:S(2)}, u32[]{:S(2)}) %collective-permute-start.34) | collective-permute-done | bytes 327712 | tf_op jit(solution)/shard_map/ppermute | solution.py:804
  341.1 15.1 %collective-permute-done.35.refs_1_ = f32[80,1024]{1,0:T(8,128)S(1)} collective-permute-done((f32[80,1024]{1,0:T(8,128)S(1)}, f32[80,1024]{1,0:T(8,128)S(1)}, u32[]{:S(2)}, u32[]{:S(2)}) %collective-permute-start.35) | collective-permute-done | bytes 327712 | tf_op jit(solution)/shard_map/ppermute | solution.py:804
  357.1 2.3 collective-permute-start.37
  359.4 3.3 collective-permute-done.36.refs_3_
  363.8 1.7 collective-permute-start.41
  365.5 1.9 collective-permute-start.39
  367.4 2.1 collective-permute-start.40
  369.5 3.9 collective-permute-done.39.refs_3_
  373.3 1.9 collective-permute-done.40.refs_4_
  375.2 1.9 widen.5
  378.8 1.3 collective-permute-start.42
  383.4 15.3 %deal.1 = (f32[1024,4096]{1,0:T(8,128)}, f32[2048,1024]{1,0:T(8,128)}, f32[496,1024]{1,0:T(8,128)}) custom-call(f32[1024,4096]{1,0:T(8,128)} %blank.3.refs_0_, f32[2048,1024]{1,0:T(8,128)} %blank.4.refs_1_, f32[496,1024]{1,0:T(8,128)} %copy-done.1, ...), custom_call_target="tpu_custom_call", output_to_operand_aliasing={{0}: (0, {}), {1}: (1, {}), {2}: (2, {})} | custom-call | flops 1 | bytes 1 | tf_op jit(solution)/shard_map/deal/pallas_call | solution.py:977
  398.8 1.6 copy-done.2
  401.5 4.6 %put.2 = (f32[1024,4096]{1,0:T(8,128)}, f32[2048,1024]{1,0:T(8,128)}, f32[496,1024]{1,0:T(8,128)S(1)}) custom-call(s32[8]{0:T(128)S(1)} %stack.56.flag_ref, f32[1024,4096]{1,0:T(8,128)} %get-tuple-element.573.refs_0_, f32[2048,1024]{1,0:T(8,128)} %get-tuple-element.574.refs_1_, ...), custom_call_target="tpu_custom_call", output_to_operand_aliasing={{0}: (1, {}), {1}: (2, {}), {2}: (3, {})} | custom-call | flops 1 | bytes 1 | tf_op jit(solution)/shard_map/put/pallas_call | solution.py:776
  406.7 3.4 collective-permute-done.48.refs_6_
  411.3 3.7 put.3
  (271 shorter events, 47.7 us)
Async XLA Ops:
  7.2 376.2 %all-gather.2.cloned.1.call-start = ((), (), s32[]{:S(2)}) async-start(), calls=%async_computation | async-start | bytes 17301504 | tf_op jit(solution)/shard_map/all_gather | solution.py:1128
  16.1 21.0 %collective-permute-start.1 = (f32[320,1024]{1,0:T(8,128)}, f32[320,1024]{1,0:T(8,128)S(1)}, u32[]{:S(2)}, u32[]{:S(2)}) collective-permute-start(f32[320,1024]{1,0:T(8,128)} %get-tuple-element.345.og_hbm.refs_2_), channel_id=1, source_target_pairs={{0,1},{1,0},{2,3},{3,2},{4,5},{5,4},{6,7},{7,6},{8,9},{9,8},{10,11... | collective-permute-start | bytes 3932168 | tf_op jit(solution)/shard_map/ppermute | solution.py:804
  32.0 5.2 %collective-permute-start = (f32[320,768]{1,0:T(8,128)}, f32[320,768]{1,0:T(8,128)S(1)}, u32[]{:S(2)}, u32[]{:S(2)}) collective-permute-start(f32[320,768]{1,0:T(8,128)} %get-tuple-element.313), channel_id=1, source_target_pairs={{0,1},{1,0},{2,3},{3,2},{4,5},{5,4},{6,7},{7,6},{8,9},{9,8},{10,11... | collective-permute-start | bytes 2949128 | tf_op jit(solution)/shard_map/ppermute | solution.py:804
  32.1 5.1 %collective-permute-start.3 = (f32[320,768]{1,0:T(8,128)}, f32[320,768]{1,0:T(8,128)}, u32[]{:S(2)}, u32[]{:S(2)}) collective-permute-start(f32[320,768]{1,0:T(8,128)} %get-tuple-element.315), channel_id=1, source_target_pairs={{0,1},{1,0},{2,3},{3,2},{4,5},{5,4},{6,7},{7,6},{8,9},{9,8},{10,11... | collective-permute-start | bytes 2949128 | tf_op jit(solution)/shard_map/ppermute | solution.py:804
  32.5 4.6 %collective-permute-start.2 = (f32[320,512]{1,0:T(8,128)}, f32[320,512]{1,0:T(8,128)S(1)}, u32[]{:S(2)}, u32[]{:S(2)}) collective-permute-start(f32[320,512]{1,0:T(8,128)} %get-tuple-element.314), channel_id=1, source_target_pairs={{0,1},{1,0},{2,3},{3,2},{4,5},{5,4},{6,7},{7,6},{8,9},{9,8},{10,11... | collective-permute-start | bytes 1966088 | tf_op jit(solution)/shard_map/ppermute | solution.py:804
  45.3 26.6 %collective-permute-start.6 = (f32[256,1024]{1,0:T(8,128)}, f32[256,1024]{1,0:T(8,128)S(1)}, u32[]{:S(2)}, u32[]{:S(2)}) collective-permute-start(f32[256,1024]{1,0:T(8,128)} %get-tuple-element.336), channel_id=1, source_target_pairs={{0,4},{4,0},{8,12},{12,8},{16,20},{20,16},{24,28},{28,24},{1,5},{5... | collective-permute-start | bytes 3145736 | tf_op jit(solution)/shard_map/ppermute | solution.py:804
  48.0 25.4 %collective-permute-start.7 = (f32[256,1024]{1,0:T(8,128)}, f32[256,1024]{1,0:T(8,128)S(1)}, u32[]{:S(2)}, u32[]{:S(2)}) collective-permute-start(f32[256,1024]{1,0:T(8,128)} %get-tuple-element.337), channel_id=1, source_target_pairs={{0,2},{1,3},{2,0},{3,1},{4,6},{5,7},{6,4},{7,5},{8,10},{9,11},{10,... | collective-permute-start | bytes 3145736 | tf_op jit(solution)/shard_map/ppermute | solution.py:804
  49.6 16.1 %copy-start.64 = (bf16[1,320,1024]{2,1,0:T(8,128)(2,1)S(1)}, bf16[1,320,1024]{2,1,0:T(8,128)(2,1)}, u32[]{:S(2)}) copy-start(bf16[1,320,1024]{2,1,0:T(8,128)(2,1)} %param.13) | copy-start | bytes 1966084
  49.6 16.1 %copy-start.77 = (bf16[320,1024]{1,0:T(8,128)(2,1)S(1)}, bf16[320,1024]{1,0:T(8,128)(2,1)}, u32[]{:S(2)}) copy-start(bf16[320,1024]{1,0:T(8,128)(2,1)} %get-tuple-element.328.refs_0_) | copy-start | bytes 1966084
  64.5 12.2 %collective-permute-start.4 = (f32[320,768]{1,0:T(8,128)}, f32[320,768]{1,0:T(8,128)}, u32[]{:S(2)}, u32[]{:S(2)}) collective-permute-start(f32[320,768]{1,0:T(8,128)} %get-tuple-element.333), channel_id=1, source_target_pairs={{0,1},{1,0},{2,3},{3,2},{4,5},{5,4},{6,7},{7,6},{8,9},{9,8},{10,11... | collective-permute-start | bytes 2949128 | tf_op jit(solution)/shard_map/ppermute | solution.py:804
  64.6 12.1 %collective-permute-start.5 = (f32[320,768]{1,0:T(8,128)}, f32[320,768]{1,0:T(8,128)}, u32[]{:S(2)}, u32[]{:S(2)}) collective-permute-start(f32[320,768]{1,0:T(8,128)} %get-tuple-element.334), channel_id=1, source_target_pairs={{0,1},{1,0},{2,3},{3,2},{4,5},{5,4},{6,7},{7,6},{8,9},{9,8},{10,11... | collective-permute-start | bytes 2949128 | tf_op jit(solution)/shard_map/ppermute | solution.py:804
  76.7 12.8 %copy-start = (bf16[320,2048]{1,0:T(8,128)(2,1)S(1)}, bf16[320,2048]{1,0:T(8,128)(2,1)}, u32[]{:S(2)}) copy-start(bf16[320,2048]{1,0:T(8,128)(2,1)} %get-tuple-element.308.act_ref) | copy-start | bytes 3932164
  76.7 12.8 %copy-start.3 = (f32[2560,128]{1,0:T(8,128)S(1)}, f32[2560,128]{1,0:T(8,128)}, u32[]{:S(2)}) copy-start(f32[2560,128]{1,0:T(8,128)} %get-tuple-element.330.gs_ref) | copy-start | bytes 3932164
  76.7 12.8 %copy-start.5 = (bf16[64,2048]{1,0:T(8,128)(2,1)S(1)}, bf16[64,2048]{1,0:T(8,128)(2,1)}, u32[]{:S(2)}) copy-start(bf16[64,2048]{1,0:T(8,128)(2,1)} %dtw_ref.11) | copy-start | bytes 786436
  76.7 12.7 %copy-start.6 = (f32[2,8,16,128]{3,2,1,0:T(8,128)S(1)}, f32[2,8,16,128]{3,2,1,0:T(8,128)}, u32[]{:S(2)}) copy-start(f32[2,8,16,128]{3,2,1,0:T(8,128)} %copy.35) | copy-start | bytes 393220
  83.6 33.8 %collective-permute-start.8 = (f32[192,1024]{1,0:T(8,128)}, f32[192,1024]{1,0:T(8,128)S(1)}, u32[]{:S(2)}, u32[]{:S(2)}) collective-permute-start(f32[192,1024]{1,0:T(8,128)} %get-tuple-element.355), channel_id=1, source_target_pairs={{0,4},{4,0},{8,12},{12,8},{16,20},{20,16},{24,28},{28,24},{1,5},{5... | collective-permute-start | bytes 2359304 | tf_op jit(solution)/shard_map/ppermute | solution.py:804
  84.1 33.4 %collective-permute-start.9 = (f32[192,1024]{1,0:T(8,128)}, f32[192,1024]{1,0:T(8,128)S(1)}, u32[]{:S(2)}, u32[]{:S(2)}) collective-permute-start(f32[192,1024]{1,0:T(8,128)} %get-tuple-element.356), channel_id=1, source_target_pairs={{0,2},{1,3},{2,0},{3,1},{4,6},{5,7},{6,4},{7,5},{8,10},{9,11},{10,... | collective-permute-start | bytes 2359304 | tf_op jit(solution)/shard_map/ppermute | solution.py:804
  85.8 28.4 %collective-permute-start.11 = (f32[128,1024]{1,0:T(8,128)}, f32[128,1024]{1,0:T(8,128)S(1)}, u32[]{:S(2)}, u32[]{:S(2)}) collective-permute-start(f32[128,1024]{1,0:T(8,128)} %copy-done.62), channel_id=1, source_target_pairs={{0,2},{1,3},{2,0},{3,1},{4,6},{5,7},{6,4},{7,5},{8,10},{9,11},{10,... | collective-permute-start | bytes 1572872 | tf_op jit(solution)/shard_map/ppermute | solution.py:804
  86.1 28.1 %collective-permute-start.12 = (f32[128,1024]{1,0:T(8,128)}, f32[128,1024]{1,0:T(8,128)S(1)}, u32[]{:S(2)}, u32[]{:S(2)}) collective-permute-start(f32[128,1024]{1,0:T(8,128)} %copy-done.61), channel_id=1, source_target_pairs={{0,4},{4,0},{8,12},{12,8},{16,20},{20,16},{24,28},{28,24},{1,5},{5... | collective-permute-start | bytes 1572872 | tf_op jit(solution)/shard_map/ppermute | solution.py:804
  87.8 29.7 %collective-permute-start.10 = (f32[128,1024]{1,0:T(8,128)}, f32[128,1024]{1,0:T(8,128)S(1)}, u32[]{:S(2)}, u32[]{:S(2)}) collective-permute-start(f32[128,1024]{1,0:T(8,128)} %get-tuple-element.357), channel_id=1, source_target_pairs={{0,8},{4,12},{8,0},{12,4},{16,24},{20,28},{24,16},{28,20},{1,9},{5... | collective-permute-start | bytes 1572872 | tf_op jit(solution)/shard_map/ppermute | solution.py:804
  92.1 22.1 %copy-start.24 = (f32[128,1024]{1,0:T(8,128)S(1)}, f32[128,1024]{1,0:T(8,128)}, u32[]{:S(2)}) copy-start(f32[128,1024]{1,0:T(8,128)} %copy-done.23) | copy-start | bytes 1572868
  115.8 26.2 %collective-permute-start.16 = (f32[128,1024]{1,0:T(8,128)}, f32[128,1024]{1,0:T(8,128)S(1)}, u32[]{:S(2)}, u32[]{:S(2)}) collective-permute-start(f32[128,1024]{1,0:T(8,128)} %get-tuple-element.395), channel_id=1, source_target_pairs={{0,8},{4,12},{8,0},{12,4},{16,24},{20,28},{24,16},{28,20},{1,9},{5... | collective-permute-start | bytes 1572872 | tf_op jit(solution)/shard_map/ppermute | solution.py:804
  121.3 24.2 %collective-permute-start.13 = (f32[96,1024]{1,0:T(8,128)}, f32[96,1024]{1,0:T(8,128)}, u32[]{:S(2)}, u32[]{:S(2)}) collective-permute-start(f32[96,1024]{1,0:T(8,128)} %get-tuple-element.391), channel_id=1, source_target_pairs={{0,2},{1,3},{2,0},{3,1},{4,6},{5,7},{6,4},{7,5},{8,10},{9,11},{10,... | collective-permute-start | bytes 1179656 | tf_op jit(solution)/shard_map/ppermute | solution.py:804
  122.9 22.6 %collective-permute-start.14 = (f32[96,1024]{1,0:T(8,128)}, f32[96,1024]{1,0:T(8,128)}, u32[]{:S(2)}, u32[]{:S(2)}) collective-permute-start(f32[96,1024]{1,0:T(8,128)} %get-tuple-element.392), channel_id=1, source_target_pairs={{0,8},{4,12},{8,0},{12,4},{16,24},{20,28},{24,16},{28,20},{1,9},{5... | collective-permute-start | bytes 1179656 | tf_op jit(solution)/shard_map/ppermute | solution.py:804
  123.3 22.2 %collective-permute-start.15 = (f32[64,1024]{1,0:T(8,128)}, f32[64,1024]{1,0:T(8,128)}, u32[]{:S(2)}, u32[]{:S(2)}) collective-permute-start(f32[64,1024]{1,0:T(8,128)} %get-tuple-element.393), channel_id=1, source_target_pairs={{0,4},{4,0},{8,12},{12,8},{16,20},{20,16},{24,28},{28,24},{1,5},{5... | collective-permute-start | bytes 786440 | tf_op jit(solution)/shard_map/ppermute | solution.py:804
  142.9 21.0 %collective-permute-start.20 = (f32[64,1024]{1,0:T(8,128)S(1)}, f32[64,1024]{1,0:T(8,128)S(1)}, u32[]{:S(2)}, u32[]{:S(2)}) collective-permute-start(f32[64,1024]{1,0:T(8,128)S(1)} %get-tuple-element.413), channel_id=1, source_target_pairs={{0,16},{4,20},{8,24},{12,28},{16,0},{20,4},{24,8},{28,12},{1,17},{... | collective-permute-start | bytes 786440 | tf_op jit(solution)/shard_map/ppermute | solution.py:804
  147.8 16.7 %collective-permute-start.17 = (f32[48,1024]{1,0:T(8,128)S(1)}, f32[48,1024]{1,0:T(8,128)S(1)}, u32[]{:S(2)}, u32[]{:S(2)}) collective-permute-start(f32[48,1024]{1,0:T(8,128)S(1)} %get-tuple-element.409), channel_id=1, source_target_pairs={{0,8},{4,12},{8,0},{12,4},{16,24},{20,28},{24,16},{28,20},{1,9},{5... | collective-permute-start | bytes 589832 | tf_op jit(solution)/shard_map/ppermute | solution.py:804
  149.5 15.0 %collective-permute-start.18 = (f32[48,1024]{1,0:T(8,128)S(1)}, f32[48,1024]{1,0:T(8,128)S(1)}, u32[]{:S(2)}, u32[]{:S(2)}) collective-permute-start(f32[48,1024]{1,0:T(8,128)S(1)} %get-tuple-element.410), channel_id=1, source_target_pairs={{0,4},{4,0},{8,12},{12,8},{16,20},{20,16},{24,28},{28,24},{1,5},{5... | collective-permute-start | bytes 589832 | tf_op jit(solution)/shard_map/ppermute | solution.py:804
  150.1 14.4 %collective-permute-start.19 = (f32[32,1024]{1,0:T(8,128)S(1)}, f32[32,1024]{1,0:T(8,128)S(1)}, u32[]{:S(2)}, u32[]{:S(2)}) collective-permute-start(f32[32,1024]{1,0:T(8,128)S(1)} %get-tuple-element.411), channel_id=1, source_target_pairs={{0,2},{1,3},{2,0},{3,1},{4,6},{5,7},{6,4},{7,5},{8,10},{9,11},{10,... | collective-permute-start | bytes 393224 | tf_op jit(solution)/shard_map/ppermute | solution.py:804
  163.9 23.3 %copy-start.39 = (f32[160,1024]{1,0:T(8,128)}, f32[160,1024]{1,0:T(8,128)S(1)}, u32[]{:S(2)}) copy-start(f32[160,1024]{1,0:T(8,128)S(1)} %get-tuple-element.466.rest_1_) | copy-start | bytes 1966084
  163.9 23.3 %copy-start.51 = (f32[64,1024]{1,0:T(8,128)}, f32[64,1024]{1,0:T(8,128)S(1)}, u32[]{:S(2)}) copy-start(f32[64,1024]{1,0:T(8,128)S(1)} %get-tuple-element.468.rest_3_) | copy-start | bytes 786436
  165.2 24.9 %collective-permute-start.21 = (f32[64,1024]{1,0:T(8,128)S(1)}, f32[64,1024]{1,0:T(8,128)S(1)}, u32[]{:S(2)}, u32[]{:S(2)}) collective-permute-start(f32[64,1024]{1,0:T(8,128)S(1)} %get-tuple-element.437), channel_id=1, source_target_pairs={{0,16},{4,20},{8,24},{12,28},{16,0},{20,4},{24,8},{28,12},{1,17},{... | collective-permute-start | bytes 786440 | tf_op jit(solution)/shard_map/ppermute | solution.py:804
  205.2 6.1 %collective-permute-start.23 = (f32[320,1024]{1,0:T(8,128)}, f32[320,1024]{1,0:T(8,128)}, u32[]{:S(2)}, u32[]{:S(2)}) collective-permute-start(f32[320,1024]{1,0:T(8,128)} %get-tuple-element.497.refs_6_), channel_id=1, source_target_pairs={{0,1},{1,0},{2,3},{3,2},{4,5},{5,4},{6,7},{7,6},{8,9},{9,8},{10,11... | collective-permute-start | bytes 3932168 | tf_op jit(solution)/shard_map/ppermute | solution.py:804
  205.3 6.0 %collective-permute-start.22 = (f32[320,1024]{1,0:T(8,128)S(1)}, f32[320,1024]{1,0:T(8,128)}, u32[]{:S(2)}, u32[]{:S(2)}) collective-permute-start(f32[320,1024]{1,0:T(8,128)S(1)} %copy-done.67), channel_id=1, source_target_pairs={{0,1},{1,0},{2,3},{3,2},{4,5},{5,4},{6,7},{7,6},{8,9},{9,8},{10,11... | collective-permute-start | bytes 3932168 | tf_op jit(solution)/shard_map/ppermute | solution.py:804
  207.0 4.2 collective-permute-start.24
  223.7 38.8 %collective-permute-start.27 = (f32[256,1024]{1,0:T(8,128)S(1)}, f32[256,1024]{1,0:T(8,128)S(1)}, u32[]{:S(2)}, u32[]{:S(2)}) collective-permute-start(f32[256,1024]{1,0:T(8,128)S(1)} %copy-done.79), channel_id=1, source_target_pairs={{0,2},{1,3},{2,0},{3,1},{4,6},{5,7},{6,4},{7,5},{8,10},{9,11},{10,... | collective-permute-start | bytes 3145736 | tf_op jit(solution)/shard_map/ppermute | solution.py:804
  225.2 29.6 %collective-permute-start.25 = (f32[192,1024]{1,0:T(8,128)}, f32[192,1024]{1,0:T(8,128)S(1)}, u32[]{:S(2)}, u32[]{:S(2)}) collective-permute-start(f32[192,1024]{1,0:T(8,128)} %get-tuple-element.502), channel_id=1, source_target_pairs={{0,4},{4,0},{8,12},{12,8},{16,20},{20,16},{24,28},{28,24},{1,5},{5... | collective-permute-start | bytes 2359304 | tf_op jit(solution)/shard_map/ppermute | solution.py:804
  226.6 35.8 %collective-permute-start.26 = (f32[192,1024]{1,0:T(8,128)}, f32[192,1024]{1,0:T(8,128)S(1)}, u32[]{:S(2)}, u32[]{:S(2)}) collective-permute-start(f32[192,1024]{1,0:T(8,128)} %get-tuple-element.503), channel_id=1, source_target_pairs={{0,8},{4,12},{8,0},{12,4},{16,24},{20,28},{24,16},{28,20},{1,9},{5... | collective-permute-start | bytes 2359304 | tf_op jit(solution)/shard_map/ppermute | solution.py:804
  234.1 28.3 %copy-start.17 = (f32[256,1024]{1,0:T(8,128)S(1)}, f32[256,1024]{1,0:T(8,128)}, u32[]{:S(2)}) copy-start(f32[256,1024]{1,0:T(8,128)} %get-tuple-element.509.refs_8_.refs_10_) | copy-start | bytes 3145732
  234.1 28.3 %copy-start.20 = (f32[192,1024]{1,0:T(8,128)S(1)}, f32[192,1024]{1,0:T(8,128)}, u32[]{:S(2)}) copy-start(f32[192,1024]{1,0:T(8,128)} %get-tuple-element.505.refs_0_.refs_2_) | copy-start | bytes 2359300
  234.1 28.3 %copy-start.21 = (f32[192,1024]{1,0:T(8,128)S(1)}, f32[192,1024]{1,0:T(8,128)}, u32[]{:S(2)}) copy-start(f32[192,1024]{1,0:T(8,128)} %get-tuple-element.507.refs_4_.refs_6_) | copy-start | bytes 2359300
  263.3 34.4 %collective-permute-start.30 = (f32[128,1024]{1,0:T(8,128)S(1)}, f32[128,1024]{1,0:T(8,128)S(1)}, u32[]{:S(2)}, u32[]{:S(2)}) collective-permute-start(f32[128,1024]{1,0:T(8,128)S(1)} %get-tuple-element.516), channel_id=1, source_target_pairs={{0,8},{4,12},{8,0},{12,4},{16,24},{20,28},{24,16},{28,20},{1,9},{5... | collective-permute-start | bytes 1572872 | tf_op jit(solution)/shard_map/ppermute | solution.py:804
  263.4 15.6 %collective-permute-start.28 = (f32[96,1024]{1,0:T(8,128)S(1)}, f32[96,1024]{1,0:T(8,128)S(1)}, u32[]{:S(2)}, u32[]{:S(2)}) collective-permute-start(f32[96,1024]{1,0:T(8,128)S(1)} %get-tuple-element.514), channel_id=1, source_target_pairs={{0,2},{1,3},{2,0},{3,1},{4,6},{5,7},{6,4},{7,5},{8,10},{9,11},{10,... | collective-permute-start | bytes 1179656 | tf_op jit(solution)/shard_map/ppermute | solution.py:804
  264.0 18.2 %collective-permute-start.29 = (f32[96,1024]{1,0:T(8,128)S(1)}, f32[96,1024]{1,0:T(8,128)S(1)}, u32[]{:S(2)}, u32[]{:S(2)}) collective-permute-start(f32[96,1024]{1,0:T(8,128)S(1)} %get-tuple-element.515), channel_id=1, source_target_pairs={{0,4},{4,0},{8,12},{12,8},{16,20},{20,16},{24,28},{28,24},{1,5},{5... | collective-permute-start | bytes 1179656 | tf_op jit(solution)/shard_map/ppermute | solution.py:804
  298.3 15.0 %collective-permute-start.33 = (f32[64,1024]{1,0:T(8,128)S(1)}, f32[64,1024]{1,0:T(8,128)S(1)}, u32[]{:S(2)}, u32[]{:S(2)}) collective-permute-start(f32[64,1024]{1,0:T(8,128)S(1)} %get-tuple-element.528), channel_id=1, source_target_pairs={{0,4},{4,0},{8,12},{12,8},{16,20},{20,16},{24,28},{28,24},{1,5},{5... | collective-permute-start | bytes 786440 | tf_op jit(solution)/shard_map/ppermute | solution.py:804
  300.5 12.8 %collective-permute-start.31 = (f32[48,1024]{1,0:T(8,128)S(1)}, f32[48,1024]{1,0:T(8,128)S(1)}, u32[]{:S(2)}, u32[]{:S(2)}) collective-permute-start(f32[48,1024]{1,0:T(8,128)S(1)} %get-tuple-element.526), channel_id=1, source_target_pairs={{0,8},{4,12},{8,0},{12,4},{16,24},{20,28},{24,16},{28,20},{1,9},{5... | collective-permute-start | bytes 589832 | tf_op jit(solution)/shard_map/ppermute | solution.py:804
  300.5 12.8 %collective-permute-start.32 = (f32[48,1024]{1,0:T(8,128)S(1)}, f32[48,1024]{1,0:T(8,128)S(1)}, u32[]{:S(2)}, u32[]{:S(2)}) collective-permute-start(f32[48,1024]{1,0:T(8,128)S(1)} %get-tuple-element.527), channel_id=1, source_target_pairs={{0,2},{1,3},{2,0},{3,1},{4,6},{5,7},{6,4},{7,5},{8,10},{9,11},{10,... | collective-permute-start | bytes 589832 | tf_op jit(solution)/shard_map/ppermute | solution.py:804
  313.9 26.5 %collective-permute-start.34 = (f32[80,1024]{1,0:T(8,128)S(1)}, f32[80,1024]{1,0:T(8,128)S(1)}, u32[]{:S(2)}, u32[]{:S(2)}) collective-permute-start(f32[80,1024]{1,0:T(8,128)S(1)} %get-tuple-element.538), channel_id=1, source_target_pairs={{0,16},{4,20},{8,24},{12,28},{16,0},{20,4},{24,8},{28,12},{1,17},{... | collective-permute-start | bytes 983048 | tf_op jit(solution)/shard_map/ppermute | solution.py:804
  341.0 15.2 %collective-permute-start.35 = (f32[80,1024]{1,0:T(8,128)S(1)}, f32[80,1024]{1,0:T(8,128)S(1)}, u32[]{:S(2)}, u32[]{:S(2)}) collective-permute-start(f32[80,1024]{1,0:T(8,128)S(1)} %last.5.refs_0_), channel_id=1, source_target_pairs={{0,16},{4,20},{8,24},{12,28},{16,0},{20,4},{24,8},{28,12},{1,17},{... | collective-permute-start | bytes 983048 | tf_op jit(solution)/shard_map/ppermute | solution.py:804
  356.7 6.4 %collective-permute-start.38 = (f32[64,1024]{1,0:T(8,128)S(1)}, f32[64,1024]{1,0:T(8,128)S(1)}, u32[]{:S(2)}, u32[]{:S(2)}) collective-permute-start(f32[64,1024]{1,0:T(8,128)S(1)} %get-tuple-element.550.refs_2_), channel_id=1, source_target_pairs={{0,4},{4,0},{8,12},{12,8},{16,20},{20,16},{24,28},{28,24},{1,5},{5... | collective-permute-start | bytes 786440 | tf_op jit(solution)/shard_map/ppermute | solution.py:804
  357.1 5.7 %collective-permute-start.36 = (f32[48,1024]{1,0:T(8,128)S(1)}, f32[48,1024]{1,0:T(8,128)S(1)}, u32[]{:S(2)}, u32[]{:S(2)}) collective-permute-start(f32[48,1024]{1,0:T(8,128)S(1)} %get-tuple-element.548.refs_0_), channel_id=1, source_target_pairs={{0,8},{4,12},{8,0},{12,4},{16,24},{20,28},{24,16},{28,20},{1,9},{5... | collective-permute-start | bytes 589832 | tf_op jit(solution)/shard_map/ppermute | solution.py:804
  357.1 6.0 %collective-permute-start.37 = (f32[48,1024]{1,0:T(8,128)S(1)}, f32[48,1024]{1,0:T(8,128)S(1)}, u32[]{:S(2)}, u32[]{:S(2)}) collective-permute-start(f32[48,1024]{1,0:T(8,128)S(1)} %get-tuple-element.549.refs_1_), channel_id=1, source_target_pairs={{0,2},{1,3},{2,0},{3,1},{4,6},{5,7},{6,4},{7,5},{8,10},{9,11},{10,... | collective-permute-start | bytes 589832 | tf_op jit(solution)/shard_map/ppermute | solution.py:804
  363.8 11.4 %collective-permute-start.41 = (f32[128,1024]{1,0:T(8,128)S(1)}, f32[128,1024]{1,0:T(8,128)S(1)}, u32[]{:S(2)}, u32[]{:S(2)}) collective-permute-start(f32[128,1024]{1,0:T(8,128)S(1)} %get-tuple-element.559.refs_2_), channel_id=1, source_target_pairs={{0,8},{4,12},{8,0},{12,4},{16,24},{20,28},{24,16},{28,20},{1,9},{5... | collective-permute-start | bytes 1572872 | tf_op jit(solution)/shard_map/ppermute | solution.py:804
  365.5 7.8 %collective-permute-start.39 = (f32[96,1024]{1,0:T(8,128)S(1)}, f32[96,1024]{1,0:T(8,128)S(1)}, u32[]{:S(2)}, u32[]{:S(2)}) collective-permute-start(f32[96,1024]{1,0:T(8,128)S(1)} %get-tuple-element.557.refs_0_), channel_id=1, source_target_pairs={{0,2},{1,3},{2,0},{3,1},{4,6},{5,7},{6,4},{7,5},{8,10},{9,11},{10,... | collective-permute-start | bytes 1179656 | tf_op jit(solution)/shard_map/ppermute | solution.py:804
  367.4 7.8 %collective-permute-start.40 = (f32[96,1024]{1,0:T(8,128)S(1)}, f32[96,1024]{1,0:T(8,128)S(1)}, u32[]{:S(2)}, u32[]{:S(2)}) collective-permute-start(f32[96,1024]{1,0:T(8,128)S(1)} %get-tuple-element.558.refs_1_), channel_id=1, source_target_pairs={{0,4},{4,0},{8,12},{12,8},{16,20},{20,16},{24,28},{28,24},{1,5},{5... | collective-permute-start | bytes 1179656 | tf_op jit(solution)/shard_map/ppermute | solution.py:804
  377.1 3.6 collective-permute-start.45
  377.1 21.7 %collective-permute-start.47 = (f32[256,1024]{1,0:T(8,128)S(1)}, f32[256,1024]{1,0:T(8,128)S(1)}, u32[]{:S(2)}, u32[]{:S(2)}) collective-permute-start(f32[256,1024]{1,0:T(8,128)S(1)} %get-tuple-element.578.refs_5_), channel_id=1, source_target_pairs={{0,1},{1,0},{2,3},{3,2},{4,5},{5,4},{6,7},{7,6},{8,9},{9,8},{10,11... | collective-permute-start | bytes 3145736 | tf_op jit(solution)/shard_map/ppermute | solution.py:804
  377.6 28.5 %collective-permute-start.44 = (f32[256,1024]{1,0:T(8,128)S(1)}, f32[256,1024]{1,0:T(8,128)S(1)}, u32[]{:S(2)}, u32[]{:S(2)}) collective-permute-start(f32[256,1024]{1,0:T(8,128)S(1)} %get-tuple-element.578.refs_5_), channel_id=1, source_target_pairs={{0,2},{1,3},{2,0},{3,1},{4,6},{5,7},{6,4},{7,5},{8,10},{9,11},{10,... | collective-permute-start | bytes 3145736 | tf_op jit(solution)/shard_map/ppermute | solution.py:804
  378.8 20.0 %collective-permute-start.46 = (f32[192,1024]{1,0:T(8,128)}, f32[192,1024]{1,0:T(8,128)}, u32[]{:S(2)}, u32[]{:S(2)}) collective-permute-start(f32[192,1024]{1,0:T(8,128)} %get-tuple-element.577.refs_4_), channel_id=1, source_target_pairs={{0,1},{1,0},{2,3},{3,2},{4,5},{5,4},{6,7},{7,6},{8,9},{9,8},{10,11... | collective-permute-start | bytes 2359304 | tf_op jit(solution)/shard_map/ppermute | solution.py:804
  378.8 27.3 %collective-permute-start.42 = (f32[192,1024]{1,0:T(8,128)}, f32[192,1024]{1,0:T(8,128)}, u32[]{:S(2)}, u32[]{:S(2)}) collective-permute-start(f32[192,1024]{1,0:T(8,128)} %get-tuple-element.576.refs_3_), channel_id=1, source_target_pairs={{0,4},{4,0},{8,12},{12,8},{16,20},{20,16},{24,28},{28,24},{1,5},{5... | collective-permute-start | bytes 2359304 | tf_op jit(solution)/shard_map/ppermute | solution.py:804
  381.6 24.5 %collective-permute-start.43 = (f32[192,1024]{1,0:T(8,128)}, f32[192,1024]{1,0:T(8,128)}, u32[]{:S(2)}, u32[]{:S(2)}) collective-permute-start(f32[192,1024]{1,0:T(8,128)} %get-tuple-element.577.refs_4_), channel_id=1, source_target_pairs={{0,8},{4,12},{8,0},{12,4},{16,24},{20,28},{24,16},{28,20},{1,9},{5... | collective-permute-start | bytes 2359304 | tf_op jit(solution)/shard_map/ppermute | solution.py:804
  406.1 5.2 %collective-permute-start.50 = (f32[256,1024]{1,0:T(8,128)S(1)}, f32[256,1024]{1,0:T(8,128)S(1)}, u32[]{:S(2)}, u32[]{:S(2)}) collective-permute-start(f32[256,1024]{1,0:T(8,128)S(1)} %collective-permute-done.44.refs_5_), channel_id=1, source_target_pairs={{0,1},{1,0},{2,3},{3,2},{4,5},{5,4},{6,7},{7,6},{8,9},{9,8},{10,11... | collective-permute-start | bytes 3145736 | tf_op jit(solution)/shard_map/ppermute | solution.py:804
  406.2 4.0 collective-permute-start.48
  406.7 4.6 %collective-permute-start.49 = (f32[192,1024]{1,0:T(8,128)}, f32[192,1024]{1,0:T(8,128)S(1)}, u32[]{:S(2)}, u32[]{:S(2)}) collective-permute-start(f32[192,1024]{1,0:T(8,128)} %collective-permute-done.43.refs_4_), channel_id=1, source_target_pairs={{0,1},{1,0},{2,3},{3,2},{4,5},{5,4},{6,7},{7,6},{8,9},{9,8},{10,11... | collective-permute-start | bytes 2359304 | tf_op jit(solution)/shard_map/ppermute | solution.py:804
  (68 other events, 257.6 us)
Sparse Core Ops, SparseCore 0:
  191.7 151.4 all-gather.1

commit v3 on v2

--- a/solution.py
+++ b/solution.py
@@ -887,14 +887,6 @@
         while self.k > 3:
             self.widen()
 
-    def origin(self, device, chunk):
-        ranks = {"rep": device % lax.axis_size("rep"), "dp": device // lax.axis_size("rep")}
-        block = 0
-        for axis, place in self.steps[chunk]:
-            block = 2 * block + (ranks[axis] >> place & 1)
-        sizes = [v << self.count for v in self.sizes]
-        return sum(sizes[:chunk]) + block * self.sizes[chunk]
-
     def widen(self):
         k = self.k
         share, got = self.order.tie(self.share, self.got)
@@ -909,12 +901,13 @@
         self.order.done(self.share[0])
         self.k = k - 1
         self.got = self.send(k - 1, self.share)
-        if k == 1:
-            self.across = [swap(v, CORE) for v in self.share]
 
     def own(self):
         n = len(self.steps)
-        return [(v, c, c, 2 * n) for c, v in enumerate(self.share)] + [(v, c, c, 2 * n + 1) for c, v in enumerate(self.across)]
+        share = self.order.tie(*self.share)
+        return [(v, c, c, 2 * n) for c, v in enumerate(share)] + [
+            (swap(v, CORE), c, c, 2 * n + 1) for c, v in enumerate(share)
+        ]
 
     def arrived(self):
         n = len(self.steps)
@@ -939,59 +932,11 @@
     return found
 
 
-def deal(targets, gathered, sets, parts):
-    n = len(targets)
-    cols = gathered.shape[1]
-    devices = lax.axis_size("dp") * lax.axis_size("rep")
-    per = 4
-    rows = gathered.shape[0] // devices
-    moves = []
-    for device in range(devices):
-        mine, start = [], 0
-        for p, layout in zip(sets, parts):
-            for c, size in enumerate(p.sizes):
-                low = p.origin(device, c)
-                for first, count, target, row, whole, col in spans_of(layout, low, low + size):
-                    mine.append((start + first, count, target, row + device % 2 * whole, col))
-                start += size
-        moves.append(mine)
-    most = max(sum(len(m) for m in moves[g : g + per]) for g in range(0, devices, per))
-
-    def body(*refs):
-        value, outs, sem = refs[n], refs[n + 1 : -1], refs[-1]
-        for g in range(0, devices, per):
-            @pl.when(pl.program_id(0) == g // per)
-            def _():
-                copies = []
-                for d in range(per):
-                    for first, count, target, row, col in moves[g + d]:
-                        copies.append(pltpu.make_async_copy(
-                            value.at[pl.ds(d * rows + first, count), :],
-                            outs[target].at[pl.ds(row, count), pl.ds(col, cols)],
-                            sem.at[len(copies)],
-                        ))
-                        copies[-1].start()
-                for copy in copies:
-                    copy.wait()
-
-    return pl.pallas_call(
-        body,
-        out_shape=[jax.ShapeDtypeStruct(t.shape, F32) for t in targets],
-        grid=(devices // per,),
-        in_specs=[pl.BlockSpec(memory_space=pltpu.HBM)] * n + [pl.BlockSpec((per * rows, cols), lambda i: (i, 0))],
-        out_specs=[pl.BlockSpec(memory_space=pltpu.HBM)] * n,
-        scratch_shapes=[pltpu.SemaphoreType.DMA((most,))],
-        input_output_aliases={k: k for k in range(n)},
-        compiler_params=pltpu.CompilerParams(vmem_limit_bytes=60 * MIB),
-        cost_estimate=CHEAP,
-        name="deal",
-    )(*targets, gathered)
-
-
 SEQUENCE = (
-    "front", "scan0", "out0", "scan1", "mixed", "p0.f", "out1", "back01", "p0.f", "p1.f", "back00", "p0.f", "p1.f", "back11",
-    "p0.e", "p1.f", "back10", "p1.e", "ag", "post0", "post1", "out2", "gn",
-    "p2.f", "p2.f", "p2.f", "p2.e", "p2.b", "p2.w", "p2.w", "p2.w", "deal", "p2.own", "p2.got",
+    "front", "scan0", "out0", "scan1", "mixed", "p0.f", "out1", "p0.f", "back01", "p0.f", "back00", "p0.e", "p0.b", "p1.f",
+    "back11", "p1.f", "p0.w", "back10", "p1.f", "p0.w", "post0", "p1.e", "p1.b", "p0.w", "post1", "out2", "p0.own", "p0.got",
+    "p1.w", "p2.f", "p2.f", "p2.f", "p1.w", "gn", "p2.e", "p2.b", "p1.w", "p1.own", "p2.w", "p2.w", "p1.got", "p2.w",
+    "p2.own", "p2.got",
 )
 PARTS = 2
 
@@ -1015,10 +960,10 @@
     gain_rows = model // 2 // (WIDE // LANES)
     order = Order()
     tie, done = order.tie, order.done
-    sets = [Reduced(order, orders(*heads)) for heads in (("xyz", "yxz"), ("xyz", "yzx", "zxy"), ("xyz", "zxy", "yzx"))]
+    sets = [Reduced(order, orders(*heads)) for heads in (("xyz", "yxz"), ("xyz", "yxz"), ("xyz", "zxy", "yzx"))]
     low = model // 2
     third = 3 * model // 8
-    heights = [[low, low], [third, third, model - 2 * third], [third, third, low]]
+    heights = [[low, low]] * 2 + [[third, third, low]]
     parts = [[(WIDE // 2, 1, b * WIDE, 0), (low, 0, 0, width + b * WIDE)] for b in range(2)]
     parts.append([(low, 0, 0, 0), (low, 0, 0, WIDE), (used + gain_rows, 2, 0, 0)])
     state = {"targets": [blank((model, 2 * width)), blank((width, model)), blank((2 * (used + gain_rows), WIDE))]}
@@ -1121,27 +1066,6 @@
         state["targets"] = put(targets, pieces, parts[p], heights[p], sets[p].flags())
         done(state["targets"][0])
 
-    def op_ag():
-        state["split"] = all(v % SUB == 0 for p in sets[:2] for v in p.sizes)
-        if state["split"]:
-            mine = jnp.concatenate([p.share[0] for p in sets[:2]])
-            state["gathered"] = lax.all_gather(mine, ("dp", "rep"), axis=0, tiled=True)
-        else:
-            for p in sets[:2]:
-                p.back()
-
-    def op_deal():
-        if state["split"]:
-            gathered, targets = tie(state["gathered"], state["targets"])
-            state["targets"] = deal(targets, gathered, sets[:2], parts[:2])
-            done(state["targets"][0])
-            return
-        for p in range(2):
-            while sets[p].k > 0:
-                sets[p].widen()
-            op_put(p, sets[p].own())
-            op_put(p, sets[p].arrived())
-
     for name in SEQUENCE:
         if name[0] == "p" and name[2] == ".":
             p, what = int(name[1]), name[3:]
@@ -1160,7 +1084,7 @@
         elif name[-1] in "012":
             {"scan": op_scan, "out": op_out, "post": op_post}[name[:-1]](int(name[-1]))
         else:
-            {"front": op_front, "gn": op_gn, "mixed": op_mixed, "ag": op_ag, "deal": op_deal}[name]()
+            {"front": op_front, "gn": op_gn, "mixed": op_mixed}[name]()
 
     grad_in, grad_out, small = state["targets"]
     lines = small.reshape(2, used + gain_rows, WIDE)

time: 433 us -> 406 us (0.938)
  between operations: 15.9 us -> 2.52 us
  waiting for transfers between devices: 145 us -> 134 us
  local copies, waits for them, and re-layouts: 25.6 us -> 18.6 us
  starting transfers between devices: 46.1 us -> 52.3 us
    pallas_call x1 -> x0, Pallas kernels: 15.3 us -> none  [deal(): pl.pallas_call(body, out_shape=[jax.ShapeDtypeStruct(t.shape, F32) for t...]
    pallas_call x2 -> x6, Pallas kernels: 8.27 us -> 22.6 us  [put(): pl.pallas_call(body, out_shape=[jax.ShapeDtypeStruct(t.shape, F32) for t...]
    ppermute x51 -> x67, waiting for transfers between devices: 145 us -> 134 us  [swap(): return lax.ppermute(value, axis, [(i, i ^ 1 << place) for i in range(size)])]
    unnamed x162 -> x146, local copies, waits for them, and re-layouts: 25.3 us -> 18.1 us
    ppermute x51 -> x67, starting transfers between devices: 46 us -> 52.3 us  [swap(): return lax.ppermute(value, axis, [(i, i ^ 1 << place) for i in range(size)])]
    pallas_call x15 -> x21, Pallas kernels: 14.3 us -> 18.7 us  [step_call(): pl.pallas_call(body, out_shape=outs, grid_spec=pltpu.PrefetchScalarGridSp...]
  transfers between devices with their start and end apart: 52 -> 67, of which waited for: 21 -> 37; matrix products, arithmetic and copies ran while one was open for 4% -> 3% of each run, Pallas kernels for 34% -> 35%
where the time goes in v3:
time: 406 us; the launch traced here: 399 us
  Pallas kernels  174 us (43%)
  waiting for transfers between devices  134 us (33%)
  starting transfers between devices  52.3 us (13%)
  local copies, waits for them, and re-layouts  18.6 us (5%)
  other arithmetic  9.78 us (2%)
  matrix products  7.96 us (2%)
    ppermute x67, waiting for transfers between devices, swap(): return lax.ppermute(value, axis, [(i, i ^ 1 << place) for i in range(size)])  134 us
    pallas_call x4, Pallas kernels, back(): pl.pallas_call(functools.partial(back_kernel, first), grid=(1,), in_specs...  59.1 us
    ppermute x67, starting transfers between devices, swap(): return lax.ppermute(value, axis, [(i, i ^ 1 << place) for i in range(size)])  52.3 us
    pallas_call x2, Pallas kernels, scan(): pl.pallas_call(functools.partial(scan_kernel, block), grid=(1,), in_specs...  29.6 us
    pallas_call x3, Pallas kernels, outer(): pl.pallas_call(body, out_shape=out_shape, grid_spec=pltpu.PrefetchScalarG...  22.9 us
    pallas_call x6, Pallas kernels, put(): pl.pallas_call(body, out_shape=[jax.ShapeDtypeStruct(t.shape, F32) for t...  22.6 us
    pallas_call x21, Pallas kernels, step_call(): pl.pallas_call(body, out_shape=outs, grid_spec=pltpu.PrefetchScalarGridSp...  18.7 us
    unnamed x146, local copies, waits for them, and re-layouts  18.1 us
  transfers between devices with their start and end apart: 67, of which 37 were waited for; matrix products, arithmetic and copies ran while one was open for 3% of the time, Pallas kernels for 35%

profile of v3, /device:TPU:0, one launch (start us, length us, event | category | flops | bytes accessed | tf_op | source)
XLA Modules:
  0.0 398.6 jit_solution(7386875193135769099)
XLA Ops:
  1.9 7.6 %front.1 = (bf16[320,1024]{1,0:T(8,128)(2,1)}, f32[320,512]{1,0:T(8,128)}, f32[320,1024]{1,0:T(8,128)}, f32[320,2048]{1,0:T(8,128)}, bf16[320,2048]{1,0:T(8,128)(2,1)}, /*index=5*/f32[320,96]{1,0:T(8,128)}) custom-call(s32[2]{0:T(128)} %pad_add_fusion.len_ref, bf16[320,1024]{1,0:T(8,128)(2,1)} %bitcast.56, bf16[320,1024]{1,0:T(8,128)(2,1)} %bitcast.60, ...), custom_call_target="tpu_custom_call" | custom-call | flops 1 | bytes 1 | tf_op jit(solution)/shard_map/front/pallas_call | solution.py:75
  10.7 14.7 %scan0.1 = (bf16[320,1024]{1,0:T(8,128)(2,1)}, bf16[320,1024]{1,0:T(8,128)(2,1)}, f32[320,768]{1,0:T(8,128)}, f32[320,768]{1,0:T(8,128)}, f32[2560,128]{1,0:T(8,...) custom-call(s32[1]{0:T(128)} %bitcast.2.core_ref, f32[320,96]{1,0:T(8,128)} %get-tuple-element.463.mp_ref, ...), custom_call_target="tpu_custom_call" | custom-call | flops 1 | bytes 1 | tf_op jit(solution)/shard_map/scan0/pallas_call | solution.py:247
  26.6 3.9 collective-permute-done.2.refs_5_.refs_1_
  32.2 6.6 %outer.3 = (f32[256,1024]{1,0:T(8,128)}, f32[256,1024]{1,0:T(8,128)}, f32[256,1024]{1,0:T(8,128)}, f32[256,1024]{1,0:T(8,128)}, f32[512,128]{1,0:T(8,128)}) custom-call(s32[3]{0:T(128)} %pad_add_fusion.1.flag_ref, bf16[320,1024]{1,0:T(8,128)(2,1)} %get-tuple-element.380.refs_0_, f32[320,768]{1,0:T(8,128)} %copy-done.58, ...), custom_call_target="tpu_custom_call" | custom-call | flops 1 | bytes 1 | tf_op jit(solution)/shard_map/outer/pallas_call | solution.py:633
  38.8 2.7 collective-permute-start.4
  41.5 1.6 collective-permute-start.5
  43.0 14.9 %scan1.1 = (bf16[320,1024]{1,0:T(8,128)(2,1)}, bf16[320,1024]{1,0:T(8,128)(2,1)}, f32[320,768]{1,0:T(8,128)}, f32[320,768]{1,0:T(8,128)}, f32[2560,128]{1,0:T(8,...) custom-call(s32[1]{0:T(128)} %bitcast.2.core_ref, f32[320,96]{1,0:T(8,128)} %get-tuple-element.463.mp_ref, ...), custom_call_target="tpu_custom_call" | custom-call | flops 1 | bytes 1 | tf_op jit(solution)/shard_map/scan1/pallas_call | solution.py:247
  58.6 4.9 %fusion.13 = bf16[320,1024]{1,0:T(8,128)(2,1)} fusion(bf16[2048,1024]{1,0:T(8,128)(2,1)} %wout_hbm.3, bf16[320,1024]{1,0:T(8,128)(2,1)} %get-tuple-element.398.refs_0_, bf16[320,1024]{1,0:T(8,128)(2,1)S(1)} %copy-done.65, pred[320]{0:T(512)(128)(4,1)S(1)} %iota_compare_fusion, bf16[1,320,1024]{2,1,0:T(8,128)(2,1)S(1)} %copy-done.53), kind=kOutput, calls=%fused_computation.23 | convolution fusion | flops 1346109440 | bytes 6816064 | tf_op jit(solution)/shard_map/dot_general | solution.py:23
  63.5 1.8 collective-permute-done.4.refs_1_.refs_3_
  65.4 1.5 collective-permute-done.5.refs_5_.refs_7_
  68.4 1.6 collective-permute-start.6
  70.5 6.6 %outer.4 = (f32[256,1024]{1,0:T(8,128)}, f32[256,1024]{1,0:T(8,128)}, f32[256,1024]{1,0:T(8,128)}, f32[256,1024]{1,0:T(8,128)}, f32[512,128]{1,0:T(8,128)}) custom-call(s32[3]{0:T(128)} %pad_add_fusion.1.flag_ref, bf16[320,1024]{1,0:T(8,128)(2,1)} %get-tuple-element.398.refs_0_, f32[320,768]{1,0:T(8,128)} %collective-permute-done.8.refs_1_.refs_7_, ...), custom_call_target="tpu_custom_call" | custom-call | flops 1 | bytes 1 | tf_op jit(solution)/shard_map/outer/pallas_call | solution.py:633
  77.1 1.6 collective-permute-start.13
  79.2 3.8 collective-permute-done.6.refs_1_.refs_3_
  88.8 1.5 fold.10
  91.6 1.6 collective-permute-start.10
  96.8 12.6 %back01.1 = (f32[160,1024]{1,0:T(8,128)S(1)}, f32[160,64]{1,0:T(8,128)S(1)}, f32[64,1024]{1,0:T(8,128)S(1)}, f32[160,128]{1,0:T(8,128)S(1)}, f32[2,16,8,128]{3,2,1,0:T(8,128)S(1)}, /*index=5*/f32[2,1024]{1,0:T(2,128)S(1)}) custom-call(f32[320,96]{1,0:T(8,128)S(1)} %copy-done.5, bf16[320,2048]{1,0:T(8,128)(2,1)S(1)} %copy-done, f32[2560,128]{1,0:T(8,128)S(1)} %copy-done.9, ...), custom_call_target="tpu_custom_call" | custom-call | flops 1 | bytes 1 | tf_op jit(solution)/shard_map/back01/pallas_call | solution.py:426
  110.5 2.6 collective-permute-start.11
  113.1 12.6 %back00.1 = (f32[160,1024]{1,0:T(8,128)S(1)}, f32[160,64]{1,0:T(8,128)S(1)}, f32[64,1024]{1,0:T(8,128)S(1)}, f32[160,128]{1,0:T(8,128)S(1)}, f32[2,16,8,128]{3,2,1,0:T(8,128)S(1)}, /*index=5*/f32[2,1024]{1,0:T(2,128)S(1)}) custom-call(f32[320,96]{1,0:T(8,128)S(1)} %copy-done.5, bf16[320,2048]{1,0:T(8,128)(2,1)S(1)} %copy-done, f32[2560,128]{1,0:T(8,128)S(1)} %copy-done.9, ...), custom_call_target="tpu_custom_call" | custom-call | flops 1 | bytes 1 | tf_op jit(solution)/shard_map/back00/pallas_call | solution.py:426
  127.7 2.6 fold.12
  132.0 12.6 %back11.1 = (f32[160,1024]{1,0:T(8,128)S(1)}, f32[160,64]{1,0:T(8,128)S(1)}, f32[64,1024]{1,0:T(8,128)S(1)}, f32[160,128]{1,0:T(8,128)S(1)}, f32[2,16,8,128]{3,2,1,0:T(8,128)S(1)}, /*index=5*/f32[2,1024]{1,0:T(2,128)S(1)}) custom-call(f32[320,96]{1,0:T(8,128)S(1)} %copy-done.5, bf16[320,2048]{1,0:T(8,128)(2,1)S(1)} %copy-done, f32[2560,128]{1,0:T(8,128)S(1)} %copy-done.7, ...), custom_call_target="tpu_custom_call" | custom-call | flops 1 | bytes 1 | tf_op jit(solution)/shard_map/back11/pallas_call | solution.py:426
  146.7 1.6 collective-permute-start.17
  148.3 21.3 %back10.1 = (f32[160,1024]{1,0:T(8,128)S(1)}, f32[160,64]{1,0:T(8,128)S(1)}, f32[64,1024]{1,0:T(8,128)S(1)}, f32[160,128]{1,0:T(8,128)S(1)}, f32[2,16,8,128]{3,2,1,0:T(8,128)S(1)}, /*index=5*/f32[2,1024]{1,0:T(2,128)S(1)}) custom-call(f32[320,96]{1,0:T(8,128)S(1)} %copy-done.6, bf16[320,2048]{1,0:T(8,128)(2,1)S(1)} %copy-done, f32[2560,128]{1,0:T(8,128)S(1)} %copy-done.7, ...), custom_call_target="tpu_custom_call" | custom-call | flops 1 | bytes 1 | tf_op jit(solution)/shard_map/back10/pallas_call | solution.py:426
  172.6 1.5 collective-permute-start.20
  174.1 2.6 collective-permute-start.21
  176.7 6.6 %post0.1 = (f32[320,1024]{1,0:T(8,128)}, f32[184,1024]{1,0:T(8,128)}) custom-call(f32[2560,128]{1,0:T(8,128)} %get-tuple-element.382.gs_ref, bf16[320,2048]{1,0:T(8,128)(2,1)} %get-tuple-element.360.act_ref, f32[320,2048]{1,0:T(8,128)} %get-tuple-element.383.inner_ref, bf16[96,2048]{1,0:T(8,128)(2,1)} %bitcast.58, f32[4,2048]{1,0:T(4,128)} %cw_ref.5, ...), custom_call_target="tpu_custom_call" | custom-call | flops 1 | bytes 1 | tf_op jit(solution)/shard_map/post0/pallas_call | solution.py:511
  184.6 1.6 widen.11
  186.3 6.6 %post1.1 = (f32[320,1024]{1,0:T(8,128)}, f32[184,1024]{1,0:T(8,128)}) custom-call(f32[2560,128]{1,0:T(8,128)} %get-tuple-element.453.gs_ref, bf16[320,2048]{1,0:T(8,128)(2,1)} %get-tuple-element.360.act_ref, f32[320,2048]{1,0:T(8,128)} %get-tuple-element.383.inner_ref, bf16[96,2048]{1,0:T(8,128)(2,1)} %bitcast.59, f32[4,2048]{1,0:T(4,128)} %cw_ref.5, ...), custom_call_target="tpu_custom_call" | custom-call | flops 1 | bytes 1 | tf_op jit(solution)/shard_map/post1/pallas_call | solution.py:511
  194.8 2.2 collective-permute-done.27.refs_13_
  197.8 9.8 %outer.5 = (f32[192,1024]{1,0:T(8,128)}, f32[192,1024]{1,0:T(8,128)}, f32[192,1024]{1,0:T(8,128)}, f32[192,1024]{1,0:T(8,128)}, f32[256,1024]{1,0:T(8,128)}, /*index=5*/f32[256,1024]{1,0:T(8,128)}, f32[512,128]{1,0:T(8,128)}) custom-call(s32[4]{0:T(128)} %pad_add_fusion.6.flag_ref, bf16[320,1024]{1,0:T(8,128)(2,1)} %get-tuple-element.534.normed_hbm.refs_4_.refs_0_, ...), custom_call_target="tpu_custom_call" | custom-call | flops 1 | bytes 1 | tf_op jit(solution)/shard_map/outer/pallas_call | solution.py:633
  212.0 4.4 %put.6 = (f32[1024,4096]{1,0:T(8,128)}, f32[2048,1024]{1,0:T(8,128)}, f32[496,1024]{1,0:T(8,128)S(1)}) custom-call(s32[6]{0:T(128)S(1)} %stack.47.flag_ref, f32[1024,4096]{1,0:T(8,128)} %blank.3.refs_0_, f32[2048,1024]{1,0:T(8,128)} %blank.4.refs_1_, f32[496,1024]{1,0:T(8,128)S(1)} %blank.5.refs_2_, ...), custom_call_target="tpu_custom_call", output_to_operand_aliasing={{0}: (1, {}), {1}: (2, {}), {2}: (3, {})} | custom-call | flops 1 | bytes 1 | tf_op jit(solution)/shard_map/put/pallas_call | solution.py:776
  216.4 17.3 %collective-permute-done.23.refs_3_ = f32[256,1024]{1,0:T(8,128)} collective-permute-done((f32[256,1024]{1,0:T(8,128)}, f32[256,1024]{1,0:T(8,128)}, u32[]{:S(2)}, u32[]{:S(2)}) %collective-permute-start.23) | collective-permute-done | bytes 1048608 | tf_op jit(solution)/shard_map/ppermute | solution.py:804
  235.1 1.5 collective-permute-start.33
  236.7 3.1 collective-permute-start.22
  239.8 4.1 %put.7 = (f32[1024,4096]{1,0:T(8,128)}, f32[2048,1024]{1,0:T(8,128)}, f32[496,1024]{1,0:T(8,128)S(1)}) custom-call(s32[6]{0:T(128)S(1)} %stack.47.flag_ref, f32[1024,4096]{1,0:T(8,128)} %get-tuple-element.558.refs_0_, f32[2048,1024]{1,0:T(8,128)} %get-tuple-element.559.refs_1_, ...), custom_call_target="tpu_custom_call", output_to_operand_aliasing={{0}: (1, {}), {1}: (2, {}), {2}: (3, {})} | custom-call | flops 1 | bytes 1 | tf_op jit(solution)/shard_map/put/pallas_call | solution.py:776
  244.0 14.9 %collective-permute-done.22.refs_1_ = f32[64,1024]{1,0:T(8,128)S(1)} collective-permute-done((f32[64,1024]{1,0:T(8,128)S(1)}, f32[64,1024]{1,0:T(8,128)S(1)}, u32[]{:S(2)}, u32[]{:S(2)}) %collective-permute-start.22) | collective-permute-done | bytes 262176 | tf_op jit(solution)/shard_map/ppermute | solution.py:804
  259.5 1.6 collective-permute-done.34.refs_5_.refs_7_
  262.0 2.1 collective-permute-start.38
  266.2 7.5 %collective-permute-done.36.refs_1_.refs_3_ = f32[96,1024]{1,0:T(8,128)S(1)} collective-permute-done((f32[96,1024]{1,0:T(8,128)S(1)}, f32[96,1024]{1,0:T(8,128)S(1)}, u32[]{:S(2)}, u32[]{:S(2)}) %collective-permute-start.36) | collective-permute-done | bytes 393248 | tf_op jit(solution)/shard_map/ppermute | solution.py:804
  274.7 2.3 collective-permute-done.38.refs_9_.refs_11_
  278.6 2.0 collective-permute-start.39
  281.8 8.6 %collective-permute-done.39.refs_1_.refs_3_ = f32[48,1024]{1,0:T(8,128)S(1)} collective-permute-done((f32[48,1024]{1,0:T(8,128)S(1)}, f32[48,1024]{1,0:T(8,128)S(1)}, u32[]{:S(2)}, u32[]{:S(2)}) %collective-permute-start.39) | collective-permute-done | bytes 196640 | tf_op jit(solution)/shard_map/ppermute | solution.py:804
  293.3 1.5 collective-permute-start.42
  295.4 3.1 fusion.14
  298.5 1.4 fusion.17
  300.0 8.9 %collective-permute-done.42.refs_3_ = f32[80,1024]{1,0:T(8,128)S(1)} collective-permute-done((f32[80,1024]{1,0:T(8,128)S(1)}, f32[80,1024]{1,0:T(8,128)S(1)}, u32[]{:S(2)}, u32[]{:S(2)}) %collective-permute-start.42) | collective-permute-done | bytes 327712 | tf_op jit(solution)/shard_map/ppermute | solution.py:804
  312.9 1.5 collective-permute-done.47.refs_6_
  314.4 2.6 put.8
  317.0 11.2 %collective-permute-done.43.refs_1_ = f32[80,1024]{1,0:T(8,128)S(1)} collective-permute-done((f32[80,1024]{1,0:T(8,128)S(1)}, f32[80,1024]{1,0:T(8,128)S(1)}, u32[]{:S(2)}, u32[]{:S(2)}) %collective-permute-start.43) | collective-permute-done | bytes 327712 | tf_op jit(solution)/shard_map/ppermute | solution.py:804
  328.7 1.8 collective-permute-start.50
  331.7 5.4 %collective-permute-done.48.refs_3_ = f32[48,1024]{1,0:T(8,128)S(1)} collective-permute-done((f32[48,1024]{1,0:T(8,128)S(1)}, f32[48,1024]{1,0:T(8,128)S(1)}, u32[]{:S(2)}, u32[]{:S(2)}) %collective-permute-start.48) | collective-permute-done | bytes 196640 | tf_op jit(solution)/shard_map/ppermute | solution.py:804
  337.1 3.2 collective-permute-done.49.refs_4_
  344.9 1.5 collective-permute-done.57.refs_6_
  346.4 2.6 put.9
  348.9 4.9 %collective-permute-done.51.refs_3_ = f32[96,1024]{1,0:T(8,128)S(1)} collective-permute-done((f32[96,1024]{1,0:T(8,128)S(1)}, f32[96,1024]{1,0:T(8,128)S(1)}, u32[]{:S(2)}, u32[]{:S(2)}) %collective-permute-start.51) | collective-permute-done | bytes 393248 | tf_op jit(solution)/shard_map/ppermute | solution.py:804
  354.4 2.2 collective-permute-done.53.refs_5_
  356.6 2.2 widen.17
  360.7 1.7 collective-permute-done.61.refs_6_
  365.2 5.2 %put.10 = (f32[1024,4096]{1,0:T(8,128)}, f32[2048,1024]{1,0:T(8,128)}, f32[496,1024]{1,0:T(8,128)S(1)}) custom-call(s32[8]{0:T(128)S(1)} %stack.52.flag_ref, f32[1024,4096]{1,0:T(8,128)} %get-tuple-element.677.refs_0_, f32[2048,1024]{1,0:T(8,128)} %get-tuple-element.678.refs_1_, ...), custom_call_target="tpu_custom_call", output_to_operand_aliasing={{0}: (1, {}), {1}: (2, {}), {2}: (3, {})} | custom-call | flops 1 | bytes 1 | tf_op jit(solution)/shard_map/put/pallas_call | solution.py:776
  370.5 10.0 %collective-permute-done.58.refs_3_ = f32[192,1024]{1,0:T(8,128)} collective-permute-done((f32[192,1024]{1,0:T(8,128)}, f32[192,1024]{1,0:T(8,128)}, u32[]{:S(2)}, u32[]{:S(2)}) %collective-permute-start.58) | collective-permute-done | bytes 786464 | tf_op jit(solution)/shard_map/ppermute | solution.py:804
  380.5 2.8 collective-permute-done.59.refs_4_
  385.2 3.1 collective-permute-done.64.refs_6_
  388.3 1.5 collective-permute-done.65.refs_7_
  389.8 3.7 put.11
  (292 shorter events, 71.1 us)
Async XLA Ops:
  9.5 21.1 %collective-permute-start.1 = (f32[320,1024]{1,0:T(8,128)}, f32[320,1024]{1,0:T(8,128)S(1)}, u32[]{:S(2)}, u32[]{:S(2)}) collective-permute-start(f32[320,1024]{1,0:T(8,128)} %get-tuple-element.400.og_hbm.refs_2_), channel_id=1, source_target_pairs={{0,1},{1,0},{2,3},{3,2},{4,5},{5,4},{6,7},{7,6},{8,9},{9,8},{10,11... | collective-permute-start | bytes 3932168 | tf_op jit(solution)/shard_map/ppermute | solution.py:804
  25.4 5.2 %collective-permute-start = (f32[320,768]{1,0:T(8,128)}, f32[320,768]{1,0:T(8,128)S(1)}, u32[]{:S(2)}, u32[]{:S(2)}) collective-permute-start(f32[320,768]{1,0:T(8,128)} %get-tuple-element.365), channel_id=1, source_target_pairs={{0,1},{1,0},{2,3},{3,2},{4,5},{5,4},{6,7},{7,6},{8,9},{9,8},{10,11... | collective-permute-start | bytes 2949128 | tf_op jit(solution)/shard_map/ppermute | solution.py:804
  25.5 5.1 %collective-permute-start.3 = (f32[320,768]{1,0:T(8,128)}, f32[320,768]{1,0:T(8,128)}, u32[]{:S(2)}, u32[]{:S(2)}) collective-permute-start(f32[320,768]{1,0:T(8,128)} %get-tuple-element.367), channel_id=1, source_target_pairs={{0,1},{1,0},{2,3},{3,2},{4,5},{5,4},{6,7},{7,6},{8,9},{9,8},{10,11... | collective-permute-start | bytes 2949128 | tf_op jit(solution)/shard_map/ppermute | solution.py:804
  26.0 4.6 %collective-permute-start.2 = (f32[320,512]{1,0:T(8,128)}, f32[320,512]{1,0:T(8,128)S(1)}, u32[]{:S(2)}, u32[]{:S(2)}) collective-permute-start(f32[320,512]{1,0:T(8,128)} %get-tuple-element.366), channel_id=1, source_target_pairs={{0,1},{1,0},{2,3},{3,2},{4,5},{5,4},{6,7},{7,6},{8,9},{9,8},{10,11... | collective-permute-start | bytes 1966088 | tf_op jit(solution)/shard_map/ppermute | solution.py:804
  38.8 26.6 %collective-permute-start.4 = (f32[256,1024]{1,0:T(8,128)}, f32[256,1024]{1,0:T(8,128)S(1)}, u32[]{:S(2)}, u32[]{:S(2)}) collective-permute-start(f32[256,1024]{1,0:T(8,128)} %get-tuple-element.385), channel_id=1, source_target_pairs={{0,4},{4,0},{8,12},{12,8},{16,20},{20,16},{24,28},{28,24},{1,5},{5... | collective-permute-start | bytes 3145736 | tf_op jit(solution)/shard_map/ppermute | solution.py:804
  41.5 25.4 %collective-permute-start.5 = (f32[256,1024]{1,0:T(8,128)}, f32[256,1024]{1,0:T(8,128)S(1)}, u32[]{:S(2)}, u32[]{:S(2)}) collective-permute-start(f32[256,1024]{1,0:T(8,128)} %get-tuple-element.386), channel_id=1, source_target_pairs={{0,2},{1,3},{2,0},{3,1},{4,6},{5,7},{6,4},{7,5},{8,10},{9,11},{10,... | collective-permute-start | bytes 3145736 | tf_op jit(solution)/shard_map/ppermute | solution.py:804
  58.0 12.5 %collective-permute-start.8 = (f32[320,768]{1,0:T(8,128)}, f32[320,768]{1,0:T(8,128)}, u32[]{:S(2)}, u32[]{:S(2)}) collective-permute-start(f32[320,768]{1,0:T(8,128)} %get-tuple-element.396), channel_id=1, source_target_pairs={{0,1},{1,0},{2,3},{3,2},{4,5},{5,4},{6,7},{7,6},{8,9},{9,8},{10,11... | collective-permute-start | bytes 2949128 | tf_op jit(solution)/shard_map/ppermute | solution.py:804
  58.0 12.5 %collective-permute-start.9 = (f32[320,768]{1,0:T(8,128)}, f32[320,768]{1,0:T(8,128)}, u32[]{:S(2)}, u32[]{:S(2)}) collective-permute-start(f32[320,768]{1,0:T(8,128)} %get-tuple-element.397), channel_id=1, source_target_pairs={{0,1},{1,0},{2,3},{3,2},{4,5},{5,4},{6,7},{7,6},{8,9},{9,8},{10,11... | collective-permute-start | bytes 2949128 | tf_op jit(solution)/shard_map/ppermute | solution.py:804
  68.4 14.6 %collective-permute-start.6 = (f32[128,1024]{1,0:T(8,128)S(1)}, f32[128,1024]{1,0:T(8,128)S(1)}, u32[]{:S(2)}, u32[]{:S(2)}) collective-permute-start(f32[128,1024]{1,0:T(8,128)S(1)} %get-tuple-element.393), channel_id=1, source_target_pairs={{0,2},{1,3},{2,0},{3,1},{4,6},{5,7},{6,4},{7,5},{8,10},{9,11},{10,... | collective-permute-start | bytes 1572872 | tf_op jit(solution)/shard_map/ppermute | solution.py:804
  70.0 14.9 %collective-permute-start.7 = (f32[128,1024]{1,0:T(8,128)S(1)}, f32[128,1024]{1,0:T(8,128)S(1)}, u32[]{:S(2)}, u32[]{:S(2)}) collective-permute-start(f32[128,1024]{1,0:T(8,128)S(1)} %get-tuple-element.394), channel_id=1, source_target_pairs={{0,4},{4,0},{8,12},{12,8},{16,20},{20,16},{24,28},{28,24},{1,5},{5... | collective-permute-start | bytes 1572872 | tf_op jit(solution)/shard_map/ppermute | solution.py:804
  77.1 50.5 %collective-permute-start.13 = (f32[256,1024]{1,0:T(8,128)}, f32[256,1024]{1,0:T(8,128)}, u32[]{:S(2)}, u32[]{:S(2)}) collective-permute-start(f32[256,1024]{1,0:T(8,128)} %get-tuple-element.441), channel_id=1, source_target_pairs={{0,4},{4,0},{8,12},{12,8},{16,20},{20,16},{24,28},{28,24},{1,5},{5... | collective-permute-start | bytes 3145736 | tf_op jit(solution)/shard_map/ppermute | solution.py:804
  78.6 49.0 %collective-permute-start.14 = (f32[256,1024]{1,0:T(8,128)}, f32[256,1024]{1,0:T(8,128)}, u32[]{:S(2)}, u32[]{:S(2)}) collective-permute-start(f32[256,1024]{1,0:T(8,128)} %get-tuple-element.442), channel_id=1, source_target_pairs={{0,2},{1,3},{2,0},{3,1},{4,6},{5,7},{6,4},{7,5},{8,10},{9,11},{10,... | collective-permute-start | bytes 3145736 | tf_op jit(solution)/shard_map/ppermute | solution.py:804
  91.6 17.9 %collective-permute-start.10 = (f32[128,1024]{1,0:T(8,128)}, f32[128,1024]{1,0:T(8,128)S(1)}, u32[]{:S(2)}, u32[]{:S(2)}) collective-permute-start(f32[128,1024]{1,0:T(8,128)} %get-tuple-element.414), channel_id=1, source_target_pairs={{0,8},{4,12},{8,0},{12,4},{16,24},{20,28},{24,16},{28,20},{1,9},{5... | collective-permute-start | bytes 1572872 | tf_op jit(solution)/shard_map/ppermute | solution.py:804
  110.5 16.5 %collective-permute-start.11 = (f32[64,1024]{1,0:T(8,128)S(1)}, f32[64,1024]{1,0:T(8,128)S(1)}, u32[]{:S(2)}, u32[]{:S(2)}) collective-permute-start(f32[64,1024]{1,0:T(8,128)S(1)} %get-tuple-element.436), channel_id=1, source_target_pairs={{0,16},{4,20},{8,24},{12,28},{16,0},{20,4},{24,8},{28,12},{1,17},{... | collective-permute-start | bytes 786440 | tf_op jit(solution)/shard_map/ppermute | solution.py:804
  130.3 14.4 %collective-permute-start.15 = (f32[128,1024]{1,0:T(8,128)S(1)}, f32[128,1024]{1,0:T(8,128)S(1)}, u32[]{:S(2)}, u32[]{:S(2)}) collective-permute-start(f32[128,1024]{1,0:T(8,128)S(1)} %get-tuple-element.449), channel_id=1, source_target_pairs={{0,2},{1,3},{2,0},{3,1},{4,6},{5,7},{6,4},{7,5},{8,10},{9,11},{10,... | collective-permute-start | bytes 1572872 | tf_op jit(solution)/shard_map/ppermute | solution.py:804
  131.1 13.6 %collective-permute-start.16 = (f32[128,1024]{1,0:T(8,128)S(1)}, f32[128,1024]{1,0:T(8,128)S(1)}, u32[]{:S(2)}, u32[]{:S(2)}) collective-permute-start(f32[128,1024]{1,0:T(8,128)S(1)} %get-tuple-element.450), channel_id=1, source_target_pairs={{0,4},{4,0},{8,12},{12,8},{16,20},{20,16},{24,28},{28,24},{1,5},{5... | collective-permute-start | bytes 1572872 | tf_op jit(solution)/shard_map/ppermute | solution.py:804
  131.7 14.4 %collective-permute-start.12 = (f32[64,1024]{1,0:T(8,128)S(1)}, f32[64,1024]{1,0:T(8,128)S(1)}, u32[]{:S(2)}, u32[]{:S(2)}) collective-permute-start(f32[64,1024]{1,0:T(8,128)S(1)} %last.3.refs_0_), channel_id=1, source_target_pairs={{0,16},{4,20},{8,24},{12,28},{16,0},{20,4},{24,8},{28,12},{1,17},{... | collective-permute-start | bytes 786440 | tf_op jit(solution)/shard_map/ppermute | solution.py:804
  145.6 24.1 %collective-permute-start.18 = (f32[128,1024]{1,0:T(8,128)S(1)}, f32[128,1024]{1,0:T(8,128)S(1)}, u32[]{:S(2)}, u32[]{:S(2)}) collective-permute-start(f32[128,1024]{1,0:T(8,128)S(1)} %get-tuple-element.470), channel_id=1, source_target_pairs={{0,8},{4,12},{8,0},{12,4},{16,24},{20,28},{24,16},{28,20},{1,9},{5... | collective-permute-start | bytes 1572872 | tf_op jit(solution)/shard_map/ppermute | solution.py:804
  146.7 24.0 %collective-permute-start.17 = (f32[128,1024]{1,0:T(8,128)S(1)}, f32[128,1024]{1,0:T(8,128)S(1)}, u32[]{:S(2)}, u32[]{:S(2)}) collective-permute-start(f32[128,1024]{1,0:T(8,128)S(1)} %widen.9.refs_0_), channel_id=1, source_target_pairs={{0,8},{4,12},{8,0},{12,4},{16,24},{20,28},{24,16},{28,20},{1,9},{5... | collective-permute-start | bytes 1572872 | tf_op jit(solution)/shard_map/ppermute | solution.py:804
  171.3 13.3 %collective-permute-start.19 = (f32[128,1024]{1,0:T(8,128)S(1)}, f32[128,1024]{1,0:T(8,128)S(1)}, u32[]{:S(2)}, u32[]{:S(2)}) collective-permute-start(f32[128,1024]{1,0:T(8,128)S(1)} %get-tuple-element.506.refs_0_), channel_id=1, source_target_pairs={{0,2},{1,3},{2,0},{3,1},{4,6},{5,7},{6,4},{7,5},{8,10},{9,11},{10,... | collective-permute-start | bytes 1572872 | tf_op jit(solution)/shard_map/ppermute | solution.py:804
  172.6 12.1 %collective-permute-start.20 = (f32[128,1024]{1,0:T(8,128)S(1)}, f32[128,1024]{1,0:T(8,128)S(1)}, u32[]{:S(2)}, u32[]{:S(2)}) collective-permute-start(f32[128,1024]{1,0:T(8,128)S(1)} %get-tuple-element.507.refs_1_), channel_id=1, source_target_pairs={{0,4},{4,0},{8,12},{12,8},{16,20},{20,16},{24,28},{28,24},{1,5},{5... | collective-permute-start | bytes 1572872 | tf_op jit(solution)/shard_map/ppermute | solution.py:804
  174.1 10.0 %collective-permute-start.21 = (f32[64,1024]{1,0:T(8,128)S(1)}, f32[64,1024]{1,0:T(8,128)S(1)}, u32[]{:S(2)}, u32[]{:S(2)}) collective-permute-start(f32[64,1024]{1,0:T(8,128)S(1)} %get-tuple-element.502), channel_id=1, source_target_pairs={{0,16},{4,20},{8,24},{12,28},{16,0},{20,4},{24,8},{28,12},{1,17},{... | collective-permute-start | bytes 786440 | tf_op jit(solution)/shard_map/ppermute | solution.py:804
  183.3 13.7 %collective-permute-start.25 = (f32[320,1024]{1,0:T(8,128)}, f32[320,1024]{1,0:T(8,128)}, u32[]{:S(2)}, u32[]{:S(2)}) collective-permute-start(f32[320,1024]{1,0:T(8,128)} %get-tuple-element.607.refs_2_), channel_id=1, source_target_pairs={{0,1},{1,0},{2,3},{3,2},{4,5},{5,4},{6,7},{7,6},{8,9},{9,8},{10,11... | collective-permute-start | bytes 3932168 | tf_op jit(solution)/shard_map/ppermute | solution.py:804
  192.9 4.1 %collective-permute-start.26 = (f32[320,1024]{1,0:T(8,128)}, f32[320,1024]{1,0:T(8,128)}, u32[]{:S(2)}, u32[]{:S(2)}) collective-permute-start(f32[320,1024]{1,0:T(8,128)} %get-tuple-element.608.refs_6_), channel_id=1, source_target_pairs={{0,1},{1,0},{2,3},{3,2},{4,5},{5,4},{6,7},{7,6},{8,9},{9,8},{10,11... | collective-permute-start | bytes 3932168 | tf_op jit(solution)/shard_map/ppermute | solution.py:804
  207.6 3.1 collective-permute-start.28
  207.9 4.1 %collective-permute-start.29 = (f32[256,1024]{1,0:T(8,128)S(1)}, f32[256,1024]{1,0:T(8,128)}, u32[]{:S(2)}, u32[]{:S(2)}) collective-permute-start(f32[256,1024]{1,0:T(8,128)S(1)} %get-tuple-element.550.refs_4_), channel_id=1, source_target_pairs={{0,1},{1,0},{2,3},{3,2},{4,5},{5,4},{6,7},{7,6},{8,9},{9,8},{10,11... | collective-permute-start | bytes 3145736 | tf_op jit(solution)/shard_map/ppermute | solution.py:804
  208.2 25.6 %collective-permute-start.23 = (f32[256,1024]{1,0:T(8,128)}, f32[256,1024]{1,0:T(8,128)}, u32[]{:S(2)}, u32[]{:S(2)}) collective-permute-start(f32[256,1024]{1,0:T(8,128)} %get-tuple-element.549.refs_3_), channel_id=1, source_target_pairs={{0,4},{4,0},{8,12},{12,8},{16,20},{20,16},{24,28},{28,24},{1,5},{5... | collective-permute-start | bytes 3145736 | tf_op jit(solution)/shard_map/ppermute | solution.py:804
  208.7 25.1 %collective-permute-start.24 = (f32[256,1024]{1,0:T(8,128)S(1)}, f32[256,1024]{1,0:T(8,128)}, u32[]{:S(2)}, u32[]{:S(2)}) collective-permute-start(f32[256,1024]{1,0:T(8,128)S(1)} %get-tuple-element.550.refs_4_), channel_id=1, source_target_pairs={{0,2},{1,3},{2,0},{3,1},{4,6},{5,7},{6,4},{7,5},{8,10},{9,11},{10,... | collective-permute-start | bytes 3145736 | tf_op jit(solution)/shard_map/ppermute | solution.py:804
  233.8 2.9 collective-permute-start.30
  233.8 6.0 %collective-permute-start.31 = (f32[256,1024]{1,0:T(8,128)}, f32[256,1024]{1,0:T(8,128)S(1)}, u32[]{:S(2)}, u32[]{:S(2)}) collective-permute-start(f32[256,1024]{1,0:T(8,128)} %collective-permute-done.24.refs_4_), channel_id=1, source_target_pairs={{0,1},{1,0},{2,3},{3,2},{4,5},{5,4},{6,7},{7,6},{8,9},{9,8},{10,11... | collective-permute-start | bytes 3145736 | tf_op jit(solution)/shard_map/ppermute | solution.py:804
  234.3 26.8 %collective-permute-start.35 = (f32[256,1024]{1,0:T(8,128)S(1)}, f32[256,1024]{1,0:T(8,128)S(1)}, u32[]{:S(2)}, u32[]{:S(2)}) collective-permute-start(f32[256,1024]{1,0:T(8,128)S(1)} %copy-done.67), channel_id=1, source_target_pairs={{0,2},{1,3},{2,0},{3,1},{4,6},{5,7},{6,4},{7,5},{8,10},{9,11},{10,... | collective-permute-start | bytes 3145736 | tf_op jit(solution)/shard_map/ppermute | solution.py:804
  235.1 24.4 %collective-permute-start.33 = (f32[192,1024]{1,0:T(8,128)S(1)}, f32[192,1024]{1,0:T(8,128)S(1)}, u32[]{:S(2)}, u32[]{:S(2)}) collective-permute-start(f32[192,1024]{1,0:T(8,128)S(1)} %copy-done.69), channel_id=1, source_target_pairs={{0,4},{4,0},{8,12},{12,8},{16,20},{20,16},{24,28},{28,24},{1,5},{5... | collective-permute-start | bytes 2359304 | tf_op jit(solution)/shard_map/ppermute | solution.py:804
  236.6 24.5 %collective-permute-start.34 = (f32[192,1024]{1,0:T(8,128)S(1)}, f32[192,1024]{1,0:T(8,128)S(1)}, u32[]{:S(2)}, u32[]{:S(2)}) collective-permute-start(f32[192,1024]{1,0:T(8,128)S(1)} %copy-done.68), channel_id=1, source_target_pairs={{0,8},{4,12},{8,0},{12,4},{16,24},{20,28},{24,16},{28,20},{1,9},{5... | collective-permute-start | bytes 2359304 | tf_op jit(solution)/shard_map/ppermute | solution.py:804
  236.7 22.2 %collective-permute-start.22 = (f32[64,1024]{1,0:T(8,128)S(1)}, f32[64,1024]{1,0:T(8,128)S(1)}, u32[]{:S(2)}, u32[]{:S(2)}) collective-permute-start(f32[64,1024]{1,0:T(8,128)S(1)} %last.4.refs_0_), channel_id=1, source_target_pairs={{0,16},{4,20},{8,24},{12,28},{16,0},{20,4},{24,8},{28,12},{1,17},{... | collective-permute-start | bytes 786440 | tf_op jit(solution)/shard_map/ppermute | solution.py:804
  262.0 14.9 %collective-permute-start.38 = (f32[128,1024]{1,0:T(8,128)S(1)}, f32[128,1024]{1,0:T(8,128)S(1)}, u32[]{:S(2)}, u32[]{:S(2)}) collective-permute-start(f32[128,1024]{1,0:T(8,128)S(1)} %get-tuple-element.584), channel_id=1, source_target_pairs={{0,8},{4,12},{8,0},{12,4},{16,24},{20,28},{24,16},{28,20},{1,9},{5... | collective-permute-start | bytes 1572872 | tf_op jit(solution)/shard_map/ppermute | solution.py:804
  264.1 9.6 %collective-permute-start.36 = (f32[96,1024]{1,0:T(8,128)S(1)}, f32[96,1024]{1,0:T(8,128)S(1)}, u32[]{:S(2)}, u32[]{:S(2)}) collective-permute-start(f32[96,1024]{1,0:T(8,128)S(1)} %get-tuple-element.582), channel_id=1, source_target_pairs={{0,2},{1,3},{2,0},{3,1},{4,6},{5,7},{6,4},{7,5},{8,10},{9,11},{10,... | collective-permute-start | bytes 1179656 | tf_op jit(solution)/shard_map/ppermute | solution.py:804
  265.4 9.3 %collective-permute-start.37 = (f32[96,1024]{1,0:T(8,128)S(1)}, f32[96,1024]{1,0:T(8,128)S(1)}, u32[]{:S(2)}, u32[]{:S(2)}) collective-permute-start(f32[96,1024]{1,0:T(8,128)S(1)} %get-tuple-element.583), channel_id=1, source_target_pairs={{0,4},{4,0},{8,12},{12,8},{16,20},{20,16},{24,28},{28,24},{1,5},{5... | collective-permute-start | bytes 1179656 | tf_op jit(solution)/shard_map/ppermute | solution.py:804
  265.9 25.2 %collective-permute-start.32 = (f32[128,1024]{1,0:T(8,128)S(1)}, f32[128,1024]{1,0:T(8,128)S(1)}, u32[]{:S(2)}, u32[]{:S(2)}) collective-permute-start(f32[128,1024]{1,0:T(8,128)S(1)} %widen.12.refs_0_), channel_id=1, source_target_pairs={{0,8},{4,12},{8,0},{12,4},{16,24},{20,28},{24,16},{28,20},{1,9},{5... | collective-permute-start | bytes 1572872 | tf_op jit(solution)/shard_map/ppermute | solution.py:804
  277.7 12.8 %collective-permute-start.41 = (f32[64,1024]{1,0:T(8,128)S(1)}, f32[64,1024]{1,0:T(8,128)S(1)}, u32[]{:S(2)}, u32[]{:S(2)}) collective-permute-start(f32[64,1024]{1,0:T(8,128)S(1)} %get-tuple-element.596), channel_id=1, source_target_pairs={{0,4},{4,0},{8,12},{12,8},{16,20},{20,16},{24,28},{28,24},{1,5},{5... | collective-permute-start | bytes 786440 | tf_op jit(solution)/shard_map/ppermute | solution.py:804
  278.6 11.9 %collective-permute-start.39 = (f32[48,1024]{1,0:T(8,128)S(1)}, f32[48,1024]{1,0:T(8,128)S(1)}, u32[]{:S(2)}, u32[]{:S(2)}) collective-permute-start(f32[48,1024]{1,0:T(8,128)S(1)} %get-tuple-element.594), channel_id=1, source_target_pairs={{0,8},{4,12},{8,0},{12,4},{16,24},{20,28},{24,16},{28,20},{1,9},{5... | collective-permute-start | bytes 589832 | tf_op jit(solution)/shard_map/ppermute | solution.py:804
  280.6 9.9 %collective-permute-start.40 = (f32[48,1024]{1,0:T(8,128)S(1)}, f32[48,1024]{1,0:T(8,128)S(1)}, u32[]{:S(2)}, u32[]{:S(2)}) collective-permute-start(f32[48,1024]{1,0:T(8,128)S(1)} %get-tuple-element.595), channel_id=1, source_target_pairs={{0,2},{1,3},{2,0},{3,1},{4,6},{5,7},{6,4},{7,5},{8,10},{9,11},{10,... | collective-permute-start | bytes 589832 | tf_op jit(solution)/shard_map/ppermute | solution.py:804
  291.8 17.6 %collective-permute-start.44 = (f32[128,1024]{1,0:T(8,128)S(1)}, f32[128,1024]{1,0:T(8,128)S(1)}, u32[]{:S(2)}, u32[]{:S(2)}) collective-permute-start(f32[128,1024]{1,0:T(8,128)S(1)} %get-tuple-element.619.refs_0_), channel_id=1, source_target_pairs={{0,2},{1,3},{2,0},{3,1},{4,6},{5,7},{6,4},{7,5},{8,10},{9,11},{10,... | collective-permute-start | bytes 1572872 | tf_op jit(solution)/shard_map/ppermute | solution.py:804
  293.3 15.5 %collective-permute-start.42 = (f32[80,1024]{1,0:T(8,128)S(1)}, f32[80,1024]{1,0:T(8,128)S(1)}, u32[]{:S(2)}, u32[]{:S(2)}) collective-permute-start(f32[80,1024]{1,0:T(8,128)S(1)} %get-tuple-element.613), channel_id=1, source_target_pairs={{0,16},{4,20},{8,24},{12,28},{16,0},{20,4},{24,8},{28,12},{1,17},{... | collective-permute-start | bytes 983048 | tf_op jit(solution)/shard_map/ppermute | solution.py:804
  294.8 14.6 %collective-permute-start.45 = (f32[128,1024]{1,0:T(8,128)S(1)}, f32[128,1024]{1,0:T(8,128)S(1)}, u32[]{:S(2)}, u32[]{:S(2)}) collective-permute-start(f32[128,1024]{1,0:T(8,128)S(1)} %get-tuple-element.620.refs_1_), channel_id=1, source_target_pairs={{0,4},{4,0},{8,12},{12,8},{16,20},{20,16},{24,28},{28,24},{1,5},{5... | collective-permute-start | bytes 1572872 | tf_op jit(solution)/shard_map/ppermute | solution.py:804
  310.2 4.1 %collective-permute-start.47 = (f32[256,1024]{1,0:T(8,128)S(1)}, f32[256,1024]{1,0:T(8,128)S(1)}, u32[]{:S(2)}, u32[]{:S(2)}) collective-permute-start(f32[256,1024]{1,0:T(8,128)S(1)} %get-tuple-element.633.refs_4_), channel_id=1, source_target_pairs={{0,1},{1,0},{2,3},{3,2},{4,5},{5,4},{6,7},{7,6},{8,9},{9,8},{10,11... | collective-permute-start | bytes 3145736 | tf_op jit(solution)/shard_map/ppermute | solution.py:804
  310.7 31.4 %collective-permute-start.54 = (f32[256,1024]{1,0:T(8,128)S(1)}, f32[256,1024]{1,0:T(8,128)S(1)}, u32[]{:S(2)}, u32[]{:S(2)}) collective-permute-start(f32[256,1024]{1,0:T(8,128)S(1)} %get-tuple-element.632.refs_3_), channel_id=1, source_target_pairs={{0,4},{4,0},{8,12},{12,8},{16,20},{20,16},{24,28},{28,24},{1,5},{5... | collective-permute-start | bytes 3145736 | tf_op jit(solution)/shard_map/ppermute | solution.py:804
  311.2 30.9 %collective-permute-start.55 = (f32[256,1024]{1,0:T(8,128)S(1)}, f32[256,1024]{1,0:T(8,128)S(1)}, u32[]{:S(2)}, u32[]{:S(2)}) collective-permute-start(f32[256,1024]{1,0:T(8,128)S(1)} %get-tuple-element.633.refs_4_), channel_id=1, source_target_pairs={{0,2},{1,3},{2,0},{3,1},{4,6},{5,7},{6,4},{7,5},{8,10},{9,11},{10,... | collective-permute-start | bytes 3145736 | tf_op jit(solution)/shard_map/ppermute | solution.py:804
  312.1 16.0 %collective-permute-start.43 = (f32[80,1024]{1,0:T(8,128)S(1)}, f32[80,1024]{1,0:T(8,128)S(1)}, u32[]{:S(2)}, u32[]{:S(2)}) collective-permute-start(f32[80,1024]{1,0:T(8,128)S(1)} %last.5.refs_0_), channel_id=1, source_target_pairs={{0,16},{4,20},{8,24},{12,28},{16,0},{20,4},{24,8},{28,12},{1,17},{... | collective-permute-start | bytes 983048 | tf_op jit(solution)/shard_map/ppermute | solution.py:804
  328.7 12.8 %collective-permute-start.50 = (f32[64,1024]{1,0:T(8,128)S(1)}, f32[64,1024]{1,0:T(8,128)S(1)}, u32[]{:S(2)}, u32[]{:S(2)}) collective-permute-start(f32[64,1024]{1,0:T(8,128)S(1)} %get-tuple-element.644.refs_2_), channel_id=1, source_target_pairs={{0,4},{4,0},{8,12},{12,8},{16,20},{20,16},{24,28},{28,24},{1,5},{5... | collective-permute-start | bytes 786440 | tf_op jit(solution)/shard_map/ppermute | solution.py:804
  330.5 6.5 %collective-permute-start.48 = (f32[48,1024]{1,0:T(8,128)S(1)}, f32[48,1024]{1,0:T(8,128)S(1)}, u32[]{:S(2)}, u32[]{:S(2)}) collective-permute-start(f32[48,1024]{1,0:T(8,128)S(1)} %get-tuple-element.642.refs_0_), channel_id=1, source_target_pairs={{0,8},{4,12},{8,0},{12,4},{16,24},{20,28},{24,16},{28,20},{1,9},{5... | collective-permute-start | bytes 589832 | tf_op jit(solution)/shard_map/ppermute | solution.py:804
  330.5 9.8 %collective-permute-start.49 = (f32[48,1024]{1,0:T(8,128)S(1)}, f32[48,1024]{1,0:T(8,128)S(1)}, u32[]{:S(2)}, u32[]{:S(2)}) collective-permute-start(f32[48,1024]{1,0:T(8,128)S(1)} %get-tuple-element.643.refs_1_), channel_id=1, source_target_pairs={{0,2},{1,3},{2,0},{3,1},{4,6},{5,7},{6,4},{7,5},{8,10},{9,11},{10,... | collective-permute-start | bytes 589832 | tf_op jit(solution)/shard_map/ppermute | solution.py:804
  342.2 4.1 %collective-permute-start.57 = (f32[256,1024]{1,0:T(8,128)S(1)}, f32[256,1024]{1,0:T(8,128)S(1)}, u32[]{:S(2)}, u32[]{:S(2)}) collective-permute-start(f32[256,1024]{1,0:T(8,128)S(1)} %collective-permute-done.55.refs_4_), channel_id=1, source_target_pairs={{0,1},{1,0},{2,3},{3,2},{4,5},{5,4},{6,7},{7,6},{8,9},{9,8},{10,11... | collective-permute-start | bytes 3145736 | tf_op jit(solution)/shard_map/ppermute | solution.py:804
  342.7 13.9 %collective-permute-start.53 = (f32[128,1024]{1,0:T(8,128)S(1)}, f32[128,1024]{1,0:T(8,128)S(1)}, u32[]{:S(2)}, u32[]{:S(2)}) collective-permute-start(f32[128,1024]{1,0:T(8,128)S(1)} %get-tuple-element.665.refs_2_), channel_id=1, source_target_pairs={{0,8},{4,12},{8,0},{12,4},{16,24},{20,28},{24,16},{28,20},{1,9},{5... | collective-permute-start | bytes 1572872 | tf_op jit(solution)/shard_map/ppermute | solution.py:804
  342.7 11.1 %collective-permute-start.51 = (f32[96,1024]{1,0:T(8,128)S(1)}, f32[96,1024]{1,0:T(8,128)S(1)}, u32[]{:S(2)}, u32[]{:S(2)}) collective-permute-start(f32[96,1024]{1,0:T(8,128)S(1)} %get-tuple-element.663.refs_0_), channel_id=1, source_target_pairs={{0,2},{1,3},{2,0},{3,1},{4,6},{5,7},{6,4},{7,5},{8,10},{9,11},{10,... | collective-permute-start | bytes 1179656 | tf_op jit(solution)/shard_map/ppermute | solution.py:804
  343.6 10.8 %collective-permute-start.52 = (f32[96,1024]{1,0:T(8,128)S(1)}, f32[96,1024]{1,0:T(8,128)S(1)}, u32[]{:S(2)}, u32[]{:S(2)}) collective-permute-start(f32[96,1024]{1,0:T(8,128)S(1)} %get-tuple-element.664.refs_1_), channel_id=1, source_target_pairs={{0,4},{4,0},{8,12},{12,8},{16,20},{20,16},{24,28},{28,24},{1,5},{5... | collective-permute-start | bytes 1179656 | tf_op jit(solution)/shard_map/ppermute | solution.py:804
  358.8 3.6 collective-permute-start.61
  358.9 5.3 %collective-permute-start.63 = (f32[256,1024]{1,0:T(8,128)}, f32[256,1024]{1,0:T(8,128)}, u32[]{:S(2)}, u32[]{:S(2)}) collective-permute-start(f32[256,1024]{1,0:T(8,128)} %get-tuple-element.682.refs_5_), channel_id=1, source_target_pairs={{0,1},{1,0},{2,3},{3,2},{4,5},{5,4},{6,7},{7,6},{8,9},{9,8},{10,11... | collective-permute-start | bytes 3145736 | tf_op jit(solution)/shard_map/ppermute | solution.py:804
  359.4 25.3 %collective-permute-start.60 = (f32[256,1024]{1,0:T(8,128)}, f32[256,1024]{1,0:T(8,128)S(1)}, u32[]{:S(2)}, u32[]{:S(2)}) collective-permute-start(f32[256,1024]{1,0:T(8,128)} %get-tuple-element.682.refs_5_), channel_id=1, source_target_pairs={{0,2},{1,3},{2,0},{3,1},{4,6},{5,7},{6,4},{7,5},{8,10},{9,11},{10,... | collective-permute-start | bytes 3145736 | tf_op jit(solution)/shard_map/ppermute | solution.py:804
  360.2 3.9 collective-permute-start.62
  360.2 20.3 %collective-permute-start.58 = (f32[192,1024]{1,0:T(8,128)}, f32[192,1024]{1,0:T(8,128)}, u32[]{:S(2)}, u32[]{:S(2)}) collective-permute-start(f32[192,1024]{1,0:T(8,128)} %get-tuple-element.680.refs_3_), channel_id=1, source_target_pairs={{0,4},{4,0},{8,12},{12,8},{16,20},{20,16},{24,28},{28,24},{1,5},{5... | collective-permute-start | bytes 2359304 | tf_op jit(solution)/shard_map/ppermute | solution.py:804
  363.4 19.9 %collective-permute-start.59 = (f32[192,1024]{1,0:T(8,128)}, f32[192,1024]{1,0:T(8,128)}, u32[]{:S(2)}, u32[]{:S(2)}) collective-permute-start(f32[192,1024]{1,0:T(8,128)} %get-tuple-element.681.refs_4_), channel_id=1, source_target_pairs={{0,8},{4,12},{8,0},{12,4},{16,24},{20,28},{24,16},{28,20},{1,9},{5... | collective-permute-start | bytes 2359304 | tf_op jit(solution)/shard_map/ppermute | solution.py:804
  384.6 5.1 %collective-permute-start.66 = (f32[256,1024]{1,0:T(8,128)S(1)}, f32[256,1024]{1,0:T(8,128)S(1)}, u32[]{:S(2)}, u32[]{:S(2)}) collective-permute-start(f32[256,1024]{1,0:T(8,128)S(1)} %collective-permute-done.60.refs_5_), channel_id=1, source_target_pairs={{0,1},{1,0},{2,3},{3,2},{4,5},{5,4},{6,7},{7,6},{8,9},{9,8},{10,11... | collective-permute-start | bytes 3145736 | tf_op jit(solution)/shard_map/ppermute | solution.py:804
  384.6 3.7 collective-permute-start.64
  385.1 4.6 %collective-permute-start.65 = (f32[192,1024]{1,0:T(8,128)}, f32[192,1024]{1,0:T(8,128)S(1)}, u32[]{:S(2)}, u32[]{:S(2)}) collective-permute-start(f32[192,1024]{1,0:T(8,128)} %collective-permute-done.59.refs_4_), channel_id=1, source_target_pairs={{0,1},{1,0},{2,3},{3,2},{4,5},{5,4},{6,7},{7,6},{8,9},{9,8},{10,11... | collective-permute-start | bytes 2359304 | tf_op jit(solution)/shard_map/ppermute | solution.py:804
  (75 other events, 419.8 us)

commit v4 on v3

--- a/solution.py
+++ b/solution.py
@@ -216,7 +216,7 @@
         branch_ref[:, cols] = branch
         into = pl.ds(j * LANES % (WIDE // 2), LANES)
 
-        @pl.when((core_ref[0] == 0) == (j * LANES >= WIDE // 2))
+        @pl.when((core_ref[1] == 0) == (j * LANES >= WIDE // 2))
         def _():
             send_ref[:, into] = branch.astype(F32)
         put_tiles(gs_ref, j, gb * gate_act)
@@ -524,14 +524,14 @@
     )(gs, act, inner, xproj, cw, cb, skip, carry, dlog, *gact, *gdtw, *two, *gdelta, *gwr)
 
 
-def outer(core, own, other, sizes, flags, weight=None, cols=(), gains=(), small=()):
+def outer(own, other, sizes, flags, bits, weight=None, cols=(), gains=(), small=()):
     length = own[0][0].shape[0]
     low, wide = own[0][0].shape[1] // 2, own[0][1].shape[1]
     halves = [v // 2 for v in sizes for _ in range(2)]
     starts = [sum(halves[:k]) for k in range(len(halves))]
     blk = 256
     total = sum(sizes)
-    at_core = len(sizes)
+    at_core = 1
     big, moves = [], []
     for c in range(2):
         for k, pieces in enumerate(([(own[c][0], None, low)], other[c][0], [(own[c][1], 0, wide)], other[c][1])):
@@ -573,7 +573,7 @@
         def each(k, act):
             c, h = k // 2, k % 2
             for flip in range(2):
-                @pl.when((flag_ref[c] == h) == bool(flip))
+                @pl.when((flag_ref[bits[c]] == h) == bool(flip))
                 def _():
                     getattr(copy(k, flip), act)()
 
@@ -667,16 +667,16 @@
     return jax.ShapeDtypeStruct((rows, cols), F32)
 
 
-def fold_call(index, kept, got, merged):
+def fold_call(flags, at, kept, got, merged):
     n = len(kept)
     ins, specs, sends, keeps = [], [], [], []
     for c in range(n):
         size, cols = kept[c].shape[0] // 2, kept[c].shape[1]
         base = 2 * c if len(got) < n else 0
         for flip in (0, 1):
-            at = lambda i, ix, c=c, flip=flip, base=0: (base + (ix[c] if flip else 1 - ix[c]), 0)
+            block = lambda i, ix, p=at[c], flip=flip, base=0: (base + (ix[p] if flip else 1 - ix[p]), 0)
             ins += [kept[c], got[c % len(got)]]
-            specs += [pl.BlockSpec((size, cols), at), pl.BlockSpec((size, cols), functools.partial(at, base=base))]
+            specs += [pl.BlockSpec((size, cols), block), pl.BlockSpec((size, cols), functools.partial(block, base=base))]
         sends.append(rows_of(size, cols))
         keeps.append(rows_of(size, cols))
     sizes = [v.shape[0] for v in sends]
@@ -695,11 +695,11 @@
                 else:
                     outs[c][...] = a[...] + b[...]
 
-    out = step_call(body, "fold", index, ins, specs, sends + keeps)
+    out = step_call(body, "fold", flags, ins, specs, sends + keeps)
     return list(out[: len(sends)]), list(out[len(sends) :])
 
 
-def last_call(index, kept, got):
+def last_call(flags, kept, got):
     n = len(kept)
     sizes = [v.shape[0] for v in kept]
     cols = kept[0].shape[1]
@@ -710,10 +710,10 @@
             at = slice(sum(sizes[:c]), sum(sizes[: c + 1]))
             refs[-1][at, :] = refs[c][...] + (refs[n + c][...] if len(got) == n else refs[n][at, :])
 
-    return step_call(body, "last", index, [*kept, *got], specs, [rows_of(sum(sizes), cols)])[0]
-
-
-def widen_call(index, sizes, share, got, merged):
+    return step_call(body, "last", flags, [*kept, *got], specs, [rows_of(sum(sizes), cols)])[0]
+
+
+def widen_call(flags, bits, sizes, share, got, merged):
     cols = share[0].shape[1]
     ins = [*share, *got]
     specs = [pl.BlockSpec(v.shape, lambda i, ix: (0, 0)) for v in ins]
@@ -723,7 +723,7 @@
         outs = refs[n + len(got) :]
         for c, size in enumerate(sizes):
             low = sum(sizes[:c])
-            for side, at in ((refs[:n], ix[c]), (refs[n : n + len(got)], 1 - ix[c])):
+            for side, at in ((refs[:n], ix[bits[c]]), (refs[n : n + len(got)], 1 - ix[bits[c]])):
                 value = side[c][...] if len(side) == len(sizes) else side[0][low : low + size, :]
                 if merged:
                     outs[0][pl.ds(pl.multiple_of(2 * low + at * size, SUB), size), :] = value
@@ -731,7 +731,7 @@
                     outs[c][pl.ds(pl.multiple_of(at * size, SUB), size), :] = value
 
     outs = [rows_of(2 * sum(sizes), cols)] if merged else [rows_of(2 * s, cols) for s in sizes]
-    return list(step_call(body, "widen", index, ins, specs, outs))
+    return list(step_call(body, "widen", flags, ins, specs, outs))
 
 
 def blank(shape):
@@ -827,14 +827,16 @@
 
 
 class Reduced:
-    def __init__(self, order, steps):
+    def __init__(self, order, steps, flags, where):
         self.order = order
         self.steps = steps
+        self.flags = flags
+        self.where = where
         self.count = len(steps[0])
         self.share = None
 
-    def index(self, k):
-        return jnp.stack([bit(s[k]) for s in self.steps]).astype(jnp.int32)
+    def places(self, k):
+        return [self.where[s[k]] for s in self.steps]
 
     def same(self, k):
         return all(s[k] == self.steps[0][k] for s in self.steps)
@@ -853,7 +855,7 @@
         k = self.k + 1
         kept, got = self.order.tie(self.kept, self.got)
         if k == self.count:
-            self.share = [last_call(self.index(0), kept, got)]
+            self.share = [last_call(self.flags, kept, got)]
             self.sizes = [v.shape[0] for v in kept]
             if any(v % SUB for v in self.sizes):
                 cut = [sum(self.sizes[:c]) for c in range(len(kept))]
@@ -873,7 +875,7 @@
             sends = [half(v, 1 - i) for v, i in zip(total, index)]
             self.kept = [half(v, i) for v, i in zip(total, index)]
         else:
-            sends, self.kept = fold_call(self.index(k), kept, got, merged)
+            sends, self.kept = fold_call(self.flags, self.places(k), kept, got, merged)
         self.order.done(self.kept[0])
         self.k = k
         self.got = self.send(k, sends)
@@ -896,30 +898,24 @@
                 jnp.where(p, jnp.concatenate([v, g]), jnp.concatenate([g, v])) for p, v, g in zip(pick, share, got)
             ]
         else:
-            self.share = widen_call(self.index(k), self.sizes, share, got, self.same(k - 1))
+            self.share = widen_call(self.flags, self.places(k), self.sizes, share, got, self.same(k - 1))
         self.sizes = [2 * v for v in self.sizes]
         self.order.done(self.share[0])
         self.k = k - 1
         self.got = self.send(k - 1, self.share)
 
+    def pieces(self, values, side):
+        halves = [p + side for p in self.places(0)]
+        values = self.order.tie(*values)
+        return [(v, c, halves[c], 1) for c, v in enumerate(values)] + [
+            (swap(v, CORE), c, halves[c], 2) for c, v in enumerate(values)
+        ]
+
     def own(self):
-        n = len(self.steps)
-        share = self.order.tie(*self.share)
-        return [(v, c, c, 2 * n) for c, v in enumerate(share)] + [
-            (swap(v, CORE), c, c, 2 * n + 1) for c, v in enumerate(share)
-        ]
+        return self.pieces(self.share, 0)
 
     def arrived(self):
-        n = len(self.steps)
-        got = self.order.tie(*self.got)
-        return [(v, c, n + c, 2 * n) for c, v in enumerate(got)] + [
-            (swap(v, CORE), c, n + c, 2 * n + 1) for c, v in enumerate(got)
-        ]
-
-    def flags(self):
-        mine = [bit(s[0]) for s in self.steps]
-        core = bit(CORE)
-        return jnp.stack(mine + [1 - i for i in mine] + [core, 1 - core]).astype(jnp.int32)
+        return self.pieces(self.got, 1)
 
 
 def spans_of(parts, low, high):
@@ -958,9 +954,15 @@
     sizes = [cols, rank, states, 2, taps + 1]
     used = -(-sum(sizes) // SUB) * SUB
     gain_rows = model // 2 // (WIDE // LANES)
+    every = orders("xyz")[0]
+    where = {s: 3 + 2 * k for k, s in enumerate(every)}
+    marks = [lengths[0], core[0], 1 - core[0]]
+    for s in every:
+        marks += [bit(s), 1 - bit(s)]
+    flags = jnp.stack([v.astype(jnp.int32) for v in marks])
     order = Order()
     tie, done = order.tie, order.done
-    sets = [Reduced(order, orders(*heads)) for heads in (("xyz", "yxz"), ("xyz", "yxz"), ("xyz", "zxy", "yzx"))]
+    sets = [Reduced(order, orders(*heads), flags, where) for heads in (("xyz", "yxz"), ("xyz", "yxz"), ("xyz", "zxy", "yzx"))]
     low = model // 2
     third = 3 * model // 8
     heights = [[low, low]] * 2 + [[third, third, low]]
@@ -971,7 +973,7 @@
 
     def op_front():
         state["front"] = front(
-            tok, cot, jnp.concatenate([lengths, core]), row(norm_gain), in_weight, conv_weight, row(conv_bias), turned
+            tok, cot, flags, row(norm_gain), in_weight, conv_weight, row(conv_bias), turned
         )
         _, send, og, _, _, mp = state["front"]
         state["og"] = swap(og, CORE)
@@ -982,7 +984,7 @@
         normed, _, og, _, act, mp = state["front"]
         mp, = tie(mp)
         scans[b] = scan(
-            b, core, mp, normed, og, act, in_weight, out_weight, dt_weight, row(dt_bias), dlog3, row(skip_gain)
+            b, flags, mp, normed, og, act, in_weight, out_weight, dt_weight, row(dt_bias), dlog3, row(skip_gain)
         )
         done(scans[b][0])
         others[b] = (swap(scans[b][2], CORE), swap(scans[b][3], CORE))
@@ -1007,13 +1009,13 @@
             [[(a, *p[1:]) for a, p in zip(array, pieces)] for array, pieces in zip(pair, cut)]
             for pair, cut in zip(arrays, other)
         ]
-        flags = jnp.concatenate([sets[b].index(0), core])
+        bits = sets[b].places(0)
         if b < 2:
-            got = outer(core, own, other, heights[b], flags, in_weight, ((1, width + b * WIDE),))
+            got = outer(own, other, heights[b], flags, bits, in_weight, ((1, width + b * WIDE),))
             gains[b] = got[-1]
         else:
             got = outer(
-                core, own, other, heights[b], flags, in_weight, ((0, 0), (1, WIDE)), (gains[0], gains[1]), small
+                own, other, heights[b], flags, bits, in_weight, ((0, 0), (1, WIDE)), (gains[0], gains[1]), small
             )
         done(got[1])
         chunks = len(heights[b])
@@ -1063,7 +1065,7 @@
     def op_put(p, pieces):
         arrays, targets = tie([v[0] for v in pieces], state["targets"])
         pieces = [(a,) + v[1:] for a, v in zip(arrays, pieces)]
-        state["targets"] = put(targets, pieces, parts[p], heights[p], sets[p].flags())
+        state["targets"] = put(targets, pieces, parts[p], heights[p], flags)
         done(state["targets"][0])
 
     for name in SEQUENCE:

time: 406 us -> 401 us (0.988)
  Pallas kernels: 174 us -> 163 us
  waiting for transfers between devices: 134 us -> 141 us
    ppermute x67, waiting for transfers between devices: 134 us -> 141 us  [swap(): return lax.ppermute(value, axis, [(i, i ^ 1 << place) for i in range(size)])]
    pallas_call x6, Pallas kernels: 22.6 us -> 15.6 us  [put(): pl.pallas_call(body, out_shape=[jax.ShapeDtypeStruct(t.shape, F32) for t...]
    pallas_call x21, Pallas kernels: 18.7 us -> 14.4 us  [step_call(): pl.pallas_call(body, out_shape=outs, grid_spec=pltpu.PrefetchScalarGridSp...]
    unnamed x146 -> x150, local copies, waits for them, and re-layouts: 18.1 us -> 18 us
  transfers between devices with their start and end apart: 67 -> 67, of which waited for: 37 -> 35; matrix products, arithmetic and copies ran while one was open for 3% -> 3% of each run, Pallas kernels for 35% -> 34%
where the time goes in v4:
time: 401 us; the launch traced here: 394 us
  Pallas kernels  163 us (41%)
  waiting for transfers between devices  141 us (35%)
  starting transfers between devices  53.1 us (13%)
  local copies, waits for them, and re-layouts  18.9 us (5%)
  matrix products  7.98 us (2%)
  other arithmetic  7.58 us (2%)
    ppermute x67, waiting for transfers between devices, swap(): return lax.ppermute(value, axis, [(i, i ^ 1 << place) for i in range(size)])  141 us
    pallas_call x4, Pallas kernels, back(): pl.pallas_call(functools.partial(back_kernel, first), grid=(1,), in_specs...  59.2 us
    ppermute x67, starting transfers between devices, swap(): return lax.ppermute(value, axis, [(i, i ^ 1 << place) for i in range(size)])  53.1 us
    pallas_call x2, Pallas kernels, scan(): pl.pallas_call(functools.partial(scan_kernel, block), grid=(1,), in_specs...  29.6 us
    pallas_call x3, Pallas kernels, outer(): pl.pallas_call(body, out_shape=out_shape, grid_spec=pltpu.PrefetchScalarG...  22.9 us
    unnamed x150, local copies, waits for them, and re-layouts  18 us
    pallas_call x6, Pallas kernels, put(): pl.pallas_call(body, out_shape=[jax.ShapeDtypeStruct(t.shape, F32) for t...  15.6 us
    pallas_call x21, Pallas kernels, step_call(): pl.pallas_call(body, out_shape=outs, grid_spec=pltpu.PrefetchScalarGridSp...  14.4 us
  transfers between devices with their start and end apart: 67, of which 35 were waited for; matrix products, arithmetic and copies ran while one was open for 3% of the time, Pallas kernels for 34%

profile of v4, /device:TPU:0, one launch (start us, length us, event | category | flops | bytes accessed | tf_op | source)
XLA Modules:
  0.0 394.0 jit_solution(3235074869955903322)
XLA Ops:
  1.9 7.7 %front.1 = (bf16[320,1024]{1,0:T(8,128)(2,1)}, f32[320,512]{1,0:T(8,128)}, f32[320,1024]{1,0:T(8,128)}, f32[320,2048]{1,0:T(8,128)}, bf16[320,2048]{1,0:T(8,128)(2,1)}, /*index=5*/f32[320,96]{1,0:T(8,128)}) custom-call(s32[11]{0:T(128)} %stack.39.len_ref.core_ref.flag_ref.ix, bf16[320,1024]{1,0:T(8,128)(2,1)} %bitcast.57, bf16[320,1024]{1,0:T(8,128)(2,1)} %bitcast.61, ...), custom_call_target="tpu_custom_call" | custom-call | flops 1 | bytes 1 | tf_op jit(solution)/shard_map/front/pallas_call | solution.py:75
  10.8 14.7 %scan0.1 = (bf16[320,1024]{1,0:T(8,128)(2,1)}, bf16[320,1024]{1,0:T(8,128)(2,1)}, f32[320,768]{1,0:T(8,128)}, f32[320,768]{1,0:T(8,128)}, f32[2560,128]{1,0:T(8,...) custom-call(s32[11]{0:T(128)} %stack.39.len_ref.core_ref.flag_ref.ix, f32[320,96]{1,0:T(8,128)} %get-tuple-element.463.mp_ref, ...), custom_call_target="tpu_custom_call" | custom-call | flops 1 | bytes 1 | tf_op jit(solution)/shard_map/scan0/pallas_call | solution.py:247
  26.1 4.5 %collective-permute-done.2.refs_5_.refs_1_ = f32[320,512]{1,0:T(8,128)S(1)} collective-permute-done((f32[320,512]{1,0:T(8,128)}, f32[320,512]{1,0:T(8,128)S(1)}, u32[]{:S(2)}, u32[]{:S(2)}) %collective-permute-start.2) | collective-permute-done | bytes 655392 | tf_op jit(solution)/shard_map/ppermute | solution.py:804
  32.6 6.6 %outer.3 = (f32[256,1024]{1,0:T(8,128)}, f32[256,1024]{1,0:T(8,128)}, f32[256,1024]{1,0:T(8,128)}, f32[256,1024]{1,0:T(8,128)}, f32[512,128]{1,0:T(8,128)}) custom-call(s32[11]{0:T(128)} %stack.39.len_ref.core_ref.flag_ref.ix, bf16[320,1024]{1,0:T(8,128)(2,1)} %get-tuple-element.380.refs_0_, f32[320,768]{1,0:T(8,128)} %copy-done.60, ...), custom_call_target="tpu_custom_call" | custom-call | flops 1 | bytes 1 | tf_op jit(solution)/shard_map/outer/pallas_call | solution.py:633
  39.2 2.7 collective-permute-start.4
  41.9 1.6 collective-permute-start.5
  43.4 14.9 %scan1.1 = (bf16[320,1024]{1,0:T(8,128)(2,1)}, bf16[320,1024]{1,0:T(8,128)(2,1)}, f32[320,768]{1,0:T(8,128)}, f32[320,768]{1,0:T(8,128)}, f32[2560,128]{1,0:T(8,...) custom-call(s32[11]{0:T(128)} %stack.39.len_ref.core_ref.flag_ref.ix, f32[320,96]{1,0:T(8,128)} %get-tuple-element.463.mp_ref, ...), custom_call_target="tpu_custom_call" | custom-call | flops 1 | bytes 1 | tf_op jit(solution)/shard_map/scan1/pallas_call | solution.py:247
  59.0 4.9 %fusion.13 = bf16[320,1024]{1,0:T(8,128)(2,1)} fusion(bf16[2048,1024]{1,0:T(8,128)(2,1)} %wout_hbm.3, bf16[320,1024]{1,0:T(8,128)(2,1)} %get-tuple-element.398.refs_0_, bf16[320,1024]{1,0:T(8,128)(2,1)S(1)} %copy-done.67, pred[320]{0:T(512)(128)(4,1)S(1)} %iota_compare_fusion, bf16[1,320,1024]{2,1,0:T(8,128)(2,1)S(1)} %copy-done.55), kind=kOutput, calls=%fused_computation.23 | convolution fusion | flops 1346109440 | bytes 6816064 | tf_op jit(solution)/shard_map/dot_general | solution.py:23
  63.9 1.9 collective-permute-done.4.refs_1_.refs_3_
  65.8 1.5 collective-permute-done.5.refs_5_.refs_7_
  67.2 1.6 fold.9
  70.4 1.6 collective-permute-start.6
  73.8 6.7 %outer.4 = (f32[256,1024]{1,0:T(8,128)}, f32[256,1024]{1,0:T(8,128)}, f32[256,1024]{1,0:T(8,128)}, f32[256,1024]{1,0:T(8,128)}, f32[512,128]{1,0:T(8,128)}) custom-call(s32[11]{0:T(128)} %stack.39.len_ref.core_ref.flag_ref.ix, bf16[320,1024]{1,0:T(8,128)(2,1)} %get-tuple-element.398.refs_0_, f32[320,768]{1,0:T(8,128)} %copy-done.59, ...), custom_call_target="tpu_custom_call" | custom-call | flops 1 | bytes 1 | tf_op jit(solution)/shard_map/outer/pallas_call | solution.py:633
  80.5 1.5 collective-permute-start.13
  82.5 1.8 collective-permute-done.6.refs_1_.refs_3_
  85.1 1.7 collective-permute-done.7.refs_5_.refs_7_
  92.5 1.6 collective-permute-start.10
  94.2 1.3 copy-done.9
  95.5 12.6 %back01.1 = (f32[160,1024]{1,0:T(8,128)S(1)}, f32[160,64]{1,0:T(8,128)S(1)}, f32[64,1024]{1,0:T(8,128)S(1)}, f32[160,128]{1,0:T(8,128)S(1)}, f32[2,16,8,128]{3,2,1,0:T(8,128)S(1)}, /*index=5*/f32[2,1024]{1,0:T(2,128)S(1)}) custom-call(f32[320,96]{1,0:T(8,128)S(1)} %copy-done.5, bf16[320,2048]{1,0:T(8,128)(2,1)S(1)} %copy-done, f32[2560,128]{1,0:T(8,128)S(1)} %copy-done.8, ...), custom_call_target="tpu_custom_call" | custom-call | flops 1 | bytes 1 | tf_op jit(solution)/shard_map/back01/pallas_call | solution.py:426
  109.1 2.6 collective-permute-start.11
  111.7 12.6 %back00.1 = (f32[160,1024]{1,0:T(8,128)S(1)}, f32[160,64]{1,0:T(8,128)S(1)}, f32[64,1024]{1,0:T(8,128)S(1)}, f32[160,128]{1,0:T(8,128)S(1)}, f32[2,16,8,128]{3,2,1,0:T(8,128)S(1)}, /*index=5*/f32[2,1024]{1,0:T(2,128)S(1)}) custom-call(f32[320,96]{1,0:T(8,128)S(1)} %copy-done.5, bf16[320,2048]{1,0:T(8,128)(2,1)S(1)} %copy-done, f32[2560,128]{1,0:T(8,128)S(1)} %copy-done.8, ...), custom_call_target="tpu_custom_call" | custom-call | flops 1 | bytes 1 | tf_op jit(solution)/shard_map/back00/pallas_call | solution.py:426
  127.6 12.6 %back11.1 = (f32[160,1024]{1,0:T(8,128)S(1)}, f32[160,64]{1,0:T(8,128)S(1)}, f32[64,1024]{1,0:T(8,128)S(1)}, f32[160,128]{1,0:T(8,128)S(1)}, f32[2,16,8,128]{3,2,1,0:T(8,128)S(1)}, /*index=5*/f32[2,1024]{1,0:T(2,128)S(1)}) custom-call(f32[320,96]{1,0:T(8,128)S(1)} %copy-done.5, bf16[320,2048]{1,0:T(8,128)(2,1)S(1)} %copy-done, f32[2560,128]{1,0:T(8,128)S(1)} %copy-done.6, ...), custom_call_target="tpu_custom_call" | custom-call | flops 1 | bytes 1 | tf_op jit(solution)/shard_map/back11/pallas_call | solution.py:426
  144.5 21.3 %back10.1 = (f32[160,1024]{1,0:T(8,128)S(1)}, f32[160,64]{1,0:T(8,128)S(1)}, f32[64,1024]{1,0:T(8,128)S(1)}, f32[160,128]{1,0:T(8,128)S(1)}, f32[2,16,8,128]{3,2,1,0:T(8,128)S(1)}, /*index=5*/f32[2,1024]{1,0:T(2,128)S(1)}) custom-call(f32[320,96]{1,0:T(8,128)S(1)} %copy-done.5, bf16[320,2048]{1,0:T(8,128)(2,1)S(1)} %copy-done, f32[2560,128]{1,0:T(8,128)S(1)} %copy-done.6, ...), custom_call_target="tpu_custom_call" | custom-call | flops 1 | bytes 1 | tf_op jit(solution)/shard_map/back10/pallas_call | solution.py:426
  168.7 1.7 collective-permute-start.20
  170.4 2.6 collective-permute-start.21
  173.0 6.5 %post0.1 = (f32[320,1024]{1,0:T(8,128)}, f32[184,1024]{1,0:T(8,128)}) custom-call(f32[2560,128]{1,0:T(8,128)} %get-tuple-element.382.gs_ref, bf16[320,2048]{1,0:T(8,128)(2,1)} %get-tuple-element.360.act_ref, f32[320,2048]{1,0:T(8,128)} %get-tuple-element.383.inner_ref, bf16[96,2048]{1,0:T(8,128)(2,1)} %bitcast.59, f32[4,2048]{1,0:T(4,128)} %cw_ref.5, ...), custom_call_target="tpu_custom_call" | custom-call | flops 1 | bytes 1 | tf_op jit(solution)/shard_map/post0/pallas_call | solution.py:511
  185.4 6.5 %post1.1 = (f32[320,1024]{1,0:T(8,128)}, f32[184,1024]{1,0:T(8,128)}) custom-call(f32[2560,128]{1,0:T(8,128)} %get-tuple-element.453.gs_ref, bf16[320,2048]{1,0:T(8,128)(2,1)} %get-tuple-element.360.act_ref, f32[320,2048]{1,0:T(8,128)} %get-tuple-element.383.inner_ref, bf16[96,2048]{1,0:T(8,128)(2,1)} %bitcast.60, f32[4,2048]{1,0:T(4,128)} %cw_ref.5, ...), custom_call_target="tpu_custom_call" | custom-call | flops 1 | bytes 1 | tf_op jit(solution)/shard_map/post1/pallas_call | solution.py:511
  193.8 2.4 collective-permute-done.27.refs_13_
  196.2 9.7 %outer.5 = (f32[192,1024]{1,0:T(8,128)}, f32[192,1024]{1,0:T(8,128)}, f32[192,1024]{1,0:T(8,128)}, f32[192,1024]{1,0:T(8,128)}, f32[256,1024]{1,0:T(8,128)}, /*index=5*/f32[256,1024]{1,0:T(8,128)}, f32[512,128]{1,0:T(8,128)}) custom-call(s32[11]{0:T(128)} %stack.39.len_ref.core_ref.flag_ref.ix, ...), custom_call_target="tpu_custom_call" | custom-call | flops 1 | bytes 1 | tf_op jit(solution)/shard_map/outer/pallas_call | solution.py:633
  208.7 1.5 collective-permute-done.29.refs_6_
  210.2 2.6 put.6
  212.8 19.0 %collective-permute-done.23.refs_3_ = f32[256,1024]{1,0:T(8,128)S(1)} collective-permute-done((f32[256,1024]{1,0:T(8,128)S(1)}, f32[256,1024]{1,0:T(8,128)S(1)}, u32[]{:S(2)}, u32[]{:S(2)}) %collective-permute-start.23) | collective-permute-done | bytes 1048608 | tf_op jit(solution)/shard_map/ppermute | solution.py:804
  233.3 1.4 collective-permute-start.33
  235.1 3.2 collective-permute-start.22
  238.3 2.6 put.7
  240.9 16.2 %collective-permute-done.22.refs_1_ = f32[64,1024]{1,0:T(8,128)S(1)} collective-permute-done((f32[64,1024]{1,0:T(8,128)S(1)}, f32[64,1024]{1,0:T(8,128)S(1)}, u32[]{:S(2)}, u32[]{:S(2)}) %collective-permute-start.22) | collective-permute-done | bytes 262176 | tf_op jit(solution)/shard_map/ppermute | solution.py:804
  257.7 1.5 collective-permute-done.34.refs_5_.refs_7_
  260.0 2.6 collective-permute-start.38
  262.6 1.4 collective-permute-start.36
  264.4 7.8 %collective-permute-done.36.refs_1_.refs_3_ = f32[96,1024]{1,0:T(8,128)S(1)} collective-permute-done((f32[96,1024]{1,0:T(8,128)S(1)}, f32[96,1024]{1,0:T(8,128)S(1)}, u32[]{:S(2)}, u32[]{:S(2)}) %collective-permute-start.36) | collective-permute-done | bytes 393248 | tf_op jit(solution)/shard_map/ppermute | solution.py:804
  273.3 2.2 collective-permute-done.38.refs_9_.refs_11_
  277.1 2.3 collective-permute-start.39
  280.5 8.5 %collective-permute-done.39.refs_1_.refs_3_ = f32[48,1024]{1,0:T(8,128)S(1)} collective-permute-done((f32[48,1024]{1,0:T(8,128)S(1)}, f32[48,1024]{1,0:T(8,128)S(1)}, u32[]{:S(2)}, u32[]{:S(2)}) %collective-permute-start.39) | collective-permute-done | bytes 196640 | tf_op jit(solution)/shard_map/ppermute | solution.py:804
  290.3 1.4 collective-permute-start.44
  292.0 1.3 collective-permute-start.42
  293.3 3.1 fusion.14
  296.4 1.4 fusion.17
  297.9 9.6 %collective-permute-done.42.refs_3_ = f32[80,1024]{1,0:T(8,128)S(1)} collective-permute-done((f32[80,1024]{1,0:T(8,128)S(1)}, f32[80,1024]{1,0:T(8,128)S(1)}, u32[]{:S(2)}, u32[]{:S(2)}) %collective-permute-start.42) | collective-permute-done | bytes 327712 | tf_op jit(solution)/shard_map/ppermute | solution.py:804
  311.5 1.5 collective-permute-done.47.refs_6_
  313.0 2.6 put.8
  315.6 11.3 %collective-permute-done.43.refs_1_ = f32[80,1024]{1,0:T(8,128)S(1)} collective-permute-done((f32[80,1024]{1,0:T(8,128)S(1)}, f32[80,1024]{1,0:T(8,128)S(1)}, u32[]{:S(2)}, u32[]{:S(2)}) %collective-permute-start.43) | collective-permute-done | bytes 327712 | tf_op jit(solution)/shard_map/ppermute | solution.py:804
  327.4 1.8 collective-permute-start.50
  330.4 5.4 %collective-permute-done.48.refs_3_ = f32[48,1024]{1,0:T(8,128)S(1)} collective-permute-done((f32[48,1024]{1,0:T(8,128)S(1)}, f32[48,1024]{1,0:T(8,128)S(1)}, u32[]{:S(2)}, u32[]{:S(2)}) %collective-permute-start.48) | collective-permute-done | bytes 196640 | tf_op jit(solution)/shard_map/ppermute | solution.py:804
  335.8 3.1 collective-permute-done.49.refs_4_
  343.5 1.5 collective-permute-done.57.refs_6_
  345.0 2.6 put.9
  347.6 4.9 %collective-permute-done.51.refs_3_ = f32[96,1024]{1,0:T(8,128)S(1)} collective-permute-done((f32[96,1024]{1,0:T(8,128)S(1)}, f32[96,1024]{1,0:T(8,128)S(1)}, u32[]{:S(2)}, u32[]{:S(2)}) %collective-permute-start.51) | collective-permute-done | bytes 393248 | tf_op jit(solution)/shard_map/ppermute | solution.py:804
  353.0 2.2 collective-permute-done.53.refs_5_
  358.6 2.3 collective-permute-done.62.refs_7_
  360.9 3.0 put.10
  363.9 13.4 %collective-permute-done.58.refs_3_ = f32[192,1024]{1,0:T(8,128)S(1)} collective-permute-done((f32[192,1024]{1,0:T(8,128)S(1)}, f32[192,1024]{1,0:T(8,128)S(1)}, u32[]{:S(2)}, u32[]{:S(2)}) %collective-permute-start.58) | collective-permute-done | bytes 786464 | tf_op jit(solution)/shard_map/ppermute | solution.py:804
  377.9 3.8 collective-permute-done.60.refs_5_
  382.2 3.3 collective-permute-done.64.refs_6_
  386.6 2.3 put.11
  (285 shorter events, 67.1 us)
Async XLA Ops:
  9.6 21.1 %collective-permute-start.1 = (f32[320,1024]{1,0:T(8,128)}, f32[320,1024]{1,0:T(8,128)S(1)}, u32[]{:S(2)}, u32[]{:S(2)}) collective-permute-start(f32[320,1024]{1,0:T(8,128)} %get-tuple-element.400.og_hbm.refs_2_), channel_id=1, source_target_pairs={{0,1},{1,0},{2,3},{3,2},{4,5},{5,4},{6,7},{7,6},{8,9},{9,8},{10,11... | collective-permute-start | bytes 3932168 | tf_op jit(solution)/shard_map/ppermute | solution.py:804
  25.5 5.2 %collective-permute-start = (f32[320,768]{1,0:T(8,128)}, f32[320,768]{1,0:T(8,128)S(1)}, u32[]{:S(2)}, u32[]{:S(2)}) collective-permute-start(f32[320,768]{1,0:T(8,128)} %get-tuple-element.365), channel_id=1, source_target_pairs={{0,1},{1,0},{2,3},{3,2},{4,5},{5,4},{6,7},{7,6},{8,9},{9,8},{10,11... | collective-permute-start | bytes 2949128 | tf_op jit(solution)/shard_map/ppermute | solution.py:804
  25.6 5.1 %collective-permute-start.3 = (f32[320,768]{1,0:T(8,128)}, f32[320,768]{1,0:T(8,128)S(1)}, u32[]{:S(2)}, u32[]{:S(2)}) collective-permute-start(f32[320,768]{1,0:T(8,128)} %get-tuple-element.367), channel_id=1, source_target_pairs={{0,1},{1,0},{2,3},{3,2},{4,5},{5,4},{6,7},{7,6},{8,9},{9,8},{10,11... | collective-permute-start | bytes 2949128 | tf_op jit(solution)/shard_map/ppermute | solution.py:804
  26.1 4.6 %collective-permute-start.2 = (f32[320,512]{1,0:T(8,128)}, f32[320,512]{1,0:T(8,128)S(1)}, u32[]{:S(2)}, u32[]{:S(2)}) collective-permute-start(f32[320,512]{1,0:T(8,128)} %get-tuple-element.366), channel_id=1, source_target_pairs={{0,1},{1,0},{2,3},{3,2},{4,5},{5,4},{6,7},{7,6},{8,9},{9,8},{10,11... | collective-permute-start | bytes 1966088 | tf_op jit(solution)/shard_map/ppermute | solution.py:804
  39.2 26.6 %collective-permute-start.4 = (f32[256,1024]{1,0:T(8,128)}, f32[256,1024]{1,0:T(8,128)S(1)}, u32[]{:S(2)}, u32[]{:S(2)}) collective-permute-start(f32[256,1024]{1,0:T(8,128)} %get-tuple-element.385), channel_id=1, source_target_pairs={{0,4},{4,0},{8,12},{12,8},{16,20},{20,16},{24,28},{28,24},{1,5},{5... | collective-permute-start | bytes 3145736 | tf_op jit(solution)/shard_map/ppermute | solution.py:804
  41.9 25.4 %collective-permute-start.5 = (f32[256,1024]{1,0:T(8,128)}, f32[256,1024]{1,0:T(8,128)S(1)}, u32[]{:S(2)}, u32[]{:S(2)}) collective-permute-start(f32[256,1024]{1,0:T(8,128)} %get-tuple-element.386), channel_id=1, source_target_pairs={{0,2},{1,3},{2,0},{3,1},{4,6},{5,7},{6,4},{7,5},{8,10},{9,11},{10,... | collective-permute-start | bytes 3145736 | tf_op jit(solution)/shard_map/ppermute | solution.py:804
  58.4 14.1 %collective-permute-start.8 = (f32[320,768]{1,0:T(8,128)}, f32[320,768]{1,0:T(8,128)S(1)}, u32[]{:S(2)}, u32[]{:S(2)}) collective-permute-start(f32[320,768]{1,0:T(8,128)} %get-tuple-element.396), channel_id=1, source_target_pairs={{0,1},{1,0},{2,3},{3,2},{4,5},{5,4},{6,7},{7,6},{8,9},{9,8},{10,11... | collective-permute-start | bytes 2949128 | tf_op jit(solution)/shard_map/ppermute | solution.py:804
  58.4 14.1 %collective-permute-start.9 = (f32[320,768]{1,0:T(8,128)}, f32[320,768]{1,0:T(8,128)S(1)}, u32[]{:S(2)}, u32[]{:S(2)}) collective-permute-start(f32[320,768]{1,0:T(8,128)} %get-tuple-element.397), channel_id=1, source_target_pairs={{0,1},{1,0},{2,3},{3,2},{4,5},{5,4},{6,7},{7,6},{8,9},{9,8},{10,11... | collective-permute-start | bytes 2949128 | tf_op jit(solution)/shard_map/ppermute | solution.py:804
  70.4 13.9 %collective-permute-start.6 = (f32[128,1024]{1,0:T(8,128)}, f32[128,1024]{1,0:T(8,128)S(1)}, u32[]{:S(2)}, u32[]{:S(2)}) collective-permute-start(f32[128,1024]{1,0:T(8,128)} %get-tuple-element.393), channel_id=1, source_target_pairs={{0,2},{1,3},{2,0},{3,1},{4,6},{5,7},{6,4},{7,5},{8,10},{9,11},{10,... | collective-permute-start | bytes 1572872 | tf_op jit(solution)/shard_map/ppermute | solution.py:804
  72.0 14.9 %collective-permute-start.7 = (f32[128,1024]{1,0:T(8,128)S(1)}, f32[128,1024]{1,0:T(8,128)S(1)}, u32[]{:S(2)}, u32[]{:S(2)}) collective-permute-start(f32[128,1024]{1,0:T(8,128)S(1)} %get-tuple-element.394), channel_id=1, source_target_pairs={{0,4},{4,0},{8,12},{12,8},{16,20},{20,16},{24,28},{28,24},{1,5},{5... | collective-permute-start | bytes 1572872 | tf_op jit(solution)/shard_map/ppermute | solution.py:804
  80.5 44.5 %collective-permute-start.13 = (f32[256,1024]{1,0:T(8,128)}, f32[256,1024]{1,0:T(8,128)S(1)}, u32[]{:S(2)}, u32[]{:S(2)}) collective-permute-start(f32[256,1024]{1,0:T(8,128)} %get-tuple-element.441), channel_id=1, source_target_pairs={{0,4},{4,0},{8,12},{12,8},{16,20},{20,16},{24,28},{28,24},{1,5},{5... | collective-permute-start | bytes 3145736 | tf_op jit(solution)/shard_map/ppermute | solution.py:804
  82.0 43.0 %collective-permute-start.14 = (f32[256,1024]{1,0:T(8,128)}, f32[256,1024]{1,0:T(8,128)S(1)}, u32[]{:S(2)}, u32[]{:S(2)}) collective-permute-start(f32[256,1024]{1,0:T(8,128)} %get-tuple-element.442), channel_id=1, source_target_pairs={{0,2},{1,3},{2,0},{3,1},{4,6},{5,7},{6,4},{7,5},{8,10},{9,11},{10,... | collective-permute-start | bytes 3145736 | tf_op jit(solution)/shard_map/ppermute | solution.py:804
  92.5 15.7 %collective-permute-start.10 = (f32[128,1024]{1,0:T(8,128)S(1)}, f32[128,1024]{1,0:T(8,128)S(1)}, u32[]{:S(2)}, u32[]{:S(2)}) collective-permute-start(f32[128,1024]{1,0:T(8,128)S(1)} %get-tuple-element.414), channel_id=1, source_target_pairs={{0,8},{4,12},{8,0},{12,4},{16,24},{20,28},{24,16},{28,20},{1,9},{5... | collective-permute-start | bytes 1572872 | tf_op jit(solution)/shard_map/ppermute | solution.py:804
  109.1 15.3 %collective-permute-start.11 = (f32[64,1024]{1,0:T(8,128)S(1)}, f32[64,1024]{1,0:T(8,128)S(1)}, u32[]{:S(2)}, u32[]{:S(2)}) collective-permute-start(f32[64,1024]{1,0:T(8,128)S(1)} %get-tuple-element.436), channel_id=1, source_target_pairs={{0,16},{4,20},{8,24},{12,28},{16,0},{20,4},{24,8},{28,12},{1,17},{... | collective-permute-start | bytes 786440 | tf_op jit(solution)/shard_map/ppermute | solution.py:804
  125.9 15.1 %collective-permute-start.15 = (f32[128,1024]{1,0:T(8,128)S(1)}, f32[128,1024]{1,0:T(8,128)S(1)}, u32[]{:S(2)}, u32[]{:S(2)}) collective-permute-start(f32[128,1024]{1,0:T(8,128)S(1)} %get-tuple-element.449), channel_id=1, source_target_pairs={{0,2},{1,3},{2,0},{3,1},{4,6},{5,7},{6,4},{7,5},{8,10},{9,11},{10,... | collective-permute-start | bytes 1572872 | tf_op jit(solution)/shard_map/ppermute | solution.py:804
  126.7 14.4 %collective-permute-start.16 = (f32[128,1024]{1,0:T(8,128)S(1)}, f32[128,1024]{1,0:T(8,128)S(1)}, u32[]{:S(2)}, u32[]{:S(2)}) collective-permute-start(f32[128,1024]{1,0:T(8,128)S(1)} %get-tuple-element.450), channel_id=1, source_target_pairs={{0,4},{4,0},{8,12},{12,8},{16,20},{20,16},{24,28},{28,24},{1,5},{5... | collective-permute-start | bytes 1572872 | tf_op jit(solution)/shard_map/ppermute | solution.py:804
  127.3 15.6 %collective-permute-start.12 = (f32[64,1024]{1,0:T(8,128)S(1)}, f32[64,1024]{1,0:T(8,128)S(1)}, u32[]{:S(2)}, u32[]{:S(2)}) collective-permute-start(f32[64,1024]{1,0:T(8,128)S(1)} %last.3.refs_0_), channel_id=1, source_target_pairs={{0,16},{4,20},{8,24},{12,28},{16,0},{20,4},{24,8},{28,12},{1,17},{... | collective-permute-start | bytes 786440 | tf_op jit(solution)/shard_map/ppermute | solution.py:804
  141.8 24.1 %collective-permute-start.18 = (f32[128,1024]{1,0:T(8,128)S(1)}, f32[128,1024]{1,0:T(8,128)S(1)}, u32[]{:S(2)}, u32[]{:S(2)}) collective-permute-start(f32[128,1024]{1,0:T(8,128)S(1)} %get-tuple-element.470), channel_id=1, source_target_pairs={{0,8},{4,12},{8,0},{12,4},{16,24},{20,28},{24,16},{28,20},{1,9},{5... | collective-permute-start | bytes 1572872 | tf_op jit(solution)/shard_map/ppermute | solution.py:804
  143.5 23.4 %collective-permute-start.17 = (f32[128,1024]{1,0:T(8,128)S(1)}, f32[128,1024]{1,0:T(8,128)S(1)}, u32[]{:S(2)}, u32[]{:S(2)}) collective-permute-start(f32[128,1024]{1,0:T(8,128)S(1)} %widen.9.refs_0_), channel_id=1, source_target_pairs={{0,8},{4,12},{8,0},{12,4},{16,24},{20,28},{24,16},{28,20},{1,9},{5... | collective-permute-start | bytes 1572872 | tf_op jit(solution)/shard_map/ppermute | solution.py:804
  167.5 13.5 %collective-permute-start.19 = (f32[128,1024]{1,0:T(8,128)S(1)}, f32[128,1024]{1,0:T(8,128)S(1)}, u32[]{:S(2)}, u32[]{:S(2)}) collective-permute-start(f32[128,1024]{1,0:T(8,128)S(1)} %get-tuple-element.506.refs_0_), channel_id=1, source_target_pairs={{0,2},{1,3},{2,0},{3,1},{4,6},{5,7},{6,4},{7,5},{8,10},{9,11},{10,... | collective-permute-start | bytes 1572872 | tf_op jit(solution)/shard_map/ppermute | solution.py:804
  168.7 13.2 %collective-permute-start.20 = (f32[128,1024]{1,0:T(8,128)S(1)}, f32[128,1024]{1,0:T(8,128)S(1)}, u32[]{:S(2)}, u32[]{:S(2)}) collective-permute-start(f32[128,1024]{1,0:T(8,128)S(1)} %get-tuple-element.507.refs_1_), channel_id=1, source_target_pairs={{0,4},{4,0},{8,12},{12,8},{16,20},{20,16},{24,28},{28,24},{1,5},{5... | collective-permute-start | bytes 1572872 | tf_op jit(solution)/shard_map/ppermute | solution.py:804
  170.4 10.1 %collective-permute-start.21 = (f32[64,1024]{1,0:T(8,128)S(1)}, f32[64,1024]{1,0:T(8,128)S(1)}, u32[]{:S(2)}, u32[]{:S(2)}) collective-permute-start(f32[64,1024]{1,0:T(8,128)S(1)} %get-tuple-element.502), channel_id=1, source_target_pairs={{0,16},{4,20},{8,24},{12,28},{16,0},{20,4},{24,8},{28,12},{1,17},{... | collective-permute-start | bytes 786440 | tf_op jit(solution)/shard_map/ppermute | solution.py:804
  179.5 16.7 %collective-permute-start.25 = (f32[320,1024]{1,0:T(8,128)}, f32[320,1024]{1,0:T(8,128)}, u32[]{:S(2)}, u32[]{:S(2)}) collective-permute-start(f32[320,1024]{1,0:T(8,128)} %get-tuple-element.607.refs_2_), channel_id=1, source_target_pairs={{0,1},{1,0},{2,3},{3,2},{4,5},{5,4},{6,7},{7,6},{8,9},{9,8},{10,11... | collective-permute-start | bytes 3932168 | tf_op jit(solution)/shard_map/ppermute | solution.py:804
  192.0 4.3 %collective-permute-start.26 = (f32[320,1024]{1,0:T(8,128)}, f32[320,1024]{1,0:T(8,128)}, u32[]{:S(2)}, u32[]{:S(2)}) collective-permute-start(f32[320,1024]{1,0:T(8,128)} %get-tuple-element.608.refs_6_), channel_id=1, source_target_pairs={{0,1},{1,0},{2,3},{3,2},{4,5},{5,4},{6,7},{7,6},{8,9},{9,8},{10,11... | collective-permute-start | bytes 3932168 | tf_op jit(solution)/shard_map/ppermute | solution.py:804
  193.2 3.0 collective-permute-start.27
  205.9 2.7 collective-permute-start.28
  206.2 4.0 %collective-permute-start.29 = (f32[256,1024]{1,0:T(8,128)S(1)}, f32[256,1024]{1,0:T(8,128)S(1)}, u32[]{:S(2)}, u32[]{:S(2)}) collective-permute-start(f32[256,1024]{1,0:T(8,128)S(1)} %get-tuple-element.550.refs_4_), channel_id=1, source_target_pairs={{0,1},{1,0},{2,3},{3,2},{4,5},{5,4},{6,7},{7,6},{8,9},{9,8},{10,11... | collective-permute-start | bytes 3145736 | tf_op jit(solution)/shard_map/ppermute | solution.py:804
  206.5 25.2 %collective-permute-start.23 = (f32[256,1024]{1,0:T(8,128)S(1)}, f32[256,1024]{1,0:T(8,128)S(1)}, u32[]{:S(2)}, u32[]{:S(2)}) collective-permute-start(f32[256,1024]{1,0:T(8,128)S(1)} %get-tuple-element.549.refs_3_), channel_id=1, source_target_pairs={{0,4},{4,0},{8,12},{12,8},{16,20},{20,16},{24,28},{28,24},{1,5},{5... | collective-permute-start | bytes 3145736 | tf_op jit(solution)/shard_map/ppermute | solution.py:804
  206.8 24.9 %collective-permute-start.24 = (f32[256,1024]{1,0:T(8,128)S(1)}, f32[256,1024]{1,0:T(8,128)S(1)}, u32[]{:S(2)}, u32[]{:S(2)}) collective-permute-start(f32[256,1024]{1,0:T(8,128)S(1)} %get-tuple-element.550.refs_4_), channel_id=1, source_target_pairs={{0,2},{1,3},{2,0},{3,1},{4,6},{5,7},{6,4},{7,5},{8,10},{9,11},{10,... | collective-permute-start | bytes 3145736 | tf_op jit(solution)/shard_map/ppermute | solution.py:804
  231.8 3.3 collective-permute-start.30
  231.8 6.5 %collective-permute-start.31 = (f32[256,1024]{1,0:T(8,128)S(1)}, f32[256,1024]{1,0:T(8,128)S(1)}, u32[]{:S(2)}, u32[]{:S(2)}) collective-permute-start(f32[256,1024]{1,0:T(8,128)S(1)} %collective-permute-done.24.refs_4_), channel_id=1, source_target_pairs={{0,1},{1,0},{2,3},{3,2},{4,5},{5,4},{6,7},{7,6},{8,9},{9,8},{10,11... | collective-permute-start | bytes 3145736 | tf_op jit(solution)/shard_map/ppermute | solution.py:804
  232.3 26.9 %collective-permute-start.35 = (f32[256,1024]{1,0:T(8,128)S(1)}, f32[256,1024]{1,0:T(8,128)S(1)}, u32[]{:S(2)}, u32[]{:S(2)}) collective-permute-start(f32[256,1024]{1,0:T(8,128)S(1)} %copy-done.69), channel_id=1, source_target_pairs={{0,2},{1,3},{2,0},{3,1},{4,6},{5,7},{6,4},{7,5},{8,10},{9,11},{10,... | collective-permute-start | bytes 3145736 | tf_op jit(solution)/shard_map/ppermute | solution.py:804
  233.3 24.5 %collective-permute-start.33 = (f32[192,1024]{1,0:T(8,128)S(1)}, f32[192,1024]{1,0:T(8,128)S(1)}, u32[]{:S(2)}, u32[]{:S(2)}) collective-permute-start(f32[192,1024]{1,0:T(8,128)S(1)} %copy-done.71), channel_id=1, source_target_pairs={{0,4},{4,0},{8,12},{12,8},{16,20},{20,16},{24,28},{28,24},{1,5},{5... | collective-permute-start | bytes 2359304 | tf_op jit(solution)/shard_map/ppermute | solution.py:804
  234.7 24.5 %collective-permute-start.34 = (f32[192,1024]{1,0:T(8,128)S(1)}, f32[192,1024]{1,0:T(8,128)S(1)}, u32[]{:S(2)}, u32[]{:S(2)}) collective-permute-start(f32[192,1024]{1,0:T(8,128)S(1)} %copy-done.70), channel_id=1, source_target_pairs={{0,8},{4,12},{8,0},{12,4},{16,24},{20,28},{24,16},{28,20},{1,9},{5... | collective-permute-start | bytes 2359304 | tf_op jit(solution)/shard_map/ppermute | solution.py:804
  235.1 22.0 %collective-permute-start.22 = (f32[64,1024]{1,0:T(8,128)S(1)}, f32[64,1024]{1,0:T(8,128)S(1)}, u32[]{:S(2)}, u32[]{:S(2)}) collective-permute-start(f32[64,1024]{1,0:T(8,128)S(1)} %last.4.refs_0_), channel_id=1, source_target_pairs={{0,16},{4,20},{8,24},{12,28},{16,0},{20,4},{24,8},{28,12},{1,17},{... | collective-permute-start | bytes 786440 | tf_op jit(solution)/shard_map/ppermute | solution.py:804
  260.0 15.4 %collective-permute-start.38 = (f32[128,1024]{1,0:T(8,128)S(1)}, f32[128,1024]{1,0:T(8,128)S(1)}, u32[]{:S(2)}, u32[]{:S(2)}) collective-permute-start(f32[128,1024]{1,0:T(8,128)S(1)} %get-tuple-element.584), channel_id=1, source_target_pairs={{0,8},{4,12},{8,0},{12,4},{16,24},{20,28},{24,16},{28,20},{1,9},{5... | collective-permute-start | bytes 1572872 | tf_op jit(solution)/shard_map/ppermute | solution.py:804
  262.6 9.6 %collective-permute-start.36 = (f32[96,1024]{1,0:T(8,128)S(1)}, f32[96,1024]{1,0:T(8,128)S(1)}, u32[]{:S(2)}, u32[]{:S(2)}) collective-permute-start(f32[96,1024]{1,0:T(8,128)S(1)} %get-tuple-element.582), channel_id=1, source_target_pairs={{0,2},{1,3},{2,0},{3,1},{4,6},{5,7},{6,4},{7,5},{8,10},{9,11},{10,... | collective-permute-start | bytes 1179656 | tf_op jit(solution)/shard_map/ppermute | solution.py:804
  264.0 9.3 %collective-permute-start.37 = (f32[96,1024]{1,0:T(8,128)S(1)}, f32[96,1024]{1,0:T(8,128)S(1)}, u32[]{:S(2)}, u32[]{:S(2)}) collective-permute-start(f32[96,1024]{1,0:T(8,128)S(1)} %get-tuple-element.583), channel_id=1, source_target_pairs={{0,4},{4,0},{8,12},{12,8},{16,20},{20,16},{24,28},{28,24},{1,5},{5... | collective-permute-start | bytes 1179656 | tf_op jit(solution)/shard_map/ppermute | solution.py:804
  264.3 25.3 %collective-permute-start.32 = (f32[128,1024]{1,0:T(8,128)S(1)}, f32[128,1024]{1,0:T(8,128)S(1)}, u32[]{:S(2)}, u32[]{:S(2)}) collective-permute-start(f32[128,1024]{1,0:T(8,128)S(1)} %widen.12.refs_0_), channel_id=1, source_target_pairs={{0,8},{4,12},{8,0},{12,4},{16,24},{20,28},{24,16},{28,20},{1,9},{5... | collective-permute-start | bytes 1572872 | tf_op jit(solution)/shard_map/ppermute | solution.py:804
  276.1 12.8 %collective-permute-start.41 = (f32[64,1024]{1,0:T(8,128)S(1)}, f32[64,1024]{1,0:T(8,128)S(1)}, u32[]{:S(2)}, u32[]{:S(2)}) collective-permute-start(f32[64,1024]{1,0:T(8,128)S(1)} %get-tuple-element.596), channel_id=1, source_target_pairs={{0,4},{4,0},{8,12},{12,8},{16,20},{20,16},{24,28},{28,24},{1,5},{5... | collective-permute-start | bytes 786440 | tf_op jit(solution)/shard_map/ppermute | solution.py:804
  277.1 11.9 %collective-permute-start.39 = (f32[48,1024]{1,0:T(8,128)S(1)}, f32[48,1024]{1,0:T(8,128)S(1)}, u32[]{:S(2)}, u32[]{:S(2)}) collective-permute-start(f32[48,1024]{1,0:T(8,128)S(1)} %get-tuple-element.594), channel_id=1, source_target_pairs={{0,8},{4,12},{8,0},{12,4},{16,24},{20,28},{24,16},{28,20},{1,9},{5... | collective-permute-start | bytes 589832 | tf_op jit(solution)/shard_map/ppermute | solution.py:804
  279.3 9.6 %collective-permute-start.40 = (f32[48,1024]{1,0:T(8,128)S(1)}, f32[48,1024]{1,0:T(8,128)S(1)}, u32[]{:S(2)}, u32[]{:S(2)}) collective-permute-start(f32[48,1024]{1,0:T(8,128)S(1)} %get-tuple-element.595), channel_id=1, source_target_pairs={{0,2},{1,3},{2,0},{3,1},{4,6},{5,7},{6,4},{7,5},{8,10},{9,11},{10,... | collective-permute-start | bytes 589832 | tf_op jit(solution)/shard_map/ppermute | solution.py:804
  290.3 17.7 %collective-permute-start.44 = (f32[128,1024]{1,0:T(8,128)S(1)}, f32[128,1024]{1,0:T(8,128)S(1)}, u32[]{:S(2)}, u32[]{:S(2)}) collective-permute-start(f32[128,1024]{1,0:T(8,128)S(1)} %get-tuple-element.619.refs_0_), channel_id=1, source_target_pairs={{0,2},{1,3},{2,0},{3,1},{4,6},{5,7},{6,4},{7,5},{8,10},{9,11},{10,... | collective-permute-start | bytes 1572872 | tf_op jit(solution)/shard_map/ppermute | solution.py:804
  292.0 15.5 %collective-permute-start.42 = (f32[80,1024]{1,0:T(8,128)S(1)}, f32[80,1024]{1,0:T(8,128)S(1)}, u32[]{:S(2)}, u32[]{:S(2)}) collective-permute-start(f32[80,1024]{1,0:T(8,128)S(1)} %get-tuple-element.613), channel_id=1, source_target_pairs={{0,16},{4,20},{8,24},{12,28},{16,0},{20,4},{24,8},{28,12},{1,17},{... | collective-permute-start | bytes 983048 | tf_op jit(solution)/shard_map/ppermute | solution.py:804
  293.3 14.8 %collective-permute-start.45 = (f32[128,1024]{1,0:T(8,128)S(1)}, f32[128,1024]{1,0:T(8,128)S(1)}, u32[]{:S(2)}, u32[]{:S(2)}) collective-permute-start(f32[128,1024]{1,0:T(8,128)S(1)} %get-tuple-element.620.refs_1_), channel_id=1, source_target_pairs={{0,4},{4,0},{8,12},{12,8},{16,20},{20,16},{24,28},{28,24},{1,5},{5... | collective-permute-start | bytes 1572872 | tf_op jit(solution)/shard_map/ppermute | solution.py:804
  308.8 4.1 %collective-permute-start.47 = (f32[256,1024]{1,0:T(8,128)S(1)}, f32[256,1024]{1,0:T(8,128)S(1)}, u32[]{:S(2)}, u32[]{:S(2)}) collective-permute-start(f32[256,1024]{1,0:T(8,128)S(1)} %get-tuple-element.633.refs_4_), channel_id=1, source_target_pairs={{0,1},{1,0},{2,3},{3,2},{4,5},{5,4},{6,7},{7,6},{8,9},{9,8},{10,11... | collective-permute-start | bytes 3145736 | tf_op jit(solution)/shard_map/ppermute | solution.py:804
  309.3 31.4 %collective-permute-start.54 = (f32[256,1024]{1,0:T(8,128)S(1)}, f32[256,1024]{1,0:T(8,128)S(1)}, u32[]{:S(2)}, u32[]{:S(2)}) collective-permute-start(f32[256,1024]{1,0:T(8,128)S(1)} %get-tuple-element.632.refs_3_), channel_id=1, source_target_pairs={{0,4},{4,0},{8,12},{12,8},{16,20},{20,16},{24,28},{28,24},{1,5},{5... | collective-permute-start | bytes 3145736 | tf_op jit(solution)/shard_map/ppermute | solution.py:804
  309.8 31.0 %collective-permute-start.55 = (f32[256,1024]{1,0:T(8,128)S(1)}, f32[256,1024]{1,0:T(8,128)S(1)}, u32[]{:S(2)}, u32[]{:S(2)}) collective-permute-start(f32[256,1024]{1,0:T(8,128)S(1)} %get-tuple-element.633.refs_4_), channel_id=1, source_target_pairs={{0,2},{1,3},{2,0},{3,1},{4,6},{5,7},{6,4},{7,5},{8,10},{9,11},{10,... | collective-permute-start | bytes 3145736 | tf_op jit(solution)/shard_map/ppermute | solution.py:804
  310.6 16.2 %collective-permute-start.43 = (f32[80,1024]{1,0:T(8,128)S(1)}, f32[80,1024]{1,0:T(8,128)S(1)}, u32[]{:S(2)}, u32[]{:S(2)}) collective-permute-start(f32[80,1024]{1,0:T(8,128)S(1)} %last.5.refs_0_), channel_id=1, source_target_pairs={{0,16},{4,20},{8,24},{12,28},{16,0},{20,4},{24,8},{28,12},{1,17},{... | collective-permute-start | bytes 983048 | tf_op jit(solution)/shard_map/ppermute | solution.py:804
  327.4 12.7 %collective-permute-start.50 = (f32[64,1024]{1,0:T(8,128)S(1)}, f32[64,1024]{1,0:T(8,128)S(1)}, u32[]{:S(2)}, u32[]{:S(2)}) collective-permute-start(f32[64,1024]{1,0:T(8,128)S(1)} %get-tuple-element.644.refs_2_), channel_id=1, source_target_pairs={{0,4},{4,0},{8,12},{12,8},{16,20},{20,16},{24,28},{28,24},{1,5},{5... | collective-permute-start | bytes 786440 | tf_op jit(solution)/shard_map/ppermute | solution.py:804
  329.3 6.5 %collective-permute-start.48 = (f32[48,1024]{1,0:T(8,128)S(1)}, f32[48,1024]{1,0:T(8,128)S(1)}, u32[]{:S(2)}, u32[]{:S(2)}) collective-permute-start(f32[48,1024]{1,0:T(8,128)S(1)} %get-tuple-element.642.refs_0_), channel_id=1, source_target_pairs={{0,8},{4,12},{8,0},{12,4},{16,24},{20,28},{24,16},{28,20},{1,9},{5... | collective-permute-start | bytes 589832 | tf_op jit(solution)/shard_map/ppermute | solution.py:804
  329.3 9.6 %collective-permute-start.49 = (f32[48,1024]{1,0:T(8,128)S(1)}, f32[48,1024]{1,0:T(8,128)S(1)}, u32[]{:S(2)}, u32[]{:S(2)}) collective-permute-start(f32[48,1024]{1,0:T(8,128)S(1)} %get-tuple-element.643.refs_1_), channel_id=1, source_target_pairs={{0,2},{1,3},{2,0},{3,1},{4,6},{5,7},{6,4},{7,5},{8,10},{9,11},{10,... | collective-permute-start | bytes 589832 | tf_op jit(solution)/shard_map/ppermute | solution.py:804
  340.8 4.1 %collective-permute-start.57 = (f32[256,1024]{1,0:T(8,128)S(1)}, f32[256,1024]{1,0:T(8,128)S(1)}, u32[]{:S(2)}, u32[]{:S(2)}) collective-permute-start(f32[256,1024]{1,0:T(8,128)S(1)} %collective-permute-done.55.refs_4_), channel_id=1, source_target_pairs={{0,1},{1,0},{2,3},{3,2},{4,5},{5,4},{6,7},{7,6},{8,9},{9,8},{10,11... | collective-permute-start | bytes 3145736 | tf_op jit(solution)/shard_map/ppermute | solution.py:804
  341.3 13.9 %collective-permute-start.53 = (f32[128,1024]{1,0:T(8,128)S(1)}, f32[128,1024]{1,0:T(8,128)S(1)}, u32[]{:S(2)}, u32[]{:S(2)}) collective-permute-start(f32[128,1024]{1,0:T(8,128)S(1)} %get-tuple-element.665.refs_2_), channel_id=1, source_target_pairs={{0,8},{4,12},{8,0},{12,4},{16,24},{20,28},{24,16},{28,20},{1,9},{5... | collective-permute-start | bytes 1572872 | tf_op jit(solution)/shard_map/ppermute | solution.py:804
  341.3 11.1 %collective-permute-start.51 = (f32[96,1024]{1,0:T(8,128)S(1)}, f32[96,1024]{1,0:T(8,128)S(1)}, u32[]{:S(2)}, u32[]{:S(2)}) collective-permute-start(f32[96,1024]{1,0:T(8,128)S(1)} %get-tuple-element.663.refs_0_), channel_id=1, source_target_pairs={{0,2},{1,3},{2,0},{3,1},{4,6},{5,7},{6,4},{7,5},{8,10},{9,11},{10,... | collective-permute-start | bytes 1179656 | tf_op jit(solution)/shard_map/ppermute | solution.py:804
  342.2 10.8 %collective-permute-start.52 = (f32[96,1024]{1,0:T(8,128)S(1)}, f32[96,1024]{1,0:T(8,128)S(1)}, u32[]{:S(2)}, u32[]{:S(2)}) collective-permute-start(f32[96,1024]{1,0:T(8,128)S(1)} %get-tuple-element.664.refs_1_), channel_id=1, source_target_pairs={{0,4},{4,0},{8,12},{12,8},{16,20},{20,16},{24,28},{28,24},{1,5},{5... | collective-permute-start | bytes 1179656 | tf_op jit(solution)/shard_map/ppermute | solution.py:804
  356.0 4.9 %collective-permute-start.63 = (f32[256,1024]{1,0:T(8,128)S(1)}, f32[256,1024]{1,0:T(8,128)S(1)}, u32[]{:S(2)}, u32[]{:S(2)}) collective-permute-start(f32[256,1024]{1,0:T(8,128)S(1)} %get-tuple-element.682.refs_5_), channel_id=1, source_target_pairs={{0,1},{1,0},{2,3},{3,2},{4,5},{5,4},{6,7},{7,6},{8,9},{9,8},{10,11... | collective-permute-start | bytes 3145736 | tf_op jit(solution)/shard_map/ppermute | solution.py:804
  356.5 25.1 %collective-permute-start.60 = (f32[256,1024]{1,0:T(8,128)S(1)}, f32[256,1024]{1,0:T(8,128)S(1)}, u32[]{:S(2)}, u32[]{:S(2)}) collective-permute-start(f32[256,1024]{1,0:T(8,128)S(1)} %get-tuple-element.682.refs_5_), channel_id=1, source_target_pairs={{0,2},{1,3},{2,0},{3,1},{4,6},{5,7},{6,4},{7,5},{8,10},{9,11},{10,... | collective-permute-start | bytes 3145736 | tf_op jit(solution)/shard_map/ppermute | solution.py:804
  357.4 3.5 collective-permute-start.62
  357.4 20.0 %collective-permute-start.58 = (f32[192,1024]{1,0:T(8,128)S(1)}, f32[192,1024]{1,0:T(8,128)S(1)}, u32[]{:S(2)}, u32[]{:S(2)}) collective-permute-start(f32[192,1024]{1,0:T(8,128)S(1)} %get-tuple-element.680.refs_3_), channel_id=1, source_target_pairs={{0,4},{4,0},{8,12},{12,8},{16,20},{20,16},{24,28},{28,24},{1,5},{5... | collective-permute-start | bytes 2359304 | tf_op jit(solution)/shard_map/ppermute | solution.py:804
  358.3 19.6 %collective-permute-start.59 = (f32[192,1024]{1,0:T(8,128)S(1)}, f32[192,1024]{1,0:T(8,128)S(1)}, u32[]{:S(2)}, u32[]{:S(2)}) collective-permute-start(f32[192,1024]{1,0:T(8,128)S(1)} %get-tuple-element.681.refs_4_), channel_id=1, source_target_pairs={{0,8},{4,12},{8,0},{12,4},{16,24},{20,28},{24,16},{28,20},{1,9},{5... | collective-permute-start | bytes 2359304 | tf_op jit(solution)/shard_map/ppermute | solution.py:804
  381.7 4.9 %collective-permute-start.66 = (f32[256,1024]{1,0:T(8,128)S(1)}, f32[256,1024]{1,0:T(8,128)S(1)}, u32[]{:S(2)}, u32[]{:S(2)}) collective-permute-start(f32[256,1024]{1,0:T(8,128)S(1)} %collective-permute-done.60.refs_5_), channel_id=1, source_target_pairs={{0,1},{1,0},{2,3},{3,2},{4,5},{5,4},{6,7},{7,6},{8,9},{9,8},{10,11... | collective-permute-start | bytes 3145736 | tf_op jit(solution)/shard_map/ppermute | solution.py:804
  381.7 3.8 collective-permute-start.64
  382.2 4.4 %collective-permute-start.65 = (f32[192,1024]{1,0:T(8,128)S(1)}, f32[192,1024]{1,0:T(8,128)S(1)}, u32[]{:S(2)}, u32[]{:S(2)}) collective-permute-start(f32[192,1024]{1,0:T(8,128)S(1)} %collective-permute-done.59.refs_4_), channel_id=1, source_target_pairs={{0,1},{1,0},{2,3},{3,2},{4,5},{5,4},{6,7},{7,6},{8,9},{9,8},{10,11... | collective-permute-start | bytes 2359304 | tf_op jit(solution)/shard_map/ppermute | solution.py:804
  (77 other events, 403.7 us)

commit v5 on v4

--- a/solution.py
+++ b/solution.py
@@ -889,6 +889,10 @@
         while self.k > 3:
             self.widen()
 
+    def wait(self):
+        self.got = self.order.tie(*self.got)
+        self.order.done(self.got)
+
     def widen(self):
         k = self.k
         share, got = self.order.tie(self.share, self.got)
@@ -930,8 +934,8 @@
 
 SEQUENCE = (
     "front", "scan0", "out0", "scan1", "mixed", "p0.f", "out1", "p0.f", "back01", "p0.f", "back00", "p0.e", "p0.b", "p1.f",
-    "back11", "p1.f", "p0.w", "back10", "p1.f", "p0.w", "post0", "p1.e", "p1.b", "p0.w", "post1", "out2", "p0.own", "p0.got",
-    "p1.w", "p2.f", "p2.f", "p2.f", "p1.w", "gn", "p2.e", "p2.b", "p1.w", "p1.own", "p2.w", "p2.w", "p1.got", "p2.w",
+    "back11", "p1.f", "p0.w", "back10", "p1.f", "p0.w", "post0", "p1.e", "p1.b", "p0.w", "post1", "out2", "gn", "p0.d", "p0.own",
+    "p1.w", "p2.f", "p2.f", "p2.f", "p1.w", "p0.got", "p2.e", "p2.b", "p1.w", "p1.own", "p2.w", "p2.w", "p1.got", "p2.w",
     "p2.own", "p2.got",
 )
 PARTS = 2
@@ -1079,6 +1083,8 @@
                 sets[p].back()
             elif what == "w":
                 sets[p].widen()
+            elif what == "d":
+                sets[p].wait()
             else:
                 op_put(p, sets[p].own() if what == "own" else sets[p].arrived())
         elif name[:4] == "back":

time: 401 us -> 391 us (0.975)
  waiting for transfers between devices: 141 us -> 124 us
    ppermute x67, waiting for transfers between devices: 141 us -> 124 us  [swap(): return lax.ppermute(value, axis, [(i, i ^ 1 << place) for i in range(size)])]
    unnamed x150 -> x144, local copies, waits for them, and re-layouts: 18 us -> 20.4 us
  transfers between devices with their start and end apart: 67 -> 67, of which waited for: 35 -> 31; matrix products, arithmetic and copies ran while one was open for 3% -> 4% of each run, Pallas kernels for 34% -> 37%
where the time goes in v5:
time: 391 us; the launch traced here: 384 us
  Pallas kernels  162 us (41%)
  waiting for transfers between devices  124 us (32%)
  starting transfers between devices  53.9 us (14%)
  local copies, waits for them, and re-layouts  21.3 us (5%)
  matrix products  11.9 us (3%)
  other arithmetic  9.09 us (2%)
    ppermute x67, waiting for transfers between devices, swap(): return lax.ppermute(value, axis, [(i, i ^ 1 << place) for i in range(size)])  124 us
    pallas_call x4, Pallas kernels, back(): pl.pallas_call(functools.partial(back_kernel, first), grid=(1,), in_specs...  59.2 us
    ppermute x67, starting transfers between devices, swap(): return lax.ppermute(value, axis, [(i, i ^ 1 << place) for i in range(size)])  53.9 us
    pallas_call x2, Pallas kernels, scan(): pl.pallas_call(functools.partial(scan_kernel, block), grid=(1,), in_specs...  29.6 us
    pallas_call x3, Pallas kernels, outer(): pl.pallas_call(body, out_shape=out_shape, grid_spec=pltpu.PrefetchScalarG...  23 us
    unnamed x144, local copies, waits for them, and re-layouts  20.4 us
    pallas_call x6, Pallas kernels, put(): pl.pallas_call(body, out_shape=[jax.ShapeDtypeStruct(t.shape, F32) for t...  15.6 us
    pallas_call x21, Pallas kernels, step_call(): pl.pallas_call(body, out_shape=outs, grid_spec=pltpu.PrefetchScalarGridSp...  13.6 us
  transfers between devices with their start and end apart: 67, of which 31 were waited for; matrix products, arithmetic and copies ran while one was open for 4% of the time, Pallas kernels for 37%

profile of v5, /device:TPU:0, one launch (start us, length us, event | category | flops | bytes accessed | tf_op | source)
XLA Modules:
  0.0 384.3 jit_solution(11247854509032939310)
XLA Ops:
  1.9 7.7 %front.1 = (bf16[320,1024]{1,0:T(8,128)(2,1)}, f32[320,512]{1,0:T(8,128)}, f32[320,1024]{1,0:T(8,128)}, f32[320,2048]{1,0:T(8,128)}, bf16[320,2048]{1,0:T(8,128)(2,1)}, /*index=5*/f32[320,96]{1,0:T(8,128)}) custom-call(s32[11]{0:T(128)} %stack.39.len_ref.core_ref.flag_ref.ix, bf16[320,1024]{1,0:T(8,128)(2,1)} %bitcast.55, bf16[320,1024]{1,0:T(8,128)(2,1)} %bitcast.59, ...), custom_call_target="tpu_custom_call" | custom-call | flops 1 | bytes 1 | tf_op jit(solution)/shard_map/front/pallas_call | solution.py:75
  10.8 14.7 %scan0.1 = (bf16[320,1024]{1,0:T(8,128)(2,1)}, bf16[320,1024]{1,0:T(8,128)(2,1)}, f32[320,768]{1,0:T(8,128)}, f32[320,768]{1,0:T(8,128)}, f32[2560,128]{1,0:T(8,...) custom-call(s32[11]{0:T(128)} %stack.39.len_ref.core_ref.flag_ref.ix, f32[320,96]{1,0:T(8,128)} %get-tuple-element.465.mp_ref, ...), custom_call_target="tpu_custom_call" | custom-call | flops 1 | bytes 1 | tf_op jit(solution)/shard_map/scan0/pallas_call | solution.py:247
  26.1 4.5 %collective-permute-done.2.refs_5_.refs_1_ = f32[320,512]{1,0:T(8,128)S(1)} collective-permute-done((f32[320,512]{1,0:T(8,128)}, f32[320,512]{1,0:T(8,128)S(1)}, u32[]{:S(2)}, u32[]{:S(2)}) %collective-permute-start.2) | collective-permute-done | bytes 655392 | tf_op jit(solution)/shard_map/ppermute | solution.py:804
  32.6 6.6 %outer.3 = (f32[256,1024]{1,0:T(8,128)}, f32[256,1024]{1,0:T(8,128)}, f32[256,1024]{1,0:T(8,128)}, f32[256,1024]{1,0:T(8,128)}, f32[512,128]{1,0:T(8,128)}) custom-call(s32[11]{0:T(128)} %stack.39.len_ref.core_ref.flag_ref.ix, bf16[320,1024]{1,0:T(8,128)(2,1)} %get-tuple-element.382.refs_0_, f32[320,768]{1,0:T(8,128)} %copy-done.58, ...), custom_call_target="tpu_custom_call" | custom-call | flops 1 | bytes 1 | tf_op jit(solution)/shard_map/outer/pallas_call | solution.py:633
  39.1 2.7 collective-permute-start.4
  41.8 1.5 collective-permute-start.5
  43.4 14.9 %scan1.1 = (bf16[320,1024]{1,0:T(8,128)(2,1)}, bf16[320,1024]{1,0:T(8,128)(2,1)}, f32[320,768]{1,0:T(8,128)}, f32[320,768]{1,0:T(8,128)}, f32[2560,128]{1,0:T(8,...) custom-call(s32[11]{0:T(128)} %stack.39.len_ref.core_ref.flag_ref.ix, f32[320,96]{1,0:T(8,128)} %get-tuple-element.465.mp_ref, ...), custom_call_target="tpu_custom_call" | custom-call | flops 1 | bytes 1 | tf_op jit(solution)/shard_map/scan1/pallas_call | solution.py:247
  58.9 4.9 %fusion.13 = bf16[320,1024]{1,0:T(8,128)(2,1)} fusion(bf16[2048,1024]{1,0:T(8,128)(2,1)} %wout_hbm.3, bf16[320,1024]{1,0:T(8,128)(2,1)} %get-tuple-element.400.refs_0_, bf16[320,1024]{1,0:T(8,128)(2,1)S(1)} %copy-done.66, pred[320]{0:T(512)(128)(4,1)S(1)} %iota_compare_fusion, bf16[1,320,1024]{2,1,0:T(8,128)(2,1)S(1)} %copy-done.53), kind=kOutput, calls=%fused_computation.23 | convolution fusion | flops 1346109440 | bytes 6816064 | tf_op jit(solution)/shard_map/dot_general | solution.py:23
  63.8 1.9 collective-permute-done.4.refs_1_.refs_3_
  65.7 1.5 collective-permute-done.5.refs_5_.refs_7_
  69.6 1.5 collective-permute-start.6
  72.9 6.7 %outer.4 = (f32[256,1024]{1,0:T(8,128)}, f32[256,1024]{1,0:T(8,128)}, f32[256,1024]{1,0:T(8,128)}, f32[256,1024]{1,0:T(8,128)}, f32[512,128]{1,0:T(8,128)}) custom-call(s32[11]{0:T(128)} %stack.39.len_ref.core_ref.flag_ref.ix, bf16[320,1024]{1,0:T(8,128)(2,1)} %get-tuple-element.400.refs_0_, f32[320,768]{1,0:T(8,128)} %copy-done.57, ...), custom_call_target="tpu_custom_call" | custom-call | flops 1 | bytes 1 | tf_op jit(solution)/shard_map/outer/pallas_call | solution.py:633
  79.6 1.6 collective-permute-start.13
  83.7 2.3 collective-permute-done.7.refs_5_.refs_7_
  91.6 1.6 collective-permute-start.10
  94.6 12.6 %back01.1 = (f32[160,1024]{1,0:T(8,128)S(1)}, f32[160,64]{1,0:T(8,128)S(1)}, f32[64,1024]{1,0:T(8,128)S(1)}, f32[160,128]{1,0:T(8,128)S(1)}, f32[2,16,8,128]{3,2,1,0:T(8,128)S(1)}, /*index=5*/f32[2,1024]{1,0:T(2,128)S(1)}) custom-call(f32[320,96]{1,0:T(8,128)S(1)} %copy-done.5, bf16[320,2048]{1,0:T(8,128)(2,1)S(1)} %copy-done, f32[2560,128]{1,0:T(8,128)S(1)} %copy-done.8, ...), custom_call_target="tpu_custom_call" | custom-call | flops 1 | bytes 1 | tf_op jit(solution)/shard_map/back01/pallas_call | solution.py:426
  108.2 2.6 collective-permute-start.11
  110.8 12.6 %back00.1 = (f32[160,1024]{1,0:T(8,128)S(1)}, f32[160,64]{1,0:T(8,128)S(1)}, f32[64,1024]{1,0:T(8,128)S(1)}, f32[160,128]{1,0:T(8,128)S(1)}, f32[2,16,8,128]{3,2,1,0:T(8,128)S(1)}, /*index=5*/f32[2,1024]{1,0:T(2,128)S(1)}) custom-call(f32[320,96]{1,0:T(8,128)S(1)} %copy-done.5, bf16[320,2048]{1,0:T(8,128)(2,1)S(1)} %copy-done, f32[2560,128]{1,0:T(8,128)S(1)} %copy-done.8, ...), custom_call_target="tpu_custom_call" | custom-call | flops 1 | bytes 1 | tf_op jit(solution)/shard_map/back00/pallas_call | solution.py:426
  128.4 12.6 %back11.1 = (f32[160,1024]{1,0:T(8,128)S(1)}, f32[160,64]{1,0:T(8,128)S(1)}, f32[64,1024]{1,0:T(8,128)S(1)}, f32[160,128]{1,0:T(8,128)S(1)}, f32[2,16,8,128]{3,2,1,0:T(8,128)S(1)}, /*index=5*/f32[2,1024]{1,0:T(2,128)S(1)}) custom-call(f32[320,96]{1,0:T(8,128)S(1)} %copy-done.5, bf16[320,2048]{1,0:T(8,128)(2,1)S(1)} %copy-done, f32[2560,128]{1,0:T(8,128)S(1)} %copy-done.6, ...), custom_call_target="tpu_custom_call" | custom-call | flops 1 | bytes 1 | tf_op jit(solution)/shard_map/back11/pallas_call | solution.py:426
  147.1 21.3 %back10.1 = (f32[160,1024]{1,0:T(8,128)S(1)}, f32[160,64]{1,0:T(8,128)S(1)}, f32[64,1024]{1,0:T(8,128)S(1)}, f32[160,128]{1,0:T(8,128)S(1)}, f32[2,16,8,128]{3,2,1,0:T(8,128)S(1)}, /*index=5*/f32[2,1024]{1,0:T(2,128)S(1)}) custom-call(f32[320,96]{1,0:T(8,128)S(1)} %copy-done.5, bf16[320,2048]{1,0:T(8,128)(2,1)S(1)} %copy-done, f32[2560,128]{1,0:T(8,128)S(1)} %copy-done.6, ...), custom_call_target="tpu_custom_call" | custom-call | flops 1 | bytes 1 | tf_op jit(solution)/shard_map/back10/pallas_call | solution.py:426
  170.1 1.5 collective-permute-start.19
  171.6 1.7 collective-permute-start.20
  173.4 2.6 collective-permute-start.21
  175.9 6.6 %post0.1 = (f32[320,1024]{1,0:T(8,128)}, f32[184,1024]{1,0:T(8,128)}) custom-call(f32[2560,128]{1,0:T(8,128)} %get-tuple-element.384.gs_ref, bf16[320,2048]{1,0:T(8,128)(2,1)} %get-tuple-element.362.act_ref, f32[320,2048]{1,0:T(8,128)} %get-tuple-element.385.inner_ref, bf16[96,2048]{1,0:T(8,128)(2,1)} %bitcast.57, f32[4,2048]{1,0:T(4,128)} %cw_ref.5, ...), custom_call_target="tpu_custom_call" | custom-call | flops 1 | bytes 1 | tf_op jit(solution)/shard_map/post0/pallas_call | solution.py:511
  185.7 6.6 %post1.1 = (f32[320,1024]{1,0:T(8,128)}, f32[184,1024]{1,0:T(8,128)}) custom-call(f32[2560,128]{1,0:T(8,128)} %get-tuple-element.455.gs_ref, bf16[320,2048]{1,0:T(8,128)(2,1)} %get-tuple-element.362.act_ref, f32[320,2048]{1,0:T(8,128)} %get-tuple-element.385.inner_ref, bf16[96,2048]{1,0:T(8,128)(2,1)} %bitcast.58, f32[4,2048]{1,0:T(4,128)} %cw_ref.5, ...), custom_call_target="tpu_custom_call" | custom-call | flops 1 | bytes 1 | tf_op jit(solution)/shard_map/post1/pallas_call | solution.py:511
  194.9 1.7 collective-permute-done.24.refs_13_
  196.6 9.7 %outer.5 = (f32[192,1024]{1,0:T(8,128)}, f32[192,1024]{1,0:T(8,128)}, f32[192,1024]{1,0:T(8,128)}, f32[192,1024]{1,0:T(8,128)}, f32[256,1024]{1,0:T(8,128)}, /*index=5*/f32[256,1024]{1,0:T(8,128)}, f32[512,128]{1,0:T(8,128)}) custom-call(s32[11]{0:T(128)} %stack.39.len_ref.core_ref.flag_ref.ix, ...), custom_call_target="tpu_custom_call" | custom-call | flops 1 | bytes 1 | tf_op jit(solution)/shard_map/outer/pallas_call | solution.py:633
  206.3 1.6 convert_element_type.19
  208.4 6.9 %fusion.14 = (f32[320]{0:T(512)S(1)}, f32[320,1024]{1,0:T(8,128)S(1)}) fusion(f32[320]{0:T(512)S(1)} %add_rsqrt_fusion, bf16[1,320,1024]{2,1,0:T(8,128)(2,1)S(1)} %copy-done.54, f32[1024]{0:T(1024)S(1)} %copy-done.67, bf16[1024,4096]{1,0:T(8,128)(2,1)} %refs_8_.1, bf16[320,1024]{1,0:T(8,128)(2,1)S(1)} %copy-done.65, bf16[320,1024]{1,0:T(8,128)(2,1)S(1)} %copy-done.64, ...), kind=kOutput, calls=%fused_computation.24 | convolution fusion | flops 2696478464 | bytes 12982784 | tf_op jit(solution)/shard_map/dot_general | solution.py:23
  215.4 1.4 fusion.17
  216.8 2.8 collective-permute-done.29.refs_3_
  220.9 1.6 collective-permute-start.25
  223.2 3.1 collective-permute-start.28
  226.8 2.6 put.6
  229.4 15.8 %collective-permute-done.28.refs_1_ = f32[64,1024]{1,0:T(8,128)S(1)} collective-permute-done((f32[64,1024]{1,0:T(8,128)S(1)}, f32[64,1024]{1,0:T(8,128)S(1)}, u32[]{:S(2)}, u32[]{:S(2)}) %collective-permute-start.28) | collective-permute-done | bytes 262176 | tf_op jit(solution)/shard_map/ppermute | solution.py:804
  248.0 2.6 collective-permute-start.35
  250.6 1.5 collective-permute-start.33
  252.5 7.7 %collective-permute-done.33.refs_1_.refs_3_ = f32[96,1024]{1,0:T(8,128)S(1)} collective-permute-done((f32[96,1024]{1,0:T(8,128)S(1)}, f32[96,1024]{1,0:T(8,128)S(1)}, u32[]{:S(2)}, u32[]{:S(2)}) %collective-permute-start.33) | collective-permute-done | bytes 393248 | tf_op jit(solution)/shard_map/ppermute | solution.py:804
  261.5 2.0 collective-permute-done.35.refs_9_.refs_11_
  264.5 2.0 collective-permute-start.36
  266.5 1.5 collective-permute-start.37
  268.1 9.0 %collective-permute-done.36.refs_1_.refs_3_ = f32[48,1024]{1,0:T(8,128)S(1)} collective-permute-done((f32[48,1024]{1,0:T(8,128)S(1)}, f32[48,1024]{1,0:T(8,128)S(1)}, u32[]{:S(2)}, u32[]{:S(2)}) %collective-permute-start.36) | collective-permute-done | bytes 196640 | tf_op jit(solution)/shard_map/ppermute | solution.py:804
  278.9 1.5 collective-permute-start.44
  282.5 2.6 put.7
  285.1 12.7 %collective-permute-done.39.refs_3_ = f32[80,1024]{1,0:T(8,128)S(1)} collective-permute-done((f32[80,1024]{1,0:T(8,128)S(1)}, f32[80,1024]{1,0:T(8,128)S(1)}, u32[]{:S(2)}, u32[]{:S(2)}) %collective-permute-start.39) | collective-permute-done | bytes 327712 | tf_op jit(solution)/shard_map/ppermute | solution.py:804
  299.7 1.7 collective-permute-start.54
  301.9 1.4 collective-permute-done.47.refs_6_
  303.3 2.6 put.8
  305.9 12.3 %collective-permute-done.43.refs_1_ = f32[80,1024]{1,0:T(8,128)S(1)} collective-permute-done((f32[80,1024]{1,0:T(8,128)S(1)}, f32[80,1024]{1,0:T(8,128)S(1)}, u32[]{:S(2)}, u32[]{:S(2)}) %collective-permute-start.43) | collective-permute-done | bytes 327712 | tf_op jit(solution)/shard_map/ppermute | solution.py:804
  319.3 1.5 collective-permute-start.49
  320.8 5.0 %collective-permute-done.48.refs_3_ = f32[48,1024]{1,0:T(8,128)S(1)} collective-permute-done((f32[48,1024]{1,0:T(8,128)S(1)}, f32[48,1024]{1,0:T(8,128)S(1)}, u32[]{:S(2)}, u32[]{:S(2)}) %collective-permute-start.48) | collective-permute-done | bytes 196640 | tf_op jit(solution)/shard_map/ppermute | solution.py:804
  325.8 4.6 %collective-permute-done.49.refs_4_ = f32[48,1024]{1,0:T(8,128)S(1)} collective-permute-done((f32[48,1024]{1,0:T(8,128)S(1)}, f32[48,1024]{1,0:T(8,128)S(1)}, u32[]{:S(2)}, u32[]{:S(2)}) %collective-permute-start.49) | collective-permute-done | bytes 196640 | tf_op jit(solution)/shard_map/ppermute | solution.py:804
  332.2 1.7 collective-permute-start.52
  333.8 1.4 collective-permute-done.57.refs_6_
  335.3 2.6 put.9
  337.9 4.9 %collective-permute-done.51.refs_3_ = f32[96,1024]{1,0:T(8,128)S(1)} collective-permute-done((f32[96,1024]{1,0:T(8,128)S(1)}, f32[96,1024]{1,0:T(8,128)S(1)}, u32[]{:S(2)}, u32[]{:S(2)}) %collective-permute-start.51) | collective-permute-done | bytes 393248 | tf_op jit(solution)/shard_map/ppermute | solution.py:804
  343.0 2.6 collective-permute-done.53.refs_5_
  347.4 1.7 collective-permute-start.58
  349.3 1.9 collective-permute-done.62.refs_7_
  351.3 3.0 put.10
  354.3 13.1 %collective-permute-done.58.refs_3_ = f32[192,1024]{1,0:T(8,128)S(1)} collective-permute-done((f32[192,1024]{1,0:T(8,128)S(1)}, f32[192,1024]{1,0:T(8,128)S(1)}, u32[]{:S(2)}, u32[]{:S(2)}) %collective-permute-start.58) | collective-permute-done | bytes 786464 | tf_op jit(solution)/shard_map/ppermute | solution.py:804
  368.7 3.3 collective-permute-done.60.refs_5_
  372.5 3.3 collective-permute-done.64.refs_6_
  376.9 2.3 put.11
  (278 shorter events, 65.7 us)
Async XLA Ops:
  9.6 21.1 %collective-permute-start.1 = (f32[320,1024]{1,0:T(8,128)}, f32[320,1024]{1,0:T(8,128)S(1)}, u32[]{:S(2)}, u32[]{:S(2)}) collective-permute-start(f32[320,1024]{1,0:T(8,128)} %get-tuple-element.402.og_hbm.refs_2_), channel_id=1, source_target_pairs={{0,1},{1,0},{2,3},{3,2},{4,5},{5,4},{6,7},{7,6},{8,9},{9,8},{10,11... | collective-permute-start | bytes 3932168 | tf_op jit(solution)/shard_map/ppermute | solution.py:804
  25.5 5.2 %collective-permute-start = (f32[320,768]{1,0:T(8,128)}, f32[320,768]{1,0:T(8,128)S(1)}, u32[]{:S(2)}, u32[]{:S(2)}) collective-permute-start(f32[320,768]{1,0:T(8,128)} %get-tuple-element.367), channel_id=1, source_target_pairs={{0,1},{1,0},{2,3},{3,2},{4,5},{5,4},{6,7},{7,6},{8,9},{9,8},{10,11... | collective-permute-start | bytes 2949128 | tf_op jit(solution)/shard_map/ppermute | solution.py:804
  25.6 5.1 %collective-permute-start.3 = (f32[320,768]{1,0:T(8,128)}, f32[320,768]{1,0:T(8,128)S(1)}, u32[]{:S(2)}, u32[]{:S(2)}) collective-permute-start(f32[320,768]{1,0:T(8,128)} %get-tuple-element.369), channel_id=1, source_target_pairs={{0,1},{1,0},{2,3},{3,2},{4,5},{5,4},{6,7},{7,6},{8,9},{9,8},{10,11... | collective-permute-start | bytes 2949128 | tf_op jit(solution)/shard_map/ppermute | solution.py:804
  26.0 4.6 %collective-permute-start.2 = (f32[320,512]{1,0:T(8,128)}, f32[320,512]{1,0:T(8,128)S(1)}, u32[]{:S(2)}, u32[]{:S(2)}) collective-permute-start(f32[320,512]{1,0:T(8,128)} %get-tuple-element.368), channel_id=1, source_target_pairs={{0,1},{1,0},{2,3},{3,2},{4,5},{5,4},{6,7},{7,6},{8,9},{9,8},{10,11... | collective-permute-start | bytes 1966088 | tf_op jit(solution)/shard_map/ppermute | solution.py:804
  39.1 26.6 %collective-permute-start.4 = (f32[256,1024]{1,0:T(8,128)}, f32[256,1024]{1,0:T(8,128)S(1)}, u32[]{:S(2)}, u32[]{:S(2)}) collective-permute-start(f32[256,1024]{1,0:T(8,128)} %get-tuple-element.387), channel_id=1, source_target_pairs={{0,4},{4,0},{8,12},{12,8},{16,20},{20,16},{24,28},{28,24},{1,5},{5... | collective-permute-start | bytes 3145736 | tf_op jit(solution)/shard_map/ppermute | solution.py:804
  41.8 25.4 %collective-permute-start.5 = (f32[256,1024]{1,0:T(8,128)}, f32[256,1024]{1,0:T(8,128)S(1)}, u32[]{:S(2)}, u32[]{:S(2)}) collective-permute-start(f32[256,1024]{1,0:T(8,128)} %get-tuple-element.388), channel_id=1, source_target_pairs={{0,2},{1,3},{2,0},{3,1},{4,6},{5,7},{6,4},{7,5},{8,10},{9,11},{10,... | collective-permute-start | bytes 3145736 | tf_op jit(solution)/shard_map/ppermute | solution.py:804
  58.3 13.3 %collective-permute-start.8 = (f32[320,768]{1,0:T(8,128)}, f32[320,768]{1,0:T(8,128)S(1)}, u32[]{:S(2)}, u32[]{:S(2)}) collective-permute-start(f32[320,768]{1,0:T(8,128)} %get-tuple-element.398), channel_id=1, source_target_pairs={{0,1},{1,0},{2,3},{3,2},{4,5},{5,4},{6,7},{7,6},{8,9},{9,8},{10,11... | collective-permute-start | bytes 2949128 | tf_op jit(solution)/shard_map/ppermute | solution.py:804
  58.4 13.3 %collective-permute-start.9 = (f32[320,768]{1,0:T(8,128)}, f32[320,768]{1,0:T(8,128)S(1)}, u32[]{:S(2)}, u32[]{:S(2)}) collective-permute-start(f32[320,768]{1,0:T(8,128)} %get-tuple-element.399), channel_id=1, source_target_pairs={{0,1},{1,0},{2,3},{3,2},{4,5},{5,4},{6,7},{7,6},{8,9},{9,8},{10,11... | collective-permute-start | bytes 2949128 | tf_op jit(solution)/shard_map/ppermute | solution.py:804
  69.6 13.3 %collective-permute-start.6 = (f32[128,1024]{1,0:T(8,128)S(1)}, f32[128,1024]{1,0:T(8,128)S(1)}, u32[]{:S(2)}, u32[]{:S(2)}) collective-permute-start(f32[128,1024]{1,0:T(8,128)S(1)} %get-tuple-element.395), channel_id=1, source_target_pairs={{0,2},{1,3},{2,0},{3,1},{4,6},{5,7},{6,4},{7,5},{8,10},{9,11},{10,... | collective-permute-start | bytes 1572872 | tf_op jit(solution)/shard_map/ppermute | solution.py:804
  71.1 14.9 %collective-permute-start.7 = (f32[128,1024]{1,0:T(8,128)S(1)}, f32[128,1024]{1,0:T(8,128)S(1)}, u32[]{:S(2)}, u32[]{:S(2)}) collective-permute-start(f32[128,1024]{1,0:T(8,128)S(1)} %get-tuple-element.396), channel_id=1, source_target_pairs={{0,4},{4,0},{8,12},{12,8},{16,20},{20,16},{24,28},{28,24},{1,5},{5... | collective-permute-start | bytes 1572872 | tf_op jit(solution)/shard_map/ppermute | solution.py:804
  79.6 46.4 %collective-permute-start.13 = (f32[256,1024]{1,0:T(8,128)}, f32[256,1024]{1,0:T(8,128)S(1)}, u32[]{:S(2)}, u32[]{:S(2)}) collective-permute-start(f32[256,1024]{1,0:T(8,128)} %get-tuple-element.443), channel_id=1, source_target_pairs={{0,4},{4,0},{8,12},{12,8},{16,20},{20,16},{24,28},{28,24},{1,5},{5... | collective-permute-start | bytes 3145736 | tf_op jit(solution)/shard_map/ppermute | solution.py:804
  81.2 44.8 %collective-permute-start.14 = (f32[256,1024]{1,0:T(8,128)}, f32[256,1024]{1,0:T(8,128)S(1)}, u32[]{:S(2)}, u32[]{:S(2)}) collective-permute-start(f32[256,1024]{1,0:T(8,128)} %get-tuple-element.444), channel_id=1, source_target_pairs={{0,2},{1,3},{2,0},{3,1},{4,6},{5,7},{6,4},{7,5},{8,10},{9,11},{10,... | collective-permute-start | bytes 3145736 | tf_op jit(solution)/shard_map/ppermute | solution.py:804
  91.6 15.7 %collective-permute-start.10 = (f32[128,1024]{1,0:T(8,128)S(1)}, f32[128,1024]{1,0:T(8,128)S(1)}, u32[]{:S(2)}, u32[]{:S(2)}) collective-permute-start(f32[128,1024]{1,0:T(8,128)S(1)} %get-tuple-element.416), channel_id=1, source_target_pairs={{0,8},{4,12},{8,0},{12,4},{16,24},{20,28},{24,16},{28,20},{1,9},{5... | collective-permute-start | bytes 1572872 | tf_op jit(solution)/shard_map/ppermute | solution.py:804
  108.2 17.2 %collective-permute-start.11 = (f32[64,1024]{1,0:T(8,128)S(1)}, f32[64,1024]{1,0:T(8,128)S(1)}, u32[]{:S(2)}, u32[]{:S(2)}) collective-permute-start(f32[64,1024]{1,0:T(8,128)S(1)} %get-tuple-element.438), channel_id=1, source_target_pairs={{0,16},{4,20},{8,24},{12,28},{16,0},{20,4},{24,8},{28,12},{1,17},{... | collective-permute-start | bytes 786440 | tf_op jit(solution)/shard_map/ppermute | solution.py:804
  127.1 16.7 %collective-permute-start.15 = (f32[128,1024]{1,0:T(8,128)S(1)}, f32[128,1024]{1,0:T(8,128)S(1)}, u32[]{:S(2)}, u32[]{:S(2)}) collective-permute-start(f32[128,1024]{1,0:T(8,128)S(1)} %get-tuple-element.451), channel_id=1, source_target_pairs={{0,2},{1,3},{2,0},{3,1},{4,6},{5,7},{6,4},{7,5},{8,10},{9,11},{10,... | collective-permute-start | bytes 1572872 | tf_op jit(solution)/shard_map/ppermute | solution.py:804
  127.7 16.1 %collective-permute-start.16 = (f32[128,1024]{1,0:T(8,128)S(1)}, f32[128,1024]{1,0:T(8,128)S(1)}, u32[]{:S(2)}, u32[]{:S(2)}) collective-permute-start(f32[128,1024]{1,0:T(8,128)S(1)} %get-tuple-element.452), channel_id=1, source_target_pairs={{0,4},{4,0},{8,12},{12,8},{16,20},{20,16},{24,28},{28,24},{1,5},{5... | collective-permute-start | bytes 1572872 | tf_op jit(solution)/shard_map/ppermute | solution.py:804
  128.0 17.5 %collective-permute-start.12 = (f32[64,1024]{1,0:T(8,128)S(1)}, f32[64,1024]{1,0:T(8,128)S(1)}, u32[]{:S(2)}, u32[]{:S(2)}) collective-permute-start(f32[64,1024]{1,0:T(8,128)S(1)} %last.3.refs_0_), channel_id=1, source_target_pairs={{0,16},{4,20},{8,24},{12,28},{16,0},{20,4},{24,8},{28,12},{1,17},{... | collective-permute-start | bytes 786440 | tf_op jit(solution)/shard_map/ppermute | solution.py:804
  144.4 24.1 %collective-permute-start.18 = (f32[128,1024]{1,0:T(8,128)S(1)}, f32[128,1024]{1,0:T(8,128)S(1)}, u32[]{:S(2)}, u32[]{:S(2)}) collective-permute-start(f32[128,1024]{1,0:T(8,128)S(1)} %get-tuple-element.472), channel_id=1, source_target_pairs={{0,8},{4,12},{8,0},{12,4},{16,24},{20,28},{24,16},{28,20},{1,9},{5... | collective-permute-start | bytes 1572872 | tf_op jit(solution)/shard_map/ppermute | solution.py:804
  146.1 23.4 %collective-permute-start.17 = (f32[128,1024]{1,0:T(8,128)S(1)}, f32[128,1024]{1,0:T(8,128)S(1)}, u32[]{:S(2)}, u32[]{:S(2)}) collective-permute-start(f32[128,1024]{1,0:T(8,128)S(1)} %widen.9.refs_0_), channel_id=1, source_target_pairs={{0,8},{4,12},{8,0},{12,4},{16,24},{20,28},{24,16},{28,20},{1,9},{5... | collective-permute-start | bytes 1572872 | tf_op jit(solution)/shard_map/ppermute | solution.py:804
  170.1 13.9 %collective-permute-start.19 = (f32[128,1024]{1,0:T(8,128)S(1)}, f32[128,1024]{1,0:T(8,128)S(1)}, u32[]{:S(2)}, u32[]{:S(2)}) collective-permute-start(f32[128,1024]{1,0:T(8,128)S(1)} %get-tuple-element.508.refs_0_), channel_id=1, source_target_pairs={{0,2},{1,3},{2,0},{3,1},{4,6},{5,7},{6,4},{7,5},{8,10},{9,11},{10,... | collective-permute-start | bytes 1572872 | tf_op jit(solution)/shard_map/ppermute | solution.py:804
  171.6 12.4 %collective-permute-start.20 = (f32[128,1024]{1,0:T(8,128)S(1)}, f32[128,1024]{1,0:T(8,128)S(1)}, u32[]{:S(2)}, u32[]{:S(2)}) collective-permute-start(f32[128,1024]{1,0:T(8,128)S(1)} %get-tuple-element.509.refs_1_), channel_id=1, source_target_pairs={{0,4},{4,0},{8,12},{12,8},{16,20},{20,16},{24,28},{28,24},{1,5},{5... | collective-permute-start | bytes 1572872 | tf_op jit(solution)/shard_map/ppermute | solution.py:804
  173.4 10.1 %collective-permute-start.21 = (f32[64,1024]{1,0:T(8,128)S(1)}, f32[64,1024]{1,0:T(8,128)S(1)}, u32[]{:S(2)}, u32[]{:S(2)}) collective-permute-start(f32[64,1024]{1,0:T(8,128)S(1)} %get-tuple-element.504), channel_id=1, source_target_pairs={{0,16},{4,20},{8,24},{12,28},{16,0},{20,4},{24,8},{28,12},{1,17},{... | collective-permute-start | bytes 786440 | tf_op jit(solution)/shard_map/ppermute | solution.py:804
  182.5 14.0 %collective-permute-start.22 = (f32[320,1024]{1,0:T(8,128)}, f32[320,1024]{1,0:T(8,128)}, u32[]{:S(2)}, u32[]{:S(2)}) collective-permute-start(f32[320,1024]{1,0:T(8,128)} %get-tuple-element.545.refs_2_), channel_id=1, source_target_pairs={{0,1},{1,0},{2,3},{3,2},{4,5},{5,4},{6,7},{7,6},{8,9},{9,8},{10,11... | collective-permute-start | bytes 3932168 | tf_op jit(solution)/shard_map/ppermute | solution.py:804
  192.3 4.3 %collective-permute-start.23 = (f32[320,1024]{1,0:T(8,128)}, f32[320,1024]{1,0:T(8,128)}, u32[]{:S(2)}, u32[]{:S(2)}) collective-permute-start(f32[320,1024]{1,0:T(8,128)} %get-tuple-element.546.refs_6_), channel_id=1, source_target_pairs={{0,1},{1,0},{2,3},{3,2},{4,5},{5,4},{6,7},{7,6},{8,9},{9,8},{10,11... | collective-permute-start | bytes 3932168 | tf_op jit(solution)/shard_map/ppermute | solution.py:804
  193.6 2.9 collective-permute-start.24
  194.0 25.6 %collective-permute-start.29 = (f32[256,1024]{1,0:T(8,128)S(1)}, f32[256,1024]{1,0:T(8,128)S(1)}, u32[]{:S(2)}, u32[]{:S(2)}) collective-permute-start(f32[256,1024]{1,0:T(8,128)S(1)} %get-tuple-element.562.refs_3_), channel_id=1, source_target_pairs={{0,4},{4,0},{8,12},{12,8},{16,20},{20,16},{24,28},{28,24},{1,5},{5... | collective-permute-start | bytes 3145736 | tf_op jit(solution)/shard_map/ppermute | solution.py:804
  194.3 25.6 %collective-permute-start.30 = (f32[256,1024]{1,0:T(8,128)}, f32[256,1024]{1,0:T(8,128)S(1)}, u32[]{:S(2)}, u32[]{:S(2)}) collective-permute-start(f32[256,1024]{1,0:T(8,128)} %copy-done.25), channel_id=1, source_target_pairs={{0,2},{1,3},{2,0},{3,1},{4,6},{5,7},{6,4},{7,5},{8,10},{9,11},{10,... | collective-permute-start | bytes 3145736 | tf_op jit(solution)/shard_map/ppermute | solution.py:804
  219.9 3.3 collective-permute-start.31
  219.9 6.3 %collective-permute-start.32 = (f32[256,1024]{1,0:T(8,128)S(1)}, f32[256,1024]{1,0:T(8,128)S(1)}, u32[]{:S(2)}, u32[]{:S(2)}) collective-permute-start(f32[256,1024]{1,0:T(8,128)S(1)} %copy-done.26), channel_id=1, source_target_pairs={{0,1},{1,0},{2,3},{3,2},{4,5},{5,4},{6,7},{7,6},{8,9},{9,8},{10,11... | collective-permute-start | bytes 3145736 | tf_op jit(solution)/shard_map/ppermute | solution.py:804
  220.4 26.8 %collective-permute-start.27 = (f32[256,1024]{1,0:T(8,128)S(1)}, f32[256,1024]{1,0:T(8,128)S(1)}, u32[]{:S(2)}, u32[]{:S(2)}) collective-permute-start(f32[256,1024]{1,0:T(8,128)S(1)} %copy-done.68), channel_id=1, source_target_pairs={{0,2},{1,3},{2,0},{3,1},{4,6},{5,7},{6,4},{7,5},{8,10},{9,11},{10,... | collective-permute-start | bytes 3145736 | tf_op jit(solution)/shard_map/ppermute | solution.py:804
  220.9 24.9 %collective-permute-start.25 = (f32[192,1024]{1,0:T(8,128)S(1)}, f32[192,1024]{1,0:T(8,128)S(1)}, u32[]{:S(2)}, u32[]{:S(2)}) collective-permute-start(f32[192,1024]{1,0:T(8,128)S(1)} %copy-done.70), channel_id=1, source_target_pairs={{0,4},{4,0},{8,12},{12,8},{16,20},{20,16},{24,28},{28,24},{1,5},{5... | collective-permute-start | bytes 2359304 | tf_op jit(solution)/shard_map/ppermute | solution.py:804
  222.6 24.6 %collective-permute-start.26 = (f32[192,1024]{1,0:T(8,128)S(1)}, f32[192,1024]{1,0:T(8,128)S(1)}, u32[]{:S(2)}, u32[]{:S(2)}) collective-permute-start(f32[192,1024]{1,0:T(8,128)S(1)} %copy-done.69), channel_id=1, source_target_pairs={{0,8},{4,12},{8,0},{12,4},{16,24},{20,28},{24,16},{28,20},{1,9},{5... | collective-permute-start | bytes 2359304 | tf_op jit(solution)/shard_map/ppermute | solution.py:804
  223.2 22.1 %collective-permute-start.28 = (f32[64,1024]{1,0:T(8,128)S(1)}, f32[64,1024]{1,0:T(8,128)S(1)}, u32[]{:S(2)}, u32[]{:S(2)}) collective-permute-start(f32[64,1024]{1,0:T(8,128)S(1)} %last.4.refs_0_), channel_id=1, source_target_pairs={{0,16},{4,20},{8,24},{12,28},{16,0},{20,4},{24,8},{28,12},{1,17},{... | collective-permute-start | bytes 786440 | tf_op jit(solution)/shard_map/ppermute | solution.py:804
  248.0 15.4 %collective-permute-start.35 = (f32[128,1024]{1,0:T(8,128)S(1)}, f32[128,1024]{1,0:T(8,128)S(1)}, u32[]{:S(2)}, u32[]{:S(2)}) collective-permute-start(f32[128,1024]{1,0:T(8,128)S(1)} %get-tuple-element.580), channel_id=1, source_target_pairs={{0,8},{4,12},{8,0},{12,4},{16,24},{20,28},{24,16},{28,20},{1,9},{5... | collective-permute-start | bytes 1572872 | tf_op jit(solution)/shard_map/ppermute | solution.py:804
  250.6 9.7 %collective-permute-start.33 = (f32[96,1024]{1,0:T(8,128)S(1)}, f32[96,1024]{1,0:T(8,128)S(1)}, u32[]{:S(2)}, u32[]{:S(2)}) collective-permute-start(f32[96,1024]{1,0:T(8,128)S(1)} %get-tuple-element.578), channel_id=1, source_target_pairs={{0,2},{1,3},{2,0},{3,1},{4,6},{5,7},{6,4},{7,5},{8,10},{9,11},{10,... | collective-permute-start | bytes 1179656 | tf_op jit(solution)/shard_map/ppermute | solution.py:804
  252.1 9.4 %collective-permute-start.34 = (f32[96,1024]{1,0:T(8,128)S(1)}, f32[96,1024]{1,0:T(8,128)S(1)}, u32[]{:S(2)}, u32[]{:S(2)}) collective-permute-start(f32[96,1024]{1,0:T(8,128)S(1)} %get-tuple-element.579), channel_id=1, source_target_pairs={{0,4},{4,0},{8,12},{12,8},{16,20},{20,16},{24,28},{28,24},{1,5},{5... | collective-permute-start | bytes 1179656 | tf_op jit(solution)/shard_map/ppermute | solution.py:804
  252.4 25.2 %collective-permute-start.40 = (f32[128,1024]{1,0:T(8,128)S(1)}, f32[128,1024]{1,0:T(8,128)S(1)}, u32[]{:S(2)}, u32[]{:S(2)}) collective-permute-start(f32[128,1024]{1,0:T(8,128)S(1)} %widen.12.refs_0_), channel_id=1, source_target_pairs={{0,8},{4,12},{8,0},{12,4},{16,24},{20,28},{24,16},{28,20},{1,9},{5... | collective-permute-start | bytes 1572872 | tf_op jit(solution)/shard_map/ppermute | solution.py:804
  264.1 12.9 %collective-permute-start.38 = (f32[64,1024]{1,0:T(8,128)S(1)}, f32[64,1024]{1,0:T(8,128)S(1)}, u32[]{:S(2)}, u32[]{:S(2)}) collective-permute-start(f32[64,1024]{1,0:T(8,128)S(1)} %get-tuple-element.592), channel_id=1, source_target_pairs={{0,4},{4,0},{8,12},{12,8},{16,20},{20,16},{24,28},{28,24},{1,5},{5... | collective-permute-start | bytes 786440 | tf_op jit(solution)/shard_map/ppermute | solution.py:804
  264.5 12.5 %collective-permute-start.36 = (f32[48,1024]{1,0:T(8,128)S(1)}, f32[48,1024]{1,0:T(8,128)S(1)}, u32[]{:S(2)}, u32[]{:S(2)}) collective-permute-start(f32[48,1024]{1,0:T(8,128)S(1)} %get-tuple-element.590), channel_id=1, source_target_pairs={{0,8},{4,12},{8,0},{12,4},{16,24},{20,28},{24,16},{28,20},{1,9},{5... | collective-permute-start | bytes 589832 | tf_op jit(solution)/shard_map/ppermute | solution.py:804
  266.5 10.5 %collective-permute-start.37 = (f32[48,1024]{1,0:T(8,128)S(1)}, f32[48,1024]{1,0:T(8,128)S(1)}, u32[]{:S(2)}, u32[]{:S(2)}) collective-permute-start(f32[48,1024]{1,0:T(8,128)S(1)} %get-tuple-element.591), channel_id=1, source_target_pairs={{0,2},{1,3},{2,0},{3,1},{4,6},{5,7},{6,4},{7,5},{8,10},{9,11},{10,... | collective-permute-start | bytes 589832 | tf_op jit(solution)/shard_map/ppermute | solution.py:804
  278.3 3.5 collective-permute-start.41
  278.4 4.1 %collective-permute-start.42 = (f32[256,1024]{1,0:T(8,128)S(1)}, f32[256,1024]{1,0:T(8,128)S(1)}, u32[]{:S(2)}, u32[]{:S(2)}) collective-permute-start(f32[256,1024]{1,0:T(8,128)S(1)} %collective-permute-done.30.refs_4_), channel_id=1, source_target_pairs={{0,1},{1,0},{2,3},{3,2},{4,5},{5,4},{6,7},{7,6},{8,9},{9,8},{10,11... | collective-permute-start | bytes 3145736 | tf_op jit(solution)/shard_map/ppermute | solution.py:804
  278.9 19.5 %collective-permute-start.44 = (f32[128,1024]{1,0:T(8,128)S(1)}, f32[128,1024]{1,0:T(8,128)S(1)}, u32[]{:S(2)}, u32[]{:S(2)}) collective-permute-start(f32[128,1024]{1,0:T(8,128)S(1)} %get-tuple-element.623.refs_0_), channel_id=1, source_target_pairs={{0,2},{1,3},{2,0},{3,1},{4,6},{5,7},{6,4},{7,5},{8,10},{9,11},{10,... | collective-permute-start | bytes 1572872 | tf_op jit(solution)/shard_map/ppermute | solution.py:804
  280.4 18.0 %collective-permute-start.45 = (f32[128,1024]{1,0:T(8,128)S(1)}, f32[128,1024]{1,0:T(8,128)S(1)}, u32[]{:S(2)}, u32[]{:S(2)}) collective-permute-start(f32[128,1024]{1,0:T(8,128)S(1)} %get-tuple-element.624.refs_1_), channel_id=1, source_target_pairs={{0,4},{4,0},{8,12},{12,8},{16,20},{20,16},{24,28},{28,24},{1,5},{5... | collective-permute-start | bytes 1572872 | tf_op jit(solution)/shard_map/ppermute | solution.py:804
  280.7 17.1 %collective-permute-start.39 = (f32[80,1024]{1,0:T(8,128)S(1)}, f32[80,1024]{1,0:T(8,128)S(1)}, u32[]{:S(2)}, u32[]{:S(2)}) collective-permute-start(f32[80,1024]{1,0:T(8,128)S(1)} %get-tuple-element.602), channel_id=1, source_target_pairs={{0,16},{4,20},{8,24},{12,28},{16,0},{20,4},{24,8},{28,12},{1,17},{... | collective-permute-start | bytes 983048 | tf_op jit(solution)/shard_map/ppermute | solution.py:804
  299.2 4.1 %collective-permute-start.47 = (f32[256,1024]{1,0:T(8,128)S(1)}, f32[256,1024]{1,0:T(8,128)S(1)}, u32[]{:S(2)}, u32[]{:S(2)}) collective-permute-start(f32[256,1024]{1,0:T(8,128)S(1)} %get-tuple-element.637.refs_4_), channel_id=1, source_target_pairs={{0,1},{1,0},{2,3},{3,2},{4,5},{5,4},{6,7},{7,6},{8,9},{9,8},{10,11... | collective-permute-start | bytes 3145736 | tf_op jit(solution)/shard_map/ppermute | solution.py:804
  299.7 31.4 %collective-permute-start.54 = (f32[256,1024]{1,0:T(8,128)S(1)}, f32[256,1024]{1,0:T(8,128)S(1)}, u32[]{:S(2)}, u32[]{:S(2)}) collective-permute-start(f32[256,1024]{1,0:T(8,128)S(1)} %get-tuple-element.636.refs_3_), channel_id=1, source_target_pairs={{0,4},{4,0},{8,12},{12,8},{16,20},{20,16},{24,28},{28,24},{1,5},{5... | collective-permute-start | bytes 3145736 | tf_op jit(solution)/shard_map/ppermute | solution.py:804
  301.3 29.7 %collective-permute-start.55 = (f32[256,1024]{1,0:T(8,128)S(1)}, f32[256,1024]{1,0:T(8,128)S(1)}, u32[]{:S(2)}, u32[]{:S(2)}) collective-permute-start(f32[256,1024]{1,0:T(8,128)S(1)} %get-tuple-element.637.refs_4_), channel_id=1, source_target_pairs={{0,2},{1,3},{2,0},{3,1},{4,6},{5,7},{6,4},{7,5},{8,10},{9,11},{10,... | collective-permute-start | bytes 3145736 | tf_op jit(solution)/shard_map/ppermute | solution.py:804
  301.8 16.3 %collective-permute-start.43 = (f32[80,1024]{1,0:T(8,128)S(1)}, f32[80,1024]{1,0:T(8,128)S(1)}, u32[]{:S(2)}, u32[]{:S(2)}) collective-permute-start(f32[80,1024]{1,0:T(8,128)S(1)} %last.5.refs_0_), channel_id=1, source_target_pairs={{0,16},{4,20},{8,24},{12,28},{16,0},{20,4},{24,8},{28,12},{1,17},{... | collective-permute-start | bytes 983048 | tf_op jit(solution)/shard_map/ppermute | solution.py:804
  318.8 11.7 %collective-permute-start.50 = (f32[64,1024]{1,0:T(8,128)S(1)}, f32[64,1024]{1,0:T(8,128)S(1)}, u32[]{:S(2)}, u32[]{:S(2)}) collective-permute-start(f32[64,1024]{1,0:T(8,128)S(1)} %get-tuple-element.648.refs_2_), channel_id=1, source_target_pairs={{0,4},{4,0},{8,12},{12,8},{16,20},{20,16},{24,28},{28,24},{1,5},{5... | collective-permute-start | bytes 786440 | tf_op jit(solution)/shard_map/ppermute | solution.py:804
  319.3 6.5 %collective-permute-start.48 = (f32[48,1024]{1,0:T(8,128)S(1)}, f32[48,1024]{1,0:T(8,128)S(1)}, u32[]{:S(2)}, u32[]{:S(2)}) collective-permute-start(f32[48,1024]{1,0:T(8,128)S(1)} %get-tuple-element.646.refs_0_), channel_id=1, source_target_pairs={{0,8},{4,12},{8,0},{12,4},{16,24},{20,28},{24,16},{28,20},{1,9},{5... | collective-permute-start | bytes 589832 | tf_op jit(solution)/shard_map/ppermute | solution.py:804
  319.3 11.1 %collective-permute-start.49 = (f32[48,1024]{1,0:T(8,128)S(1)}, f32[48,1024]{1,0:T(8,128)S(1)}, u32[]{:S(2)}, u32[]{:S(2)}) collective-permute-start(f32[48,1024]{1,0:T(8,128)S(1)} %get-tuple-element.647.refs_1_), channel_id=1, source_target_pairs={{0,2},{1,3},{2,0},{3,1},{4,6},{5,7},{6,4},{7,5},{8,10},{9,11},{10,... | collective-permute-start | bytes 589832 | tf_op jit(solution)/shard_map/ppermute | solution.py:804
  331.2 4.1 %collective-permute-start.57 = (f32[256,1024]{1,0:T(8,128)S(1)}, f32[256,1024]{1,0:T(8,128)S(1)}, u32[]{:S(2)}, u32[]{:S(2)}) collective-permute-start(f32[256,1024]{1,0:T(8,128)S(1)} %collective-permute-done.55.refs_4_), channel_id=1, source_target_pairs={{0,1},{1,0},{2,3},{3,2},{4,5},{5,4},{6,7},{7,6},{8,9},{9,8},{10,11... | collective-permute-start | bytes 3145736 | tf_op jit(solution)/shard_map/ppermute | solution.py:804
  331.6 13.9 %collective-permute-start.53 = (f32[128,1024]{1,0:T(8,128)S(1)}, f32[128,1024]{1,0:T(8,128)S(1)}, u32[]{:S(2)}, u32[]{:S(2)}) collective-permute-start(f32[128,1024]{1,0:T(8,128)S(1)} %get-tuple-element.669.refs_2_), channel_id=1, source_target_pairs={{0,8},{4,12},{8,0},{12,4},{16,24},{20,28},{24,16},{28,20},{1,9},{5... | collective-permute-start | bytes 1572872 | tf_op jit(solution)/shard_map/ppermute | solution.py:804
  331.7 11.1 %collective-permute-start.51 = (f32[96,1024]{1,0:T(8,128)S(1)}, f32[96,1024]{1,0:T(8,128)S(1)}, u32[]{:S(2)}, u32[]{:S(2)}) collective-permute-start(f32[96,1024]{1,0:T(8,128)S(1)} %get-tuple-element.667.refs_0_), channel_id=1, source_target_pairs={{0,2},{1,3},{2,0},{3,1},{4,6},{5,7},{6,4},{7,5},{8,10},{9,11},{10,... | collective-permute-start | bytes 1179656 | tf_op jit(solution)/shard_map/ppermute | solution.py:804
  332.2 10.8 %collective-permute-start.52 = (f32[96,1024]{1,0:T(8,128)S(1)}, f32[96,1024]{1,0:T(8,128)S(1)}, u32[]{:S(2)}, u32[]{:S(2)}) collective-permute-start(f32[96,1024]{1,0:T(8,128)S(1)} %get-tuple-element.668.refs_1_), channel_id=1, source_target_pairs={{0,4},{4,0},{8,12},{12,8},{16,20},{20,16},{24,28},{28,24},{1,5},{5... | collective-permute-start | bytes 1179656 | tf_op jit(solution)/shard_map/ppermute | solution.py:804
  346.4 4.9 %collective-permute-start.63 = (f32[256,1024]{1,0:T(8,128)S(1)}, f32[256,1024]{1,0:T(8,128)S(1)}, u32[]{:S(2)}, u32[]{:S(2)}) collective-permute-start(f32[256,1024]{1,0:T(8,128)S(1)} %get-tuple-element.686.refs_5_), channel_id=1, source_target_pairs={{0,1},{1,0},{2,3},{3,2},{4,5},{5,4},{6,7},{7,6},{8,9},{9,8},{10,11... | collective-permute-start | bytes 3145736 | tf_op jit(solution)/shard_map/ppermute | solution.py:804
  346.9 25.1 %collective-permute-start.60 = (f32[256,1024]{1,0:T(8,128)S(1)}, f32[256,1024]{1,0:T(8,128)S(1)}, u32[]{:S(2)}, u32[]{:S(2)}) collective-permute-start(f32[256,1024]{1,0:T(8,128)S(1)} %get-tuple-element.686.refs_5_), channel_id=1, source_target_pairs={{0,2},{1,3},{2,0},{3,1},{4,6},{5,7},{6,4},{7,5},{8,10},{9,11},{10,... | collective-permute-start | bytes 3145736 | tf_op jit(solution)/shard_map/ppermute | solution.py:804
  347.4 3.9 %collective-permute-start.62 = (f32[192,1024]{1,0:T(8,128)S(1)}, f32[192,1024]{1,0:T(8,128)S(1)}, u32[]{:S(2)}, u32[]{:S(2)}) collective-permute-start(f32[192,1024]{1,0:T(8,128)S(1)} %get-tuple-element.685.refs_4_), channel_id=1, source_target_pairs={{0,1},{1,0},{2,3},{3,2},{4,5},{5,4},{6,7},{7,6},{8,9},{9,8},{10,11... | collective-permute-start | bytes 2359304 | tf_op jit(solution)/shard_map/ppermute | solution.py:804
  347.4 20.0 %collective-permute-start.58 = (f32[192,1024]{1,0:T(8,128)S(1)}, f32[192,1024]{1,0:T(8,128)S(1)}, u32[]{:S(2)}, u32[]{:S(2)}) collective-permute-start(f32[192,1024]{1,0:T(8,128)S(1)} %get-tuple-element.684.refs_3_), channel_id=1, source_target_pairs={{0,4},{4,0},{8,12},{12,8},{16,20},{20,16},{24,28},{28,24},{1,5},{5... | collective-permute-start | bytes 2359304 | tf_op jit(solution)/shard_map/ppermute | solution.py:804
  349.1 19.7 %collective-permute-start.59 = (f32[192,1024]{1,0:T(8,128)S(1)}, f32[192,1024]{1,0:T(8,128)S(1)}, u32[]{:S(2)}, u32[]{:S(2)}) collective-permute-start(f32[192,1024]{1,0:T(8,128)S(1)} %get-tuple-element.685.refs_4_), channel_id=1, source_target_pairs={{0,8},{4,12},{8,0},{12,4},{16,24},{20,28},{24,16},{28,20},{1,9},{5... | collective-permute-start | bytes 2359304 | tf_op jit(solution)/shard_map/ppermute | solution.py:804
  372.0 4.9 %collective-permute-start.66 = (f32[256,1024]{1,0:T(8,128)S(1)}, f32[256,1024]{1,0:T(8,128)S(1)}, u32[]{:S(2)}, u32[]{:S(2)}) collective-permute-start(f32[256,1024]{1,0:T(8,128)S(1)} %collective-permute-done.60.refs_5_), channel_id=1, source_target_pairs={{0,1},{1,0},{2,3},{3,2},{4,5},{5,4},{6,7},{7,6},{8,9},{9,8},{10,11... | collective-permute-start | bytes 3145736 | tf_op jit(solution)/shard_map/ppermute | solution.py:804
  372.0 3.8 collective-permute-start.64
  372.5 4.4 %collective-permute-start.65 = (f32[192,1024]{1,0:T(8,128)S(1)}, f32[192,1024]{1,0:T(8,128)S(1)}, u32[]{:S(2)}, u32[]{:S(2)}) collective-permute-start(f32[192,1024]{1,0:T(8,128)S(1)} %collective-permute-done.59.refs_4_), channel_id=1, source_target_pairs={{0,1},{1,0},{2,3},{3,2},{4,5},{5,4},{6,7},{7,6},{8,9},{9,8},{10,11... | collective-permute-start | bytes 2359304 | tf_op jit(solution)/shard_map/ppermute | solution.py:804
  (74 other events, 294.8 us)
